TPU v7x, 32 devices: a whole 2x2x4 slice. The times are simulated.
32 devices in a mesh: groups: 2 (over x), box: 16 (over z, y, core).
Axes of the slice: x: 2, y: 2, z: 4, core: 2. Of those that a mesh axis runs over, the one named last changes fastest.
Arguments:
- scene_image: bfloat16 [32768, 512], P(('groups', 'box')), parts along dimension 0, may hold values from -6 to 6
- echoes: bfloat16 [32768, 1024], P(('groups', 'box')), parts along dimension 0, may hold values from -6 to 6
- pixel_slot: int32 [32, 1024], P(('groups', 'box')), parts along dimension 0, may hold values from 0 to 1023, each once within a row
- pulse_slot: int32 [32, 1024], P(('groups', 'box')), parts along dimension 0, may hold values from 0 to 1023, each once within a row
- level_perm: int32 [4, 16, 1024], P(None, 'box'), may hold values from 0 to 1023, each once within a row
- target_leaf: bfloat16 [512, 128], replicated, may hold values from -0.25 to 0.25
- source_leaf: bfloat16 [128, 1024], replicated, may hold values from -0.5 to 0.5
- panels: bfloat16 [4, 16, 4, 128, 128], P(None, 'box'), may hold values from -0.375 to 0.375
Outputs:
- new_image: bfloat16 [32768, 512], P(('groups', 'box')), parts along dimension 0
There are 2 independent parts, one for each index of `groups`. A program takes and returns all parts, laid end to end along the dimension named above; an argument that names none is the same for every part. Nothing has to cross between parts.
Inputs may be any that keep to these rules, and one draw needn't show every extreme that they name: `pixel_slot`: each box's row is a permutation of 0 .. 1023. `pulse_slot`: each box's row is a permutation of 0 .. 1023. `level_perm`: each level's row for each box is a permutation of 0 .. 1023.
All inputs are finite; a program needn't handle non-finite values.
Results may differ from a plain program's by a relative error of at most 0.012.
Values may be sent and summed in bfloat16 or wider, within the bound.
No kernel may reach another device: no remote copies, remote signals or barrier semaphores. Data moves between devices by JAX's collectives and lax.ppermute only.
A program may use at most 64 MiB of HBM per device.

v0:
```python
import jax
import jax.numpy as jnp
from jax import lax
from jax.sharding import PartitionSpec as P

step_size = 0.1


def swapped(value, axis, apart):
    return lax.ppermute(value, axis, [(i, i ^ 1 << apart) for i in range(lax.axis_size(axis))])


def pick_block(blocks, which):
    return lax.dynamic_index_in_dim(blocks, which, 0, keepdims=False)


def selector(slots):
    columns = lax.broadcasted_iota(jnp.int32, (slots.shape[0], slots.shape[0]), 1)
    return (slots[:, None] == columns).astype(jnp.bfloat16)


def take_rows(slots, values):
    return jnp.dot(selector(slots), values, preferred_element_type=jnp.float32).astype(jnp.bfloat16)


def place_rows(slots, values):
    placed = lax.dot_general(
        selector(slots), values, (((0,), (0,)), ((), ())), preferred_element_type=jnp.float32
    )
    return placed.astype(jnp.bfloat16)


def on_device(
    scene_image, echoes, pixel_slot, pulse_slot, level_perm, target_leaf, source_leaf, panels
):
    levels = lax.axis_size("box").bit_length() - 1
    position = lax.axis_index("box")
    rows_dev = scene_image.shape[0]
    half_rows = rows_dev // 2
    coef_width = target_leaf.shape[1]
    pixel_rows = pixel_slot[0]
    pulse_rows = pulse_slot[0]
    leafed = jnp.dot(scene_image, target_leaf, preferred_element_type=jnp.float32).astype(
        jnp.bfloat16
    )
    coefficients = take_rows(pixel_rows, leafed)
    for level_index in range(levels):
        bit_value = position // 2**level_index % 2
        blocks = panels[level_index, 0]
        permuted = take_rows(level_perm[level_index, 0], coefficients)
        own_half = lax.dynamic_slice_in_dim(permuted, bit_value * half_rows, half_rows, 0)
        outgoing = lax.dynamic_slice_in_dim(permuted, (1 - bit_value) * half_rows, half_rows, 0)
        partner_half = swapped(outgoing, "box", level_index)
        own_weight = jnp.concatenate(
            [pick_block(blocks, bit_value), pick_block(blocks, 2 + bit_value)], axis=1
        )
        partner_weight = jnp.concatenate(
            [pick_block(blocks, 1 - bit_value), pick_block(blocks, 3 - bit_value)], axis=1
        )
        mixture = jnp.dot(own_half, own_weight, preferred_element_type=jnp.float32)
        mixture = mixture + jnp.dot(
            partner_half, partner_weight, preferred_element_type=jnp.float32
        )
        coefficients = jnp.concatenate(
            [mixture[:, :coef_width], mixture[:, coef_width:]], axis=0
        ).astype(jnp.bfloat16)
    pulse_coefs = take_rows(pulse_rows, coefficients)
    predicted = jnp.dot(pulse_coefs, source_leaf, preferred_element_type=jnp.float32)
    residual = (predicted - echoes.astype(jnp.float32)).astype(jnp.bfloat16)
    backward = lax.dot_general(
        residual, source_leaf, (((1,), (1,)), ((), ())), preferred_element_type=jnp.float32
    )
    coefficients = place_rows(pulse_rows, backward.astype(jnp.bfloat16))
    for level_index in reversed(range(levels)):
        bit_value = position // 2**level_index % 2
        blocks = panels[level_index, 0]
        stacked = jnp.concatenate([coefficients[:half_rows], coefficients[half_rows:]], axis=1)
        own_weight = jnp.concatenate(
            [pick_block(blocks, bit_value).T, pick_block(blocks, 2 + bit_value).T], axis=0
        )
        other_weight = jnp.concatenate(
            [pick_block(blocks, 1 - bit_value).T, pick_block(blocks, 3 - bit_value).T], axis=0
        )
        own_grad = jnp.dot(stacked, own_weight, preferred_element_type=jnp.float32).astype(
            jnp.bfloat16
        )
        partner_rows, partner_map = swapped((stacked, other_weight), "box", level_index)
        returned = jnp.dot(partner_rows, partner_map, preferred_element_type=jnp.float32).astype(
            jnp.bfloat16
        )
        permuted_grad = jnp.where(
            bit_value == 0,
            jnp.concatenate([own_grad, returned], axis=0),
            jnp.concatenate([returned, own_grad], axis=0),
        )
        coefficients = place_rows(level_perm[level_index, 0], permuted_grad)
    pixel_coefs = place_rows(pixel_rows, coefficients)
    gradient = lax.dot_general(
        pixel_coefs, target_leaf, (((1,), (1,)), ((), ())), preferred_element_type=jnp.float32
    )
    return (scene_image.astype(jnp.float32) - step_size * gradient).astype(jnp.bfloat16)


def solution(mesh):
    return jax.shard_map(
        on_device,
        mesh=mesh,
        in_specs=(
            P(("groups", "box"), None),
            P(("groups", "box"), None),
            P(("groups", "box"), None),
            P(("groups", "box"), None),
            P(None, "box", None),
            P(),
            P(),
            P(None, "box", None, None, None),
        ),
        out_specs=P(("groups", "box"), None),
        check_vma=False,
    )
```

profile of v0, /device:TPU:0, one launch (start us, length us, event | category | flops | bytes accessed | tf_op | source)
XLA Modules:
  0.0 78.2 jit_solution(2841095059713310778)
XLA Ops:
  0.0 0.8 fusion.162
  0.8 2.8 %fusion.29 = bf16[1024,128]{1,0:T(8,128)(2,1)S(1)} fusion(s32[1024]{0:T(1024)} %bitcast.117, bf16[1024,512]{1,0:T(8,128)(2,1)} %param.8, bf16[512,128]{1,0:T(8,128)(2,1)} %param.13), kind=kOutput, calls=%fused_computation.41 | convolution fusion | flops 403963904 | bytes 1445888 | tf_op jit(solution)/shard_map/dot_general | solution.py:23
  3.6 0.8 %fusion.31 = bf16[1024,128]{1,0:T(8,128)(2,1)S(1)} fusion(bf16[1024,128]{1,0:T(8,128)(2,1)S(1)} %fusion.29, s32[1024]{0:T(1024)S(1)} %bitcast.107), kind=kOutput, calls=%fused_computation.43 | convolution fusion | flops 269615104 | bytes 528384 | tf_op jit(solution)/shard_map/dot_general | solution.py:23
  4.5 0.5 collective-permute-start
  5.4 0.6 collective-permute-done
  6.2 0.8 %fusion.33 = bf16[1024,128]{1,0:T(8,128)(2,1)S(1)} fusion(s32[1024]{0:T(1024)S(1)} %bitcast.109, bf16[512,128]{1,0:T(8,128)(2,1)S(1)} %get-tuple-element.24, bf16[512,128]{1,0:T(8,128)(2,1)S(1)} %get-tuple-element.23), kind=kOutput, calls=%fused_computation.45 | convolution fusion | flops 270139392 | bytes 528384 | tf_op jit(solution)/shard_map/dot_general | solution.py:23
  7.1 2.9 %collective-permute-start.1 = (bf16[512,128]{1,0:T(8,128)(2,1)S(1)}, bf16[512,128]{1,0:T(8,128)(2,1)S(1)}, u32[]{:S(2)}, u32[]{:S(2)}) collective-permute-start(bf16[512,128]{1,0:T(8,128)(2,1)S(1)} %constant_dynamic-slice_fusion.2), channel_id=1, source_target_pairs={{0,2},{1,3},{2,0},{3,1},{4,6},{5,7},{6,4},{7,5},{8,10},{9,11},{10,... | collective-permute-start | bytes 393224 | tf_op jit(solution)/shard_map/ppermute | solution.py:10
  10.3 3.5 %collective-permute-done.1 = bf16[512,128]{1,0:T(8,128)(2,1)S(1)} collective-permute-done((bf16[512,128]{1,0:T(8,128)(2,1)S(1)}, bf16[512,128]{1,0:T(8,128)(2,1)S(1)}, u32[]{:S(2)}, u32[]{:S(2)}) %collective-permute-start.1) | collective-permute-done | bytes 131104 | tf_op jit(solution)/shard_map/ppermute | solution.py:10
  14.1 0.8 %fusion.35 = bf16[1024,128]{1,0:T(8,128)(2,1)S(1)} fusion(s32[1024]{0:T(1024)S(1)} %bitcast.111, bf16[512,128]{1,0:T(8,128)(2,1)S(1)} %get-tuple-element.22, bf16[512,128]{1,0:T(8,128)(2,1)S(1)} %get-tuple-element.21), kind=kOutput, calls=%fused_computation.47 | convolution fusion | flops 270139392 | bytes 528384 | tf_op jit(solution)/shard_map/dot_general | solution.py:23
  14.9 1.9 %collective-permute-start.2 = (bf16[512,128]{1,0:T(8,128)(2,1)S(1)}, bf16[512,128]{1,0:T(8,128)(2,1)S(1)}, u32[]{:S(2)}, u32[]{:S(2)}) collective-permute-start(bf16[512,128]{1,0:T(8,128)(2,1)S(1)} %constant_dynamic-slice_fusion.1), channel_id=1, source_target_pairs={{0,4},{1,5},{2,6},{3,7},{4,0},{5,1},{6,2},{7,3},{8,12},{9,13},{10,... | collective-permute-start | bytes 393224 | tf_op jit(solution)/shard_map/ppermute | solution.py:10
  17.1 2.9 %collective-permute-done.2 = bf16[512,128]{1,0:T(8,128)(2,1)S(1)} collective-permute-done((bf16[512,128]{1,0:T(8,128)(2,1)S(1)}, bf16[512,128]{1,0:T(8,128)(2,1)S(1)}, u32[]{:S(2)}, u32[]{:S(2)}) %collective-permute-start.2) | collective-permute-done | bytes 131104 | tf_op jit(solution)/shard_map/ppermute | solution.py:10
  20.3 0.8 %fusion.37 = bf16[1024,128]{1,0:T(8,128)(2,1)S(1)} fusion(s32[1024]{0:T(1024)S(1)} %bitcast.113, bf16[512,128]{1,0:T(8,128)(2,1)S(1)} %get-tuple-element.20, bf16[512,128]{1,0:T(8,128)(2,1)S(1)} %get-tuple-element.19), kind=kOutput, calls=%fused_computation.49 | convolution fusion | flops 270139392 | bytes 528384 | tf_op jit(solution)/shard_map/dot_general | solution.py:23
  21.1 2.8 %collective-permute-start.3 = (bf16[512,128]{1,0:T(8,128)(2,1)S(1)}, bf16[512,128]{1,0:T(8,128)(2,1)S(1)}, u32[]{:S(2)}, u32[]{:S(2)}) collective-permute-start(bf16[512,128]{1,0:T(8,128)(2,1)S(1)} %constant_dynamic-slice_fusion), channel_id=1, source_target_pairs={{0,8},{1,9},{2,10},{3,11},{4,12},{5,13},{6,14},{7,15},{8,0},{9,1},... | collective-permute-start | bytes 393224 | tf_op jit(solution)/shard_map/ppermute | solution.py:10
  24.2 4.8 %collective-permute-done.3 = bf16[512,128]{1,0:T(8,128)(2,1)S(1)} collective-permute-done((bf16[512,128]{1,0:T(8,128)(2,1)S(1)}, bf16[512,128]{1,0:T(8,128)(2,1)S(1)}, u32[]{:S(2)}, u32[]{:S(2)}) %collective-permute-start.3) | collective-permute-done | bytes 131104 | tf_op jit(solution)/shard_map/ppermute | solution.py:10
  29.3 0.8 %fusion.39 = bf16[1024,128]{1,0:T(8,128)(2,1)S(1)} fusion(s32[1024]{0:T(1024)S(1)} %bitcast.115, bf16[512,128]{1,0:T(8,128)(2,1)S(1)} %get-tuple-element.18, bf16[512,128]{1,0:T(8,128)(2,1)S(1)} %get-tuple-element.17), kind=kOutput, calls=%fused_computation.51 | convolution fusion | flops 270139392 | bytes 528384 | tf_op jit(solution)/shard_map/dot_general | solution.py:23
  30.1 2.9 %fusion.41 = bf16[1024,128]{1,0:T(8,128)(2,1)S(1)} fusion(bf16[128,1024]{1,0:T(8,128)(2,1)S(1)} %copy-done, bf16[1024,1024]{1,0:T(8,128)(2,1)} %param.9, bf16[1024,128]{1,0:T(8,128)(2,1)S(1)} %fusion.39), kind=kOutput, calls=%fused_computation.54 | convolution fusion | flops 540147712 | bytes 2883584 | tf_op jit(solution)/shard_map/dot_general | solution.py:70
  33.1 1.0 %fusion.40 = bf16[1024,128]{0,1:T(8,128)(2,1)S(1)} fusion(bf16[1024,128]{1,0:T(8,128)(2,1)S(1)} %fusion.41, s32[1024]{0:T(1024)S(1)} %bitcast.116), kind=kOutput, calls=%fused_computation.52 | convolution fusion | flops 269615104 | bytes 528384 | tf_op jit(solution)/shard_map/dot_general | solution.py:27
  34.2 0.9 %collective-permute-start.4 = (bf16[512,256]{0,1:T(8,128)(2,1)S(1)}, bf16[512,256]{0,1:T(8,128)(2,1)S(1)}, u32[]{:S(2)}, u32[]{:S(2)}) collective-permute-start(bf16[512,256]{0,1:T(8,128)(2,1)S(1)} %pad_maximum_fusion), channel_id=1, source_target_pairs={{0,8},{1,9},{2,10},{3,11},{4,12},{5,13},{6,14},{7,15},{8,0},{9,1},... | collective-permute-start | bytes 786440 | tf_op jit(solution)/shard_map/ppermute | solution.py:10
  35.1 2.1 %collective-permute-start.5 = (bf16[256,128]{0,1:T(8,128)(2,1)S(1)}, bf16[256,128]{0,1:T(8,128)(2,1)S(1)}, u32[]{:S(2)}, u32[]{:S(2)}) collective-permute-start(bf16[256,128]{0,1:T(8,128)(2,1)S(1)} %pad_maximum_fusion.4), channel_id=1, source_target_pairs={{0,8},{1,9},{2,10},{3,11},{4,12},{5,13},{6,14},{7,15},{8,0},{9,1},... | collective-permute-start | bytes 196616 | tf_op jit(solution)/shard_map/ppermute | solution.py:10
  37.5 11.7 %collective-permute-done.5 = bf16[256,128]{0,1:T(8,128)(2,1)S(1)} collective-permute-done((bf16[256,128]{0,1:T(8,128)(2,1)S(1)}, bf16[256,128]{0,1:T(8,128)(2,1)S(1)}, u32[]{:S(2)}, u32[]{:S(2)}) %collective-permute-start.5) | collective-permute-done | bytes 65568 | tf_op jit(solution)/shard_map/ppermute | solution.py:10
  49.5 1.0 %fusion.38 = bf16[1024,128]{0,1:T(8,128)(2,1)S(1)} fusion(s32[1024]{0:T(1024)S(1)} %bitcast.114, bf16[512,128]{1,0:T(8,128)(2,1)S(1)} %convolution_convert_fusion.7, bf16[512,128]{1,0:T(8,128)(2,1)S(1)} %convolution_convert_fusion.8, pred[]{:T(512)S(6)} %eq.123), kind=kOutput, calls=%fused_computation.50 | convolution fusion | flops 270794752 | bytes 528385 | tf_op jit(solution)/shard_map/dot_general | solution.py:27
  50.7 2.1 %collective-permute-start.7 = (bf16[256,128]{0,1:T(8,128)(2,1)S(1)}, bf16[256,128]{0,1:T(8,128)(2,1)S(1)}, u32[]{:S(2)}, u32[]{:S(2)}) collective-permute-start(bf16[256,128]{0,1:T(8,128)(2,1)S(1)} %pad_maximum_fusion.5), channel_id=1, source_target_pairs={{0,4},{1,5},{2,6},{3,7},{4,0},{5,1},{6,2},{7,3},{8,12},{9,13},{10,... | collective-permute-start | bytes 196616 | tf_op jit(solution)/shard_map/ppermute | solution.py:10
  53.0 7.3 %collective-permute-done.7 = bf16[256,128]{0,1:T(8,128)(2,1)S(1)} collective-permute-done((bf16[256,128]{0,1:T(8,128)(2,1)S(1)}, bf16[256,128]{0,1:T(8,128)(2,1)S(1)}, u32[]{:S(2)}, u32[]{:S(2)}) %collective-permute-start.7) | collective-permute-done | bytes 65568 | tf_op jit(solution)/shard_map/ppermute | solution.py:10
  60.6 1.0 %fusion.36 = bf16[1024,128]{0,1:T(8,128)(2,1)S(1)} fusion(s32[1024]{0:T(1024)S(1)} %bitcast.112, bf16[512,128]{1,0:T(8,128)(2,1)S(1)} %convolution_convert_fusion.5, bf16[512,128]{1,0:T(8,128)(2,1)S(1)} %convolution_convert_fusion.6, pred[]{:T(512)S(6)} %eq.119), kind=kOutput, calls=%fused_computation.48 | convolution fusion | flops 270794752 | bytes 528385 | tf_op jit(solution)/shard_map/dot_general | solution.py:27
  61.9 2.1 %collective-permute-start.9 = (bf16[256,128]{0,1:T(8,128)(2,1)S(1)}, bf16[256,128]{0,1:T(8,128)(2,1)S(1)}, u32[]{:S(2)}, u32[]{:S(2)}) collective-permute-start(bf16[256,128]{0,1:T(8,128)(2,1)S(1)} %pad_maximum_fusion.6), channel_id=1, source_target_pairs={{0,2},{1,3},{2,0},{3,1},{4,6},{5,7},{6,4},{7,5},{8,10},{9,11},{10,... | collective-permute-start | bytes 196616 | tf_op jit(solution)/shard_map/ppermute | solution.py:10
  64.3 6.4 %collective-permute-done.9 = bf16[256,128]{0,1:T(8,128)(2,1)S(1)} collective-permute-done((bf16[256,128]{0,1:T(8,128)(2,1)S(1)}, bf16[256,128]{0,1:T(8,128)(2,1)S(1)}, u32[]{:S(2)}, u32[]{:S(2)}) %collective-permute-start.9) | collective-permute-done | bytes 65568 | tf_op jit(solution)/shard_map/ppermute | solution.py:10
  71.0 1.0 %fusion.34 = bf16[1024,128]{0,1:T(8,128)(2,1)S(1)} fusion(s32[1024]{0:T(1024)S(1)} %bitcast.110, bf16[512,128]{1,0:T(8,128)(2,1)S(1)} %convolution_convert_fusion.3, bf16[512,128]{1,0:T(8,128)(2,1)S(1)} %convolution_convert_fusion.4, pred[]{:T(512)S(6)} %eq.115), kind=kOutput, calls=%fused_computation.46 | convolution fusion | flops 270794752 | bytes 528385 | tf_op jit(solution)/shard_map/dot_general | solution.py:27
  72.2 0.6 collective-permute-start.11
  73.0 0.8 collective-permute-done.11
  73.8 0.3 convolution_convert_fusion.1
  74.1 2.7 %fusion.30 = bf16[1024,128]{1,0:T(8,128)(2,1)S(1)} fusion(s32[1024]{0:T(1024)S(1)} %bitcast.118, s32[1024]{0:T(1024)S(1)} %bitcast.108, bf16[512,128]{1,0:T(8,128)(2,1)S(1)} %convolution_convert_fusion.1, bf16[512,128]{1,0:T(8,128)(2,1)S(1)} %convolution_convert_fusion.2, pred[]{:T(512)S(6)} %eq.111), kind=kOutput, calls=%fused_computation.42 | convolution fusion | flops 540409856 | bytes 532481 | tf_op jit(solution)/shard_map/dot_general | solution.py:27
  76.8 1.4 %subtract_convert_fusion.1 = bf16[1024,512]{1,0:T(8,128)(2,1)} fusion(bf16[1024,512]{1,0:T(8,128)(2,1)S(1)} %copy-done.1, bf16[1024,128]{1,0:T(8,128)(2,1)S(1)} %fusion.30, bf16[512,128]{1,0:T(8,128)(2,1)S(1)} %copy-done.3), kind=kOutput, calls=%fused_computation.19 | convolution fusion | flops 136314880 | bytes 2490368 | tf_op jit(solution)/shard_map/dot_general | solution.py:98
  (59 shorter events, 4.5 us)
Async XLA Ops:
  0.0 30.1 %copy-start = (bf16[128,1024]{1,0:T(8,128)(2,1)S(1)}, bf16[128,1024]{1,0:T(8,128)(2,1)}, u32[]{:S(2)}) copy-start(bf16[128,1024]{1,0:T(8,128)(2,1)} %param.14) | copy-start | bytes 786436
  0.8 4.2 %copy-start.2 = (bf16[4,1,4,128,128]{4,3,2,1,0:T(8,128)(2,1)S(1)}, bf16[4,1,4,128,128]{4,3,2,1,0:T(8,128)(2,1)}, u32[]{:S(2)}) copy-start(bf16[4,1,4,128,128]{4,3,2,1,0:T(8,128)(2,1)} %param.15) | copy-start | bytes 1572868
  4.5 1.5 %collective-permute-start = (bf16[512,128]{1,0:T(8,128)(2,1)S(1)}, bf16[512,128]{1,0:T(8,128)(2,1)S(1)}, u32[]{:S(2)}, u32[]{:S(2)}) collective-permute-start(bf16[512,128]{1,0:T(8,128)(2,1)S(1)} %constant_dynamic-slice_fusion.3), channel_id=1, source_target_pairs={{0,1},{1,0},{2,3},{3,2},{4,5},{5,4},{6,7},{7,6},{8,9},{9,8},{10,11... | collective-permute-start | bytes 393224 | tf_op jit(solution)/shard_map/ppermute | solution.py:10
  7.1 6.7 %collective-permute-start.1 = (bf16[512,128]{1,0:T(8,128)(2,1)S(1)}, bf16[512,128]{1,0:T(8,128)(2,1)S(1)}, u32[]{:S(2)}, u32[]{:S(2)}) collective-permute-start(bf16[512,128]{1,0:T(8,128)(2,1)S(1)} %constant_dynamic-slice_fusion.2), channel_id=1, source_target_pairs={{0,2},{1,3},{2,0},{3,1},{4,6},{5,7},{6,4},{7,5},{8,10},{9,11},{10,... | collective-permute-start | bytes 393224 | tf_op jit(solution)/shard_map/ppermute | solution.py:10
  14.9 5.1 %collective-permute-start.2 = (bf16[512,128]{1,0:T(8,128)(2,1)S(1)}, bf16[512,128]{1,0:T(8,128)(2,1)S(1)}, u32[]{:S(2)}, u32[]{:S(2)}) collective-permute-start(bf16[512,128]{1,0:T(8,128)(2,1)S(1)} %constant_dynamic-slice_fusion.1), channel_id=1, source_target_pairs={{0,4},{1,5},{2,6},{3,7},{4,0},{5,1},{6,2},{7,3},{8,12},{9,13},{10,... | collective-permute-start | bytes 393224 | tf_op jit(solution)/shard_map/ppermute | solution.py:10
  20.3 9.0 %copy-start.4 = (s32[1,1024]{1,0:T(1,128)S(1)}, s32[1,1024]{1,0:T(1,128)}, u32[]{:S(2)}) copy-start(s32[1,1024]{1,0:T(1,128)} %param.11) | copy-start | bytes 12292
  21.1 7.9 %collective-permute-start.3 = (bf16[512,128]{1,0:T(8,128)(2,1)S(1)}, bf16[512,128]{1,0:T(8,128)(2,1)S(1)}, u32[]{:S(2)}, u32[]{:S(2)}) collective-permute-start(bf16[512,128]{1,0:T(8,128)(2,1)S(1)} %constant_dynamic-slice_fusion), channel_id=1, source_target_pairs={{0,8},{1,9},{2,10},{3,11},{4,12},{5,13},{6,14},{7,15},{8,0},{9,1},... | collective-permute-start | bytes 393224 | tf_op jit(solution)/shard_map/ppermute | solution.py:10
  34.2 15.1 %collective-permute-start.4 = (bf16[512,256]{0,1:T(8,128)(2,1)S(1)}, bf16[512,256]{0,1:T(8,128)(2,1)S(1)}, u32[]{:S(2)}, u32[]{:S(2)}) collective-permute-start(bf16[512,256]{0,1:T(8,128)(2,1)S(1)} %pad_maximum_fusion), channel_id=1, source_target_pairs={{0,8},{1,9},{2,10},{3,11},{4,12},{5,13},{6,14},{7,15},{8,0},{9,1},... | collective-permute-start | bytes 786440 | tf_op jit(solution)/shard_map/ppermute | solution.py:10
  35.1 14.1 %collective-permute-start.5 = (bf16[256,128]{0,1:T(8,128)(2,1)S(1)}, bf16[256,128]{0,1:T(8,128)(2,1)S(1)}, u32[]{:S(2)}, u32[]{:S(2)}) collective-permute-start(bf16[256,128]{0,1:T(8,128)(2,1)S(1)} %pad_maximum_fusion.4), channel_id=1, source_target_pairs={{0,8},{1,9},{2,10},{3,11},{4,12},{5,13},{6,14},{7,15},{8,0},{9,1},... | collective-permute-start | bytes 196616 | tf_op jit(solution)/shard_map/ppermute | solution.py:10
  50.6 9.7 %collective-permute-start.6 = (bf16[512,256]{0,1:T(8,128)(2,1)S(1)}, bf16[512,256]{0,1:T(8,128)(2,1)S(1)}, u32[]{:S(2)}, u32[]{:S(2)}) collective-permute-start(bf16[512,256]{0,1:T(8,128)(2,1)S(1)} %pad_maximum_fusion.1), channel_id=1, source_target_pairs={{0,4},{1,5},{2,6},{3,7},{4,0},{5,1},{6,2},{7,3},{8,12},{9,13},{10,... | collective-permute-start | bytes 786440 | tf_op jit(solution)/shard_map/ppermute | solution.py:10
  50.7 9.6 %collective-permute-start.7 = (bf16[256,128]{0,1:T(8,128)(2,1)S(1)}, bf16[256,128]{0,1:T(8,128)(2,1)S(1)}, u32[]{:S(2)}, u32[]{:S(2)}) collective-permute-start(bf16[256,128]{0,1:T(8,128)(2,1)S(1)} %pad_maximum_fusion.5), channel_id=1, source_target_pairs={{0,4},{1,5},{2,6},{3,7},{4,0},{5,1},{6,2},{7,3},{8,12},{9,13},{10,... | collective-permute-start | bytes 196616 | tf_op jit(solution)/shard_map/ppermute | solution.py:10
  61.7 9.0 %collective-permute-start.8 = (bf16[512,256]{0,1:T(8,128)(2,1)S(1)}, bf16[512,256]{0,1:T(8,128)(2,1)S(1)}, u32[]{:S(2)}, u32[]{:S(2)}) collective-permute-start(bf16[512,256]{0,1:T(8,128)(2,1)S(1)} %pad_maximum_fusion.2), channel_id=1, source_target_pairs={{0,2},{1,3},{2,0},{3,1},{4,6},{5,7},{6,4},{7,5},{8,10},{9,11},{10,... | collective-permute-start | bytes 786440 | tf_op jit(solution)/shard_map/ppermute | solution.py:10
  61.9 8.8 %collective-permute-start.9 = (bf16[256,128]{0,1:T(8,128)(2,1)S(1)}, bf16[256,128]{0,1:T(8,128)(2,1)S(1)}, u32[]{:S(2)}, u32[]{:S(2)}) collective-permute-start(bf16[256,128]{0,1:T(8,128)(2,1)S(1)} %pad_maximum_fusion.6), channel_id=1, source_target_pairs={{0,2},{1,3},{2,0},{3,1},{4,6},{5,7},{6,4},{7,5},{8,10},{9,11},{10,... | collective-permute-start | bytes 196616 | tf_op jit(solution)/shard_map/ppermute | solution.py:10
  71.0 3.1 %copy-start.5 = (s32[1,1024]{1,0:T(1,128)S(1)}, s32[1,1024]{1,0:T(1,128)}, u32[]{:S(2)}) copy-start(s32[1,1024]{1,0:T(1,128)} %param.10) | copy-start | bytes 12292
  72.1 1.7 %collective-permute-start.10 = (bf16[512,256]{0,1:T(8,128)(2,1)S(1)}, bf16[512,256]{0,1:T(8,128)(2,1)S(1)}, u32[]{:S(2)}, u32[]{:S(2)}) collective-permute-start(bf16[512,256]{0,1:T(8,128)(2,1)S(1)} %pad_maximum_fusion.3), channel_id=1, source_target_pairs={{0,1},{1,0},{2,3},{3,2},{4,5},{5,4},{6,7},{7,6},{8,9},{9,8},{10,11... | collective-permute-start | bytes 786440 | tf_op jit(solution)/shard_map/ppermute | solution.py:10
  72.2 1.6 %collective-permute-start.11 = (bf16[256,128]{0,1:T(8,128)(2,1)S(1)}, bf16[256,128]{0,1:T(8,128)(2,1)S(1)}, u32[]{:S(2)}, u32[]{:S(2)}) collective-permute-start(bf16[256,128]{0,1:T(8,128)(2,1)S(1)} %pad_maximum_fusion.7), channel_id=1, source_target_pairs={{0,1},{1,0},{2,3},{3,2},{4,5},{5,4},{6,7},{7,6},{8,9},{9,8},{10,11... | collective-permute-start | bytes 196616 | tf_op jit(solution)/shard_map/ppermute | solution.py:10
  74.0 2.7 %copy-start.1 = (bf16[1024,512]{1,0:T(8,128)(2,1)S(1)}, bf16[1024,512]{1,0:T(8,128)(2,1)}, u32[]{:S(2)}) copy-start(bf16[1024,512]{1,0:T(8,128)(2,1)} %param.8) | copy-start | bytes 3145732
  74.0 2.7 %copy-start.3 = (bf16[512,128]{1,0:T(8,128)(2,1)S(1)}, bf16[512,128]{1,0:T(8,128)(2,1)}, u32[]{:S(2)}) copy-start(bf16[512,128]{1,0:T(8,128)(2,1)} %param.13) | copy-start | bytes 393220
where the time goes:
time: 78.4 us; the launch traced here: 78.2 us
  waiting for transfers between devices  38.1 us (49%)
  matrix products  21.8 us (28%)
  starting transfers between devices  16.3 us (21%)
  local copies, waits for them, and re-layouts  1.23 us (2%)
    ppermute x12, waiting for transfers between devices, swapped(): lax.ppermute(value, axis, [(i, i ^ 1 << apart) for i in range(lax.axis_si...  38.1 us
    ppermute x12, starting transfers between devices, swapped(): lax.ppermute(value, axis, [(i, i ^ 1 << apart) for i in range(lax.axis_si...  16.3 us
    dot_general x6, matrix products, take_rows(): jnp.dot(selector(slots), values, preferred_element_type=jnp.float32)  6.94 us
    dot_general x5, matrix products, place_rows(): lax.dot_general(selector(slots), values, (((0,), (0,)), ((), ())), prefer...  6.81 us
    dot_general x1, matrix products, on_device(): lax.dot_general(residual, source_leaf, (((1,), (1,)), ((), ())), preferre...  2.95 us
  transfers between devices with their start and end apart: 12, of which 8 were waited for; matrix products, arithmetic and copies ran while one was open for 3% of the time, Pallas kernels for 0%

commit v1 on v0

v1 whole, which is shorter than its diff:
```python
import functools

import jax
import jax.numpy as jnp
from jax import lax
from jax.experimental import pallas as pl
from jax.experimental.pallas import tpu as pltpu
from jax.sharding import PartitionSpec as P

step_size = 0.1
wide = jnp.float32
thin = jnp.bfloat16
lanes = 128
depth = 256


def swapped(value, axis, apart):
    return lax.ppermute(value, axis, [(i, i ^ 1 << apart) for i in range(lax.axis_size(axis))])


def mul(left, right):
    return jnp.dot(left, right, preferred_element_type=wide)


def mul_t(left, right):
    return lax.dot_general(left, right, (((1,), (1,)), ((), ())), preferred_element_type=wide)


def bit_of(level):
    return lax.axis_index("box") // 2**level % 2


def half_row(row_ref, bit):
    half = row_ref.shape[1] // 2
    return row_ref[:, pl.ds(pl.multiple_of(bit * half, half), half)]


def column(row):
    parts = []
    for at in range(0, row.shape[1], lanes):
        parts.append(jnp.broadcast_to(row[:, at : at + lanes], (lanes, lanes)).T)
    return jnp.concatenate(parts, axis=0)


def one_hot(hits):
    return jnp.where(hits, 1.0, 0.0).astype(thin)


def take(row, values):
    slots = column(row)
    lane = lax.broadcasted_iota(jnp.int32, slots.shape, 1)
    total = None
    for at in range(0, values.shape[0], depth):
        chosen = jnp.concatenate(
            [one_hot(slots == lane + (at + more)) for more in range(0, depth, lanes)], axis=1
        )
        part = mul(chosen, values[at : at + depth])
        total = part if total is None else total + part
    return total


def place(row, values, rows):
    total = None
    target = lax.broadcasted_iota(jnp.int32, (rows, depth), 0)
    for at in range(0, values.shape[0], depth):
        chosen = one_hot(target == row[:, at : at + depth])
        part = mul(chosen, values[at : at + depth])
        total = part if total is None else total + part
    return total


def compose(outer, inner):
    digits = jnp.concatenate([outer // 256, outer % 256], axis=0).astype(wide)
    digits = jnp.pad(digits, ((0, 14), (0, 0))).astype(thin)
    total = None
    target = lax.broadcasted_iota(jnp.int32, (depth, inner.shape[1]), 0)
    for at in range(0, outer.shape[1], depth):
        chosen = one_hot(target + at == inner)
        part = mul(digits[:, at : at + depth], chosen)
        total = part if total is None else total + part
    return (total[0:1] * 256 + total[1:2]).astype(jnp.int32)


def stack(values):
    half = values.shape[0] // 2
    return jnp.concatenate([values[:half], values[half:]], axis=1)


def unstack(values):
    width = values.shape[1] // 2
    return jnp.concatenate([values[:, :width], values[:, width:]], axis=0)


def pair_weight(panel_ref, which):
    return jnp.concatenate([panel_ref[0, which], panel_ref[0, 2 + which]], axis=1)


def first_kernel(scene_ref, leaf_ref, pixel_ref, perm_ref, leafed_ref, slots_ref, out_ref):
    slots = compose(pixel_ref[...], half_row(perm_ref, 1 - bit_of(0)))
    slots_ref[...] = slots
    leafed = mul(scene_ref[...], leaf_ref[...]).astype(thin)
    leafed_ref[...] = leafed
    out_ref[...] = take(slots, leafed).astype(thin)


def first_own_kernel(leafed_ref, pixel_ref, perm_ref, panel_ref, slots_ref, part_ref):
    bit = bit_of(0)
    slots = compose(pixel_ref[...], half_row(perm_ref, bit))
    slots_ref[...] = slots
    own = take(slots, leafed_ref[...]).astype(thin)
    part_ref[...] = mul(own, pair_weight(panel_ref, bit))


def own_kernel(level, coef_ref, perm_ref, panel_ref, part_ref):
    bit = bit_of(level)
    own = take(half_row(perm_ref, bit), coef_ref[...]).astype(thin)
    part_ref[...] = mul(own, pair_weight(panel_ref, bit))


def mix(level, arrived_ref, part_ref, panel_ref):
    mixture = part_ref[...] + mul(arrived_ref[...], pair_weight(panel_ref, 1 - bit_of(level)))
    return unstack(mixture.astype(thin))


def forward_kernel(level, arrived_ref, part_ref, panel_ref, perm_ref, coef_ref, out_ref):
    coefficients = mix(level, arrived_ref, part_ref, panel_ref)
    coef_ref[...] = coefficients
    out_ref[...] = take(half_row(perm_ref, 1 - bit_of(level + 1)), coefficients).astype(thin)


def echo_kernel(echo_ref, leaf_ref, slots_ref, back_ref, gram_ref):
    leaf = leaf_ref[...]
    gram = mul_t(leaf, leaf)
    high = gram.astype(thin)
    low = (gram - high.astype(wide)).astype(thin)
    gram_ref[...] = jnp.concatenate([high, low], axis=0)
    back = mul_t(echo_ref[...], leaf).astype(thin)
    back_ref[...] = place(slots_ref[...], back, back.shape[0])


def centre_kernel(level, arrived_ref, part_ref, panel_ref, echo_ref, gram_ref, coef_ref, out_ref):
    coefficients = mix(level, arrived_ref, part_ref, panel_ref)
    twice = jnp.concatenate([coefficients, coefficients], axis=1)
    back = (mul(twice, gram_ref[...]) - echo_ref[...]).astype(thin)
    coef_ref[...] = back
    out_ref[...] = mul_t(stack(back), pair_weight(panel_ref, 1 - bit_of(level))).astype(thin)


def own_back_kernel(level, coef_ref, panel_ref, perm_ref, placed_ref):
    bit = bit_of(level)
    own = mul_t(stack(coef_ref[...]), pair_weight(panel_ref, bit)).astype(thin)
    row = perm_ref[...] if perm_ref.shape[1] == own.shape[0] else half_row(perm_ref, bit)
    placed_ref[...] = place(row, own, coef_ref.shape[0]).astype(thin)


def backward_kernel(level, arrived_ref, placed_ref, perm_ref, panel_ref, coef_ref, out_ref):
    row = half_row(perm_ref, 1 - bit_of(level + 1))
    back = place(row, arrived_ref[...], placed_ref.shape[0]) + placed_ref[...].astype(wide)
    back = back.astype(thin)
    coef_ref[...] = back
    out_ref[...] = mul_t(stack(back), pair_weight(panel_ref, 1 - bit_of(level))).astype(thin)


def last_kernel(arrived_ref, placed_ref, slots_ref, leaf_ref, scene_ref, image_ref):
    back = place(slots_ref[...], arrived_ref[...], placed_ref.shape[0])
    back = (back + placed_ref[...].astype(wide)).astype(thin)
    gradient = mul_t(back, leaf_ref[...])
    image_ref[...] = (scene_ref[...].astype(wide) - step_size * gradient).astype(thin)


def call(kernel, outs, *operands, work=1):
    whole = pl.BlockSpec(memory_space=pltpu.VMEM)
    shapes = tuple(jax.ShapeDtypeStruct(shape, kind) for shape, kind in outs)
    got = pl.pallas_call(
        kernel,
        out_shape=shapes,
        in_specs=[whole] * len(operands),
        out_specs=tuple(whole for _ in shapes),
        compiler_params=pltpu.CompilerParams(vmem_limit_bytes=16 * 2**20),
        cost_estimate=pl.CostEstimate(
            flops=work * 10**8, bytes_accessed=10**6, transcendentals=0
        ),
    )(*operands)
    return got[0] if len(outs) == 1 else got


def on_device(
    scene_image, echoes, pixel_slot, pulse_slot, level_perm, target_leaf, source_leaf, panels
):
    levels = lax.axis_size("box").bit_length() - 1
    rows = scene_image.shape[0]
    half = rows // 2
    width = target_leaf.shape[1]
    column_of = ((rows, width), thin)
    row_half = ((1, half), jnp.int32)
    sent = ((half, width), thin)
    mixed = ((half, 2 * width), wide)
    perms = [level_perm[level] for level in range(levels)]
    blocks = [panels[level] for level in range(levels)]

    leafed, out_slots, outgoing = call(
        first_kernel, [column_of, row_half, sent], scene_image, target_leaf, pixel_slot, perms[0]
    )
    arrived = swapped(outgoing, "box", 0)
    own_slots, part = call(
        first_own_kernel, [row_half, mixed], leafed, pixel_slot, perms[0], blocks[0]
    )
    for level in range(1, levels):
        coefficients, outgoing = call(
            functools.partial(forward_kernel, level - 1),
            [column_of, sent],
            arrived,
            part,
            blocks[level - 1],
            perms[level],
        )
        arrived = swapped(outgoing, "box", level)
        part = call(
            functools.partial(own_kernel, level),
            [mixed],
            coefficients,
            perms[level],
            blocks[level],
        )

    echo_back, gram = call(
        echo_kernel,
        [((rows, width), wide), ((2 * width, width), thin)],
        echoes,
        source_leaf,
        pulse_slot,
    )
    last = levels - 1
    coefficients, outgoing = call(
        functools.partial(centre_kernel, last),
        [column_of, sent],
        arrived,
        part,
        blocks[last],
        echo_back,
        gram,
    )
    for level in reversed(range(levels)):
        arrived = swapped(outgoing, "box", level)
        placed = call(
            functools.partial(own_back_kernel, level),
            [column_of],
            coefficients,
            blocks[level],
            perms[level] if level else own_slots,
        )
        if level:
            coefficients, outgoing = call(
                functools.partial(backward_kernel, level - 1),
                [column_of, sent],
                arrived,
                placed,
                perms[level],
                blocks[level - 1],
            )
    return call(
        last_kernel,
        [((rows, scene_image.shape[1]), thin)],
        arrived,
        placed,
        out_slots,
        target_leaf,
        scene_image,
    )


def solution(mesh):
    return jax.shard_map(
        on_device,
        mesh=mesh,
        in_specs=(
            P(("groups", "box"), None),
            P(("groups", "box"), None),
            P(("groups", "box"), None),
            P(("groups", "box"), None),
            P(None, "box", None),
            P(),
            P(),
            P(None, "box", None, None, None),
        ),
        out_specs=P(("groups", "box"), None),
        check_vma=False,
    )
```

time: 78.4 us -> 54.5 us (0.70)
  matrix products: 21.8 us -> 0 us
  Pallas kernels: 0 us -> 16.1 us
  waiting for transfers between devices: 38.1 us -> 24.1 us
  starting transfers between devices: 16.3 us -> 9.15 us
  local copies, waits for them, and re-layouts: 1.23 us -> 4.73 us
    dot_general x29 -> x0, matrix products: 21.8 us -> none  [the longest x6 6.94 us: take_rows(): jnp.dot(selector(slots), values, preferred_element_type=jnp.float32)]
    pallas_call x0 -> x18, Pallas kernels: none -> 16.1 us  [call(): pl.pallas_call(kernel, out_shape=shapes, in_specs=[whole] * len(operands)...]
    ppermute x12 -> x8, waiting for transfers between devices: 38.1 us -> 24.1 us  [swapped(): lax.ppermute(value, axis, [(i, i ^ 1 << apart) for i in range(lax.axis_si...]
    ppermute x12 -> x8, starting transfers between devices: 16.3 us -> 9.15 us  [swapped(): lax.ppermute(value, axis, [(i, i ^ 1 << apart) for i in range(lax.axis_si...]
    unnamed x12 -> x18, local copies, waits for them, and re-layouts: 0.03 us -> 2.84 us
    squeeze x0 -> x2, local copies, waits for them, and re-layouts: none -> 1.88 us  [the longest x1 1.13 us: on_device(): blocks = [panels[level] for level in range(levels)]]
    slice x10 -> x0, local copies, waits for them, and re-layouts: 0.97 us -> none  [the longest x1 0.78 us: on_device(): coefficients = place_rows(level_perm[level_index, 0], permuted_grad)]
  transfers between devices with their start and end apart: 12 -> 8, of which waited for: 8 -> 7; matrix products, arithmetic and copies ran while one was open for 3% -> 2% of each run, Pallas kernels for 0% -> 15%
where the time goes in v1:
time: 54.5 us; the launch traced here: 54.2 us
  waiting for transfers between devices  24.1 us (44%)
  Pallas kernels  16.1 us (30%)
  starting transfers between devices  9.15 us (17%)
  local copies, waits for them, and re-layouts  4.73 us (9%)
    ppermute x8, waiting for transfers between devices, swapped(): lax.ppermute(value, axis, [(i, i ^ 1 << apart) for i in range(lax.axis_si...  24.1 us
    pallas_call x18, Pallas kernels, call(): pl.pallas_call(kernel, out_shape=shapes, in_specs=[whole] * len(operands)...  16.1 us
    ppermute x8, starting transfers between devices, swapped(): lax.ppermute(value, axis, [(i, i ^ 1 << apart) for i in range(lax.axis_si...  9.15 us
    unnamed x18, local copies, waits for them, and re-layouts  2.84 us
    squeeze x1, local copies, waits for them, and re-layouts, on_device(): blocks = [panels[level] for level in range(levels)]  1.13 us
  transfers between devices with their start and end apart: 8, of which 7 were waited for; matrix products, arithmetic and copies ran while one was open for 2% of the time, Pallas kernels for 15%

profile of v1, /device:TPU:0, one launch (start us, length us, event | category | flops | bytes accessed | tf_op | source)
XLA Modules:
  0.0 54.2 jit_solution(3065257019701625736)
XLA Ops:
  0.0 0.8 %slice_bitcast_fusion.4 = (s32[1,1024]{1,0:T(1,128)S(1)}, s32[1,1024]{1,0:T(1,128)S(1)}, s32[1,1024]{1,0:T(1,128)S(1)}, s32[1,1024]{1,0:T(1,128)S(1)}) fusion(s32[4,1,1024]{2,1,0:T(1,128)} %param.12), kind=kLoop, calls=%fused_computation.4 | loop fusion | bytes 32768 | tf_op jit(solution)/shard_map/squeeze | solution.py:198
  0.8 1.2 %copy-done = bf16[1024,512]{1,0:T(8,128)(2,1)S(1)} copy-done((bf16[1024,512]{1,0:T(8,128)(2,1)S(1)}, bf16[1024,512]{1,0:T(8,128)(2,1)}, u32[]{:S(2)}) %copy-start) | copy-done | bytes 1048600
  2.0 0.9 %copy-done.3 = bf16[512,128]{1,0:T(8,128)(2,1)S(1)} copy-done((bf16[512,128]{1,0:T(8,128)(2,1)S(1)}, bf16[512,128]{1,0:T(8,128)(2,1)}, u32[]{:S(2)}) %copy-start.3) | copy-done | bytes 131096
  2.9 0.7 %copy-done.6 = s32[1,1024]{1,0:T(1,128)S(1)} copy-done((s32[1,1024]{1,0:T(1,128)S(1)}, s32[1,1024]{1,0:T(1,128)}, u32[]{:S(2)}) %copy-start.6) | copy-done | bytes 4120
  3.6 1.4 %shard_map.82 = (bf16[1024,128]{1,0:T(8,128)(2,1)S(1)}, s32[1,512]{1,0:T(1,128)S(1)}, bf16[512,128]{1,0:T(8,128)(2,1)S(1)}) custom-call(bf16[1024,512]{1,0:T(8,128)(2,1)S(1)} %copy-done, bf16[512,128]{1,0:T(8,128)(2,1)S(1)} %copy-done.3, s32[1,1024]{1,0:T(1,128)S(1)} %copy-done.6, s32[1,1024]{1,0:T(1,128)S(1)} %get-tuple-element.53.perm_ref), custom_call_target="tpu_custom_call" | custom-call | flops 100000000 | bytes 1000000 | tf_op jit(solution)/shard_map/pallas_call | solution.py:174
  5.5 1.1 %slice_bitcast_fusion = (bf16[1,4,128,128]{3,2,1,0:T(8,128)(2,1)S(1)}, bf16[1,4,128,128]{3,2,1,0:T(8,128)(2,1)S(1)}, bf16[1,4,128,128]{3,2,1,0:T(8,128)(2,1)S(1)}, bf16[1,4,128,128]{3,2,1,0:T(8,128)(2,1)S(1)}) fusion(bf16[4,1,4,128,128]{4,3,2,1,0:T(8,128)(2,1)} %param.15), kind=kLoop, calls=%fused_computation | loop fusion | bytes 1048576 | tf_op jit(solution)/shard_map/squeeze | solution.py:199
  6.7 0.9 %shard_map.83 = (s32[1,512]{1,0:T(1,128)S(1)}, f32[512,256]{1,0:T(8,128)S(1)}) custom-call(bf16[1024,128]{1,0:T(8,128)(2,1)S(1)} %get-tuple-element.27.leafed_ref, s32[1,1024]{1,0:T(1,128)S(1)} %copy-done.7, s32[1,1024]{1,0:T(1,128)S(1)} %get-tuple-element.53.perm_ref, bf16[1,4,128,128]{3,2,1,0:T(8,128)(2,1)S(1)} %get-tuple-element.49.panel_ref), custom_call_target="tpu_custom_call" | custom-call | flops 100000000 | bytes 1000000 | tf_op jit(solution)/shard_map/pallas_call | solution.py:174
  7.6 0.7 %shard_map.84 = (bf16[1024,128]{1,0:T(8,128)(2,1)S(1)}, bf16[512,128]{1,0:T(8,128)(2,1)S(1)}) custom-call(bf16[512,128]{1,0:T(8,128)(2,1)S(1)} %collective-permute-done.arrived_ref, f32[512,256]{1,0:T(8,128)S(1)} %get-tuple-element.28.part_ref, bf16[1,4,128,128]{3,2,1,0:T(8,128)(2,1)S(1)} %get-tuple-element.49.panel_ref, ...), custom_call_target="tpu_custom_call" | custom-call | flops 100000000 | bytes 1000000 | tf_op jit(solution)/shard_map/pallas_call | solution.py:174
  8.4 2.6 %collective-permute-start.1 = (bf16[512,128]{1,0:T(8,128)(2,1)S(1)}, bf16[512,128]{1,0:T(8,128)(2,1)S(1)}, u32[]{:S(2)}, u32[]{:S(2)}) collective-permute-start(bf16[512,128]{1,0:T(8,128)(2,1)S(1)} %get-tuple-element.29), channel_id=1, source_target_pairs={{0,2},{1,3},{2,0},{3,1},{4,6},{5,7},{6,4},{7,5},{8,10},{9,11},{10,... | collective-permute-start | bytes 393224 | tf_op jit(solution)/shard_map/ppermute | solution.py:18
  11.0 0.7 %shard_map.85.part_ref = f32[512,256]{1,0:T(8,128)S(1)} custom-call(bf16[1024,128]{1,0:T(8,128)(2,1)S(1)} %get-tuple-element.30.coef_ref, s32[1,1024]{1,0:T(1,128)S(1)} %get-tuple-element.52.perm_ref, bf16[1,4,128,128]{3,2,1,0:T(8,128)(2,1)S(1)} %get-tuple-element.48.panel_ref), custom_call_target="tpu_custom_call" | custom-call | flops 100000000 | bytes 1000000 | tf_op jit(solution)/shard_map/pallas_call | solution.py:174
  11.6 3.5 %collective-permute-done.1.arrived_ref = bf16[512,128]{1,0:T(8,128)(2,1)S(1)} collective-permute-done((bf16[512,128]{1,0:T(8,128)(2,1)S(1)}, bf16[512,128]{1,0:T(8,128)(2,1)S(1)}, u32[]{:S(2)}, u32[]{:S(2)}) %collective-permute-start.1) | collective-permute-done | bytes 131104 | tf_op jit(solution)/shard_map/ppermute | solution.py:18
  15.1 0.7 %shard_map.86 = (bf16[1024,128]{1,0:T(8,128)(2,1)S(1)}, bf16[512,128]{1,0:T(8,128)(2,1)S(1)}) custom-call(bf16[512,128]{1,0:T(8,128)(2,1)S(1)} %collective-permute-done.1.arrived_ref, f32[512,256]{1,0:T(8,128)S(1)} %shard_map.85.part_ref, bf16[1,4,128,128]{3,2,1,0:T(8,128)(2,1)S(1)} %get-tuple-element.48.panel_ref, s32[1,1024]{1,0:T(1,128)S(1)} %get-tuple-element.54.perm_ref), custom_call_target="tpu_custom_call" | custom-call | flops 100000000 | bytes 1000000 | tf_op jit(solution)/shard_map/pallas_call | solution.py:174
  15.8 1.9 %collective-permute-start.2 = (bf16[512,128]{1,0:T(8,128)(2,1)S(1)}, bf16[512,128]{1,0:T(8,128)(2,1)S(1)}, u32[]{:S(2)}, u32[]{:S(2)}) collective-permute-start(bf16[512,128]{1,0:T(8,128)(2,1)S(1)} %get-tuple-element.31), channel_id=1, source_target_pairs={{0,4},{1,5},{2,6},{3,7},{4,0},{5,1},{6,2},{7,3},{8,12},{9,13},{10,... | collective-permute-start | bytes 393224 | tf_op jit(solution)/shard_map/ppermute | solution.py:18
  17.7 0.7 %shard_map.87.part_ref = f32[512,256]{1,0:T(8,128)S(1)} custom-call(bf16[1024,128]{1,0:T(8,128)(2,1)S(1)} %get-tuple-element.32.coef_ref, s32[1,1024]{1,0:T(1,128)S(1)} %get-tuple-element.54.perm_ref, bf16[1,4,128,128]{3,2,1,0:T(8,128)(2,1)S(1)} %get-tuple-element.50.panel_ref), custom_call_target="tpu_custom_call" | custom-call | flops 100000000 | bytes 1000000 | tf_op jit(solution)/shard_map/pallas_call | solution.py:174
  18.4 2.8 %collective-permute-done.2.arrived_ref = bf16[512,128]{1,0:T(8,128)(2,1)S(1)} collective-permute-done((bf16[512,128]{1,0:T(8,128)(2,1)S(1)}, bf16[512,128]{1,0:T(8,128)(2,1)S(1)}, u32[]{:S(2)}, u32[]{:S(2)}) %collective-permute-start.2) | collective-permute-done | bytes 131104 | tf_op jit(solution)/shard_map/ppermute | solution.py:18
  21.2 0.7 %shard_map.88 = (bf16[1024,128]{1,0:T(8,128)(2,1)S(1)}, bf16[512,128]{1,0:T(8,128)(2,1)S(1)}) custom-call(bf16[512,128]{1,0:T(8,128)(2,1)S(1)} %collective-permute-done.2.arrived_ref, f32[512,256]{1,0:T(8,128)S(1)} %shard_map.87.part_ref, bf16[1,4,128,128]{3,2,1,0:T(8,128)(2,1)S(1)} %get-tuple-element.50.panel_ref, s32[1,1024]{1,0:T(1,128)S(1)} %get-tuple-element.51.perm_ref), custom_call_target="tpu_custom_call" | custom-call | flops 100000000 | bytes 1000000 | tf_op jit(solution)/shard_map/pallas_call | solution.py:174
  21.9 2.7 %collective-permute-start.3 = (bf16[512,128]{1,0:T(8,128)(2,1)S(1)}, bf16[512,128]{1,0:T(8,128)(2,1)S(1)}, u32[]{:S(2)}, u32[]{:S(2)}) collective-permute-start(bf16[512,128]{1,0:T(8,128)(2,1)S(1)} %get-tuple-element.33), channel_id=1, source_target_pairs={{0,8},{1,9},{2,10},{3,11},{4,12},{5,13},{6,14},{7,15},{8,0},{9,1},... | collective-permute-start | bytes 393224 | tf_op jit(solution)/shard_map/ppermute | solution.py:18
  24.6 2.2 %shard_map.90 = (f32[1024,128]{1,0:T(8,128)S(1)}, bf16[256,128]{1,0:T(8,128)(2,1)S(1)}) custom-call(bf16[1024,1024]{1,0:T(8,128)(2,1)S(1)} %copy-done.2, bf16[128,1024]{1,0:T(8,128)(2,1)S(1)} %copy-done.5, s32[1,1024]{1,0:T(1,128)S(1)} %copy-done.8), custom_call_target="tpu_custom_call" | custom-call | flops 100000000 | bytes 1000000 | tf_op jit(solution)/shard_map/pallas_call | solution.py:174
  26.9 0.7 %shard_map.89.part_ref = f32[512,256]{1,0:T(8,128)S(1)} custom-call(bf16[1024,128]{1,0:T(8,128)(2,1)S(1)} %get-tuple-element.34.coef_ref, s32[1,1024]{1,0:T(1,128)S(1)} %get-tuple-element.51.perm_ref, bf16[1,4,128,128]{3,2,1,0:T(8,128)(2,1)S(1)} %get-tuple-element.47.panel_ref), custom_call_target="tpu_custom_call" | custom-call | flops 100000000 | bytes 1000000 | tf_op jit(solution)/shard_map/pallas_call | solution.py:174
  27.6 2.6 %collective-permute-done.3.arrived_ref = bf16[512,128]{1,0:T(8,128)(2,1)S(1)} collective-permute-done((bf16[512,128]{1,0:T(8,128)(2,1)S(1)}, bf16[512,128]{1,0:T(8,128)(2,1)S(1)}, u32[]{:S(2)}, u32[]{:S(2)}) %collective-permute-start.3) | collective-permute-done | bytes 131104 | tf_op jit(solution)/shard_map/ppermute | solution.py:18
  30.1 0.7 %shard_map.91 = (bf16[1024,128]{1,0:T(8,128)(2,1)S(1)}, bf16[512,128]{1,0:T(8,128)(2,1)S(1)}) custom-call(bf16[512,128]{1,0:T(8,128)(2,1)S(1)} %collective-permute-done.3.arrived_ref, f32[512,256]{1,0:T(8,128)S(1)} %shard_map.89.part_ref, bf16[1,4,128,128]{3,2,1,0:T(8,128)(2,1)S(1)} %get-tuple-element.47.panel_ref, ...), custom_call_target="tpu_custom_call" | custom-call | flops 100000000 | bytes 1000000 | tf_op jit(solution)/shard_map/pallas_call | solution.py:174
  31.3 0.8 %shard_map.92.placed_ref = bf16[1024,128]{1,0:T(8,128)(2,1)S(1)} custom-call(bf16[1024,128]{1,0:T(8,128)(2,1)S(1)} %get-tuple-element.38.coef_ref, bf16[1,4,128,128]{3,2,1,0:T(8,128)(2,1)S(1)} %get-tuple-element.47.panel_ref, s32[1,1024]{1,0:T(1,128)S(1)} %get-tuple-element.51.perm_ref), custom_call_target="tpu_custom_call" | custom-call | flops 100000000 | bytes 1000000 | tf_op jit(solution)/shard_map/pallas_call | solution.py:174
  32.1 7.1 %collective-permute-done.4.arrived_ref = bf16[512,128]{1,0:T(8,128)(2,1)S(1)} collective-permute-done((bf16[512,128]{1,0:T(8,128)(2,1)S(1)}, bf16[512,128]{1,0:T(8,128)(2,1)S(1)}, u32[]{:S(2)}, u32[]{:S(2)}) %collective-permute-start.4) | collective-permute-done | bytes 131104 | tf_op jit(solution)/shard_map/ppermute | solution.py:18
  39.9 0.8 %shard_map.94.placed_ref = bf16[1024,128]{1,0:T(8,128)(2,1)S(1)} custom-call(bf16[1024,128]{1,0:T(8,128)(2,1)S(1)} %get-tuple-element.40.coef_ref, bf16[1,4,128,128]{3,2,1,0:T(8,128)(2,1)S(1)} %get-tuple-element.50.panel_ref, s32[1,1024]{1,0:T(1,128)S(1)} %get-tuple-element.54.perm_ref), custom_call_target="tpu_custom_call" | custom-call | flops 100000000 | bytes 1000000 | tf_op jit(solution)/shard_map/pallas_call | solution.py:174
  40.6 4.2 %collective-permute-done.5.arrived_ref = bf16[512,128]{1,0:T(8,128)(2,1)S(1)} collective-permute-done((bf16[512,128]{1,0:T(8,128)(2,1)S(1)}, bf16[512,128]{1,0:T(8,128)(2,1)S(1)}, u32[]{:S(2)}, u32[]{:S(2)}) %collective-permute-start.5) | collective-permute-done | bytes 131104 | tf_op jit(solution)/shard_map/ppermute | solution.py:18
  44.8 0.6 %shard_map.95 = (bf16[1024,128]{1,0:T(8,128)(2,1)S(1)}, bf16[512,128]{1,0:T(8,128)(2,1)S(1)}) custom-call(bf16[512,128]{1,0:T(8,128)(2,1)S(1)} %collective-permute-done.5.arrived_ref, bf16[1024,128]{1,0:T(8,128)(2,1)S(1)} %shard_map.94.placed_ref, s32[1,1024]{1,0:T(1,128)S(1)} %get-tuple-element.54.perm_ref, ...), custom_call_target="tpu_custom_call" | custom-call | flops 100000000 | bytes 1000000 | tf_op jit(solution)/shard_map/pallas_call | solution.py:174
  45.4 0.9 %collective-permute-start.6 = (bf16[512,128]{1,0:T(8,128)(2,1)S(1)}, bf16[512,128]{1,0:T(8,128)(2,1)S(1)}, u32[]{:S(2)}, u32[]{:S(2)}) collective-permute-start(bf16[512,128]{1,0:T(8,128)(2,1)S(1)} %get-tuple-element.41), channel_id=1, source_target_pairs={{0,2},{1,3},{2,0},{3,1},{4,6},{5,7},{6,4},{7,5},{8,10},{9,11},{10,... | collective-permute-start | bytes 393224 | tf_op jit(solution)/shard_map/ppermute | solution.py:18
  46.3 0.8 %shard_map.96.placed_ref = bf16[1024,128]{1,0:T(8,128)(2,1)S(1)} custom-call(bf16[1024,128]{1,0:T(8,128)(2,1)S(1)} %get-tuple-element.42.coef_ref, bf16[1,4,128,128]{3,2,1,0:T(8,128)(2,1)S(1)} %get-tuple-element.48.panel_ref, s32[1,1024]{1,0:T(1,128)S(1)} %get-tuple-element.52.perm_ref), custom_call_target="tpu_custom_call" | custom-call | flops 100000000 | bytes 1000000 | tf_op jit(solution)/shard_map/pallas_call | solution.py:174
  47.1 3.4 %collective-permute-done.6.arrived_ref = bf16[512,128]{1,0:T(8,128)(2,1)S(1)} collective-permute-done((bf16[512,128]{1,0:T(8,128)(2,1)S(1)}, bf16[512,128]{1,0:T(8,128)(2,1)S(1)}, u32[]{:S(2)}, u32[]{:S(2)}) %collective-permute-start.6) | collective-permute-done | bytes 131104 | tf_op jit(solution)/shard_map/ppermute | solution.py:18
  50.5 0.6 %shard_map.97 = (bf16[1024,128]{1,0:T(8,128)(2,1)S(1)}, bf16[512,128]{1,0:T(8,128)(2,1)S(1)}) custom-call(bf16[512,128]{1,0:T(8,128)(2,1)S(1)} %collective-permute-done.6.arrived_ref, bf16[1024,128]{1,0:T(8,128)(2,1)S(1)} %shard_map.96.placed_ref, s32[1,1024]{1,0:T(1,128)S(1)} %get-tuple-element.52.perm_ref, ...), custom_call_target="tpu_custom_call" | custom-call | flops 100000000 | bytes 1000000 | tf_op jit(solution)/shard_map/pallas_call | solution.py:174
  51.2 0.8 %shard_map.98.placed_ref = bf16[1024,128]{1,0:T(8,128)(2,1)S(1)} custom-call(bf16[1024,128]{1,0:T(8,128)(2,1)S(1)} %get-tuple-element.44.coef_ref, bf16[1,4,128,128]{3,2,1,0:T(8,128)(2,1)S(1)} %get-tuple-element.49.panel_ref, s32[1,512]{1,0:T(1,128)S(1)} %get-tuple-element.45.perm_ref), custom_call_target="tpu_custom_call" | custom-call | flops 100000000 | bytes 1000000 | tf_op jit(solution)/shard_map/pallas_call | solution.py:174
  52.5 1.7 %shard_map.99 = bf16[1024,512]{1,0:T(8,128)(2,1)} custom-call(bf16[512,128]{1,0:T(8,128)(2,1)S(1)} %collective-permute-done.7.arrived_ref, bf16[1024,128]{1,0:T(8,128)(2,1)S(1)} %shard_map.98.placed_ref, s32[1,512]{1,0:T(1,128)S(1)} %get-tuple-element.46.slots_ref, bf16[512,128]{1,0:T(8,128)(2,1)S(1)} %copy-done.4, bf16[1024,512]{1,0:T(8,128)(2,1)S(1)} %copy-done.1), custom_call_target="tpu_custom_call" | custom-call | flops 100000000 | bytes 1000000 | tf_op jit(solution)/shard_map/pallas_call | solution.py:174
  (22 shorter events, 2.4 us)
Async XLA Ops:
  0.0 6.6 %copy-start.7 = (s32[1,1024]{1,0:T(1,128)S(1)}, s32[1,1024]{1,0:T(1,128)}, u32[]{:S(2)}) copy-start(s32[1,1024]{1,0:T(1,128)} %pixel_ref.3) | copy-start | bytes 12292
  0.8 1.2 %copy-start = (bf16[1024,512]{1,0:T(8,128)(2,1)S(1)}, bf16[1024,512]{1,0:T(8,128)(2,1)}, u32[]{:S(2)}) copy-start(bf16[1024,512]{1,0:T(8,128)(2,1)} %scene_ref.3) | copy-start | bytes 3145732
  2.0 0.9 %copy-start.3 = (bf16[512,128]{1,0:T(8,128)(2,1)S(1)}, bf16[512,128]{1,0:T(8,128)(2,1)}, u32[]{:S(2)}) copy-start(bf16[512,128]{1,0:T(8,128)(2,1)} %leaf_ref.5) | copy-start | bytes 393220
  2.9 0.7 %copy-start.6 = (s32[1,1024]{1,0:T(1,128)S(1)}, s32[1,1024]{1,0:T(1,128)}, u32[]{:S(2)}) copy-start(s32[1,1024]{1,0:T(1,128)} %pixel_ref.3) | copy-start | bytes 12292
  5.0 2.6 %collective-permute-start = (bf16[512,128]{1,0:T(8,128)(2,1)S(1)}, bf16[512,128]{1,0:T(8,128)(2,1)S(1)}, u32[]{:S(2)}, u32[]{:S(2)}) collective-permute-start(bf16[512,128]{1,0:T(8,128)(2,1)S(1)} %get-tuple-element.26), channel_id=1, source_target_pairs={{0,1},{1,0},{2,3},{3,2},{4,5},{5,4},{6,7},{7,6},{8,9},{9,8},{10,11... | collective-permute-start | bytes 393224 | tf_op jit(solution)/shard_map/ppermute | solution.py:18
  7.6 17.0 %copy-start.2 = (bf16[1024,1024]{1,0:T(8,128)(2,1)S(1)}, bf16[1024,1024]{1,0:T(8,128)(2,1)}, u32[]{:S(2)}) copy-start(bf16[1024,1024]{1,0:T(8,128)(2,1)} %echo_ref.1) | copy-start | bytes 6291460
  7.6 17.0 %copy-start.5 = (bf16[128,1024]{1,0:T(8,128)(2,1)S(1)}, bf16[128,1024]{1,0:T(8,128)(2,1)}, u32[]{:S(2)}) copy-start(bf16[128,1024]{1,0:T(8,128)(2,1)} %leaf_ref.4) | copy-start | bytes 786436
  7.6 17.0 %copy-start.8 = (s32[1,1024]{1,0:T(1,128)S(1)}, s32[1,1024]{1,0:T(1,128)}, u32[]{:S(2)}) copy-start(s32[1,1024]{1,0:T(1,128)} %slots_ref.1) | copy-start | bytes 12292
  8.4 6.8 %collective-permute-start.1 = (bf16[512,128]{1,0:T(8,128)(2,1)S(1)}, bf16[512,128]{1,0:T(8,128)(2,1)S(1)}, u32[]{:S(2)}, u32[]{:S(2)}) collective-permute-start(bf16[512,128]{1,0:T(8,128)(2,1)S(1)} %get-tuple-element.29), channel_id=1, source_target_pairs={{0,2},{1,3},{2,0},{3,1},{4,6},{5,7},{6,4},{7,5},{8,10},{9,11},{10,... | collective-permute-start | bytes 393224 | tf_op jit(solution)/shard_map/ppermute | solution.py:18
  15.8 5.4 %collective-permute-start.2 = (bf16[512,128]{1,0:T(8,128)(2,1)S(1)}, bf16[512,128]{1,0:T(8,128)(2,1)S(1)}, u32[]{:S(2)}, u32[]{:S(2)}) collective-permute-start(bf16[512,128]{1,0:T(8,128)(2,1)S(1)} %get-tuple-element.31), channel_id=1, source_target_pairs={{0,4},{1,5},{2,6},{3,7},{4,0},{5,1},{6,2},{7,3},{8,12},{9,13},{10,... | collective-permute-start | bytes 393224 | tf_op jit(solution)/shard_map/ppermute | solution.py:18
  21.9 8.2 %collective-permute-start.3 = (bf16[512,128]{1,0:T(8,128)(2,1)S(1)}, bf16[512,128]{1,0:T(8,128)(2,1)S(1)}, u32[]{:S(2)}, u32[]{:S(2)}) collective-permute-start(bf16[512,128]{1,0:T(8,128)(2,1)S(1)} %get-tuple-element.33), channel_id=1, source_target_pairs={{0,8},{1,9},{2,10},{3,11},{4,12},{5,13},{6,14},{7,15},{8,0},{9,1},... | collective-permute-start | bytes 393224 | tf_op jit(solution)/shard_map/ppermute | solution.py:18
  30.8 8.3 %collective-permute-start.4 = (bf16[512,128]{1,0:T(8,128)(2,1)S(1)}, bf16[512,128]{1,0:T(8,128)(2,1)S(1)}, u32[]{:S(2)}, u32[]{:S(2)}) collective-permute-start(bf16[512,128]{1,0:T(8,128)(2,1)S(1)} %get-tuple-element.37), channel_id=1, source_target_pairs={{0,8},{1,9},{2,10},{3,11},{4,12},{5,13},{6,14},{7,15},{8,0},{9,1},... | collective-permute-start | bytes 393224 | tf_op jit(solution)/shard_map/ppermute | solution.py:18
  31.3 21.2 %copy-start.1 = (bf16[1024,512]{1,0:T(8,128)(2,1)S(1)}, bf16[1024,512]{1,0:T(8,128)(2,1)}, u32[]{:S(2)}) copy-start(bf16[1024,512]{1,0:T(8,128)(2,1)} %scene_ref.3) | copy-start | bytes 3145732
  31.3 21.2 %copy-start.4 = (bf16[512,128]{1,0:T(8,128)(2,1)S(1)}, bf16[512,128]{1,0:T(8,128)(2,1)}, u32[]{:S(2)}) copy-start(bf16[512,128]{1,0:T(8,128)(2,1)} %leaf_ref.5) | copy-start | bytes 393220
  39.8 5.0 %collective-permute-start.5 = (bf16[512,128]{1,0:T(8,128)(2,1)S(1)}, bf16[512,128]{1,0:T(8,128)(2,1)S(1)}, u32[]{:S(2)}, u32[]{:S(2)}) collective-permute-start(bf16[512,128]{1,0:T(8,128)(2,1)S(1)} %get-tuple-element.39), channel_id=1, source_target_pairs={{0,4},{1,5},{2,6},{3,7},{4,0},{5,1},{6,2},{7,3},{8,12},{9,13},{10,... | collective-permute-start | bytes 393224 | tf_op jit(solution)/shard_map/ppermute | solution.py:18
  45.4 5.0 %collective-permute-start.6 = (bf16[512,128]{1,0:T(8,128)(2,1)S(1)}, bf16[512,128]{1,0:T(8,128)(2,1)S(1)}, u32[]{:S(2)}, u32[]{:S(2)}) collective-permute-start(bf16[512,128]{1,0:T(8,128)(2,1)S(1)} %get-tuple-element.41), channel_id=1, source_target_pairs={{0,2},{1,3},{2,0},{3,1},{4,6},{5,7},{6,4},{7,5},{8,10},{9,11},{10,... | collective-permute-start | bytes 393224 | tf_op jit(solution)/shard_map/ppermute | solution.py:18
  51.1 1.4 %collective-permute-start.7 = (bf16[512,128]{1,0:T(8,128)(2,1)S(1)}, bf16[512,128]{1,0:T(8,128)(2,1)S(1)}, u32[]{:S(2)}, u32[]{:S(2)}) collective-permute-start(bf16[512,128]{1,0:T(8,128)(2,1)S(1)} %get-tuple-element.43), channel_id=1, source_target_pairs={{0,1},{1,0},{2,3},{3,2},{4,5},{5,4},{6,7},{7,6},{8,9},{9,8},{10,11... | collective-permute-start | bytes 393224 | tf_op jit(solution)/shard_map/ppermute | solution.py:18

commit v2 on v1

v2 whole, which is shorter than its diff:
```python
import functools

import jax
import jax.numpy as jnp
from jax import lax
from jax.experimental import pallas as pl
from jax.experimental.pallas import tpu as pltpu
from jax.sharding import PartitionSpec as P

step_size = 0.1
wide = jnp.float32
thin = jnp.bfloat16
lanes = 128
depth = 256
scene_chunks = 4


def swapped(value, axis, apart):
    return lax.ppermute(value, axis, [(i, i ^ 1 << apart) for i in range(lax.axis_size(axis))])


def mul(left, right):
    return jnp.dot(left, right, preferred_element_type=wide)


def mul_t(left, right):
    return lax.dot_general(left, right, (((1,), (1,)), ((), ())), preferred_element_type=wide)


def bit_of(level):
    return lax.axis_index("box") // 2**level % 2


def half_row(perm_ref, level, which):
    half = perm_ref.shape[2] // 2
    return perm_ref[level, :, pl.ds(pl.multiple_of(which * half, half), half)]


def column(row):
    parts = []
    for at in range(0, row.shape[1], lanes):
        parts.append(jnp.broadcast_to(row[:, at : at + lanes], (lanes, lanes)).T)
    return jnp.concatenate(parts, axis=0)


def one_hot(hits):
    return jnp.where(hits, 1.0, 0.0).astype(thin)


def take(row, values):
    slots = column(row)
    lane = lax.broadcasted_iota(jnp.int32, slots.shape, 1)
    total = None
    for at in range(0, values.shape[0], depth):
        chosen = jnp.concatenate(
            [one_hot(slots == lane + (at + more)) for more in range(0, depth, lanes)], axis=1
        )
        part = mul(chosen, values[at : at + depth])
        total = part if total is None else total + part
    return total


def place(row, values, rows):
    total = None
    target = lax.broadcasted_iota(jnp.int32, (rows, depth), 0)
    for at in range(0, values.shape[0], depth):
        chosen = one_hot(target == row[:, at : at + depth])
        part = mul(chosen, values[at : at + depth])
        total = part if total is None else total + part
    return total


def compose(outer, inner):
    digits = jnp.concatenate([outer // 256, outer % 256], axis=0).astype(wide)
    digits = jnp.pad(digits, ((0, 14), (0, 0))).astype(thin)
    total = None
    target = lax.broadcasted_iota(jnp.int32, (depth, inner.shape[1]), 0)
    for at in range(0, outer.shape[1], depth):
        chosen = one_hot(target + at == inner)
        part = mul(digits[:, at : at + depth], chosen)
        total = part if total is None else total + part
    return (total[0:1] * 256 + total[1:2]).astype(jnp.int32)


def stack(values):
    half = values.shape[0] // 2
    return jnp.concatenate([values[:half], values[half:]], axis=1)


def unstack(values):
    width = values.shape[1] // 2
    return jnp.concatenate([values[:, :width], values[:, width:]], axis=0)


def pair_weight(panel_ref, level, which):
    return jnp.concatenate(
        [panel_ref[level, 0, which], panel_ref[level, 0, 2 + which]], axis=1
    )


def first_kernel(
    scene_in, leaf_in, pixel_in, perm_in, panel_in,
    scene_ref, leaf_ref, pixel_ref, perm_ref, panel_ref, leafed_ref, slots_ref, out_ref, done,
):
    rows = scene_ref.shape[0]
    half = rows // 2
    chunk = rows // scene_chunks
    parts = [pl.ds(at * chunk, chunk) for at in range(scene_chunks)]
    pairs = [(pixel_in, pixel_ref), (perm_in, perm_ref), (leaf_in, leaf_ref)]
    pairs += [(scene_in.at[part], scene_ref.at[part]) for part in parts]
    pairs += [(panel_in, panel_ref)]
    loads = [
        pltpu.make_async_copy(source, target, done.at[at])
        for at, (source, target) in enumerate(pairs)
    ]
    for load in loads:
        load.start()
    loads[0].wait()
    loads[1].wait()
    slots = compose(pixel_ref[...], half_row(perm_ref, 0, 1 - bit_of(0)))
    slots_ref[...] = slots
    loads[2].wait()
    for at, part in enumerate(parts):
        loads[3 + at].wait()
        leafed_ref[part] = mul(scene_ref[part], leaf_ref[...]).astype(thin)
    out_ref[...] = take(slots, leafed_ref[...]).astype(thin)
    loads[-1].wait()


def first_own_kernel(leafed_ref, pixel_ref, perm_ref, panel_ref, slots_ref, part_ref):
    bit = bit_of(0)
    slots = compose(pixel_ref[...], half_row(perm_ref, 0, bit))
    slots_ref[...] = slots
    own = take(slots, leafed_ref[...]).astype(thin)
    part_ref[...] = mul(own, pair_weight(panel_ref, 0, bit))


def own_kernel(level, coef_ref, perm_ref, panel_ref, part_ref):
    bit = bit_of(level)
    own = take(half_row(perm_ref, level, bit), coef_ref[...]).astype(thin)
    part_ref[...] = mul(own, pair_weight(panel_ref, level, bit))


def own_echo_kernel(
    level, coef_ref, perm_ref, panel_ref, echo_in, leaf_in, slots_in,
    part_ref, back_ref, gram_ref, echo, leaf, slots, done,
):
    rows = coef_ref.shape[0]
    chunk = rows // scene_chunks
    parts = [pl.ds(at * chunk, chunk) for at in range(scene_chunks)]
    pairs = [(slots_in, slots), (leaf_in, leaf)]
    pairs += [(echo_in.at[part], echo.at[part]) for part in parts]
    loads = [
        pltpu.make_async_copy(source, target, done.at[at])
        for at, (source, target) in enumerate(pairs)
    ]
    for load in loads:
        load.start()
    own_kernel(level, coef_ref, perm_ref, panel_ref, part_ref)
    loads[0].wait()
    loads[1].wait()
    gram = mul_t(leaf[...], leaf[...])
    high = gram.astype(thin)
    low = (gram - high.astype(wide)).astype(thin)
    gram_ref[...] = jnp.concatenate([high, low], axis=0)
    back = []
    for at, part in enumerate(parts):
        loads[2 + at].wait()
        back.append(mul_t(echo[part], leaf[...]).astype(thin))
    back_ref[...] = place(slots[...], jnp.concatenate(back, axis=0), rows)


def mix(level, arrived_ref, part_ref, panel_ref):
    weight = pair_weight(panel_ref, level, 1 - bit_of(level))
    mixture = part_ref[...] + mul(arrived_ref[...], weight)
    return unstack(mixture.astype(thin))


def forward_kernel(level, arrived_ref, part_ref, panel_ref, perm_ref, coef_ref, out_ref):
    coefficients = mix(level, arrived_ref, part_ref, panel_ref)
    coef_ref[...] = coefficients
    slots = half_row(perm_ref, level + 1, 1 - bit_of(level + 1))
    out_ref[...] = take(slots, coefficients).astype(thin)


def centre_kernel(level, arrived_ref, part_ref, panel_ref, echo_ref, gram_ref, coef_ref, out_ref):
    coefficients = mix(level, arrived_ref, part_ref, panel_ref)
    twice = jnp.concatenate([coefficients, coefficients], axis=1)
    back = (mul(twice, gram_ref[...]) - echo_ref[...]).astype(thin)
    coef_ref[...] = back
    weight = pair_weight(panel_ref, level, 1 - bit_of(level))
    out_ref[...] = mul_t(stack(back), weight).astype(thin)


def own_back_kernel(level, coef_ref, panel_ref, perm_ref, placed_ref):
    bit = bit_of(level)
    own = mul_t(stack(coef_ref[...]), pair_weight(panel_ref, level, bit)).astype(thin)
    row = half_row(perm_ref, level, bit) if level else perm_ref[...]
    placed_ref[...] = place(row, own, coef_ref.shape[0]).astype(thin)


def backward_kernel(level, arrived_ref, placed_ref, perm_ref, panel_ref, coef_ref, out_ref):
    row = half_row(perm_ref, level + 1, 1 - bit_of(level + 1))
    back = place(row, arrived_ref[...], placed_ref.shape[0]) + placed_ref[...].astype(wide)
    back = back.astype(thin)
    coef_ref[...] = back
    weight = pair_weight(panel_ref, level, 1 - bit_of(level))
    out_ref[...] = mul_t(stack(back), weight).astype(thin)


def last_kernel(arrived_ref, placed_ref, slots_ref, leaf_ref, scene_ref, image_ref, image, sent):
    rows = scene_ref.shape[0]
    chunk = rows // scene_chunks
    back = place(slots_ref[...], arrived_ref[...], rows)
    back = (back + placed_ref[...].astype(wide)).astype(thin)
    stores = []
    for at in range(scene_chunks):
        part = pl.ds(at * chunk, chunk)
        gradient = mul_t(back[at * chunk : (at + 1) * chunk], leaf_ref[...])
        image[part] = (scene_ref[part].astype(wide) - step_size * gradient).astype(thin)
        stores.append(pltpu.make_async_copy(image.at[part], image_ref.at[part], sent.at[at]))
        stores[-1].start()
    for store in stores:
        store.wait()


def call(kernel, outs, *operands, far=(), far_out=False, scratch=()):
    shapes = tuple(jax.ShapeDtypeStruct(shape, kind) for shape, kind in outs)
    near, off = pl.BlockSpec(memory_space=pltpu.VMEM), pl.BlockSpec(memory_space=pltpu.HBM)
    away = tuple(pltpu.with_memory_space_constraint(array, pltpu.HBM) for array in far)
    got = pl.pallas_call(
        kernel,
        out_shape=shapes,
        in_specs=[near] * len(operands) + [off] * len(far),
        out_specs=tuple(off if far_out else near for _ in shapes),
        scratch_shapes=scratch,
        compiler_params=pltpu.CompilerParams(vmem_limit_bytes=16 * 2**20),
        cost_estimate=pl.CostEstimate(flops=10**8, bytes_accessed=10**6, transcendentals=0),
    )(*operands, *away)
    return got[0] if len(outs) == 1 else got


def like(array):
    return (array.shape, array.dtype)


def on_device(
    scene_image, echoes, pixel_slot, pulse_slot, level_perm, target_leaf, source_leaf, panels
):
    levels = lax.axis_size("box").bit_length() - 1
    rows, samples = scene_image.shape
    half = rows // 2
    width = target_leaf.shape[1]
    column_of = ((rows, width), thin)
    row_half = ((1, half), jnp.int32)
    sent = ((half, width), thin)
    mixed = ((half, 2 * width), wide)

    far = (scene_image, target_leaf, pixel_slot, level_perm, panels)
    scene_near, leaf_near, pixel_near, perms, blocks, leafed, out_slots, outgoing = call(
        first_kernel,
        [like(array) for array in far] + [column_of, row_half, sent],
        far=far,
        scratch=[pltpu.SemaphoreType.DMA((4 + scene_chunks,))],
    )
    arrived = swapped(outgoing, "box", 0)
    own_slots, part = call(
        first_own_kernel, [row_half, mixed], leafed, pixel_near, perms, blocks
    )
    for level in range(1, levels):
        coefficients, outgoing = call(
            functools.partial(forward_kernel, level - 1),
            [column_of, sent],
            arrived,
            part,
            blocks,
            perms,
        )
        arrived = swapped(outgoing, "box", level)
        if level == 1:
            part, echo_back, gram = call(
                functools.partial(own_echo_kernel, level),
                [mixed, ((rows, width), wide), ((2 * width, width), thin)],
                coefficients,
                perms,
                blocks,
                far=(echoes, source_leaf, pulse_slot),
                scratch=[
                    pltpu.VMEM(echoes.shape, thin),
                    pltpu.VMEM(source_leaf.shape, thin),
                    pltpu.VMEM(pulse_slot.shape, jnp.int32),
                    pltpu.SemaphoreType.DMA((2 + scene_chunks,)),
                ],
            )
        else:
            part = call(
                functools.partial(own_kernel, level), [mixed], coefficients, perms, blocks
            )

    last = levels - 1
    coefficients, outgoing = call(
        functools.partial(centre_kernel, last),
        [column_of, sent],
        arrived,
        part,
        blocks,
        echo_back,
        gram,
    )
    for level in reversed(range(levels)):
        arrived = swapped(outgoing, "box", level)
        placed = call(
            functools.partial(own_back_kernel, level),
            [column_of],
            coefficients,
            blocks,
            perms if level else own_slots,
        )
        if level:
            coefficients, outgoing = call(
                functools.partial(backward_kernel, level - 1),
                [column_of, sent],
                arrived,
                placed,
                perms,
                blocks,
            )
    return call(
        last_kernel,
        [((rows, samples), thin)],
        arrived,
        placed,
        out_slots,
        leaf_near,
        scene_near,
        far_out=True,
        scratch=[
            pltpu.VMEM((rows, samples), thin),
            pltpu.SemaphoreType.DMA((scene_chunks,)),
        ],
    )


def solution(mesh):
    return jax.shard_map(
        on_device,
        mesh=mesh,
        in_specs=(
            P(("groups", "box"), None),
            P(("groups", "box"), None),
            P(("groups", "box"), None),
            P(("groups", "box"), None),
            P(None, "box", None),
            P(),
            P(),
            P(None, "box", None, None, None),
        ),
        out_specs=P(("groups", "box"), None),
        check_vma=False,
    )
```

time: 54.5 us -> 48.9 us (0.90)
  local copies, waits for them, and re-layouts: 4.73 us -> 0 us
  waiting for transfers between devices: 24.1 us -> 20.8 us
  Pallas kernels: 16.1 us -> 17.4 us
  starting transfers between devices: 9.15 us -> 10.4 us
    ppermute x8, waiting for transfers between devices: 24.1 us -> 20.8 us  [swapped(): lax.ppermute(value, axis, [(i, i ^ 1 << apart) for i in range(lax.axis_si...]
    unnamed x18 -> x0, local copies, waits for them, and re-layouts: 2.84 us -> none
    squeeze x2 -> x0, local copies, waits for them, and re-layouts: 1.88 us -> none  [the longest x1 1.13 us: on_device(): blocks = [panels[level] for level in range(levels)]]
    pallas_call x18 -> x17, Pallas kernels: 16.1 us -> 17.4 us  [call(): pl.pallas_call(kernel, out_shape=shapes, in_specs=[near] * len(operands)...]
    ppermute x8, starting transfers between devices: 9.15 us -> 10.4 us  [swapped(): lax.ppermute(value, axis, [(i, i ^ 1 << apart) for i in range(lax.axis_si...]
  transfers between devices with their start and end apart: 8 -> 8, of which waited for: 7 -> 8; matrix products, arithmetic and copies ran while one was open for 2% -> 0% of each run, Pallas kernels for 15% -> 18%
where the time goes in v2:
time: 48.9 us; the launch traced here: 48.8 us
  waiting for transfers between devices  20.8 us (43%)
  Pallas kernels  17.4 us (36%)
  starting transfers between devices  10.4 us (21%)
    ppermute x8, waiting for transfers between devices, swapped(): lax.ppermute(value, axis, [(i, i ^ 1 << apart) for i in range(lax.axis_si...  20.8 us
    pallas_call x17, Pallas kernels, call(): pl.pallas_call(kernel, out_shape=shapes, in_specs=[near] * len(operands)...  17.4 us
    ppermute x8, starting transfers between devices, swapped(): lax.ppermute(value, axis, [(i, i ^ 1 << apart) for i in range(lax.axis_si...  10.4 us
  transfers between devices with their start and end apart: 8, of which 8 were waited for; matrix products, arithmetic and copies ran while one was open for 0% of the time, Pallas kernels for 18%

profile of v2, /device:TPU:0, one launch (start us, length us, event | category | flops | bytes accessed | tf_op | source)
XLA Modules:
  0.0 48.8 jit_solution(9662401526618407526)
XLA Ops:
  0.0 2.4 %shard_map.82 = (bf16[1024,512]{1,0:T(8,128)(2,1)S(1)}, bf16[512,128]{1,0:T(8,128)(2,1)S(1)}, s32[1,1024]{1,0:T(1,128)S(1)}, s32[4,1,1024]{2,1,0:T(1,128)S(1)}, ...) custom-call(bf16[1024,512]{1,0:T(8,128)(2,1)} %scene_in.1, ...), custom_call_target="tpu_custom_call" | custom-call | flops 100000000 | bytes 1000000 | tf_op jit(solution)/shard_map/pallas_call | solution.py:231
  2.4 0.5 %collective-permute-start = (bf16[512,128]{1,0:T(8,128)(2,1)S(1)}, bf16[512,128]{1,0:T(8,128)(2,1)S(1)}, u32[]{:S(2)}, u32[]{:S(2)}) collective-permute-start(bf16[512,128]{1,0:T(8,128)(2,1)S(1)} %get-tuple-element.32), channel_id=1, source_target_pairs={{0,1},{1,0},{2,3},{3,2},{4,5},{5,4},{6,7},{7,6},{8,9},{9,8},{10,11... | collective-permute-start | bytes 393224 | tf_op jit(solution)/shard_map/ppermute | solution.py:19
  2.9 0.9 %shard_map.83 = (s32[1,512]{1,0:T(1,128)S(1)}, f32[512,256]{1,0:T(8,128)S(1)}) custom-call(bf16[1024,128]{1,0:T(8,128)(2,1)S(1)} %get-tuple-element.33.leafed_ref, s32[1,1024]{1,0:T(1,128)S(1)} %get-tuple-element.34.pixel_ref, s32[4,1,1024]{2,1,0:T(1,128)S(1)} %get-tuple-element.35.perm_ref, bf16[4,1,4,128,128]{4,3,2,1,0:T(8,128)(2,1)S(1)} %get-tuple-element.36.panel_ref), custom_call_target="tpu_custom_call" | custom-call | flops 100000000 | bytes 1000000 | tf_op jit(solution)/shard_map/pallas_call | solution.py:231
  3.9 0.7 %shard_map.84 = (bf16[1024,128]{1,0:T(8,128)(2,1)S(1)}, bf16[512,128]{1,0:T(8,128)(2,1)S(1)}) custom-call(bf16[512,128]{1,0:T(8,128)(2,1)S(1)} %collective-permute-done.arrived_ref, f32[512,256]{1,0:T(8,128)S(1)} %get-tuple-element.37.part_ref, bf16[4,1,4,128,128]{4,3,2,1,0:T(8,128)(2,1)S(1)} %get-tuple-element.36.panel_ref, ...), custom_call_target="tpu_custom_call" | custom-call | flops 100000000 | bytes 1000000 | tf_op jit(solution)/shard_map/pallas_call | solution.py:231
  4.6 2.9 %collective-permute-start.1 = (bf16[512,128]{1,0:T(8,128)(2,1)S(1)}, bf16[512,128]{1,0:T(8,128)(2,1)S(1)}, u32[]{:S(2)}, u32[]{:S(2)}) collective-permute-start(bf16[512,128]{1,0:T(8,128)(2,1)S(1)} %get-tuple-element.38), channel_id=1, source_target_pairs={{0,2},{1,3},{2,0},{3,1},{4,6},{5,7},{6,4},{7,5},{8,10},{9,11},{10,... | collective-permute-start | bytes 393224 | tf_op jit(solution)/shard_map/ppermute | solution.py:19
  7.6 3.4 %shard_map.85 = (f32[512,256]{1,0:T(8,128)S(1)}, f32[1024,128]{1,0:T(8,128)S(1)}, bf16[256,128]{1,0:T(8,128)(2,1)S(1)}) custom-call(bf16[1024,128]{1,0:T(8,128)(2,1)S(1)} %get-tuple-element.39.coef_ref, s32[4,1,1024]{2,1,0:T(1,128)S(1)} %get-tuple-element.35.perm_ref, bf16[4,1,4,128,128]{4,3,2,1,0:T(8,128)(2,1)S(1)} %get-tuple-element.36.panel_ref, ...), custom_call_target="tpu_custom_call" | custom-call | flops 100000000 | bytes 1000000 | tf_op jit(solution)/shard_map/pallas_call | solution.py:231
  11.0 0.4 collective-permute-done.1.arrived_ref
  11.4 0.7 %shard_map.86 = (bf16[1024,128]{1,0:T(8,128)(2,1)S(1)}, bf16[512,128]{1,0:T(8,128)(2,1)S(1)}) custom-call(bf16[512,128]{1,0:T(8,128)(2,1)S(1)} %collective-permute-done.1.arrived_ref, f32[512,256]{1,0:T(8,128)S(1)} %get-tuple-element.40.part_ref, bf16[4,1,4,128,128]{4,3,2,1,0:T(8,128)(2,1)S(1)} %get-tuple-element.36.panel_ref, ...), custom_call_target="tpu_custom_call" | custom-call | flops 100000000 | bytes 1000000 | tf_op jit(solution)/shard_map/pallas_call | solution.py:231
  12.1 1.9 %collective-permute-start.2 = (bf16[512,128]{1,0:T(8,128)(2,1)S(1)}, bf16[512,128]{1,0:T(8,128)(2,1)S(1)}, u32[]{:S(2)}, u32[]{:S(2)}) collective-permute-start(bf16[512,128]{1,0:T(8,128)(2,1)S(1)} %get-tuple-element.41), channel_id=1, source_target_pairs={{0,4},{1,5},{2,6},{3,7},{4,0},{5,1},{6,2},{7,3},{8,12},{9,13},{10,... | collective-permute-start | bytes 393224 | tf_op jit(solution)/shard_map/ppermute | solution.py:19
  13.9 0.7 %shard_map.87.part_ref = f32[512,256]{1,0:T(8,128)S(1)} custom-call(bf16[1024,128]{1,0:T(8,128)(2,1)S(1)} %get-tuple-element.42.coef_ref, s32[4,1,1024]{2,1,0:T(1,128)S(1)} %get-tuple-element.35.perm_ref, bf16[4,1,4,128,128]{4,3,2,1,0:T(8,128)(2,1)S(1)} %get-tuple-element.36.panel_ref), custom_call_target="tpu_custom_call" | custom-call | flops 100000000 | bytes 1000000 | tf_op jit(solution)/shard_map/pallas_call | solution.py:231
  14.6 2.6 %collective-permute-done.2.arrived_ref = bf16[512,128]{1,0:T(8,128)(2,1)S(1)} collective-permute-done((bf16[512,128]{1,0:T(8,128)(2,1)S(1)}, bf16[512,128]{1,0:T(8,128)(2,1)S(1)}, u32[]{:S(2)}, u32[]{:S(2)}) %collective-permute-start.2) | collective-permute-done | bytes 131104 | tf_op jit(solution)/shard_map/ppermute | solution.py:19
  17.2 0.7 %shard_map.88 = (bf16[1024,128]{1,0:T(8,128)(2,1)S(1)}, bf16[512,128]{1,0:T(8,128)(2,1)S(1)}) custom-call(bf16[512,128]{1,0:T(8,128)(2,1)S(1)} %collective-permute-done.2.arrived_ref, f32[512,256]{1,0:T(8,128)S(1)} %shard_map.87.part_ref, bf16[4,1,4,128,128]{4,3,2,1,0:T(8,128)(2,1)S(1)} %get-tuple-element.36.panel_ref, ...), custom_call_target="tpu_custom_call" | custom-call | flops 100000000 | bytes 1000000 | tf_op jit(solution)/shard_map/pallas_call | solution.py:231
  17.9 2.8 %collective-permute-start.3 = (bf16[512,128]{1,0:T(8,128)(2,1)S(1)}, bf16[512,128]{1,0:T(8,128)(2,1)S(1)}, u32[]{:S(2)}, u32[]{:S(2)}) collective-permute-start(bf16[512,128]{1,0:T(8,128)(2,1)S(1)} %get-tuple-element.43), channel_id=1, source_target_pairs={{0,8},{1,9},{2,10},{3,11},{4,12},{5,13},{6,14},{7,15},{8,0},{9,1},... | collective-permute-start | bytes 393224 | tf_op jit(solution)/shard_map/ppermute | solution.py:19
  20.7 0.7 %shard_map.89.part_ref = f32[512,256]{1,0:T(8,128)S(1)} custom-call(bf16[1024,128]{1,0:T(8,128)(2,1)S(1)} %get-tuple-element.44.coef_ref, s32[4,1,1024]{2,1,0:T(1,128)S(1)} %get-tuple-element.35.perm_ref, bf16[4,1,4,128,128]{4,3,2,1,0:T(8,128)(2,1)S(1)} %get-tuple-element.36.panel_ref), custom_call_target="tpu_custom_call" | custom-call | flops 100000000 | bytes 1000000 | tf_op jit(solution)/shard_map/pallas_call | solution.py:231
  21.4 4.4 %collective-permute-done.3.arrived_ref = bf16[512,128]{1,0:T(8,128)(2,1)S(1)} collective-permute-done((bf16[512,128]{1,0:T(8,128)(2,1)S(1)}, bf16[512,128]{1,0:T(8,128)(2,1)S(1)}, u32[]{:S(2)}, u32[]{:S(2)}) %collective-permute-start.3) | collective-permute-done | bytes 131104 | tf_op jit(solution)/shard_map/ppermute | solution.py:19
  25.8 0.7 %shard_map.90 = (bf16[1024,128]{1,0:T(8,128)(2,1)S(1)}, bf16[512,128]{1,0:T(8,128)(2,1)S(1)}) custom-call(bf16[512,128]{1,0:T(8,128)(2,1)S(1)} %collective-permute-done.3.arrived_ref, f32[512,256]{1,0:T(8,128)S(1)} %shard_map.89.part_ref, bf16[4,1,4,128,128]{4,3,2,1,0:T(8,128)(2,1)S(1)} %get-tuple-element.36.panel_ref, ...), custom_call_target="tpu_custom_call" | custom-call | flops 100000000 | bytes 1000000 | tf_op jit(solution)/shard_map/pallas_call | solution.py:231
  26.5 0.9 %collective-permute-start.4 = (bf16[512,128]{1,0:T(8,128)(2,1)S(1)}, bf16[512,128]{1,0:T(8,128)(2,1)S(1)}, u32[]{:S(2)}, u32[]{:S(2)}) collective-permute-start(bf16[512,128]{1,0:T(8,128)(2,1)S(1)} %get-tuple-element.47), channel_id=1, source_target_pairs={{0,8},{1,9},{2,10},{3,11},{4,12},{5,13},{6,14},{7,15},{8,0},{9,1},... | collective-permute-start | bytes 393224 | tf_op jit(solution)/shard_map/ppermute | solution.py:19
  27.4 0.8 %shard_map.91.placed_ref = bf16[1024,128]{1,0:T(8,128)(2,1)S(1)} custom-call(bf16[1024,128]{1,0:T(8,128)(2,1)S(1)} %get-tuple-element.48.coef_ref, bf16[4,1,4,128,128]{4,3,2,1,0:T(8,128)(2,1)S(1)} %get-tuple-element.36.panel_ref, s32[4,1,1024]{2,1,0:T(1,128)S(1)} %get-tuple-element.35.perm_ref), custom_call_target="tpu_custom_call" | custom-call | flops 100000000 | bytes 1000000 | tf_op jit(solution)/shard_map/pallas_call | solution.py:231
  28.2 5.7 %collective-permute-done.4.arrived_ref = bf16[512,128]{1,0:T(8,128)(2,1)S(1)} collective-permute-done((bf16[512,128]{1,0:T(8,128)(2,1)S(1)}, bf16[512,128]{1,0:T(8,128)(2,1)S(1)}, u32[]{:S(2)}, u32[]{:S(2)}) %collective-permute-start.4) | collective-permute-done | bytes 131104 | tf_op jit(solution)/shard_map/ppermute | solution.py:19
  33.9 0.6 %shard_map.92 = (bf16[1024,128]{1,0:T(8,128)(2,1)S(1)}, bf16[512,128]{1,0:T(8,128)(2,1)S(1)}) custom-call(bf16[512,128]{1,0:T(8,128)(2,1)S(1)} %collective-permute-done.4.arrived_ref, bf16[1024,128]{1,0:T(8,128)(2,1)S(1)} %shard_map.91.placed_ref, s32[4,1,1024]{2,1,0:T(1,128)S(1)} %get-tuple-element.35.perm_ref, ...), custom_call_target="tpu_custom_call" | custom-call | flops 100000000 | bytes 1000000 | tf_op jit(solution)/shard_map/pallas_call | solution.py:231
  34.5 0.1 collective-permute-start.5
  34.6 0.8 %shard_map.93.placed_ref = bf16[1024,128]{1,0:T(8,128)(2,1)S(1)} custom-call(bf16[1024,128]{1,0:T(8,128)(2,1)S(1)} %get-tuple-element.50.coef_ref, bf16[4,1,4,128,128]{4,3,2,1,0:T(8,128)(2,1)S(1)} %get-tuple-element.36.panel_ref, s32[4,1,1024]{2,1,0:T(1,128)S(1)} %get-tuple-element.35.perm_ref), custom_call_target="tpu_custom_call" | custom-call | flops 100000000 | bytes 1000000 | tf_op jit(solution)/shard_map/pallas_call | solution.py:231
  35.4 4.2 %collective-permute-done.5.arrived_ref = bf16[512,128]{1,0:T(8,128)(2,1)S(1)} collective-permute-done((bf16[512,128]{1,0:T(8,128)(2,1)S(1)}, bf16[512,128]{1,0:T(8,128)(2,1)S(1)}, u32[]{:S(2)}, u32[]{:S(2)}) %collective-permute-start.5) | collective-permute-done | bytes 131104 | tf_op jit(solution)/shard_map/ppermute | solution.py:19
  39.5 0.6 %shard_map.94 = (bf16[1024,128]{1,0:T(8,128)(2,1)S(1)}, bf16[512,128]{1,0:T(8,128)(2,1)S(1)}) custom-call(bf16[512,128]{1,0:T(8,128)(2,1)S(1)} %collective-permute-done.5.arrived_ref, bf16[1024,128]{1,0:T(8,128)(2,1)S(1)} %shard_map.93.placed_ref, s32[4,1,1024]{2,1,0:T(1,128)S(1)} %get-tuple-element.35.perm_ref, ...), custom_call_target="tpu_custom_call" | custom-call | flops 100000000 | bytes 1000000 | tf_op jit(solution)/shard_map/pallas_call | solution.py:231
  40.2 1.2 %collective-permute-start.6 = (bf16[512,128]{1,0:T(8,128)(2,1)S(1)}, bf16[512,128]{1,0:T(8,128)(2,1)S(1)}, u32[]{:S(2)}, u32[]{:S(2)}) collective-permute-start(bf16[512,128]{1,0:T(8,128)(2,1)S(1)} %get-tuple-element.51), channel_id=1, source_target_pairs={{0,2},{1,3},{2,0},{3,1},{4,6},{5,7},{6,4},{7,5},{8,10},{9,11},{10,... | collective-permute-start | bytes 393224 | tf_op jit(solution)/shard_map/ppermute | solution.py:19
  41.4 0.8 %shard_map.95.placed_ref = bf16[1024,128]{1,0:T(8,128)(2,1)S(1)} custom-call(bf16[1024,128]{1,0:T(8,128)(2,1)S(1)} %get-tuple-element.52.coef_ref, bf16[4,1,4,128,128]{4,3,2,1,0:T(8,128)(2,1)S(1)} %get-tuple-element.36.panel_ref, s32[4,1,1024]{2,1,0:T(1,128)S(1)} %get-tuple-element.35.perm_ref), custom_call_target="tpu_custom_call" | custom-call | flops 100000000 | bytes 1000000 | tf_op jit(solution)/shard_map/pallas_call | solution.py:231
  42.2 3.0 %collective-permute-done.6.arrived_ref = bf16[512,128]{1,0:T(8,128)(2,1)S(1)} collective-permute-done((bf16[512,128]{1,0:T(8,128)(2,1)S(1)}, bf16[512,128]{1,0:T(8,128)(2,1)S(1)}, u32[]{:S(2)}, u32[]{:S(2)}) %collective-permute-start.6) | collective-permute-done | bytes 131104 | tf_op jit(solution)/shard_map/ppermute | solution.py:19
  45.2 0.6 %shard_map.96 = (bf16[1024,128]{1,0:T(8,128)(2,1)S(1)}, bf16[512,128]{1,0:T(8,128)(2,1)S(1)}) custom-call(bf16[512,128]{1,0:T(8,128)(2,1)S(1)} %collective-permute-done.6.arrived_ref, bf16[1024,128]{1,0:T(8,128)(2,1)S(1)} %shard_map.95.placed_ref, s32[4,1,1024]{2,1,0:T(1,128)S(1)} %get-tuple-element.35.perm_ref, ...), custom_call_target="tpu_custom_call" | custom-call | flops 100000000 | bytes 1000000 | tf_op jit(solution)/shard_map/pallas_call | solution.py:231
  45.8 0.1 collective-permute-start.7
  45.9 0.8 %shard_map.97.placed_ref = bf16[1024,128]{1,0:T(8,128)(2,1)S(1)} custom-call(bf16[1024,128]{1,0:T(8,128)(2,1)S(1)} %get-tuple-element.54.coef_ref, bf16[4,1,4,128,128]{4,3,2,1,0:T(8,128)(2,1)S(1)} %get-tuple-element.36.panel_ref, s32[1,512]{1,0:T(1,128)S(1)} %get-tuple-element.55.perm_ref), custom_call_target="tpu_custom_call" | custom-call | flops 100000000 | bytes 1000000 | tf_op jit(solution)/shard_map/pallas_call | solution.py:231
  46.7 0.6 %collective-permute-done.7.arrived_ref = bf16[512,128]{1,0:T(8,128)(2,1)S(1)} collective-permute-done((bf16[512,128]{1,0:T(8,128)(2,1)S(1)}, bf16[512,128]{1,0:T(8,128)(2,1)S(1)}, u32[]{:S(2)}, u32[]{:S(2)}) %collective-permute-start.7) | collective-permute-done | bytes 131104 | tf_op jit(solution)/shard_map/ppermute | solution.py:19
  47.3 1.5 %shard_map.98 = bf16[1024,512]{1,0:T(8,128)(2,1)} custom-call(bf16[512,128]{1,0:T(8,128)(2,1)S(1)} %collective-permute-done.7.arrived_ref, bf16[1024,128]{1,0:T(8,128)(2,1)S(1)} %shard_map.97.placed_ref, s32[1,512]{1,0:T(1,128)S(1)} %get-tuple-element.56.slots_ref, bf16[512,128]{1,0:T(8,128)(2,1)S(1)} %get-tuple-element.57.leaf_ref, ...), custom_call_target="tpu_custom_call" | custom-call | flops 100000000 | bytes 1000000 | tf_op jit(solution)/shard_map/pallas_call | solution.py:231
  (1 shorter events, 0.1 us)
Async XLA Ops:
  2.4 1.5 %collective-permute-start = (bf16[512,128]{1,0:T(8,128)(2,1)S(1)}, bf16[512,128]{1,0:T(8,128)(2,1)S(1)}, u32[]{:S(2)}, u32[]{:S(2)}) collective-permute-start(bf16[512,128]{1,0:T(8,128)(2,1)S(1)} %get-tuple-element.32), channel_id=1, source_target_pairs={{0,1},{1,0},{2,3},{3,2},{4,5},{5,4},{6,7},{7,6},{8,9},{9,8},{10,11... | collective-permute-start | bytes 393224 | tf_op jit(solution)/shard_map/ppermute | solution.py:19
  4.6 6.8 %collective-permute-start.1 = (bf16[512,128]{1,0:T(8,128)(2,1)S(1)}, bf16[512,128]{1,0:T(8,128)(2,1)S(1)}, u32[]{:S(2)}, u32[]{:S(2)}) collective-permute-start(bf16[512,128]{1,0:T(8,128)(2,1)S(1)} %get-tuple-element.38), channel_id=1, source_target_pairs={{0,2},{1,3},{2,0},{3,1},{4,6},{5,7},{6,4},{7,5},{8,10},{9,11},{10,... | collective-permute-start | bytes 393224 | tf_op jit(solution)/shard_map/ppermute | solution.py:19
  12.1 5.1 %collective-permute-start.2 = (bf16[512,128]{1,0:T(8,128)(2,1)S(1)}, bf16[512,128]{1,0:T(8,128)(2,1)S(1)}, u32[]{:S(2)}, u32[]{:S(2)}) collective-permute-start(bf16[512,128]{1,0:T(8,128)(2,1)S(1)} %get-tuple-element.41), channel_id=1, source_target_pairs={{0,4},{1,5},{2,6},{3,7},{4,0},{5,1},{6,2},{7,3},{8,12},{9,13},{10,... | collective-permute-start | bytes 393224 | tf_op jit(solution)/shard_map/ppermute | solution.py:19
  17.9 7.9 %collective-permute-start.3 = (bf16[512,128]{1,0:T(8,128)(2,1)S(1)}, bf16[512,128]{1,0:T(8,128)(2,1)S(1)}, u32[]{:S(2)}, u32[]{:S(2)}) collective-permute-start(bf16[512,128]{1,0:T(8,128)(2,1)S(1)} %get-tuple-element.43), channel_id=1, source_target_pairs={{0,8},{1,9},{2,10},{3,11},{4,12},{5,13},{6,14},{7,15},{8,0},{9,1},... | collective-permute-start | bytes 393224 | tf_op jit(solution)/shard_map/ppermute | solution.py:19
  26.5 7.4 %collective-permute-start.4 = (bf16[512,128]{1,0:T(8,128)(2,1)S(1)}, bf16[512,128]{1,0:T(8,128)(2,1)S(1)}, u32[]{:S(2)}, u32[]{:S(2)}) collective-permute-start(bf16[512,128]{1,0:T(8,128)(2,1)S(1)} %get-tuple-element.47), channel_id=1, source_target_pairs={{0,8},{1,9},{2,10},{3,11},{4,12},{5,13},{6,14},{7,15},{8,0},{9,1},... | collective-permute-start | bytes 393224 | tf_op jit(solution)/shard_map/ppermute | solution.py:19
  34.5 5.0 %collective-permute-start.5 = (bf16[512,128]{1,0:T(8,128)(2,1)S(1)}, bf16[512,128]{1,0:T(8,128)(2,1)S(1)}, u32[]{:S(2)}, u32[]{:S(2)}) collective-permute-start(bf16[512,128]{1,0:T(8,128)(2,1)S(1)} %get-tuple-element.49), channel_id=1, source_target_pairs={{0,4},{1,5},{2,6},{3,7},{4,0},{5,1},{6,2},{7,3},{8,12},{9,13},{10,... | collective-permute-start | bytes 393224 | tf_op jit(solution)/shard_map/ppermute | solution.py:19
  40.2 5.0 %collective-permute-start.6 = (bf16[512,128]{1,0:T(8,128)(2,1)S(1)}, bf16[512,128]{1,0:T(8,128)(2,1)S(1)}, u32[]{:S(2)}, u32[]{:S(2)}) collective-permute-start(bf16[512,128]{1,0:T(8,128)(2,1)S(1)} %get-tuple-element.51), channel_id=1, source_target_pairs={{0,2},{1,3},{2,0},{3,1},{4,6},{5,7},{6,4},{7,5},{8,10},{9,11},{10,... | collective-permute-start | bytes 393224 | tf_op jit(solution)/shard_map/ppermute | solution.py:19
  45.8 1.4 %collective-permute-start.7 = (bf16[512,128]{1,0:T(8,128)(2,1)S(1)}, bf16[512,128]{1,0:T(8,128)(2,1)S(1)}, u32[]{:S(2)}, u32[]{:S(2)}) collective-permute-start(bf16[512,128]{1,0:T(8,128)(2,1)S(1)} %get-tuple-element.53), channel_id=1, source_target_pairs={{0,1},{1,0},{2,3},{3,2},{4,5},{5,4},{6,7},{7,6},{8,9},{9,8},{10,11... | collective-permute-start | bytes 393224 | tf_op jit(solution)/shard_map/ppermute | solution.py:19

commit v3 on v2

--- a/solution.py
+++ b/solution.py
@@ -96,6 +96,12 @@
     return jnp.concatenate(
         [panel_ref[level, 0, which], panel_ref[level, 0, 2 + which]], axis=1
     )
+
+
+def pair_weights(panel_ref, level):
+    bit = bit_of(level)
+    own, other = pair_weight(panel_ref, level, bit), pair_weight(panel_ref, level, 1 - bit)
+    return jnp.concatenate([own, other], axis=0)
 
 
 def first_kernel(
@@ -141,9 +147,18 @@
     part_ref[...] = mul(own, pair_weight(panel_ref, level, bit))
 
 
-def own_echo_kernel(
-    level, coef_ref, perm_ref, panel_ref, echo_in, leaf_in, slots_in,
-    part_ref, back_ref, gram_ref, echo, leaf, slots, done,
+def split(values):
+    high = values.astype(thin)
+    return jnp.concatenate([high, (values - high.astype(wide)).astype(thin)], axis=0)
+
+
+def twice(values):
+    return jnp.concatenate([values, values], axis=1)
+
+
+def own_map_kernel(
+    level, last, coef_ref, perm_ref, panel_ref, echo_in, leaf_in, slots_in,
+    part_ref, own_map_ref, other_map_ref, sent_map_ref, back_ref, echo, leaf, slots, done,
 ):
     rows = coef_ref.shape[0]
     chunk = rows // scene_chunks
@@ -159,15 +174,27 @@
     own_kernel(level, coef_ref, perm_ref, panel_ref, part_ref)
     loads[0].wait()
     loads[1].wait()
-    gram = mul_t(leaf[...], leaf[...])
-    high = gram.astype(thin)
-    low = (gram - high.astype(wide)).astype(thin)
-    gram_ref[...] = jnp.concatenate([high, low], axis=0)
+    gram = split(mul_t(leaf[...], leaf[...]))
+    both = pair_weights(panel_ref, last)
+    width = both.shape[0] // 2
+    scaled = stack(mul(twice(unstack(both)), gram))
+    pair = mul_t(split(scaled), both)
+    maps = pair[: 2 * width] + pair[2 * width :]
+    own_map_ref[...] = split(maps[:width])
+    other_map_ref[...] = split(maps[width:, :width])
+    sent_map_ref[...] = split(maps[width:, width:])
     back = []
     for at, part in enumerate(parts):
         loads[2 + at].wait()
         back.append(mul_t(echo[part], leaf[...]).astype(thin))
-    back_ref[...] = place(slots[...], jnp.concatenate(back, axis=0), rows)
+    back_ref[...] = place(slots[...], jnp.concatenate(back, axis=0), rows).astype(thin)
+
+
+def own_echo_kernel(
+    level, last, coef_ref, perm_ref, panel_ref, back_ref, part_ref, echo_part_ref
+):
+    own_kernel(level, coef_ref, perm_ref, panel_ref, part_ref)
+    echo_part_ref[...] = mul_t(stack(back_ref[...]), pair_weights(panel_ref, last))
 
 
 def mix(level, arrived_ref, part_ref, panel_ref):
@@ -183,13 +210,22 @@
     out_ref[...] = take(slots, coefficients).astype(thin)
 
 
-def centre_kernel(level, arrived_ref, part_ref, panel_ref, echo_ref, gram_ref, coef_ref, out_ref):
-    coefficients = mix(level, arrived_ref, part_ref, panel_ref)
-    twice = jnp.concatenate([coefficients, coefficients], axis=1)
-    back = (mul(twice, gram_ref[...]) - echo_ref[...]).astype(thin)
-    coef_ref[...] = back
-    weight = pair_weight(panel_ref, level, 1 - bit_of(level))
-    out_ref[...] = mul_t(stack(back), weight).astype(thin)
+def bracket_kernel(
+    level, coef_ref, perm_ref, map_ref, echo_part_ref, sent_ref, arrived_map_ref,
+    part_ref, rest_ref, out_ref,
+):
+    own = take(half_row(perm_ref, level, bit_of(level)), coef_ref[...]).astype(thin)
+    both = mul(twice(own), map_ref[...]) - echo_part_ref[...]
+    width = own.shape[1]
+    part_ref[...] = both[:, :width]
+    out_ref[...] = both[:, width:].astype(thin)
+    rest_ref[...] = mul(twice(sent_ref[...]), arrived_map_ref[...])
+
+
+def join_kernel(level, arrived_ref, part_ref, map_ref, perm_ref, placed_ref):
+    own = part_ref[...] + mul(twice(arrived_ref[...]), map_ref[...])
+    row = half_row(perm_ref, level, bit_of(level))
+    placed_ref[...] = place(row, own.astype(thin), placed_ref.shape[0]).astype(thin)
 
 
 def own_back_kernel(level, coef_ref, panel_ref, perm_ref, placed_ref):
@@ -199,9 +235,13 @@
     placed_ref[...] = place(row, own, coef_ref.shape[0]).astype(thin)
 
 
-def backward_kernel(level, arrived_ref, placed_ref, perm_ref, panel_ref, coef_ref, out_ref):
+def backward_kernel(level, arrived_ref, placed_ref, perm_ref, panel_ref, *refs):
+    *rest_ref, coef_ref, out_ref = refs
+    arrived = arrived_ref[...]
+    if rest_ref:
+        arrived = (arrived.astype(wide) + rest_ref[0][...]).astype(thin)
     row = half_row(perm_ref, level + 1, 1 - bit_of(level + 1))
-    back = place(row, arrived_ref[...], placed_ref.shape[0]) + placed_ref[...].astype(wide)
+    back = place(row, arrived, placed_ref.shape[0]) + placed_ref[...].astype(wide)
     back = back.astype(thin)
     coef_ref[...] = back
     weight = pair_weight(panel_ref, level, 1 - bit_of(level))
@@ -235,7 +275,7 @@
         out_specs=tuple(off if far_out else near for _ in shapes),
         scratch_shapes=scratch,
         compiler_params=pltpu.CompilerParams(vmem_limit_bytes=16 * 2**20),
-        cost_estimate=pl.CostEstimate(flops=10**8, bytes_accessed=10**6, transcendentals=0),
+        cost_estimate=pl.CostEstimate(flops=10**6, bytes_accessed=10**4, transcendentals=0),
     )(*operands, *away)
     return got[0] if len(outs) == 1 else got
 
@@ -267,6 +307,7 @@
     own_slots, part = call(
         first_own_kernel, [row_half, mixed], leafed, pixel_near, perms, blocks
     )
+    last = levels - 1
     for level in range(1, levels):
         coefficients, outgoing = call(
             functools.partial(forward_kernel, level - 1),
@@ -278,9 +319,10 @@
         )
         arrived = swapped(outgoing, "box", level)
         if level == 1:
-            part, echo_back, gram = call(
-                functools.partial(own_echo_kernel, level),
-                [mixed, ((rows, width), wide), ((2 * width, width), thin)],
+            narrow_map = ((2 * width, width), thin)
+            part, own_map, other_map, sent_map, echo_back = call(
+                functools.partial(own_map_kernel, level, last),
+                [mixed, ((2 * width, 2 * width), thin), narrow_map, narrow_map, column_of],
                 coefficients,
                 perms,
                 blocks,
@@ -292,23 +334,47 @@
                     pltpu.SemaphoreType.DMA((2 + scene_chunks,)),
                 ],
             )
-        else:
+            arrived_map = swapped(sent_map, "box", last)
+        elif level == 2:
+            part, echo_part = call(
+                functools.partial(own_echo_kernel, level, last),
+                [mixed, mixed],
+                coefficients,
+                perms,
+                blocks,
+                echo_back,
+            )
+        elif level < last:
             part = call(
                 functools.partial(own_kernel, level), [mixed], coefficients, perms, blocks
             )
-
-    last = levels - 1
-    coefficients, outgoing = call(
-        functools.partial(centre_kernel, last),
-        [column_of, sent],
-        arrived,
-        part,
-        blocks,
-        echo_back,
-        gram,
-    )
-    for level in reversed(range(levels)):
-        arrived = swapped(outgoing, "box", level)
+    half_wide = ((half, width), wide)
+    part, rest, bracket = call(
+        functools.partial(bracket_kernel, last),
+        [half_wide, half_wide, sent],
+        coefficients,
+        perms,
+        own_map,
+        echo_part,
+        outgoing,
+        arrived_map,
+    )
+    arrived_bracket = swapped(bracket, "box", last)
+    placed = call(
+        functools.partial(join_kernel, last), [column_of], arrived, part, other_map, perms
+    )
+    arrived, more = arrived_bracket, (rest,)
+    for level in reversed(range(last)):
+        coefficients, outgoing = call(
+            functools.partial(backward_kernel, level),
+            [column_of, sent],
+            arrived,
+            placed,
+            perms,
+            blocks,
+            *more,
+        )
+        arrived, more = swapped(outgoing, "box", level), ()
         placed = call(
             functools.partial(own_back_kernel, level),
             [column_of],
@@ -316,15 +382,6 @@
             blocks,
             perms if level else own_slots,
         )
-        if level:
-            coefficients, outgoing = call(
-                functools.partial(backward_kernel, level - 1),
-                [column_of, sent],
-                arrived,
-                placed,
-                perms,
-                blocks,
-            )
     return call(
         last_kernel,
         [((rows, samples), thin)],

time: 48.9 us -> 47.5 us (0.971)
  waiting for transfers between devices: 20.8 us -> 17.3 us
  starting transfers between devices: 10.4 us -> 12.2 us
    ppermute x8 -> x9, waiting for transfers between devices: 20.8 us -> 17.3 us  [swapped(): lax.ppermute(value, axis, [(i, i ^ 1 << apart) for i in range(lax.axis_si...]
    ppermute x8 -> x9, starting transfers between devices: 10.4 us -> 12.2 us  [swapped(): lax.ppermute(value, axis, [(i, i ^ 1 << apart) for i in range(lax.axis_si...]
    pallas_call x17 -> x16, Pallas kernels: 17.4 us -> 17.8 us  [call(): pl.pallas_call(kernel, out_shape=shapes, in_specs=[near] * len(operands)...]
  transfers between devices with their start and end apart: 8 -> 9, of which waited for: 8 -> 7; matrix products, arithmetic and copies ran while one was open for 0% -> 0% of each run, Pallas kernels for 18% -> 22%
where the time goes in v3:
time: 47.5 us; the launch traced here: 47.3 us
  Pallas kernels  17.8 us (37%)
  waiting for transfers between devices  17.3 us (36%)
  starting transfers between devices  12.2 us (26%)
    pallas_call x16, Pallas kernels, call(): pl.pallas_call(kernel, out_shape=shapes, in_specs=[near] * len(operands)...  17.8 us
    ppermute x9, waiting for transfers between devices, swapped(): lax.ppermute(value, axis, [(i, i ^ 1 << apart) for i in range(lax.axis_si...  17.3 us
    ppermute x9, starting transfers between devices, swapped(): lax.ppermute(value, axis, [(i, i ^ 1 << apart) for i in range(lax.axis_si...  12.2 us
  transfers between devices with their start and end apart: 9, of which 7 were waited for; matrix products, arithmetic and copies ran while one was open for 0% of the time, Pallas kernels for 22%

profile of v3, /device:TPU:0, one launch (start us, length us, event | category | flops | bytes accessed | tf_op | source)
XLA Modules:
  0.0 47.3 jit_solution(2435599076093850776)
XLA Ops:
  0.0 2.4 %shard_map.82 = (bf16[1024,512]{1,0:T(8,128)(2,1)S(1)}, bf16[512,128]{1,0:T(8,128)(2,1)S(1)}, s32[1,1024]{1,0:T(1,128)S(1)}, s32[4,1,1024]{2,1,0:T(1,128)S(1)}, ...) custom-call(bf16[1024,512]{1,0:T(8,128)(2,1)} %scene_in.1, ...), custom_call_target="tpu_custom_call" | custom-call | flops 1000000 | bytes 10000 | tf_op jit(solution)/shard_map/pallas_call | solution.py:271
  2.4 0.5 %collective-permute-start = (bf16[512,128]{1,0:T(8,128)(2,1)S(1)}, bf16[512,128]{1,0:T(8,128)(2,1)S(1)}, u32[]{:S(2)}, u32[]{:S(2)}) collective-permute-start(bf16[512,128]{1,0:T(8,128)(2,1)S(1)} %get-tuple-element.37), channel_id=1, source_target_pairs={{0,1},{1,0},{2,3},{3,2},{4,5},{5,4},{6,7},{7,6},{8,9},{9,8},{10,11... | collective-permute-start | bytes 393224 | tf_op jit(solution)/shard_map/ppermute | solution.py:19
  2.9 0.9 %shard_map.83 = (s32[1,512]{1,0:T(1,128)S(1)}, f32[512,256]{1,0:T(8,128)S(1)}) custom-call(bf16[1024,128]{1,0:T(8,128)(2,1)S(1)} %get-tuple-element.38.leafed_ref, s32[1,1024]{1,0:T(1,128)S(1)} %get-tuple-element.39.pixel_ref, s32[4,1,1024]{2,1,0:T(1,128)S(1)} %get-tuple-element.40.perm_ref, bf16[4,1,4,128,128]{4,3,2,1,0:T(8,128)(2,1)S(1)} %get-tuple-element.41.panel_ref), custom_call_target="tpu_custom_call" | custom-call | flops 1000000 | bytes 10000 | tf_op jit(solution)/shard_map/pallas_call | solution.py:271
  3.8 0.1 collective-permute-done.arrived_ref
  3.9 0.7 %shard_map.84 = (bf16[1024,128]{1,0:T(8,128)(2,1)S(1)}, bf16[512,128]{1,0:T(8,128)(2,1)S(1)}) custom-call(bf16[512,128]{1,0:T(8,128)(2,1)S(1)} %collective-permute-done.arrived_ref, f32[512,256]{1,0:T(8,128)S(1)} %get-tuple-element.42.part_ref, bf16[4,1,4,128,128]{4,3,2,1,0:T(8,128)(2,1)S(1)} %get-tuple-element.41.panel_ref, ...), custom_call_target="tpu_custom_call" | custom-call | flops 1000000 | bytes 10000 | tf_op jit(solution)/shard_map/pallas_call | solution.py:271
  4.6 2.9 %collective-permute-start.1 = (bf16[512,128]{1,0:T(8,128)(2,1)S(1)}, bf16[512,128]{1,0:T(8,128)(2,1)S(1)}, u32[]{:S(2)}, u32[]{:S(2)}) collective-permute-start(bf16[512,128]{1,0:T(8,128)(2,1)S(1)} %get-tuple-element.43), channel_id=1, source_target_pairs={{0,2},{1,3},{2,0},{3,1},{4,6},{5,7},{6,4},{7,5},{8,10},{9,11},{10,... | collective-permute-start | bytes 393224 | tf_op jit(solution)/shard_map/ppermute | solution.py:19
  7.6 4.0 %shard_map.85 = (f32[512,256]{1,0:T(8,128)S(1)}, bf16[256,256]{1,0:T(8,128)(2,1)S(1)}, bf16[256,128]{1,0:T(8,128)(2,1)S(1)}, bf16[256,128]{1,0:T(8,128)(2,1)S(1)}, bf16[1024,128]{1,0:T(8,128)(2,1)S(1)}) custom-call(bf16[1024,128]{1,0:T(8,128)(2,1)S(1)} %get-tuple-element.44.coef_ref, s32[4,1,1024]{2,1,0:T(1,128)S(1)} %get-tuple-element.40.perm_ref, ...), custom_call_target="tpu_custom_call" | custom-call | flops 1000000 | bytes 10000 | tf_op jit(solution)/shard_map/pallas_call | solution.py:271
  11.6 0.7 %shard_map.86 = (bf16[1024,128]{1,0:T(8,128)(2,1)S(1)}, bf16[512,128]{1,0:T(8,128)(2,1)S(1)}) custom-call(bf16[512,128]{1,0:T(8,128)(2,1)S(1)} %collective-permute-done.1.arrived_ref, f32[512,256]{1,0:T(8,128)S(1)} %get-tuple-element.45.part_ref, bf16[4,1,4,128,128]{4,3,2,1,0:T(8,128)(2,1)S(1)} %get-tuple-element.41.panel_ref, ...), custom_call_target="tpu_custom_call" | custom-call | flops 1000000 | bytes 10000 | tf_op jit(solution)/shard_map/pallas_call | solution.py:271
  12.3 1.6 %collective-permute-start.2 = (bf16[512,128]{1,0:T(8,128)(2,1)S(1)}, bf16[512,128]{1,0:T(8,128)(2,1)S(1)}, u32[]{:S(2)}, u32[]{:S(2)}) collective-permute-start(bf16[512,128]{1,0:T(8,128)(2,1)S(1)} %get-tuple-element.46), channel_id=1, source_target_pairs={{0,4},{1,5},{2,6},{3,7},{4,0},{5,1},{6,2},{7,3},{8,12},{9,13},{10,... | collective-permute-start | bytes 393224 | tf_op jit(solution)/shard_map/ppermute | solution.py:19
  14.0 2.6 %collective-permute-start.3 = (bf16[256,128]{1,0:T(8,128)(2,1)S(1)}, bf16[256,128]{1,0:T(8,128)(2,1)S(1)}, u32[]{:S(2)}, u32[]{:S(2)}) collective-permute-start(bf16[256,128]{1,0:T(8,128)(2,1)S(1)} %get-tuple-element.54), channel_id=1, source_target_pairs={{0,8},{1,9},{2,10},{3,11},{4,12},{5,13},{6,14},{7,15},{8,0},{9,1},... | collective-permute-start | bytes 196616 | tf_op jit(solution)/shard_map/ppermute | solution.py:19
  16.5 0.9 %shard_map.87 = (f32[512,256]{1,0:T(8,128)S(1)}, f32[512,256]{1,0:T(8,128)S(1)}) custom-call(bf16[1024,128]{1,0:T(8,128)(2,1)S(1)} %get-tuple-element.47.coef_ref, s32[4,1,1024]{2,1,0:T(1,128)S(1)} %get-tuple-element.40.perm_ref, bf16[4,1,4,128,128]{4,3,2,1,0:T(8,128)(2,1)S(1)} %get-tuple-element.41.panel_ref, bf16[1024,128]{1,0:T(8,128)(2,1)S(1)} %get-tuple-element.48.back_ref), custom_call_target="tpu_custom_call" | custom-call | flops 1000000 | bytes 10000 | tf_op jit(solution)/shard_map/pallas_call | solution.py:271
  17.5 0.9 %collective-permute-done.2.arrived_ref = bf16[512,128]{1,0:T(8,128)(2,1)S(1)} collective-permute-done((bf16[512,128]{1,0:T(8,128)(2,1)S(1)}, bf16[512,128]{1,0:T(8,128)(2,1)S(1)}, u32[]{:S(2)}, u32[]{:S(2)}) %collective-permute-start.2) | collective-permute-done | bytes 131104 | tf_op jit(solution)/shard_map/ppermute | solution.py:19
  18.4 0.7 %shard_map.88 = (bf16[1024,128]{1,0:T(8,128)(2,1)S(1)}, bf16[512,128]{1,0:T(8,128)(2,1)S(1)}) custom-call(bf16[512,128]{1,0:T(8,128)(2,1)S(1)} %collective-permute-done.2.arrived_ref, f32[512,256]{1,0:T(8,128)S(1)} %get-tuple-element.49.part_ref, bf16[4,1,4,128,128]{4,3,2,1,0:T(8,128)(2,1)S(1)} %get-tuple-element.41.panel_ref, ...), custom_call_target="tpu_custom_call" | custom-call | flops 1000000 | bytes 10000 | tf_op jit(solution)/shard_map/pallas_call | solution.py:271
  19.1 2.6 %collective-permute-start.5 = (bf16[512,128]{1,0:T(8,128)(2,1)S(1)}, bf16[512,128]{1,0:T(8,128)(2,1)S(1)}, u32[]{:S(2)}, u32[]{:S(2)}) collective-permute-start(bf16[512,128]{1,0:T(8,128)(2,1)S(1)} %get-tuple-element.53.sent_ref), channel_id=1, source_target_pairs={{0,8},{1,9},{2,10},{3,11},{4,12},{5,13},{6,14},{7,15},{8,0},{9,1},... | collective-permute-start | bytes 393224 | tf_op jit(solution)/shard_map/ppermute | solution.py:19
  21.7 0.9 %shard_map.89 = (f32[512,128]{1,0:T(8,128)S(1)}, f32[512,128]{1,0:T(8,128)S(1)}, bf16[512,128]{1,0:T(8,128)(2,1)S(1)}) custom-call(bf16[1024,128]{1,0:T(8,128)(2,1)S(1)} %get-tuple-element.50.coef_ref, s32[4,1,1024]{2,1,0:T(1,128)S(1)} %get-tuple-element.40.perm_ref, bf16[256,256]{1,0:T(8,128)(2,1)S(1)} %get-tuple-element.51.map_ref, ...), custom_call_target="tpu_custom_call" | custom-call | flops 1000000 | bytes 10000 | tf_op jit(solution)/shard_map/pallas_call | solution.py:271
  22.6 0.4 collective-permute-start.4
  23.0 7.8 %collective-permute-done.5.arrived_ref = bf16[512,128]{1,0:T(8,128)(2,1)S(1)} collective-permute-done((bf16[512,128]{1,0:T(8,128)(2,1)S(1)}, bf16[512,128]{1,0:T(8,128)(2,1)S(1)}, u32[]{:S(2)}, u32[]{:S(2)}) %collective-permute-start.5) | collective-permute-done | bytes 131104 | tf_op jit(solution)/shard_map/ppermute | solution.py:19
  30.8 0.8 %shard_map.90.placed_ref = bf16[1024,128]{1,0:T(8,128)(2,1)S(1)} custom-call(bf16[512,128]{1,0:T(8,128)(2,1)S(1)} %collective-permute-done.5.arrived_ref, f32[512,128]{1,0:T(8,128)S(1)} %get-tuple-element.56.part_ref, bf16[256,128]{1,0:T(8,128)(2,1)S(1)} %get-tuple-element.57.map_ref, s32[4,1,1024]{2,1,0:T(1,128)S(1)} %get-tuple-element.40.perm_ref), custom_call_target="tpu_custom_call" | custom-call | flops 1000000 | bytes 10000 | tf_op jit(solution)/shard_map/pallas_call | solution.py:271
  31.6 0.8 %collective-permute-done.4.arrived_ref = bf16[512,128]{1,0:T(8,128)(2,1)S(1)} collective-permute-done((bf16[512,128]{1,0:T(8,128)(2,1)S(1)}, bf16[512,128]{1,0:T(8,128)(2,1)S(1)}, u32[]{:S(2)}, u32[]{:S(2)}) %collective-permute-start.4) | collective-permute-done | bytes 131104 | tf_op jit(solution)/shard_map/ppermute | solution.py:19
  32.4 0.6 %shard_map.91 = (bf16[1024,128]{1,0:T(8,128)(2,1)S(1)}, bf16[512,128]{1,0:T(8,128)(2,1)S(1)}) custom-call(bf16[512,128]{1,0:T(8,128)(2,1)S(1)} %collective-permute-done.4.arrived_ref, bf16[1024,128]{1,0:T(8,128)(2,1)S(1)} %shard_map.90.placed_ref, s32[4,1,1024]{2,1,0:T(1,128)S(1)} %get-tuple-element.40.perm_ref, ...), custom_call_target="tpu_custom_call" | custom-call | flops 1000000 | bytes 10000 | tf_op jit(solution)/shard_map/pallas_call | solution.py:271
  33.1 0.5 %collective-permute-start.6 = (bf16[512,128]{1,0:T(8,128)(2,1)S(1)}, bf16[512,128]{1,0:T(8,128)(2,1)S(1)}, u32[]{:S(2)}, u32[]{:S(2)}) collective-permute-start(bf16[512,128]{1,0:T(8,128)(2,1)S(1)} %get-tuple-element.59), channel_id=1, source_target_pairs={{0,4},{1,5},{2,6},{3,7},{4,0},{5,1},{6,2},{7,3},{8,12},{9,13},{10,... | collective-permute-start | bytes 393224 | tf_op jit(solution)/shard_map/ppermute | solution.py:19
  33.5 0.8 %shard_map.92.placed_ref = bf16[1024,128]{1,0:T(8,128)(2,1)S(1)} custom-call(bf16[1024,128]{1,0:T(8,128)(2,1)S(1)} %get-tuple-element.60.coef_ref, bf16[4,1,4,128,128]{4,3,2,1,0:T(8,128)(2,1)S(1)} %get-tuple-element.41.panel_ref, s32[4,1,1024]{2,1,0:T(1,128)S(1)} %get-tuple-element.40.perm_ref), custom_call_target="tpu_custom_call" | custom-call | flops 1000000 | bytes 10000 | tf_op jit(solution)/shard_map/pallas_call | solution.py:271
  34.3 3.8 %collective-permute-done.6.arrived_ref = bf16[512,128]{1,0:T(8,128)(2,1)S(1)} collective-permute-done((bf16[512,128]{1,0:T(8,128)(2,1)S(1)}, bf16[512,128]{1,0:T(8,128)(2,1)S(1)}, u32[]{:S(2)}, u32[]{:S(2)}) %collective-permute-start.6) | collective-permute-done | bytes 131104 | tf_op jit(solution)/shard_map/ppermute | solution.py:19
  38.1 0.6 %shard_map.93 = (bf16[1024,128]{1,0:T(8,128)(2,1)S(1)}, bf16[512,128]{1,0:T(8,128)(2,1)S(1)}) custom-call(bf16[512,128]{1,0:T(8,128)(2,1)S(1)} %collective-permute-done.6.arrived_ref, bf16[1024,128]{1,0:T(8,128)(2,1)S(1)} %shard_map.92.placed_ref, s32[4,1,1024]{2,1,0:T(1,128)S(1)} %get-tuple-element.40.perm_ref, ...), custom_call_target="tpu_custom_call" | custom-call | flops 1000000 | bytes 10000 | tf_op jit(solution)/shard_map/pallas_call | solution.py:271
  38.7 0.9 %collective-permute-start.7 = (bf16[512,128]{1,0:T(8,128)(2,1)S(1)}, bf16[512,128]{1,0:T(8,128)(2,1)S(1)}, u32[]{:S(2)}, u32[]{:S(2)}) collective-permute-start(bf16[512,128]{1,0:T(8,128)(2,1)S(1)} %get-tuple-element.61), channel_id=1, source_target_pairs={{0,2},{1,3},{2,0},{3,1},{4,6},{5,7},{6,4},{7,5},{8,10},{9,11},{10,... | collective-permute-start | bytes 393224 | tf_op jit(solution)/shard_map/ppermute | solution.py:19
  39.6 0.8 %shard_map.94.placed_ref = bf16[1024,128]{1,0:T(8,128)(2,1)S(1)} custom-call(bf16[1024,128]{1,0:T(8,128)(2,1)S(1)} %get-tuple-element.62.coef_ref, bf16[4,1,4,128,128]{4,3,2,1,0:T(8,128)(2,1)S(1)} %get-tuple-element.41.panel_ref, s32[4,1,1024]{2,1,0:T(1,128)S(1)} %get-tuple-element.40.perm_ref), custom_call_target="tpu_custom_call" | custom-call | flops 1000000 | bytes 10000 | tf_op jit(solution)/shard_map/pallas_call | solution.py:271
  40.4 3.3 %collective-permute-done.7.arrived_ref = bf16[512,128]{1,0:T(8,128)(2,1)S(1)} collective-permute-done((bf16[512,128]{1,0:T(8,128)(2,1)S(1)}, bf16[512,128]{1,0:T(8,128)(2,1)S(1)}, u32[]{:S(2)}, u32[]{:S(2)}) %collective-permute-start.7) | collective-permute-done | bytes 131104 | tf_op jit(solution)/shard_map/ppermute | solution.py:19
  43.8 0.6 %shard_map.95 = (bf16[1024,128]{1,0:T(8,128)(2,1)S(1)}, bf16[512,128]{1,0:T(8,128)(2,1)S(1)}) custom-call(bf16[512,128]{1,0:T(8,128)(2,1)S(1)} %collective-permute-done.7.arrived_ref, bf16[1024,128]{1,0:T(8,128)(2,1)S(1)} %shard_map.94.placed_ref, s32[4,1,1024]{2,1,0:T(1,128)S(1)} %get-tuple-element.40.perm_ref, ...), custom_call_target="tpu_custom_call" | custom-call | flops 1000000 | bytes 10000 | tf_op jit(solution)/shard_map/pallas_call | solution.py:271
  44.4 0.1 collective-permute-start.8
  44.5 0.8 %shard_map.96.placed_ref = bf16[1024,128]{1,0:T(8,128)(2,1)S(1)} custom-call(bf16[1024,128]{1,0:T(8,128)(2,1)S(1)} %get-tuple-element.64.coef_ref, bf16[4,1,4,128,128]{4,3,2,1,0:T(8,128)(2,1)S(1)} %get-tuple-element.41.panel_ref, s32[1,512]{1,0:T(1,128)S(1)} %get-tuple-element.65.perm_ref), custom_call_target="tpu_custom_call" | custom-call | flops 1000000 | bytes 10000 | tf_op jit(solution)/shard_map/pallas_call | solution.py:271
  45.3 0.6 %collective-permute-done.8.arrived_ref = bf16[512,128]{1,0:T(8,128)(2,1)S(1)} collective-permute-done((bf16[512,128]{1,0:T(8,128)(2,1)S(1)}, bf16[512,128]{1,0:T(8,128)(2,1)S(1)}, u32[]{:S(2)}, u32[]{:S(2)}) %collective-permute-start.8) | collective-permute-done | bytes 131104 | tf_op jit(solution)/shard_map/ppermute | solution.py:19
  45.8 1.5 %shard_map.97 = bf16[1024,512]{1,0:T(8,128)(2,1)} custom-call(bf16[512,128]{1,0:T(8,128)(2,1)S(1)} %collective-permute-done.8.arrived_ref, bf16[1024,128]{1,0:T(8,128)(2,1)S(1)} %shard_map.96.placed_ref, s32[1,512]{1,0:T(1,128)S(1)} %get-tuple-element.66.slots_ref, bf16[512,128]{1,0:T(8,128)(2,1)S(1)} %get-tuple-element.67.leaf_ref, ...), custom_call_target="tpu_custom_call" | custom-call | flops 1000000 | bytes 10000 | tf_op jit(solution)/shard_map/pallas_call | solution.py:271
  (2 shorter events, 0.0 us)
Async XLA Ops:
  2.4 1.5 %collective-permute-start = (bf16[512,128]{1,0:T(8,128)(2,1)S(1)}, bf16[512,128]{1,0:T(8,128)(2,1)S(1)}, u32[]{:S(2)}, u32[]{:S(2)}) collective-permute-start(bf16[512,128]{1,0:T(8,128)(2,1)S(1)} %get-tuple-element.37), channel_id=1, source_target_pairs={{0,1},{1,0},{2,3},{3,2},{4,5},{5,4},{6,7},{7,6},{8,9},{9,8},{10,11... | collective-permute-start | bytes 393224 | tf_op jit(solution)/shard_map/ppermute | solution.py:19
  4.6 7.0 %collective-permute-start.1 = (bf16[512,128]{1,0:T(8,128)(2,1)S(1)}, bf16[512,128]{1,0:T(8,128)(2,1)S(1)}, u32[]{:S(2)}, u32[]{:S(2)}) collective-permute-start(bf16[512,128]{1,0:T(8,128)(2,1)S(1)} %get-tuple-element.43), channel_id=1, source_target_pairs={{0,2},{1,3},{2,0},{3,1},{4,6},{5,7},{6,4},{7,5},{8,10},{9,11},{10,... | collective-permute-start | bytes 393224 | tf_op jit(solution)/shard_map/ppermute | solution.py:19
  12.3 6.0 %collective-permute-start.2 = (bf16[512,128]{1,0:T(8,128)(2,1)S(1)}, bf16[512,128]{1,0:T(8,128)(2,1)S(1)}, u32[]{:S(2)}, u32[]{:S(2)}) collective-permute-start(bf16[512,128]{1,0:T(8,128)(2,1)S(1)} %get-tuple-element.46), channel_id=1, source_target_pairs={{0,4},{1,5},{2,6},{3,7},{4,0},{5,1},{6,2},{7,3},{8,12},{9,13},{10,... | collective-permute-start | bytes 393224 | tf_op jit(solution)/shard_map/ppermute | solution.py:19
  14.0 7.8 %collective-permute-start.3 = (bf16[256,128]{1,0:T(8,128)(2,1)S(1)}, bf16[256,128]{1,0:T(8,128)(2,1)S(1)}, u32[]{:S(2)}, u32[]{:S(2)}) collective-permute-start(bf16[256,128]{1,0:T(8,128)(2,1)S(1)} %get-tuple-element.54), channel_id=1, source_target_pairs={{0,8},{1,9},{2,10},{3,11},{4,12},{5,13},{6,14},{7,15},{8,0},{9,1},... | collective-permute-start | bytes 196616 | tf_op jit(solution)/shard_map/ppermute | solution.py:19
  19.1 11.7 %collective-permute-start.5 = (bf16[512,128]{1,0:T(8,128)(2,1)S(1)}, bf16[512,128]{1,0:T(8,128)(2,1)S(1)}, u32[]{:S(2)}, u32[]{:S(2)}) collective-permute-start(bf16[512,128]{1,0:T(8,128)(2,1)S(1)} %get-tuple-element.53.sent_ref), channel_id=1, source_target_pairs={{0,8},{1,9},{2,10},{3,11},{4,12},{5,13},{6,14},{7,15},{8,0},{9,1},... | collective-permute-start | bytes 393224 | tf_op jit(solution)/shard_map/ppermute | solution.py:19
  22.6 9.8 %collective-permute-start.4 = (bf16[512,128]{1,0:T(8,128)(2,1)S(1)}, bf16[512,128]{1,0:T(8,128)(2,1)S(1)}, u32[]{:S(2)}, u32[]{:S(2)}) collective-permute-start(bf16[512,128]{1,0:T(8,128)(2,1)S(1)} %get-tuple-element.55), channel_id=1, source_target_pairs={{0,8},{1,9},{2,10},{3,11},{4,12},{5,13},{6,14},{7,15},{8,0},{9,1},... | collective-permute-start | bytes 393224 | tf_op jit(solution)/shard_map/ppermute | solution.py:19
  33.1 5.0 %collective-permute-start.6 = (bf16[512,128]{1,0:T(8,128)(2,1)S(1)}, bf16[512,128]{1,0:T(8,128)(2,1)S(1)}, u32[]{:S(2)}, u32[]{:S(2)}) collective-permute-start(bf16[512,128]{1,0:T(8,128)(2,1)S(1)} %get-tuple-element.59), channel_id=1, source_target_pairs={{0,4},{1,5},{2,6},{3,7},{4,0},{5,1},{6,2},{7,3},{8,12},{9,13},{10,... | collective-permute-start | bytes 393224 | tf_op jit(solution)/shard_map/ppermute | solution.py:19
  38.7 5.0 %collective-permute-start.7 = (bf16[512,128]{1,0:T(8,128)(2,1)S(1)}, bf16[512,128]{1,0:T(8,128)(2,1)S(1)}, u32[]{:S(2)}, u32[]{:S(2)}) collective-permute-start(bf16[512,128]{1,0:T(8,128)(2,1)S(1)} %get-tuple-element.61), channel_id=1, source_target_pairs={{0,2},{1,3},{2,0},{3,1},{4,6},{5,7},{6,4},{7,5},{8,10},{9,11},{10,... | collective-permute-start | bytes 393224 | tf_op jit(solution)/shard_map/ppermute | solution.py:19
  44.4 1.4 %collective-permute-start.8 = (bf16[512,128]{1,0:T(8,128)(2,1)S(1)}, bf16[512,128]{1,0:T(8,128)(2,1)S(1)}, u32[]{:S(2)}, u32[]{:S(2)}) collective-permute-start(bf16[512,128]{1,0:T(8,128)(2,1)S(1)} %get-tuple-element.63), channel_id=1, source_target_pairs={{0,1},{1,0},{2,3},{3,2},{4,5},{5,4},{6,7},{7,6},{8,9},{9,8},{10,11... | collective-permute-start | bytes 393224 | tf_op jit(solution)/shard_map/ppermute | solution.py:19

commit v4 on v3

--- a/solution.py
+++ b/solution.py
@@ -47,39 +47,55 @@
     return jnp.where(hits, 1.0, 0.0).astype(thin)
 
 
-def take(row, values):
+def fold(slots, half):
+    return jnp.where(slots < half, slots, slots - half)
+
+
+def take(row, both):
+    half, width = both.shape[0], both.shape[1] // 2
     slots = column(row)
+    within = fold(slots, half)
     lane = lax.broadcasted_iota(jnp.int32, slots.shape, 1)
     total = None
+    for at in range(0, half, depth):
+        chosen = jnp.concatenate(
+            [one_hot(within == lane + (at + more)) for more in range(0, depth, lanes)], axis=1
+        )
+        part = mul(chosen, both[at : at + depth])
+        total = part if total is None else total + part
+    return jnp.where(slots < half, total[:, :width], total[:, width:])
+
+
+def place(row, values, half):
+    low = column(row) < half
+    values = values.astype(wide)
+    zeros = jnp.zeros_like(values)
+    spread = jnp.concatenate([jnp.where(low, values, zeros), jnp.where(low, zeros, values)], axis=1)
+    spread = spread.astype(thin)
+    within = fold(row, half)
+    total = None
+    target = lax.broadcasted_iota(jnp.int32, (half, depth), 0)
     for at in range(0, values.shape[0], depth):
-        chosen = jnp.concatenate(
-            [one_hot(slots == lane + (at + more)) for more in range(0, depth, lanes)], axis=1
-        )
-        part = mul(chosen, values[at : at + depth])
+        chosen = one_hot(target == within[:, at : at + depth])
+        part = mul(chosen, spread[at : at + depth])
         total = part if total is None else total + part
     return total
 
 
-def place(row, values, rows):
-    total = None
-    target = lax.broadcasted_iota(jnp.int32, (rows, depth), 0)
-    for at in range(0, values.shape[0], depth):
-        chosen = one_hot(target == row[:, at : at + depth])
-        part = mul(chosen, values[at : at + depth])
-        total = part if total is None else total + part
-    return total
-
-
 def compose(outer, inner):
+    half = outer.shape[1] // 2
     digits = jnp.concatenate([outer // 256, outer % 256], axis=0).astype(wide)
-    digits = jnp.pad(digits, ((0, 14), (0, 0))).astype(thin)
+    digits = jnp.concatenate([digits[:, :half], digits[:, half:]], axis=0)
+    digits = jnp.pad(digits, ((0, 12), (0, 0))).astype(thin)
+    within = fold(inner, half)
     total = None
     target = lax.broadcasted_iota(jnp.int32, (depth, inner.shape[1]), 0)
-    for at in range(0, outer.shape[1], depth):
-        chosen = one_hot(target + at == inner)
+    for at in range(0, half, depth):
+        chosen = one_hot(target + at == within)
         part = mul(digits[:, at : at + depth], chosen)
         total = part if total is None else total + part
-    return (total[0:1] * 256 + total[1:2]).astype(jnp.int32)
+    picked = jnp.where(inner < half, total[0:2], total[2:4])
+    return (picked[0:1] * 256 + picked[1:2]).astype(jnp.int32)
 
 
 def stack(values):
@@ -109,7 +125,7 @@
     scene_ref, leaf_ref, pixel_ref, perm_ref, panel_ref, leafed_ref, slots_ref, out_ref, done,
 ):
     rows = scene_ref.shape[0]
-    half = rows // 2
+    half, width = rows // 2, leaf_ref.shape[1]
     chunk = rows // scene_chunks
     parts = [pl.ds(at * chunk, chunk) for at in range(scene_chunks)]
     pairs = [(pixel_in, pixel_ref), (perm_in, perm_ref), (leaf_in, leaf_ref)]
@@ -128,7 +144,10 @@
     loads[2].wait()
     for at, part in enumerate(parts):
         loads[3 + at].wait()
-        leafed_ref[part] = mul(scene_ref[part], leaf_ref[...]).astype(thin)
+        side, first = divmod(at * chunk, half)
+        leafed_ref[pl.ds(first, chunk), pl.ds(side * width, width)] = mul(
+            scene_ref[part], leaf_ref[...]
+        ).astype(thin)
     out_ref[...] = take(slots, leafed_ref[...]).astype(thin)
     loads[-1].wait()
 
@@ -160,7 +179,7 @@
     level, last, coef_ref, perm_ref, panel_ref, echo_in, leaf_in, slots_in,
     part_ref, own_map_ref, other_map_ref, sent_map_ref, back_ref, echo, leaf, slots, done,
 ):
-    rows = coef_ref.shape[0]
+    rows = echo.shape[0]
     chunk = rows // scene_chunks
     parts = [pl.ds(at * chunk, chunk) for at in range(scene_chunks)]
     pairs = [(slots_in, slots), (leaf_in, leaf)]
@@ -187,20 +206,20 @@
     for at, part in enumerate(parts):
         loads[2 + at].wait()
         back.append(mul_t(echo[part], leaf[...]).astype(thin))
-    back_ref[...] = place(slots[...], jnp.concatenate(back, axis=0), rows).astype(thin)
+    back_ref[...] = place(slots[...], jnp.concatenate(back, axis=0), rows // 2).astype(thin)
 
 
 def own_echo_kernel(
     level, last, coef_ref, perm_ref, panel_ref, back_ref, part_ref, echo_part_ref
 ):
     own_kernel(level, coef_ref, perm_ref, panel_ref, part_ref)
-    echo_part_ref[...] = mul_t(stack(back_ref[...]), pair_weights(panel_ref, last))
+    echo_part_ref[...] = mul_t(back_ref[...], pair_weights(panel_ref, last))
 
 
 def mix(level, arrived_ref, part_ref, panel_ref):
     weight = pair_weight(panel_ref, level, 1 - bit_of(level))
     mixture = part_ref[...] + mul(arrived_ref[...], weight)
-    return unstack(mixture.astype(thin))
+    return mixture.astype(thin)
 
 
 def forward_kernel(level, arrived_ref, part_ref, panel_ref, perm_ref, coef_ref, out_ref):
@@ -230,7 +249,7 @@
 
 def own_back_kernel(level, coef_ref, panel_ref, perm_ref, placed_ref):
     bit = bit_of(level)
-    own = mul_t(stack(coef_ref[...]), pair_weight(panel_ref, level, bit)).astype(thin)
+    own = mul_t(coef_ref[...], pair_weight(panel_ref, level, bit)).astype(thin)
     row = half_row(perm_ref, level, bit) if level else perm_ref[...]
     placed_ref[...] = place(row, own, coef_ref.shape[0]).astype(thin)
 
@@ -245,14 +264,14 @@
     back = back.astype(thin)
     coef_ref[...] = back
     weight = pair_weight(panel_ref, level, 1 - bit_of(level))
-    out_ref[...] = mul_t(stack(back), weight).astype(thin)
+    out_ref[...] = mul_t(back, weight).astype(thin)
 
 
 def last_kernel(arrived_ref, placed_ref, slots_ref, leaf_ref, scene_ref, image_ref, image, sent):
     rows = scene_ref.shape[0]
     chunk = rows // scene_chunks
-    back = place(slots_ref[...], arrived_ref[...], rows)
-    back = (back + placed_ref[...].astype(wide)).astype(thin)
+    back = place(slots_ref[...], arrived_ref[...], rows // 2)
+    back = unstack((back + placed_ref[...].astype(wide)).astype(thin))
     stores = []
     for at in range(scene_chunks):
         part = pl.ds(at * chunk, chunk)
@@ -291,7 +310,7 @@
     rows, samples = scene_image.shape
     half = rows // 2
     width = target_leaf.shape[1]
-    column_of = ((rows, width), thin)
+    column_of = ((half, 2 * width), thin)
     row_half = ((1, half), jnp.int32)
     sent = ((half, width), thin)
     mixed = ((half, 2 * width), wide)

time: 47.5 us -> 46.8 us (0.985)
  Pallas kernels: 17.8 us -> 16 us
  waiting for transfers between devices: 17.3 us -> 18 us
    pallas_call x16, Pallas kernels: 17.8 us -> 16 us  [call(): pl.pallas_call(kernel, out_shape=shapes, in_specs=[near] * len(operands)...]
    ppermute x9, waiting for transfers between devices: 17.3 us -> 18 us  [swapped(): lax.ppermute(value, axis, [(i, i ^ 1 << apart) for i in range(lax.axis_si...]
  transfers between devices with their start and end apart: 9 -> 9, of which waited for: 7 -> 8; matrix products, arithmetic and copies ran while one was open for 0% -> 0% of each run, Pallas kernels for 22% -> 20%
where the time goes in v4:
time: 46.8 us; the launch traced here: 46.6 us
  waiting for transfers between devices  18 us (38%)
  Pallas kernels  16 us (34%)
  starting transfers between devices  12.4 us (26%)
    ppermute x9, waiting for transfers between devices, swapped(): lax.ppermute(value, axis, [(i, i ^ 1 << apart) for i in range(lax.axis_si...  18 us
    pallas_call x16, Pallas kernels, call(): pl.pallas_call(kernel, out_shape=shapes, in_specs=[near] * len(operands)...  16 us
    ppermute x9, starting transfers between devices, swapped(): lax.ppermute(value, axis, [(i, i ^ 1 << apart) for i in range(lax.axis_si...  12.4 us
  transfers between devices with their start and end apart: 9, of which 8 were waited for; matrix products, arithmetic and copies ran while one was open for 0% of the time, Pallas kernels for 20%

profile of v4, /device:TPU:0, one launch (start us, length us, event | category | flops | bytes accessed | tf_op | source)
XLA Modules:
  0.0 46.6 jit_solution(7946106733011023361)
XLA Ops:
  0.0 2.3 %shard_map.82 = (bf16[1024,512]{1,0:T(8,128)(2,1)S(1)}, bf16[512,128]{1,0:T(8,128)(2,1)S(1)}, s32[1,1024]{1,0:T(1,128)S(1)}, s32[4,1,1024]{2,1,0:T(1,128)S(1)}, ...) custom-call(bf16[1024,512]{1,0:T(8,128)(2,1)} %scene_in.1, ...), custom_call_target="tpu_custom_call" | custom-call | flops 1000000 | bytes 10000 | tf_op jit(solution)/shard_map/pallas_call | solution.py:290
  2.3 0.5 %collective-permute-start = (bf16[512,128]{1,0:T(8,128)(2,1)S(1)}, bf16[512,128]{1,0:T(8,128)(2,1)S(1)}, u32[]{:S(2)}, u32[]{:S(2)}) collective-permute-start(bf16[512,128]{1,0:T(8,128)(2,1)S(1)} %get-tuple-element.37), channel_id=1, source_target_pairs={{0,1},{1,0},{2,3},{3,2},{4,5},{5,4},{6,7},{7,6},{8,9},{9,8},{10,11... | collective-permute-start | bytes 393224 | tf_op jit(solution)/shard_map/ppermute | solution.py:19
  2.8 0.7 %shard_map.83 = (s32[1,512]{1,0:T(1,128)S(1)}, f32[512,256]{1,0:T(8,128)S(1)}) custom-call(bf16[512,256]{1,0:T(8,128)(2,1)S(1)} %get-tuple-element.38.leafed_ref, s32[1,1024]{1,0:T(1,128)S(1)} %get-tuple-element.39.pixel_ref, s32[4,1,1024]{2,1,0:T(1,128)S(1)} %get-tuple-element.40.perm_ref, bf16[4,1,4,128,128]{4,3,2,1,0:T(8,128)(2,1)S(1)} %get-tuple-element.41.panel_ref), custom_call_target="tpu_custom_call" | custom-call | flops 1000000 | bytes 10000 | tf_op jit(solution)/shard_map/pallas_call | solution.py:290
  3.5 0.3 collective-permute-done.arrived_ref
  3.8 0.6 %shard_map.84 = (bf16[512,256]{1,0:T(8,128)(2,1)S(1)}, bf16[512,128]{1,0:T(8,128)(2,1)S(1)}) custom-call(bf16[512,128]{1,0:T(8,128)(2,1)S(1)} %collective-permute-done.arrived_ref, f32[512,256]{1,0:T(8,128)S(1)} %get-tuple-element.42.part_ref, bf16[4,1,4,128,128]{4,3,2,1,0:T(8,128)(2,1)S(1)} %get-tuple-element.41.panel_ref, ...), custom_call_target="tpu_custom_call" | custom-call | flops 1000000 | bytes 10000 | tf_op jit(solution)/shard_map/pallas_call | solution.py:290
  4.4 2.9 %collective-permute-start.1 = (bf16[512,128]{1,0:T(8,128)(2,1)S(1)}, bf16[512,128]{1,0:T(8,128)(2,1)S(1)}, u32[]{:S(2)}, u32[]{:S(2)}) collective-permute-start(bf16[512,128]{1,0:T(8,128)(2,1)S(1)} %get-tuple-element.43), channel_id=1, source_target_pairs={{0,2},{1,3},{2,0},{3,1},{4,6},{5,7},{6,4},{7,5},{8,10},{9,11},{10,... | collective-permute-start | bytes 393224 | tf_op jit(solution)/shard_map/ppermute | solution.py:19
  7.3 3.7 %shard_map.85 = (f32[512,256]{1,0:T(8,128)S(1)}, bf16[256,256]{1,0:T(8,128)(2,1)S(1)}, bf16[256,128]{1,0:T(8,128)(2,1)S(1)}, bf16[256,128]{1,0:T(8,128)(2,1)S(1)}, bf16[512,256]{1,0:T(8,128)(2,1)S(1)}) custom-call(bf16[512,256]{1,0:T(8,128)(2,1)S(1)} %get-tuple-element.44.coef_ref, s32[4,1,1024]{2,1,0:T(1,128)S(1)} %get-tuple-element.40.perm_ref, ...), custom_call_target="tpu_custom_call" | custom-call | flops 1000000 | bytes 10000 | tf_op jit(solution)/shard_map/pallas_call | solution.py:290
  11.1 0.1 collective-permute-done.1.arrived_ref
  11.2 0.6 %shard_map.86 = (bf16[512,256]{1,0:T(8,128)(2,1)S(1)}, bf16[512,128]{1,0:T(8,128)(2,1)S(1)}) custom-call(bf16[512,128]{1,0:T(8,128)(2,1)S(1)} %collective-permute-done.1.arrived_ref, f32[512,256]{1,0:T(8,128)S(1)} %get-tuple-element.45.part_ref, bf16[4,1,4,128,128]{4,3,2,1,0:T(8,128)(2,1)S(1)} %get-tuple-element.41.panel_ref, ...), custom_call_target="tpu_custom_call" | custom-call | flops 1000000 | bytes 10000 | tf_op jit(solution)/shard_map/pallas_call | solution.py:290
  11.8 1.9 %collective-permute-start.2 = (bf16[512,128]{1,0:T(8,128)(2,1)S(1)}, bf16[512,128]{1,0:T(8,128)(2,1)S(1)}, u32[]{:S(2)}, u32[]{:S(2)}) collective-permute-start(bf16[512,128]{1,0:T(8,128)(2,1)S(1)} %get-tuple-element.46), channel_id=1, source_target_pairs={{0,4},{1,5},{2,6},{3,7},{4,0},{5,1},{6,2},{7,3},{8,12},{9,13},{10,... | collective-permute-start | bytes 393224 | tf_op jit(solution)/shard_map/ppermute | solution.py:19
  13.6 2.6 %collective-permute-start.3 = (bf16[256,128]{1,0:T(8,128)(2,1)S(1)}, bf16[256,128]{1,0:T(8,128)(2,1)S(1)}, u32[]{:S(2)}, u32[]{:S(2)}) collective-permute-start(bf16[256,128]{1,0:T(8,128)(2,1)S(1)} %get-tuple-element.54), channel_id=1, source_target_pairs={{0,8},{1,9},{2,10},{3,11},{4,12},{5,13},{6,14},{7,15},{8,0},{9,1},... | collective-permute-start | bytes 196616 | tf_op jit(solution)/shard_map/ppermute | solution.py:19
  16.2 0.8 %shard_map.87 = (f32[512,256]{1,0:T(8,128)S(1)}, f32[512,256]{1,0:T(8,128)S(1)}) custom-call(bf16[512,256]{1,0:T(8,128)(2,1)S(1)} %get-tuple-element.47.coef_ref, s32[4,1,1024]{2,1,0:T(1,128)S(1)} %get-tuple-element.40.perm_ref, bf16[4,1,4,128,128]{4,3,2,1,0:T(8,128)(2,1)S(1)} %get-tuple-element.41.panel_ref, bf16[512,256]{1,0:T(8,128)(2,1)S(1)} %get-tuple-element.48.back_ref), custom_call_target="tpu_custom_call" | custom-call | flops 1000000 | bytes 10000 | tf_op jit(solution)/shard_map/pallas_call | solution.py:290
  17.0 0.8 %collective-permute-done.2.arrived_ref = bf16[512,128]{1,0:T(8,128)(2,1)S(1)} collective-permute-done((bf16[512,128]{1,0:T(8,128)(2,1)S(1)}, bf16[512,128]{1,0:T(8,128)(2,1)S(1)}, u32[]{:S(2)}, u32[]{:S(2)}) %collective-permute-start.2) | collective-permute-done | bytes 131104 | tf_op jit(solution)/shard_map/ppermute | solution.py:19
  17.7 0.6 %shard_map.88 = (bf16[512,256]{1,0:T(8,128)(2,1)S(1)}, bf16[512,128]{1,0:T(8,128)(2,1)S(1)}) custom-call(bf16[512,128]{1,0:T(8,128)(2,1)S(1)} %collective-permute-done.2.arrived_ref, f32[512,256]{1,0:T(8,128)S(1)} %get-tuple-element.49.part_ref, bf16[4,1,4,128,128]{4,3,2,1,0:T(8,128)(2,1)S(1)} %get-tuple-element.41.panel_ref, ...), custom_call_target="tpu_custom_call" | custom-call | flops 1000000 | bytes 10000 | tf_op jit(solution)/shard_map/pallas_call | solution.py:290
  18.4 2.6 %collective-permute-start.5 = (bf16[512,128]{1,0:T(8,128)(2,1)S(1)}, bf16[512,128]{1,0:T(8,128)(2,1)S(1)}, u32[]{:S(2)}, u32[]{:S(2)}) collective-permute-start(bf16[512,128]{1,0:T(8,128)(2,1)S(1)} %get-tuple-element.53.sent_ref), channel_id=1, source_target_pairs={{0,8},{1,9},{2,10},{3,11},{4,12},{5,13},{6,14},{7,15},{8,0},{9,1},... | collective-permute-start | bytes 393224 | tf_op jit(solution)/shard_map/ppermute | solution.py:19
  21.0 0.7 %shard_map.89 = (f32[512,128]{1,0:T(8,128)S(1)}, f32[512,128]{1,0:T(8,128)S(1)}, bf16[512,128]{1,0:T(8,128)(2,1)S(1)}) custom-call(bf16[512,256]{1,0:T(8,128)(2,1)S(1)} %get-tuple-element.50.coef_ref, s32[4,1,1024]{2,1,0:T(1,128)S(1)} %get-tuple-element.40.perm_ref, bf16[256,256]{1,0:T(8,128)(2,1)S(1)} %get-tuple-element.51.map_ref, ...), custom_call_target="tpu_custom_call" | custom-call | flops 1000000 | bytes 10000 | tf_op jit(solution)/shard_map/pallas_call | solution.py:290
  21.8 0.4 collective-permute-start.4
  22.2 8.1 %collective-permute-done.5.arrived_ref = bf16[512,128]{1,0:T(8,128)(2,1)S(1)} collective-permute-done((bf16[512,128]{1,0:T(8,128)(2,1)S(1)}, bf16[512,128]{1,0:T(8,128)(2,1)S(1)}, u32[]{:S(2)}, u32[]{:S(2)}) %collective-permute-start.5) | collective-permute-done | bytes 131104 | tf_op jit(solution)/shard_map/ppermute | solution.py:19
  30.3 0.6 %shard_map.90.placed_ref = bf16[512,256]{1,0:T(8,128)(2,1)S(1)} custom-call(bf16[512,128]{1,0:T(8,128)(2,1)S(1)} %collective-permute-done.5.arrived_ref, f32[512,128]{1,0:T(8,128)S(1)} %get-tuple-element.56.part_ref, bf16[256,128]{1,0:T(8,128)(2,1)S(1)} %get-tuple-element.57.map_ref, s32[4,1,1024]{2,1,0:T(1,128)S(1)} %get-tuple-element.40.perm_ref), custom_call_target="tpu_custom_call" | custom-call | flops 1000000 | bytes 10000 | tf_op jit(solution)/shard_map/pallas_call | solution.py:290
  30.9 0.8 %collective-permute-done.4.arrived_ref = bf16[512,128]{1,0:T(8,128)(2,1)S(1)} collective-permute-done((bf16[512,128]{1,0:T(8,128)(2,1)S(1)}, bf16[512,128]{1,0:T(8,128)(2,1)S(1)}, u32[]{:S(2)}, u32[]{:S(2)}) %collective-permute-start.4) | collective-permute-done | bytes 131104 | tf_op jit(solution)/shard_map/ppermute | solution.py:19
  31.7 0.6 %shard_map.91 = (bf16[512,256]{1,0:T(8,128)(2,1)S(1)}, bf16[512,128]{1,0:T(8,128)(2,1)S(1)}) custom-call(bf16[512,128]{1,0:T(8,128)(2,1)S(1)} %collective-permute-done.4.arrived_ref, bf16[512,256]{1,0:T(8,128)(2,1)S(1)} %shard_map.90.placed_ref, s32[4,1,1024]{2,1,0:T(1,128)S(1)} %get-tuple-element.40.perm_ref, ...), custom_call_target="tpu_custom_call" | custom-call | flops 1000000 | bytes 10000 | tf_op jit(solution)/shard_map/pallas_call | solution.py:290
  32.3 0.1 collective-permute-start.6
  32.3 0.7 %shard_map.92.placed_ref = bf16[512,256]{1,0:T(8,128)(2,1)S(1)} custom-call(bf16[512,256]{1,0:T(8,128)(2,1)S(1)} %get-tuple-element.60.coef_ref, bf16[4,1,4,128,128]{4,3,2,1,0:T(8,128)(2,1)S(1)} %get-tuple-element.41.panel_ref, s32[4,1,1024]{2,1,0:T(1,128)S(1)} %get-tuple-element.40.perm_ref), custom_call_target="tpu_custom_call" | custom-call | flops 1000000 | bytes 10000 | tf_op jit(solution)/shard_map/pallas_call | solution.py:290
  33.0 4.3 %collective-permute-done.6.arrived_ref = bf16[512,128]{1,0:T(8,128)(2,1)S(1)} collective-permute-done((bf16[512,128]{1,0:T(8,128)(2,1)S(1)}, bf16[512,128]{1,0:T(8,128)(2,1)S(1)}, u32[]{:S(2)}, u32[]{:S(2)}) %collective-permute-start.6) | collective-permute-done | bytes 131104 | tf_op jit(solution)/shard_map/ppermute | solution.py:19
  37.3 0.6 %shard_map.93 = (bf16[512,256]{1,0:T(8,128)(2,1)S(1)}, bf16[512,128]{1,0:T(8,128)(2,1)S(1)}) custom-call(bf16[512,128]{1,0:T(8,128)(2,1)S(1)} %collective-permute-done.6.arrived_ref, bf16[512,256]{1,0:T(8,128)(2,1)S(1)} %shard_map.92.placed_ref, s32[4,1,1024]{2,1,0:T(1,128)S(1)} %get-tuple-element.40.perm_ref, ...), custom_call_target="tpu_custom_call" | custom-call | flops 1000000 | bytes 10000 | tf_op jit(solution)/shard_map/pallas_call | solution.py:290
  37.9 1.3 %collective-permute-start.7 = (bf16[512,128]{1,0:T(8,128)(2,1)S(1)}, bf16[512,128]{1,0:T(8,128)(2,1)S(1)}, u32[]{:S(2)}, u32[]{:S(2)}) collective-permute-start(bf16[512,128]{1,0:T(8,128)(2,1)S(1)} %get-tuple-element.61), channel_id=1, source_target_pairs={{0,2},{1,3},{2,0},{3,1},{4,6},{5,7},{6,4},{7,5},{8,10},{9,11},{10,... | collective-permute-start | bytes 393224 | tf_op jit(solution)/shard_map/ppermute | solution.py:19
  39.2 0.6 %shard_map.94.placed_ref = bf16[512,256]{1,0:T(8,128)(2,1)S(1)} custom-call(bf16[512,256]{1,0:T(8,128)(2,1)S(1)} %get-tuple-element.62.coef_ref, bf16[4,1,4,128,128]{4,3,2,1,0:T(8,128)(2,1)S(1)} %get-tuple-element.41.panel_ref, s32[4,1,1024]{2,1,0:T(1,128)S(1)} %get-tuple-element.40.perm_ref), custom_call_target="tpu_custom_call" | custom-call | flops 1000000 | bytes 10000 | tf_op jit(solution)/shard_map/pallas_call | solution.py:290
  39.9 3.1 %collective-permute-done.7.arrived_ref = bf16[512,128]{1,0:T(8,128)(2,1)S(1)} collective-permute-done((bf16[512,128]{1,0:T(8,128)(2,1)S(1)}, bf16[512,128]{1,0:T(8,128)(2,1)S(1)}, u32[]{:S(2)}, u32[]{:S(2)}) %collective-permute-start.7) | collective-permute-done | bytes 131104 | tf_op jit(solution)/shard_map/ppermute | solution.py:19
  42.9 0.6 %shard_map.95 = (bf16[512,256]{1,0:T(8,128)(2,1)S(1)}, bf16[512,128]{1,0:T(8,128)(2,1)S(1)}) custom-call(bf16[512,128]{1,0:T(8,128)(2,1)S(1)} %collective-permute-done.7.arrived_ref, bf16[512,256]{1,0:T(8,128)(2,1)S(1)} %shard_map.94.placed_ref, s32[4,1,1024]{2,1,0:T(1,128)S(1)} %get-tuple-element.40.perm_ref, ...), custom_call_target="tpu_custom_call" | custom-call | flops 1000000 | bytes 10000 | tf_op jit(solution)/shard_map/pallas_call | solution.py:290
  43.6 0.6 %shard_map.96.placed_ref = bf16[512,256]{1,0:T(8,128)(2,1)S(1)} custom-call(bf16[512,256]{1,0:T(8,128)(2,1)S(1)} %get-tuple-element.64.coef_ref, bf16[4,1,4,128,128]{4,3,2,1,0:T(8,128)(2,1)S(1)} %get-tuple-element.41.panel_ref, s32[1,512]{1,0:T(1,128)S(1)} %get-tuple-element.65.perm_ref), custom_call_target="tpu_custom_call" | custom-call | flops 1000000 | bytes 10000 | tf_op jit(solution)/shard_map/pallas_call | solution.py:290
  44.2 0.7 %collective-permute-done.8.arrived_ref = bf16[512,128]{1,0:T(8,128)(2,1)S(1)} collective-permute-done((bf16[512,128]{1,0:T(8,128)(2,1)S(1)}, bf16[512,128]{1,0:T(8,128)(2,1)S(1)}, u32[]{:S(2)}, u32[]{:S(2)}) %collective-permute-start.8) | collective-permute-done | bytes 131104 | tf_op jit(solution)/shard_map/ppermute | solution.py:19
  44.9 1.7 %shard_map.97 = bf16[1024,512]{1,0:T(8,128)(2,1)} custom-call(bf16[512,128]{1,0:T(8,128)(2,1)S(1)} %collective-permute-done.8.arrived_ref, bf16[512,256]{1,0:T(8,128)(2,1)S(1)} %shard_map.96.placed_ref, s32[1,512]{1,0:T(1,128)S(1)} %get-tuple-element.66.slots_ref, bf16[512,128]{1,0:T(8,128)(2,1)S(1)} %get-tuple-element.67.leaf_ref, ...), custom_call_target="tpu_custom_call" | custom-call | flops 1000000 | bytes 10000 | tf_op jit(solution)/shard_map/pallas_call | solution.py:290
  (2 shorter events, 0.1 us)
Async XLA Ops:
  2.3 1.5 %collective-permute-start = (bf16[512,128]{1,0:T(8,128)(2,1)S(1)}, bf16[512,128]{1,0:T(8,128)(2,1)S(1)}, u32[]{:S(2)}, u32[]{:S(2)}) collective-permute-start(bf16[512,128]{1,0:T(8,128)(2,1)S(1)} %get-tuple-element.37), channel_id=1, source_target_pairs={{0,1},{1,0},{2,3},{3,2},{4,5},{5,4},{6,7},{7,6},{8,9},{9,8},{10,11... | collective-permute-start | bytes 393224 | tf_op jit(solution)/shard_map/ppermute | solution.py:19
  4.4 6.8 %collective-permute-start.1 = (bf16[512,128]{1,0:T(8,128)(2,1)S(1)}, bf16[512,128]{1,0:T(8,128)(2,1)S(1)}, u32[]{:S(2)}, u32[]{:S(2)}) collective-permute-start(bf16[512,128]{1,0:T(8,128)(2,1)S(1)} %get-tuple-element.43), channel_id=1, source_target_pairs={{0,2},{1,3},{2,0},{3,1},{4,6},{5,7},{6,4},{7,5},{8,10},{9,11},{10,... | collective-permute-start | bytes 393224 | tf_op jit(solution)/shard_map/ppermute | solution.py:19
  11.8 6.0 %collective-permute-start.2 = (bf16[512,128]{1,0:T(8,128)(2,1)S(1)}, bf16[512,128]{1,0:T(8,128)(2,1)S(1)}, u32[]{:S(2)}, u32[]{:S(2)}) collective-permute-start(bf16[512,128]{1,0:T(8,128)(2,1)S(1)} %get-tuple-element.46), channel_id=1, source_target_pairs={{0,4},{1,5},{2,6},{3,7},{4,0},{5,1},{6,2},{7,3},{8,12},{9,13},{10,... | collective-permute-start | bytes 393224 | tf_op jit(solution)/shard_map/ppermute | solution.py:19
  13.6 7.4 %collective-permute-start.3 = (bf16[256,128]{1,0:T(8,128)(2,1)S(1)}, bf16[256,128]{1,0:T(8,128)(2,1)S(1)}, u32[]{:S(2)}, u32[]{:S(2)}) collective-permute-start(bf16[256,128]{1,0:T(8,128)(2,1)S(1)} %get-tuple-element.54), channel_id=1, source_target_pairs={{0,8},{1,9},{2,10},{3,11},{4,12},{5,13},{6,14},{7,15},{8,0},{9,1},... | collective-permute-start | bytes 196616 | tf_op jit(solution)/shard_map/ppermute | solution.py:19
  18.4 11.9 %collective-permute-start.5 = (bf16[512,128]{1,0:T(8,128)(2,1)S(1)}, bf16[512,128]{1,0:T(8,128)(2,1)S(1)}, u32[]{:S(2)}, u32[]{:S(2)}) collective-permute-start(bf16[512,128]{1,0:T(8,128)(2,1)S(1)} %get-tuple-element.53.sent_ref), channel_id=1, source_target_pairs={{0,8},{1,9},{2,10},{3,11},{4,12},{5,13},{6,14},{7,15},{8,0},{9,1},... | collective-permute-start | bytes 393224 | tf_op jit(solution)/shard_map/ppermute | solution.py:19
  21.8 9.9 %collective-permute-start.4 = (bf16[512,128]{1,0:T(8,128)(2,1)S(1)}, bf16[512,128]{1,0:T(8,128)(2,1)S(1)}, u32[]{:S(2)}, u32[]{:S(2)}) collective-permute-start(bf16[512,128]{1,0:T(8,128)(2,1)S(1)} %get-tuple-element.55), channel_id=1, source_target_pairs={{0,8},{1,9},{2,10},{3,11},{4,12},{5,13},{6,14},{7,15},{8,0},{9,1},... | collective-permute-start | bytes 393224 | tf_op jit(solution)/shard_map/ppermute | solution.py:19
  32.3 5.0 %collective-permute-start.6 = (bf16[512,128]{1,0:T(8,128)(2,1)S(1)}, bf16[512,128]{1,0:T(8,128)(2,1)S(1)}, u32[]{:S(2)}, u32[]{:S(2)}) collective-permute-start(bf16[512,128]{1,0:T(8,128)(2,1)S(1)} %get-tuple-element.59), channel_id=1, source_target_pairs={{0,4},{1,5},{2,6},{3,7},{4,0},{5,1},{6,2},{7,3},{8,12},{9,13},{10,... | collective-permute-start | bytes 393224 | tf_op jit(solution)/shard_map/ppermute | solution.py:19
  37.9 5.0 %collective-permute-start.7 = (bf16[512,128]{1,0:T(8,128)(2,1)S(1)}, bf16[512,128]{1,0:T(8,128)(2,1)S(1)}, u32[]{:S(2)}, u32[]{:S(2)}) collective-permute-start(bf16[512,128]{1,0:T(8,128)(2,1)S(1)} %get-tuple-element.61), channel_id=1, source_target_pairs={{0,2},{1,3},{2,0},{3,1},{4,6},{5,7},{6,4},{7,5},{8,10},{9,11},{10,... | collective-permute-start | bytes 393224 | tf_op jit(solution)/shard_map/ppermute | solution.py:19
  43.5 1.4 %collective-permute-start.8 = (bf16[512,128]{1,0:T(8,128)(2,1)S(1)}, bf16[512,128]{1,0:T(8,128)(2,1)S(1)}, u32[]{:S(2)}, u32[]{:S(2)}) collective-permute-start(bf16[512,128]{1,0:T(8,128)(2,1)S(1)} %get-tuple-element.63), channel_id=1, source_target_pairs={{0,1},{1,0},{2,3},{3,2},{4,5},{5,4},{6,7},{7,6},{8,9},{9,8},{10,11... | collective-permute-start | bytes 393224 | tf_op jit(solution)/shard_map/ppermute | solution.py:19

commit v5 on v4

--- a/solution.py
+++ b/solution.py
@@ -11,7 +11,6 @@
 wide = jnp.float32
 thin = jnp.bfloat16
 lanes = 128
-depth = 256
 scene_chunks = 4
 
 
@@ -51,35 +50,39 @@
     return jnp.where(slots < half, slots, slots - half)
 
 
-def take(row, both):
-    half, width = both.shape[0], both.shape[1] // 2
+def take_plan(row):
+    half = row.shape[1]
     slots = column(row)
     within = fold(slots, half)
     lane = lax.broadcasted_iota(jnp.int32, slots.shape, 1)
-    total = None
-    for at in range(0, half, depth):
-        chosen = jnp.concatenate(
-            [one_hot(within == lane + (at + more)) for more in range(0, depth, lanes)], axis=1
-        )
-        part = mul(chosen, both[at : at + depth])
-        total = part if total is None else total + part
-    return jnp.where(slots < half, total[:, :width], total[:, width:])
-
-
-def place(row, values, half):
-    low = column(row) < half
-    values = values.astype(wide)
-    zeros = jnp.zeros_like(values)
-    spread = jnp.concatenate([jnp.where(low, values, zeros), jnp.where(low, zeros, values)], axis=1)
-    spread = spread.astype(thin)
-    within = fold(row, half)
-    total = None
-    target = lax.broadcasted_iota(jnp.int32, (half, depth), 0)
-    for at in range(0, values.shape[0], depth):
-        chosen = one_hot(target == within[:, at : at + depth])
-        part = mul(chosen, spread[at : at + depth])
-        total = part if total is None else total + part
-    return total
+    chosen = [one_hot(within == lane + at) for at in range(0, half, lanes)]
+    return jnp.concatenate(chosen, axis=1), jnp.where(slots < half, 1.0, 0.0)
+
+
+def take(plan, both):
+    chosen, low = plan
+    total = mul(chosen, both)
+    width = both.shape[1] // 2
+    return jnp.where(low > 0.5, total[:, :width], total[:, width:])
+
+
+def place_plan(row, half):
+    target = lax.broadcasted_iota(jnp.int32, (half, row.shape[1]), 0)
+    return one_hot(target == fold(row, half)), one_hot(column(row) < half)
+
+
+def place(plan, values):
+    chosen, low = plan
+    return mul(chosen, jnp.concatenate([values * low, values * (1 - low)], axis=1))
+
+
+def read(refs):
+    return tuple(ref[...] for ref in refs)
+
+
+def write(refs, values):
+    for ref, value in zip(refs, values):
+        ref[...] = value
 
 
 def compose(outer, inner):
@@ -87,13 +90,8 @@
     digits = jnp.concatenate([outer // 256, outer % 256], axis=0).astype(wide)
     digits = jnp.concatenate([digits[:, :half], digits[:, half:]], axis=0)
     digits = jnp.pad(digits, ((0, 12), (0, 0))).astype(thin)
-    within = fold(inner, half)
-    total = None
-    target = lax.broadcasted_iota(jnp.int32, (depth, inner.shape[1]), 0)
-    for at in range(0, half, depth):
-        chosen = one_hot(target + at == within)
-        part = mul(digits[:, at : at + depth], chosen)
-        total = part if total is None else total + part
+    target = lax.broadcasted_iota(jnp.int32, (half, inner.shape[1]), 0)
+    total = mul(digits, one_hot(target == fold(inner, half)))
     picked = jnp.where(inner < half, total[0:2], total[2:4])
     return (picked[0:1] * 256 + picked[1:2]).astype(jnp.int32)
 
@@ -141,14 +139,14 @@
     loads[1].wait()
     slots = compose(pixel_ref[...], half_row(perm_ref, 0, 1 - bit_of(0)))
     slots_ref[...] = slots
-    loads[2].wait()
+    for load in loads[2:-1]:
+        load.wait()
     for at, part in enumerate(parts):
-        loads[3 + at].wait()
         side, first = divmod(at * chunk, half)
         leafed_ref[pl.ds(first, chunk), pl.ds(side * width, width)] = mul(
             scene_ref[part], leaf_ref[...]
         ).astype(thin)
-    out_ref[...] = take(slots, leafed_ref[...]).astype(thin)
+    out_ref[...] = take(take_plan(slots), leafed_ref[...]).astype(thin)
     loads[-1].wait()
 
 
@@ -156,13 +154,13 @@
     bit = bit_of(0)
     slots = compose(pixel_ref[...], half_row(perm_ref, 0, bit))
     slots_ref[...] = slots
-    own = take(slots, leafed_ref[...]).astype(thin)
+    own = take(take_plan(slots), leafed_ref[...]).astype(thin)
     part_ref[...] = mul(own, pair_weight(panel_ref, 0, bit))
 
 
 def own_kernel(level, coef_ref, perm_ref, panel_ref, part_ref):
     bit = bit_of(level)
-    own = take(half_row(perm_ref, level, bit), coef_ref[...]).astype(thin)
+    own = take(take_plan(half_row(perm_ref, level, bit)), coef_ref[...]).astype(thin)
     part_ref[...] = mul(own, pair_weight(panel_ref, level, bit))
 
 
@@ -201,12 +199,13 @@
     maps = pair[: 2 * width] + pair[2 * width :]
     own_map_ref[...] = split(maps[:width])
     other_map_ref[...] = split(maps[width:, :width])
-    sent_map_ref[...] = split(maps[width:, width:])
+    sent_map_ref[...] = maps[width:, width:].astype(thin)
     back = []
     for at, part in enumerate(parts):
         loads[2 + at].wait()
         back.append(mul_t(echo[part], leaf[...]).astype(thin))
-    back_ref[...] = place(slots[...], jnp.concatenate(back, axis=0), rows // 2).astype(thin)
+    plan = place_plan(slots[...], rows // 2)
+    back_ref[...] = place(plan, jnp.concatenate(back, axis=0)).astype(thin)
 
 
 def own_echo_kernel(
@@ -225,52 +224,61 @@
 def forward_kernel(level, arrived_ref, part_ref, panel_ref, perm_ref, coef_ref, out_ref):
     coefficients = mix(level, arrived_ref, part_ref, panel_ref)
     coef_ref[...] = coefficients
-    slots = half_row(perm_ref, level + 1, 1 - bit_of(level + 1))
-    out_ref[...] = take(slots, coefficients).astype(thin)
+    plan = take_plan(half_row(perm_ref, level + 1, 1 - bit_of(level + 1)))
+    out_ref[...] = take(plan, coefficients).astype(thin)
 
 
 def bracket_kernel(
     level, coef_ref, perm_ref, map_ref, echo_part_ref, sent_ref, arrived_map_ref,
     part_ref, rest_ref, out_ref,
 ):
-    own = take(half_row(perm_ref, level, bit_of(level)), coef_ref[...]).astype(thin)
+    plan = take_plan(half_row(perm_ref, level, bit_of(level)))
+    own = take(plan, coef_ref[...]).astype(thin)
     both = mul(twice(own), map_ref[...]) - echo_part_ref[...]
     width = own.shape[1]
     part_ref[...] = both[:, :width]
     out_ref[...] = both[:, width:].astype(thin)
-    rest_ref[...] = mul(twice(sent_ref[...]), arrived_map_ref[...])
-
-
-def join_kernel(level, arrived_ref, part_ref, map_ref, perm_ref, placed_ref):
+    rest_ref[...] = mul(sent_ref[...], arrived_map_ref[...])
+
+
+def join_kernel(level, arrived_ref, part_ref, map_ref, perm_ref, placed_ref, *plan_refs):
+    bit, half = bit_of(level), placed_ref.shape[0]
     own = part_ref[...] + mul(twice(arrived_ref[...]), map_ref[...])
-    row = half_row(perm_ref, level, bit_of(level))
-    placed_ref[...] = place(row, own.astype(thin), placed_ref.shape[0]).astype(thin)
-
-
-def own_back_kernel(level, coef_ref, panel_ref, perm_ref, placed_ref):
-    bit = bit_of(level)
+    plan = place_plan(half_row(perm_ref, level, bit), half)
+    placed_ref[...] = place(plan, own.astype(thin)).astype(thin)
+    write(plan_refs, place_plan(half_row(perm_ref, level, 1 - bit), half))
+
+
+def own_back_kernel(level, coef_ref, panel_ref, own_ref, other_ref, placed_ref, *plan_refs):
+    bit, half = bit_of(level), placed_ref.shape[0]
     own = mul_t(coef_ref[...], pair_weight(panel_ref, level, bit)).astype(thin)
-    row = half_row(perm_ref, level, bit) if level else perm_ref[...]
-    placed_ref[...] = place(row, own, coef_ref.shape[0]).astype(thin)
-
-
-def backward_kernel(level, arrived_ref, placed_ref, perm_ref, panel_ref, *refs):
+    rows = [own_ref[...], other_ref[...]]
+    if level:
+        rows = [half_row(own_ref, level, bit), half_row(other_ref, level, 1 - bit)]
+    placed_ref[...] = place(place_plan(rows[0], half), own).astype(thin)
+    write(plan_refs, place_plan(rows[1], half))
+
+
+def backward_kernel(
+    level, arrived_ref, placed_ref, chosen_ref, low_ref, panel_ref, *refs
+):
     *rest_ref, coef_ref, out_ref = refs
     arrived = arrived_ref[...]
     if rest_ref:
         arrived = (arrived.astype(wide) + rest_ref[0][...]).astype(thin)
-    row = half_row(perm_ref, level + 1, 1 - bit_of(level + 1))
-    back = place(row, arrived, placed_ref.shape[0]) + placed_ref[...].astype(wide)
+    back = place(read((chosen_ref, low_ref)), arrived) + placed_ref[...].astype(wide)
     back = back.astype(thin)
     coef_ref[...] = back
     weight = pair_weight(panel_ref, level, 1 - bit_of(level))
     out_ref[...] = mul_t(back, weight).astype(thin)
 
 
-def last_kernel(arrived_ref, placed_ref, slots_ref, leaf_ref, scene_ref, image_ref, image, sent):
+def last_kernel(
+    arrived_ref, placed_ref, chosen_ref, low_ref, leaf_ref, scene_ref, image_ref, image, sent
+):
     rows = scene_ref.shape[0]
     chunk = rows // scene_chunks
-    back = place(slots_ref[...], arrived_ref[...], rows // 2)
+    back = place(read((chosen_ref, low_ref)), arrived_ref[...])
     back = unstack((back + placed_ref[...].astype(wide)).astype(thin))
     stores = []
     for at in range(scene_chunks):
@@ -323,6 +331,7 @@
         scratch=[pltpu.SemaphoreType.DMA((4 + scene_chunks,))],
     )
     arrived = swapped(outgoing, "box", 0)
+    place_like = [((half, half), thin), ((half, lanes), thin)]
     own_slots, part = call(
         first_own_kernel, [row_half, mixed], leafed, pixel_near, perms, blocks
     )
@@ -341,7 +350,7 @@
             narrow_map = ((2 * width, width), thin)
             part, own_map, other_map, sent_map, echo_back = call(
                 functools.partial(own_map_kernel, level, last),
-                [mixed, ((2 * width, 2 * width), thin), narrow_map, narrow_map, column_of],
+                [mixed, ((2 * width, 2 * width), thin), narrow_map, ((width, width), thin), column_of],
                 coefficients,
                 perms,
                 blocks,
@@ -365,7 +374,11 @@
             )
         elif level < last:
             part = call(
-                functools.partial(own_kernel, level), [mixed], coefficients, perms, blocks
+                functools.partial(own_kernel, level),
+                [mixed],
+                coefficients,
+                perms,
+                blocks,
             )
     half_wide = ((half, width), wide)
     part, rest, bracket = call(
@@ -379,8 +392,13 @@
         arrived_map,
     )
     arrived_bracket = swapped(bracket, "box", last)
-    placed = call(
-        functools.partial(join_kernel, last), [column_of], arrived, part, other_map, perms
+    placed, *plan = call(
+        functools.partial(join_kernel, last),
+        [column_of] + place_like,
+        arrived,
+        part,
+        other_map,
+        perms,
     )
     arrived, more = arrived_bracket, (rest,)
     for level in reversed(range(last)):
@@ -389,24 +407,24 @@
             [column_of, sent],
             arrived,
             placed,
-            perms,
+            *plan,
             blocks,
             *more,
         )
         arrived, more = swapped(outgoing, "box", level), ()
-        placed = call(
+        placed, *plan = call(
             functools.partial(own_back_kernel, level),
-            [column_of],
+            [column_of] + place_like,
             coefficients,
             blocks,
-            perms if level else own_slots,
+            *((perms, perms) if level else (own_slots, out_slots)),
         )
     return call(
         last_kernel,
         [((rows, samples), thin)],
         arrived,
         placed,
-        out_slots,
+        *plan,
         leaf_near,
         scene_near,
         far_out=True,

time: 46.8 us -> 45.8 us (0.979)
  Pallas kernels: 16 us -> 15 us
    pallas_call x16, Pallas kernels: 16 us -> 15 us  [call(): pl.pallas_call(kernel, out_shape=shapes, in_specs=[near] * len(operands)...]
  transfers between devices with their start and end apart: 9 -> 9, of which waited for: 8 -> 8; matrix products, arithmetic and copies ran while one was open for 0% -> 0% of each run, Pallas kernels for 20% -> 19%
where the time goes in v5:
time: 45.8 us; the launch traced here: 45.6 us
  waiting for transfers between devices  17.9 us (39%)
  Pallas kernels  15 us (33%)
  starting transfers between devices  12.6 us (28%)
    ppermute x9, waiting for transfers between devices, swapped(): lax.ppermute(value, axis, [(i, i ^ 1 << apart) for i in range(lax.axis_si...  17.9 us
    pallas_call x16, Pallas kernels, call(): pl.pallas_call(kernel, out_shape=shapes, in_specs=[near] * len(operands)...  15 us
    ppermute x9, starting transfers between devices, swapped(): lax.ppermute(value, axis, [(i, i ^ 1 << apart) for i in range(lax.axis_si...  12.6 us
  transfers between devices with their start and end apart: 9, of which 8 were waited for; matrix products, arithmetic and copies ran while one was open for 0% of the time, Pallas kernels for 19%

profile of v5, /device:TPU:0, one launch (start us, length us, event | category | flops | bytes accessed | tf_op | source)
XLA Modules:
  0.0 45.6 jit_solution(4841357895922148817)
XLA Ops:
  0.0 2.1 %shard_map.82 = (bf16[1024,512]{1,0:T(8,128)(2,1)S(1)}, bf16[512,128]{1,0:T(8,128)(2,1)S(1)}, s32[1,1024]{1,0:T(1,128)S(1)}, s32[4,1,1024]{2,1,0:T(1,128)S(1)}, ...) custom-call(bf16[1024,512]{1,0:T(8,128)(2,1)} %scene_in.1, ...), custom_call_target="tpu_custom_call" | custom-call | flops 1000000 | bytes 10000 | tf_op jit(solution)/shard_map/pallas_call | solution.py:298
  2.1 0.5 %collective-permute-start = (bf16[512,128]{1,0:T(8,128)(2,1)S(1)}, bf16[512,128]{1,0:T(8,128)(2,1)S(1)}, u32[]{:S(2)}, u32[]{:S(2)}) collective-permute-start(bf16[512,128]{1,0:T(8,128)(2,1)S(1)} %get-tuple-element.49), channel_id=1, source_target_pairs={{0,1},{1,0},{2,3},{3,2},{4,5},{5,4},{6,7},{7,6},{8,9},{9,8},{10,11... | collective-permute-start | bytes 393224 | tf_op jit(solution)/shard_map/ppermute | solution.py:18
  2.6 0.7 %shard_map.83 = (s32[1,512]{1,0:T(1,128)S(1)}, f32[512,256]{1,0:T(8,128)S(1)}) custom-call(bf16[512,256]{1,0:T(8,128)(2,1)S(1)} %get-tuple-element.50.leafed_ref, s32[1,1024]{1,0:T(1,128)S(1)} %get-tuple-element.51.pixel_ref, s32[4,1,1024]{2,1,0:T(1,128)S(1)} %get-tuple-element.52.perm_ref.own_ref.other_ref, ...), custom_call_target="tpu_custom_call" | custom-call | flops 1000000 | bytes 10000 | tf_op jit(solution)/shard_map/pallas_call | solution.py:298
  3.3 0.3 collective-permute-done.arrived_ref
  3.6 0.6 %shard_map.84 = (bf16[512,256]{1,0:T(8,128)(2,1)S(1)}, bf16[512,128]{1,0:T(8,128)(2,1)S(1)}) custom-call(bf16[512,128]{1,0:T(8,128)(2,1)S(1)} %collective-permute-done.arrived_ref, f32[512,256]{1,0:T(8,128)S(1)} %get-tuple-element.54.part_ref, bf16[4,1,4,128,128]{4,3,2,1,0:T(8,128)(2,1)S(1)} %get-tuple-element.53.panel_ref, ...), custom_call_target="tpu_custom_call" | custom-call | flops 1000000 | bytes 10000 | tf_op jit(solution)/shard_map/pallas_call | solution.py:298
  4.2 2.9 %collective-permute-start.1 = (bf16[512,128]{1,0:T(8,128)(2,1)S(1)}, bf16[512,128]{1,0:T(8,128)(2,1)S(1)}, u32[]{:S(2)}, u32[]{:S(2)}) collective-permute-start(bf16[512,128]{1,0:T(8,128)(2,1)S(1)} %get-tuple-element.55), channel_id=1, source_target_pairs={{0,2},{1,3},{2,0},{3,1},{4,6},{5,7},{6,4},{7,5},{8,10},{9,11},{10,... | collective-permute-start | bytes 393224 | tf_op jit(solution)/shard_map/ppermute | solution.py:18
  7.1 3.7 %shard_map.85 = (f32[512,256]{1,0:T(8,128)S(1)}, bf16[256,256]{1,0:T(8,128)(2,1)S(1)}, bf16[256,128]{1,0:T(8,128)(2,1)S(1)}, bf16[128,128]{1,0:T(8,128)(2,1)S(1)}, bf16[512,256]{1,0:T(8,128)(2,1)S(1)}) custom-call(bf16[512,256]{1,0:T(8,128)(2,1)S(1)} %get-tuple-element.56.coef_ref, s32[4,1,1024]{2,1,0:T(1,128)S(1)} %get-tuple-element.52.perm_ref.own_ref.other_ref, ...), custom_call_target="tpu_custom_call" | custom-call | flops 1000000 | bytes 10000 | tf_op jit(solution)/shard_map/pallas_call | solution.py:298
  10.8 0.1 collective-permute-done.1.arrived_ref
  10.9 0.6 %shard_map.86 = (bf16[512,256]{1,0:T(8,128)(2,1)S(1)}, bf16[512,128]{1,0:T(8,128)(2,1)S(1)}) custom-call(bf16[512,128]{1,0:T(8,128)(2,1)S(1)} %collective-permute-done.1.arrived_ref, f32[512,256]{1,0:T(8,128)S(1)} %get-tuple-element.57.part_ref, bf16[4,1,4,128,128]{4,3,2,1,0:T(8,128)(2,1)S(1)} %get-tuple-element.53.panel_ref, ...), custom_call_target="tpu_custom_call" | custom-call | flops 1000000 | bytes 10000 | tf_op jit(solution)/shard_map/pallas_call | solution.py:298
  11.5 1.9 %collective-permute-start.2 = (bf16[512,128]{1,0:T(8,128)(2,1)S(1)}, bf16[512,128]{1,0:T(8,128)(2,1)S(1)}, u32[]{:S(2)}, u32[]{:S(2)}) collective-permute-start(bf16[512,128]{1,0:T(8,128)(2,1)S(1)} %get-tuple-element.58), channel_id=1, source_target_pairs={{0,4},{1,5},{2,6},{3,7},{4,0},{5,1},{6,2},{7,3},{8,12},{9,13},{10,... | collective-permute-start | bytes 393224 | tf_op jit(solution)/shard_map/ppermute | solution.py:18
  13.3 2.6 %collective-permute-start.3 = (bf16[128,128]{1,0:T(8,128)(2,1)S(1)}, bf16[128,128]{1,0:T(8,128)(2,1)S(1)}, u32[]{:S(2)}, u32[]{:S(2)}) collective-permute-start(bf16[128,128]{1,0:T(8,128)(2,1)S(1)} %get-tuple-element.66), channel_id=1, source_target_pairs={{0,8},{1,9},{2,10},{3,11},{4,12},{5,13},{6,14},{7,15},{8,0},{9,1},... | collective-permute-start | bytes 98312 | tf_op jit(solution)/shard_map/ppermute | solution.py:18
  15.9 0.8 %shard_map.87 = (f32[512,256]{1,0:T(8,128)S(1)}, f32[512,256]{1,0:T(8,128)S(1)}) custom-call(bf16[512,256]{1,0:T(8,128)(2,1)S(1)} %get-tuple-element.59.coef_ref, s32[4,1,1024]{2,1,0:T(1,128)S(1)} %get-tuple-element.52.perm_ref.own_ref.other_ref, bf16[4,1,4,128,128]{4,3,2,1,0:T(8,128)(2,1)S(1)} %get-tuple-element.53.panel_ref, ...), custom_call_target="tpu_custom_call" | custom-call | flops 1000000 | bytes 10000 | tf_op jit(solution)/shard_map/pallas_call | solution.py:298
  16.7 0.4 collective-permute-done.2.arrived_ref
  17.1 0.6 %shard_map.88 = (bf16[512,256]{1,0:T(8,128)(2,1)S(1)}, bf16[512,128]{1,0:T(8,128)(2,1)S(1)}) custom-call(bf16[512,128]{1,0:T(8,128)(2,1)S(1)} %collective-permute-done.2.arrived_ref, f32[512,256]{1,0:T(8,128)S(1)} %get-tuple-element.61.part_ref, bf16[4,1,4,128,128]{4,3,2,1,0:T(8,128)(2,1)S(1)} %get-tuple-element.53.panel_ref, ...), custom_call_target="tpu_custom_call" | custom-call | flops 1000000 | bytes 10000 | tf_op jit(solution)/shard_map/pallas_call | solution.py:298
  17.7 2.6 %collective-permute-start.5 = (bf16[512,128]{1,0:T(8,128)(2,1)S(1)}, bf16[512,128]{1,0:T(8,128)(2,1)S(1)}, u32[]{:S(2)}, u32[]{:S(2)}) collective-permute-start(bf16[512,128]{1,0:T(8,128)(2,1)S(1)} %get-tuple-element.65.sent_ref), channel_id=1, source_target_pairs={{0,8},{1,9},{2,10},{3,11},{4,12},{5,13},{6,14},{7,15},{8,0},{9,1},... | collective-permute-start | bytes 393224 | tf_op jit(solution)/shard_map/ppermute | solution.py:18
  20.3 0.6 %shard_map.89 = (f32[512,128]{1,0:T(8,128)S(1)}, f32[512,128]{1,0:T(8,128)S(1)}, bf16[512,128]{1,0:T(8,128)(2,1)S(1)}) custom-call(bf16[512,256]{1,0:T(8,128)(2,1)S(1)} %get-tuple-element.62.coef_ref, s32[4,1,1024]{2,1,0:T(1,128)S(1)} %get-tuple-element.52.perm_ref.own_ref.other_ref, bf16[256,256]{1,0:T(8,128)(2,1)S(1)} %get-tuple-element.63.map_ref, ...), custom_call_target="tpu_custom_call" | custom-call | flops 1000000 | bytes 10000 | tf_op jit(solution)/shard_map/pallas_call | solution.py:298
  21.0 0.5 %collective-permute-start.4 = (bf16[512,128]{1,0:T(8,128)(2,1)S(1)}, bf16[512,128]{1,0:T(8,128)(2,1)S(1)}, u32[]{:S(2)}, u32[]{:S(2)}) collective-permute-start(bf16[512,128]{1,0:T(8,128)(2,1)S(1)} %get-tuple-element.67), channel_id=1, source_target_pairs={{0,8},{1,9},{2,10},{3,11},{4,12},{5,13},{6,14},{7,15},{8,0},{9,1},... | collective-permute-start | bytes 393224 | tf_op jit(solution)/shard_map/ppermute | solution.py:18
  21.5 8.2 %collective-permute-done.5.arrived_ref = bf16[512,128]{1,0:T(8,128)(2,1)S(1)} collective-permute-done((bf16[512,128]{1,0:T(8,128)(2,1)S(1)}, bf16[512,128]{1,0:T(8,128)(2,1)S(1)}, u32[]{:S(2)}, u32[]{:S(2)}) %collective-permute-start.5) | collective-permute-done | bytes 131104 | tf_op jit(solution)/shard_map/ppermute | solution.py:18
  29.7 0.6 %shard_map.90 = (bf16[512,256]{1,0:T(8,128)(2,1)S(1)}, bf16[512,512]{1,0:T(8,128)(2,1)S(1)}, bf16[512,128]{1,0:T(8,128)(2,1)S(1)}) custom-call(bf16[512,128]{1,0:T(8,128)(2,1)S(1)} %collective-permute-done.5.arrived_ref, f32[512,128]{1,0:T(8,128)S(1)} %get-tuple-element.68.part_ref, bf16[256,128]{1,0:T(8,128)(2,1)S(1)} %get-tuple-element.69.map_ref, ...), custom_call_target="tpu_custom_call" | custom-call | flops 1000000 | bytes 10000 | tf_op jit(solution)/shard_map/pallas_call | solution.py:298
  30.2 0.8 %collective-permute-done.4.arrived_ref = bf16[512,128]{1,0:T(8,128)(2,1)S(1)} collective-permute-done((bf16[512,128]{1,0:T(8,128)(2,1)S(1)}, bf16[512,128]{1,0:T(8,128)(2,1)S(1)}, u32[]{:S(2)}, u32[]{:S(2)}) %collective-permute-start.4) | collective-permute-done | bytes 131104 | tf_op jit(solution)/shard_map/ppermute | solution.py:18
  31.1 0.5 %shard_map.91 = (bf16[512,256]{1,0:T(8,128)(2,1)S(1)}, bf16[512,128]{1,0:T(8,128)(2,1)S(1)}) custom-call(bf16[512,128]{1,0:T(8,128)(2,1)S(1)} %collective-permute-done.4.arrived_ref, bf16[512,256]{1,0:T(8,128)(2,1)S(1)} %get-tuple-element.70.placed_ref, bf16[512,512]{1,0:T(8,128)(2,1)S(1)} %get-tuple-element.71.chosen_ref, ...), custom_call_target="tpu_custom_call" | custom-call | flops 1000000 | bytes 10000 | tf_op jit(solution)/shard_map/pallas_call | solution.py:298
  31.6 0.2 collective-permute-start.6
  31.7 0.6 %shard_map.92 = (bf16[512,256]{1,0:T(8,128)(2,1)S(1)}, bf16[512,512]{1,0:T(8,128)(2,1)S(1)}, bf16[512,128]{1,0:T(8,128)(2,1)S(1)}) custom-call(bf16[512,256]{1,0:T(8,128)(2,1)S(1)} %get-tuple-element.75.coef_ref, bf16[4,1,4,128,128]{4,3,2,1,0:T(8,128)(2,1)S(1)} %get-tuple-element.53.panel_ref, ...), custom_call_target="tpu_custom_call" | custom-call | flops 1000000 | bytes 10000 | tf_op jit(solution)/shard_map/pallas_call | solution.py:298
  32.3 4.3 %collective-permute-done.6.arrived_ref = bf16[512,128]{1,0:T(8,128)(2,1)S(1)} collective-permute-done((bf16[512,128]{1,0:T(8,128)(2,1)S(1)}, bf16[512,128]{1,0:T(8,128)(2,1)S(1)}, u32[]{:S(2)}, u32[]{:S(2)}) %collective-permute-start.6) | collective-permute-done | bytes 131104 | tf_op jit(solution)/shard_map/ppermute | solution.py:18
  36.6 0.5 %shard_map.93 = (bf16[512,256]{1,0:T(8,128)(2,1)S(1)}, bf16[512,128]{1,0:T(8,128)(2,1)S(1)}) custom-call(bf16[512,128]{1,0:T(8,128)(2,1)S(1)} %collective-permute-done.6.arrived_ref, bf16[512,256]{1,0:T(8,128)(2,1)S(1)} %get-tuple-element.76.placed_ref, bf16[512,512]{1,0:T(8,128)(2,1)S(1)} %get-tuple-element.77.chosen_ref, ...), custom_call_target="tpu_custom_call" | custom-call | flops 1000000 | bytes 10000 | tf_op jit(solution)/shard_map/pallas_call | solution.py:298
  37.1 1.3 %collective-permute-start.7 = (bf16[512,128]{1,0:T(8,128)(2,1)S(1)}, bf16[512,128]{1,0:T(8,128)(2,1)S(1)}, u32[]{:S(2)}, u32[]{:S(2)}) collective-permute-start(bf16[512,128]{1,0:T(8,128)(2,1)S(1)} %get-tuple-element.79), channel_id=1, source_target_pairs={{0,2},{1,3},{2,0},{3,1},{4,6},{5,7},{6,4},{7,5},{8,10},{9,11},{10,... | collective-permute-start | bytes 393224 | tf_op jit(solution)/shard_map/ppermute | solution.py:18
  38.4 0.6 %shard_map.94 = (bf16[512,256]{1,0:T(8,128)(2,1)S(1)}, bf16[512,512]{1,0:T(8,128)(2,1)S(1)}, bf16[512,128]{1,0:T(8,128)(2,1)S(1)}) custom-call(bf16[512,256]{1,0:T(8,128)(2,1)S(1)} %get-tuple-element.80.coef_ref, bf16[4,1,4,128,128]{4,3,2,1,0:T(8,128)(2,1)S(1)} %get-tuple-element.53.panel_ref, ...), custom_call_target="tpu_custom_call" | custom-call | flops 1000000 | bytes 10000 | tf_op jit(solution)/shard_map/pallas_call | solution.py:298
  39.0 3.1 %collective-permute-done.7.arrived_ref = bf16[512,128]{1,0:T(8,128)(2,1)S(1)} collective-permute-done((bf16[512,128]{1,0:T(8,128)(2,1)S(1)}, bf16[512,128]{1,0:T(8,128)(2,1)S(1)}, u32[]{:S(2)}, u32[]{:S(2)}) %collective-permute-start.7) | collective-permute-done | bytes 131104 | tf_op jit(solution)/shard_map/ppermute | solution.py:18
  42.1 0.5 %shard_map.95 = (bf16[512,256]{1,0:T(8,128)(2,1)S(1)}, bf16[512,128]{1,0:T(8,128)(2,1)S(1)}) custom-call(bf16[512,128]{1,0:T(8,128)(2,1)S(1)} %collective-permute-done.7.arrived_ref, bf16[512,256]{1,0:T(8,128)(2,1)S(1)} %get-tuple-element.81.placed_ref, bf16[512,512]{1,0:T(8,128)(2,1)S(1)} %get-tuple-element.82.chosen_ref, ...), custom_call_target="tpu_custom_call" | custom-call | flops 1000000 | bytes 10000 | tf_op jit(solution)/shard_map/pallas_call | solution.py:298
  42.7 0.6 %shard_map.96 = (bf16[512,256]{1,0:T(8,128)(2,1)S(1)}, bf16[512,512]{1,0:T(8,128)(2,1)S(1)}, bf16[512,128]{1,0:T(8,128)(2,1)S(1)}) custom-call(bf16[512,256]{1,0:T(8,128)(2,1)S(1)} %get-tuple-element.85.coef_ref, bf16[4,1,4,128,128]{4,3,2,1,0:T(8,128)(2,1)S(1)} %get-tuple-element.53.panel_ref, s32[1,512]{1,0:T(1,128)S(1)} %get-tuple-element.86.own_ref, ...), custom_call_target="tpu_custom_call" | custom-call | flops 1000000 | bytes 10000 | tf_op jit(solution)/shard_map/pallas_call | solution.py:298
  43.3 0.7 %collective-permute-done.8.arrived_ref = bf16[512,128]{1,0:T(8,128)(2,1)S(1)} collective-permute-done((bf16[512,128]{1,0:T(8,128)(2,1)S(1)}, bf16[512,128]{1,0:T(8,128)(2,1)S(1)}, u32[]{:S(2)}, u32[]{:S(2)}) %collective-permute-start.8) | collective-permute-done | bytes 131104 | tf_op jit(solution)/shard_map/ppermute | solution.py:18
  44.0 1.6 %shard_map.97 = bf16[1024,512]{1,0:T(8,128)(2,1)} custom-call(bf16[512,128]{1,0:T(8,128)(2,1)S(1)} %collective-permute-done.8.arrived_ref, bf16[512,256]{1,0:T(8,128)(2,1)S(1)} %get-tuple-element.88.placed_ref, bf16[512,512]{1,0:T(8,128)(2,1)S(1)} %get-tuple-element.89.chosen_ref, bf16[512,128]{1,0:T(8,128)(2,1)S(1)} %get-tuple-element.90.low_ref, ...), custom_call_target="tpu_custom_call" | custom-call | flops 1000000 | bytes 10000 | tf_op jit(solution)/shard_map/pallas_call | solution.py:298
  (2 shorter events, 0.1 us)
Async XLA Ops:
  2.1 1.5 %collective-permute-start = (bf16[512,128]{1,0:T(8,128)(2,1)S(1)}, bf16[512,128]{1,0:T(8,128)(2,1)S(1)}, u32[]{:S(2)}, u32[]{:S(2)}) collective-permute-start(bf16[512,128]{1,0:T(8,128)(2,1)S(1)} %get-tuple-element.49), channel_id=1, source_target_pairs={{0,1},{1,0},{2,3},{3,2},{4,5},{5,4},{6,7},{7,6},{8,9},{9,8},{10,11... | collective-permute-start | bytes 393224 | tf_op jit(solution)/shard_map/ppermute | solution.py:18
  4.2 6.8 %collective-permute-start.1 = (bf16[512,128]{1,0:T(8,128)(2,1)S(1)}, bf16[512,128]{1,0:T(8,128)(2,1)S(1)}, u32[]{:S(2)}, u32[]{:S(2)}) collective-permute-start(bf16[512,128]{1,0:T(8,128)(2,1)S(1)} %get-tuple-element.55), channel_id=1, source_target_pairs={{0,2},{1,3},{2,0},{3,1},{4,6},{5,7},{6,4},{7,5},{8,10},{9,11},{10,... | collective-permute-start | bytes 393224 | tf_op jit(solution)/shard_map/ppermute | solution.py:18
  11.5 5.6 %collective-permute-start.2 = (bf16[512,128]{1,0:T(8,128)(2,1)S(1)}, bf16[512,128]{1,0:T(8,128)(2,1)S(1)}, u32[]{:S(2)}, u32[]{:S(2)}) collective-permute-start(bf16[512,128]{1,0:T(8,128)(2,1)S(1)} %get-tuple-element.58), channel_id=1, source_target_pairs={{0,4},{1,5},{2,6},{3,7},{4,0},{5,1},{6,2},{7,3},{8,12},{9,13},{10,... | collective-permute-start | bytes 393224 | tf_op jit(solution)/shard_map/ppermute | solution.py:18
  13.3 7.0 %collective-permute-start.3 = (bf16[128,128]{1,0:T(8,128)(2,1)S(1)}, bf16[128,128]{1,0:T(8,128)(2,1)S(1)}, u32[]{:S(2)}, u32[]{:S(2)}) collective-permute-start(bf16[128,128]{1,0:T(8,128)(2,1)S(1)} %get-tuple-element.66), channel_id=1, source_target_pairs={{0,8},{1,9},{2,10},{3,11},{4,12},{5,13},{6,14},{7,15},{8,0},{9,1},... | collective-permute-start | bytes 98312 | tf_op jit(solution)/shard_map/ppermute | solution.py:18
  17.7 12.0 %collective-permute-start.5 = (bf16[512,128]{1,0:T(8,128)(2,1)S(1)}, bf16[512,128]{1,0:T(8,128)(2,1)S(1)}, u32[]{:S(2)}, u32[]{:S(2)}) collective-permute-start(bf16[512,128]{1,0:T(8,128)(2,1)S(1)} %get-tuple-element.65.sent_ref), channel_id=1, source_target_pairs={{0,8},{1,9},{2,10},{3,11},{4,12},{5,13},{6,14},{7,15},{8,0},{9,1},... | collective-permute-start | bytes 393224 | tf_op jit(solution)/shard_map/ppermute | solution.py:18
  21.0 10.1 %collective-permute-start.4 = (bf16[512,128]{1,0:T(8,128)(2,1)S(1)}, bf16[512,128]{1,0:T(8,128)(2,1)S(1)}, u32[]{:S(2)}, u32[]{:S(2)}) collective-permute-start(bf16[512,128]{1,0:T(8,128)(2,1)S(1)} %get-tuple-element.67), channel_id=1, source_target_pairs={{0,8},{1,9},{2,10},{3,11},{4,12},{5,13},{6,14},{7,15},{8,0},{9,1},... | collective-permute-start | bytes 393224 | tf_op jit(solution)/shard_map/ppermute | solution.py:18
  31.6 5.0 %collective-permute-start.6 = (bf16[512,128]{1,0:T(8,128)(2,1)S(1)}, bf16[512,128]{1,0:T(8,128)(2,1)S(1)}, u32[]{:S(2)}, u32[]{:S(2)}) collective-permute-start(bf16[512,128]{1,0:T(8,128)(2,1)S(1)} %get-tuple-element.74), channel_id=1, source_target_pairs={{0,4},{1,5},{2,6},{3,7},{4,0},{5,1},{6,2},{7,3},{8,12},{9,13},{10,... | collective-permute-start | bytes 393224 | tf_op jit(solution)/shard_map/ppermute | solution.py:18
  37.1 5.0 %collective-permute-start.7 = (bf16[512,128]{1,0:T(8,128)(2,1)S(1)}, bf16[512,128]{1,0:T(8,128)(2,1)S(1)}, u32[]{:S(2)}, u32[]{:S(2)}) collective-permute-start(bf16[512,128]{1,0:T(8,128)(2,1)S(1)} %get-tuple-element.79), channel_id=1, source_target_pairs={{0,2},{1,3},{2,0},{3,1},{4,6},{5,7},{6,4},{7,5},{8,10},{9,11},{10,... | collective-permute-start | bytes 393224 | tf_op jit(solution)/shard_map/ppermute | solution.py:18
  42.6 1.4 %collective-permute-start.8 = (bf16[512,128]{1,0:T(8,128)(2,1)S(1)}, bf16[512,128]{1,0:T(8,128)(2,1)S(1)}, u32[]{:S(2)}, u32[]{:S(2)}) collective-permute-start(bf16[512,128]{1,0:T(8,128)(2,1)S(1)} %get-tuple-element.84), channel_id=1, source_target_pairs={{0,1},{1,0},{2,3},{3,2},{4,5},{5,4},{6,7},{7,6},{8,9},{9,8},{10,11... | collective-permute-start | bytes 393224 | tf_op jit(solution)/shard_map/ppermute | solution.py:18

commit v6 on v5

--- a/solution.py
+++ b/solution.py
@@ -74,15 +74,6 @@
 def place(plan, values):
     chosen, low = plan
     return mul(chosen, jnp.concatenate([values * low, values * (1 - low)], axis=1))
-
-
-def read(refs):
-    return tuple(ref[...] for ref in refs)
-
-
-def write(refs, values):
-    for ref, value in zip(refs, values):
-        ref[...] = value
 
 
 def compose(outer, inner):
@@ -173,24 +164,54 @@
     return jnp.concatenate([values, values], axis=1)
 
 
-def own_map_kernel(
-    level, last, coef_ref, perm_ref, panel_ref, echo_in, leaf_in, slots_in,
-    part_ref, own_map_ref, other_map_ref, sent_map_ref, back_ref, echo, leaf, slots, done,
-):
+def echo_loads(echo_in, leaf_in, slots_in, echo, leaf, slots, done):
     rows = echo.shape[0]
     chunk = rows // scene_chunks
     parts = [pl.ds(at * chunk, chunk) for at in range(scene_chunks)]
     pairs = [(slots_in, slots), (leaf_in, leaf)]
     pairs += [(echo_in.at[part], echo.at[part]) for part in parts]
-    loads = [
+    return [
         pltpu.make_async_copy(source, target, done.at[at])
         for at, (source, target) in enumerate(pairs)
     ]
-    for load in loads:
-        load.start()
+
+
+def echo_back(loads, echo, leaf, slots, back_ref):
+    half = echo.shape[0] // 2
+    chunk = echo.shape[0] // scene_chunks
+    loads[0].wait()
+    plan = place_plan(slots[...], half)
+    loads[1].wait()
+    back = []
+    for at in range(scene_chunks):
+        loads[2 + at].wait()
+        back.append(mul_t(echo[pl.ds(at * chunk, chunk)], leaf[...]).astype(thin))
+    back_ref[...] = place(plan, jnp.concatenate(back, axis=0)).astype(thin)
+
+
+def own_map_kernel(
+    level, last, coef_ref, perm_ref, panel_ref, echo_in, leaf_in, slots_in,
+    part_ref, own_map_ref, other_map_ref, sent_map_ref, back_ref, echo, leaf, slots, done,
+):
+    loads = echo_loads(echo_in, leaf_in, slots_in, echo, leaf, slots, done)
+    early = bit_of(0) == 0
+
+    @pl.when(early)
+    def _():
+        for load in loads:
+            load.start()
+
+    @pl.when(jnp.logical_not(early))
+    def _():
+        loads[1].start()
+        loads[1].wait()
+
     own_kernel(level, coef_ref, perm_ref, panel_ref, part_ref)
-    loads[0].wait()
-    loads[1].wait()
+
+    @pl.when(early)
+    def _():
+        echo_back(loads, echo, leaf, slots, back_ref)
+
     gram = split(mul_t(leaf[...], leaf[...]))
     both = pair_weights(panel_ref, last)
     width = both.shape[0] // 2
@@ -200,19 +221,6 @@
     own_map_ref[...] = split(maps[:width])
     other_map_ref[...] = split(maps[width:, :width])
     sent_map_ref[...] = maps[width:, width:].astype(thin)
-    back = []
-    for at, part in enumerate(parts):
-        loads[2 + at].wait()
-        back.append(mul_t(echo[part], leaf[...]).astype(thin))
-    plan = place_plan(slots[...], rows // 2)
-    back_ref[...] = place(plan, jnp.concatenate(back, axis=0)).astype(thin)
-
-
-def own_echo_kernel(
-    level, last, coef_ref, perm_ref, panel_ref, back_ref, part_ref, echo_part_ref
-):
-    own_kernel(level, coef_ref, perm_ref, panel_ref, part_ref)
-    echo_part_ref[...] = mul_t(back_ref[...], pair_weights(panel_ref, last))
 
 
 def mix(level, arrived_ref, part_ref, panel_ref):
@@ -228,10 +236,47 @@
     out_ref[...] = take(plan, coefficients).astype(thin)
 
 
+def own_echo_kernel(
+    level, last, coef_ref, perm_ref, panel_ref, back_ref, part_ref, echo_part_ref
+):
+    own_kernel(level, coef_ref, perm_ref, panel_ref, part_ref)
+
+    @pl.when(bit_of(0) == 0)
+    def _():
+        echo_part_ref[...] = mul_t(back_ref[...], pair_weights(panel_ref, last))
+
+
+def make_plans(perm_ref, slots_refs, chosen_ref, low_ref):
+    half = chosen_ref.shape[1]
+    for level in range(perm_ref.shape[0]):
+        bit = bit_of(level)
+        for side in range(2):
+            row = half_row(perm_ref, level, bit if side == 0 else 1 - bit)
+            if level == 0:
+                row = slots_refs[side][...]
+            chosen_ref[2 * level + side], low_ref[2 * level + side] = place_plan(row, half)
+
+
 def bracket_kernel(
-    level, coef_ref, perm_ref, map_ref, echo_part_ref, sent_ref, arrived_map_ref,
-    part_ref, rest_ref, out_ref,
-):
+    level, coef_ref, perm_ref, map_ref, panel_ref, early_ref, own_slots_ref, out_slots_ref,
+    sent_ref, arrived_map_ref, echo_in, leaf_in, slots_in,
+    part_ref, rest_ref, out_ref, chosen_ref, low_ref, echo_part_ref, back_ref, echo, leaf, slots, done,
+):
+    loads = echo_loads(echo_in, leaf_in, slots_in, echo, leaf, slots, done)
+    early = bit_of(0) == 0
+
+    @pl.when(early)
+    def _():
+        echo_part_ref[...] = early_ref[...]
+
+    @pl.when(jnp.logical_not(early))
+    def _():
+        for load in loads:
+            load.start()
+        make_plans(perm_ref, (own_slots_ref, out_slots_ref), chosen_ref, low_ref)
+        echo_back(loads, echo, leaf, slots, back_ref)
+        echo_part_ref[...] = mul_t(back_ref[...], pair_weights(panel_ref, level))
+
     plan = take_plan(half_row(perm_ref, level, bit_of(level)))
     own = take(plan, coef_ref[...]).astype(thin)
     both = mul(twice(own), map_ref[...]) - echo_part_ref[...]
@@ -241,32 +286,39 @@
     rest_ref[...] = mul(sent_ref[...], arrived_map_ref[...])
 
 
-def join_kernel(level, arrived_ref, part_ref, map_ref, perm_ref, placed_ref, *plan_refs):
-    bit, half = bit_of(level), placed_ref.shape[0]
+def plan_kernel(
+    perm_ref, own_slots_ref, out_slots_ref, chosen_in, low_in, chosen_ref, low_ref
+):
+    del chosen_in, low_in
+
+    @pl.when(bit_of(0) == 0)
+    def _():
+        make_plans(perm_ref, (own_slots_ref, out_slots_ref), chosen_ref, low_ref)
+
+
+def planned(level, side, chosen_ref, low_ref):
+    return chosen_ref[2 * level + side], low_ref[2 * level + side]
+
+
+def join_kernel(level, arrived_ref, part_ref, map_ref, chosen_ref, low_ref, placed_ref):
     own = part_ref[...] + mul(twice(arrived_ref[...]), map_ref[...])
-    plan = place_plan(half_row(perm_ref, level, bit), half)
+    plan = planned(level, 0, chosen_ref, low_ref)
     placed_ref[...] = place(plan, own.astype(thin)).astype(thin)
-    write(plan_refs, place_plan(half_row(perm_ref, level, 1 - bit), half))
-
-
-def own_back_kernel(level, coef_ref, panel_ref, own_ref, other_ref, placed_ref, *plan_refs):
-    bit, half = bit_of(level), placed_ref.shape[0]
-    own = mul_t(coef_ref[...], pair_weight(panel_ref, level, bit)).astype(thin)
-    rows = [own_ref[...], other_ref[...]]
-    if level:
-        rows = [half_row(own_ref, level, bit), half_row(other_ref, level, 1 - bit)]
-    placed_ref[...] = place(place_plan(rows[0], half), own).astype(thin)
-    write(plan_refs, place_plan(rows[1], half))
-
-
-def backward_kernel(
-    level, arrived_ref, placed_ref, chosen_ref, low_ref, panel_ref, *refs
-):
+
+
+def own_back_kernel(level, coef_ref, panel_ref, chosen_ref, low_ref, placed_ref):
+    own = mul_t(coef_ref[...], pair_weight(panel_ref, level, bit_of(level))).astype(thin)
+    plan = planned(level, 0, chosen_ref, low_ref)
+    placed_ref[...] = place(plan, own).astype(thin)
+
+
+def backward_kernel(level, arrived_ref, placed_ref, chosen_ref, low_ref, panel_ref, *refs):
     *rest_ref, coef_ref, out_ref = refs
     arrived = arrived_ref[...]
     if rest_ref:
         arrived = (arrived.astype(wide) + rest_ref[0][...]).astype(thin)
-    back = place(read((chosen_ref, low_ref)), arrived) + placed_ref[...].astype(wide)
+    plan = planned(level + 1, 1, chosen_ref, low_ref)
+    back = place(plan, arrived) + placed_ref[...].astype(wide)
     back = back.astype(thin)
     coef_ref[...] = back
     weight = pair_weight(panel_ref, level, 1 - bit_of(level))
@@ -278,7 +330,7 @@
 ):
     rows = scene_ref.shape[0]
     chunk = rows // scene_chunks
-    back = place(read((chosen_ref, low_ref)), arrived_ref[...])
+    back = place(planned(0, 1, chosen_ref, low_ref), arrived_ref[...])
     back = unstack((back + placed_ref[...].astype(wide)).astype(thin))
     stores = []
     for at in range(scene_chunks):
@@ -291,7 +343,7 @@
         store.wait()
 
 
-def call(kernel, outs, *operands, far=(), far_out=False, scratch=()):
+def call(kernel, outs, *operands, far=(), far_out=False, scratch=(), aliases={}):
     shapes = tuple(jax.ShapeDtypeStruct(shape, kind) for shape, kind in outs)
     near, off = pl.BlockSpec(memory_space=pltpu.VMEM), pl.BlockSpec(memory_space=pltpu.HBM)
     away = tuple(pltpu.with_memory_space_constraint(array, pltpu.HBM) for array in far)
@@ -301,6 +353,7 @@
         in_specs=[near] * len(operands) + [off] * len(far),
         out_specs=tuple(off if far_out else near for _ in shapes),
         scratch_shapes=scratch,
+        input_output_aliases=aliases,
         compiler_params=pltpu.CompilerParams(vmem_limit_bytes=16 * 2**20),
         cost_estimate=pl.CostEstimate(flops=10**6, bytes_accessed=10**4, transcendentals=0),
     )(*operands, *away)
@@ -336,6 +389,12 @@
         first_own_kernel, [row_half, mixed], leafed, pixel_near, perms, blocks
     )
     last = levels - 1
+    echo_scratch = [
+        pltpu.VMEM(echoes.shape, thin),
+        pltpu.VMEM(source_leaf.shape, thin),
+        pltpu.VMEM(pulse_slot.shape, jnp.int32),
+        pltpu.SemaphoreType.DMA((2 + scene_chunks,)),
+    ]
     for level in range(1, levels):
         coefficients, outgoing = call(
             functools.partial(forward_kernel, level - 1),
@@ -348,29 +407,24 @@
         arrived = swapped(outgoing, "box", level)
         if level == 1:
             narrow_map = ((2 * width, width), thin)
-            part, own_map, other_map, sent_map, echo_back = call(
+            part, own_map, other_map, sent_map, early = call(
                 functools.partial(own_map_kernel, level, last),
                 [mixed, ((2 * width, 2 * width), thin), narrow_map, ((width, width), thin), column_of],
                 coefficients,
                 perms,
                 blocks,
                 far=(echoes, source_leaf, pulse_slot),
-                scratch=[
-                    pltpu.VMEM(echoes.shape, thin),
-                    pltpu.VMEM(source_leaf.shape, thin),
-                    pltpu.VMEM(pulse_slot.shape, jnp.int32),
-                    pltpu.SemaphoreType.DMA((2 + scene_chunks,)),
-                ],
+                scratch=echo_scratch,
             )
             arrived_map = swapped(sent_map, "box", last)
         elif level == 2:
-            part, echo_part = call(
+            part, early = call(
                 functools.partial(own_echo_kernel, level, last),
                 [mixed, mixed],
                 coefficients,
                 perms,
                 blocks,
-                echo_back,
+                early,
             )
         elif level < last:
             part = call(
@@ -381,24 +435,29 @@
                 blocks,
             )
     half_wide = ((half, width), wide)
-    part, rest, bracket = call(
+    plan_like = [((2 * levels, half, half), thin), ((2 * levels, half, lanes), thin)]
+    part, rest, bracket, *plans = call(
         functools.partial(bracket_kernel, last),
-        [half_wide, half_wide, sent],
+        [half_wide, half_wide, sent] + plan_like,
         coefficients,
         perms,
         own_map,
-        echo_part,
+        blocks,
+        early,
+        own_slots,
+        out_slots,
         outgoing,
         arrived_map,
+        far=(echoes, source_leaf, pulse_slot),
+        scratch=[pltpu.VMEM((half, 2 * width), wide), pltpu.VMEM((half, 2 * width), thin)]
+        + echo_scratch,
     )
     arrived_bracket = swapped(bracket, "box", last)
-    placed, *plan = call(
-        functools.partial(join_kernel, last),
-        [column_of] + place_like,
-        arrived,
-        part,
-        other_map,
-        perms,
+    plans = call(
+        plan_kernel, plan_like, perms, own_slots, out_slots, *plans, aliases={3: 0, 4: 1}
+    )
+    placed = call(
+        functools.partial(join_kernel, last), [column_of], arrived, part, other_map, *plans
     )
     arrived, more = arrived_bracket, (rest,)
     for level in reversed(range(last)):
@@ -407,24 +466,20 @@
             [column_of, sent],
             arrived,
             placed,
-            *plan,
+            *plans,
             blocks,
             *more,
         )
         arrived, more = swapped(outgoing, "box", level), ()
-        placed, *plan = call(
-            functools.partial(own_back_kernel, level),
-            [column_of] + place_like,
-            coefficients,
-            blocks,
-            *((perms, perms) if level else (own_slots, out_slots)),
+        placed = call(
+            functools.partial(own_back_kernel, level), [column_of], coefficients, blocks, *plans
         )
     return call(
         last_kernel,
         [((rows, samples), thin)],
         arrived,
         placed,
-        *plan,
+        *plans,
         leaf_near,
         scene_near,
         far_out=True,

time: 45.8 us -> 45.6 us (level)
  waiting for transfers between devices: 17.9 us -> 10.8 us
  starting transfers between devices: 12.6 us -> 17.2 us
  Pallas kernels: 15 us -> 17.1 us
    ppermute x9, waiting for transfers between devices: 17.9 us -> 10.8 us  [swapped(): lax.ppermute(value, axis, [(i, i ^ 1 << apart) for i in range(lax.axis_si...]
    ppermute x9, starting transfers between devices: 12.6 us -> 17.2 us  [swapped(): lax.ppermute(value, axis, [(i, i ^ 1 << apart) for i in range(lax.axis_si...]
    pallas_call x16 -> x17, Pallas kernels: 15 us -> 17.1 us  [call(): pl.pallas_call(kernel, out_shape=shapes, in_specs=[near] * len(operands)...]
  transfers between devices with their start and end apart: 9 -> 9, of which waited for: 8 -> 7; matrix products, arithmetic and copies ran while one was open for 0% -> 0% of each run, Pallas kernels for 19% -> 24%
where the time goes in v6:
time: 45.6 us; the launch traced here: 45.4 us
  starting transfers between devices  17.2 us (38%)
  Pallas kernels  17.1 us (38%)
  waiting for transfers between devices  10.8 us (24%)
    ppermute x9, starting transfers between devices, swapped(): lax.ppermute(value, axis, [(i, i ^ 1 << apart) for i in range(lax.axis_si...  17.2 us
    pallas_call x17, Pallas kernels, call(): pl.pallas_call(kernel, out_shape=shapes, in_specs=[near] * len(operands)...  17.1 us
    ppermute x9, waiting for transfers between devices, swapped(): lax.ppermute(value, axis, [(i, i ^ 1 << apart) for i in range(lax.axis_si...  10.8 us
  transfers between devices with their start and end apart: 9, of which 7 were waited for; matrix products, arithmetic and copies ran while one was open for 0% of the time, Pallas kernels for 24%

profile of v6, /device:TPU:0, one launch (start us, length us, event | category | flops | bytes accessed | tf_op | source)
XLA Modules:
  0.0 45.4 jit_solution(10788265622314088654)
XLA Ops:
  0.0 2.1 %shard_map.82 = (bf16[1024,512]{1,0:T(8,128)(2,1)S(1)}, bf16[512,128]{1,0:T(8,128)(2,1)S(1)}, s32[1,1024]{1,0:T(1,128)S(1)}, s32[4,1,1024]{2,1,0:T(1,128)S(1)}, ...) custom-call(bf16[1024,512]{1,0:T(8,128)(2,1)} %scene_in.1, ...), custom_call_target="tpu_custom_call" | custom-call | flops 1000000 | bytes 10000 | tf_op jit(solution)/shard_map/pallas_call | solution.py:350
  2.1 0.5 %collective-permute-start = (bf16[512,128]{1,0:T(8,128)(2,1)S(1)}, bf16[512,128]{1,0:T(8,128)(2,1)S(1)}, u32[]{:S(2)}, u32[]{:S(2)}) collective-permute-start(bf16[512,128]{1,0:T(8,128)(2,1)S(1)} %get-tuple-element.41), channel_id=1, source_target_pairs={{0,1},{1,0},{2,3},{3,2},{4,5},{5,4},{6,7},{7,6},{8,9},{9,8},{10,11... | collective-permute-start | bytes 393224 | tf_op jit(solution)/shard_map/ppermute | solution.py:18
  2.6 0.7 %shard_map.83 = (s32[1,512]{1,0:T(1,128)S(1)}, f32[512,256]{1,0:T(8,128)S(1)}) custom-call(bf16[512,256]{1,0:T(8,128)(2,1)S(1)} %get-tuple-element.42.leafed_ref, s32[1,1024]{1,0:T(1,128)S(1)} %get-tuple-element.43.pixel_ref, s32[4,1,1024]{2,1,0:T(1,128)S(1)} %get-tuple-element.44.perm_ref, bf16[4,1,4,128,128]{4,3,2,1,0:T(8,128)(2,1)S(1)} %get-tuple-element.45.panel_ref), custom_call_target="tpu_custom_call" | custom-call | flops 1000000 | bytes 10000 | tf_op jit(solution)/shard_map/pallas_call | solution.py:350
  3.3 0.3 collective-permute-done.arrived_ref
  3.6 0.6 %shard_map.84 = (bf16[512,256]{1,0:T(8,128)(2,1)S(1)}, bf16[512,128]{1,0:T(8,128)(2,1)S(1)}) custom-call(bf16[512,128]{1,0:T(8,128)(2,1)S(1)} %collective-permute-done.arrived_ref, f32[512,256]{1,0:T(8,128)S(1)} %get-tuple-element.46.part_ref, bf16[4,1,4,128,128]{4,3,2,1,0:T(8,128)(2,1)S(1)} %get-tuple-element.45.panel_ref, ...), custom_call_target="tpu_custom_call" | custom-call | flops 1000000 | bytes 10000 | tf_op jit(solution)/shard_map/pallas_call | solution.py:350
  4.2 2.9 %collective-permute-start.1 = (bf16[512,128]{1,0:T(8,128)(2,1)S(1)}, bf16[512,128]{1,0:T(8,128)(2,1)S(1)}, u32[]{:S(2)}, u32[]{:S(2)}) collective-permute-start(bf16[512,128]{1,0:T(8,128)(2,1)S(1)} %get-tuple-element.47), channel_id=1, source_target_pairs={{0,2},{1,3},{2,0},{3,1},{4,6},{5,7},{6,4},{7,5},{8,10},{9,11},{10,... | collective-permute-start | bytes 393224 | tf_op jit(solution)/shard_map/ppermute | solution.py:18
  7.1 3.8 %shard_map.85 = (f32[512,256]{1,0:T(8,128)S(1)}, bf16[256,256]{1,0:T(8,128)(2,1)S(1)}, bf16[256,128]{1,0:T(8,128)(2,1)S(1)}, bf16[128,128]{1,0:T(8,128)(2,1)S(1)}, bf16[512,256]{1,0:T(8,128)(2,1)S(1)}) custom-call(bf16[512,256]{1,0:T(8,128)(2,1)S(1)} %get-tuple-element.48.coef_ref, s32[4,1,1024]{2,1,0:T(1,128)S(1)} %get-tuple-element.44.perm_ref, ...), custom_call_target="tpu_custom_call" | custom-call | flops 1000000 | bytes 10000 | tf_op jit(solution)/shard_map/pallas_call | solution.py:350
  11.0 0.6 %shard_map.86 = (bf16[512,256]{1,0:T(8,128)(2,1)S(1)}, bf16[512,128]{1,0:T(8,128)(2,1)S(1)}) custom-call(bf16[512,128]{1,0:T(8,128)(2,1)S(1)} %collective-permute-done.1.arrived_ref, f32[512,256]{1,0:T(8,128)S(1)} %get-tuple-element.49.part_ref, bf16[4,1,4,128,128]{4,3,2,1,0:T(8,128)(2,1)S(1)} %get-tuple-element.45.panel_ref, ...), custom_call_target="tpu_custom_call" | custom-call | flops 1000000 | bytes 10000 | tf_op jit(solution)/shard_map/pallas_call | solution.py:350
  11.5 1.8 %collective-permute-start.2 = (bf16[512,128]{1,0:T(8,128)(2,1)S(1)}, bf16[512,128]{1,0:T(8,128)(2,1)S(1)}, u32[]{:S(2)}, u32[]{:S(2)}) collective-permute-start(bf16[512,128]{1,0:T(8,128)(2,1)S(1)} %get-tuple-element.50), channel_id=1, source_target_pairs={{0,4},{1,5},{2,6},{3,7},{4,0},{5,1},{6,2},{7,3},{8,12},{9,13},{10,... | collective-permute-start | bytes 393224 | tf_op jit(solution)/shard_map/ppermute | solution.py:18
  13.3 2.6 %collective-permute-start.3 = (bf16[128,128]{1,0:T(8,128)(2,1)S(1)}, bf16[128,128]{1,0:T(8,128)(2,1)S(1)}, u32[]{:S(2)}, u32[]{:S(2)}) collective-permute-start(bf16[128,128]{1,0:T(8,128)(2,1)S(1)} %get-tuple-element.60), channel_id=1, source_target_pairs={{0,8},{1,9},{2,10},{3,11},{4,12},{5,13},{6,14},{7,15},{8,0},{9,1},... | collective-permute-start | bytes 98312 | tf_op jit(solution)/shard_map/ppermute | solution.py:18
  15.9 0.8 %shard_map.87 = (f32[512,256]{1,0:T(8,128)S(1)}, f32[512,256]{1,0:T(8,128)S(1)}) custom-call(bf16[512,256]{1,0:T(8,128)(2,1)S(1)} %get-tuple-element.51.coef_ref, s32[4,1,1024]{2,1,0:T(1,128)S(1)} %get-tuple-element.44.perm_ref, bf16[4,1,4,128,128]{4,3,2,1,0:T(8,128)(2,1)S(1)} %get-tuple-element.45.panel_ref, bf16[512,256]{1,0:T(8,128)(2,1)S(1)} %get-tuple-element.52.back_ref), custom_call_target="tpu_custom_call" | custom-call | flops 1000000 | bytes 10000 | tf_op jit(solution)/shard_map/pallas_call | solution.py:350
  16.7 0.2 collective-permute-done.2.arrived_ref
  16.9 0.6 %shard_map.88 = (bf16[512,256]{1,0:T(8,128)(2,1)S(1)}, bf16[512,128]{1,0:T(8,128)(2,1)S(1)}) custom-call(bf16[512,128]{1,0:T(8,128)(2,1)S(1)} %collective-permute-done.2.arrived_ref, f32[512,256]{1,0:T(8,128)S(1)} %get-tuple-element.53.part_ref, bf16[4,1,4,128,128]{4,3,2,1,0:T(8,128)(2,1)S(1)} %get-tuple-element.45.panel_ref, ...), custom_call_target="tpu_custom_call" | custom-call | flops 1000000 | bytes 10000 | tf_op jit(solution)/shard_map/pallas_call | solution.py:350
  17.5 2.6 %collective-permute-start.5 = (bf16[512,128]{1,0:T(8,128)(2,1)S(1)}, bf16[512,128]{1,0:T(8,128)(2,1)S(1)}, u32[]{:S(2)}, u32[]{:S(2)}) collective-permute-start(bf16[512,128]{1,0:T(8,128)(2,1)S(1)} %get-tuple-element.59.sent_ref), channel_id=1, source_target_pairs={{0,8},{1,9},{2,10},{3,11},{4,12},{5,13},{6,14},{7,15},{8,0},{9,1},... | collective-permute-start | bytes 393224 | tf_op jit(solution)/shard_map/ppermute | solution.py:18
  20.1 0.7 %shard_map.89 = (f32[512,128]{1,0:T(8,128)S(1)}, f32[512,128]{1,0:T(8,128)S(1)}, bf16[512,128]{1,0:T(8,128)(2,1)S(1)}, bf16[8,512,512]{2,1,0:T(8,128)(2,1)S(1)}, bf16[8,512,128]{2,1,0:T(8,128)(2,1)S(1)}) custom-call(bf16[512,256]{1,0:T(8,128)(2,1)S(1)} %get-tuple-element.54.coef_ref, s32[4,1,1024]{2,1,0:T(1,128)S(1)} %get-tuple-element.44.perm_ref, ...), custom_call_target="tpu_custom_call" | custom-call | flops 1000000 | bytes 10000 | tf_op jit(solution)/shard_map/pallas_call | solution.py:350
  20.8 0.7 %collective-permute-start.4 = (bf16[512,128]{1,0:T(8,128)(2,1)S(1)}, bf16[512,128]{1,0:T(8,128)(2,1)S(1)}, u32[]{:S(2)}, u32[]{:S(2)}) collective-permute-start(bf16[512,128]{1,0:T(8,128)(2,1)S(1)} %get-tuple-element.61), channel_id=1, source_target_pairs={{0,8},{1,9},{2,10},{3,11},{4,12},{5,13},{6,14},{7,15},{8,0},{9,1},... | collective-permute-start | bytes 393224 | tf_op jit(solution)/shard_map/ppermute | solution.py:18
  21.5 2.0 %shard_map.90 = (bf16[8,512,512]{2,1,0:T(8,128)(2,1)S(1)}, bf16[8,512,128]{2,1,0:T(8,128)(2,1)S(1)}) custom-call(s32[4,1,1024]{2,1,0:T(1,128)S(1)} %get-tuple-element.44.perm_ref, s32[1,512]{1,0:T(1,128)S(1)} %get-tuple-element.57.own_slots_ref, s32[1,512]{1,0:T(1,128)S(1)} %get-tuple-element.58.out_slots_ref, ...), custom_call_target="tpu_custom_call", output_to_operand_aliasing={{0}: (3, {}), {1}: (4, {})} | custom-call | flops 1000000 | bytes 10000 | tf_op jit(solution)/shard_map/pallas_call | solution.py:350
  23.5 1.5 %collective-permute-done.5.arrived_ref = bf16[512,128]{1,0:T(8,128)(2,1)S(1)} collective-permute-done((bf16[512,128]{1,0:T(8,128)(2,1)S(1)}, bf16[512,128]{1,0:T(8,128)(2,1)S(1)}, u32[]{:S(2)}, u32[]{:S(2)}) %collective-permute-start.5) | collective-permute-done | bytes 131104 | tf_op jit(solution)/shard_map/ppermute | solution.py:18
  25.0 0.6 %shard_map.91.placed_ref = bf16[512,256]{1,0:T(8,128)(2,1)S(1)} custom-call(bf16[512,128]{1,0:T(8,128)(2,1)S(1)} %collective-permute-done.5.arrived_ref, f32[512,128]{1,0:T(8,128)S(1)} %get-tuple-element.62.part_ref, bf16[256,128]{1,0:T(8,128)(2,1)S(1)} %get-tuple-element.63.map_ref, bf16[8,512,512]{2,1,0:T(8,128)(2,1)S(1)} %get-tuple-element.66.chosen_ref, ...), custom_call_target="tpu_custom_call" | custom-call | flops 1000000 | bytes 10000 | tf_op jit(solution)/shard_map/pallas_call | solution.py:350
  25.6 1.2 %collective-permute-done.4.arrived_ref = bf16[512,128]{1,0:T(8,128)(2,1)S(1)} collective-permute-done((bf16[512,128]{1,0:T(8,128)(2,1)S(1)}, bf16[512,128]{1,0:T(8,128)(2,1)S(1)}, u32[]{:S(2)}, u32[]{:S(2)}) %collective-permute-start.4) | collective-permute-done | bytes 131104 | tf_op jit(solution)/shard_map/ppermute | solution.py:18
  26.7 0.5 %shard_map.92 = (bf16[512,256]{1,0:T(8,128)(2,1)S(1)}, bf16[512,128]{1,0:T(8,128)(2,1)S(1)}) custom-call(bf16[512,128]{1,0:T(8,128)(2,1)S(1)} %collective-permute-done.4.arrived_ref, bf16[512,256]{1,0:T(8,128)(2,1)S(1)} %shard_map.91.placed_ref, bf16[8,512,512]{2,1,0:T(8,128)(2,1)S(1)} %get-tuple-element.66.chosen_ref, ...), custom_call_target="tpu_custom_call" | custom-call | flops 1000000 | bytes 10000 | tf_op jit(solution)/shard_map/pallas_call | solution.py:350
  27.2 4.4 %collective-permute-start.6 = (bf16[512,128]{1,0:T(8,128)(2,1)S(1)}, bf16[512,128]{1,0:T(8,128)(2,1)S(1)}, u32[]{:S(2)}, u32[]{:S(2)}) collective-permute-start(bf16[512,128]{1,0:T(8,128)(2,1)S(1)} %get-tuple-element.69), channel_id=1, source_target_pairs={{0,4},{1,5},{2,6},{3,7},{4,0},{5,1},{6,2},{7,3},{8,12},{9,13},{10,... | collective-permute-start | bytes 393224 | tf_op jit(solution)/shard_map/ppermute | solution.py:18
  31.6 0.6 %shard_map.93.placed_ref = bf16[512,256]{1,0:T(8,128)(2,1)S(1)} custom-call(bf16[512,256]{1,0:T(8,128)(2,1)S(1)} %get-tuple-element.70.coef_ref, bf16[4,1,4,128,128]{4,3,2,1,0:T(8,128)(2,1)S(1)} %get-tuple-element.45.panel_ref, bf16[8,512,512]{2,1,0:T(8,128)(2,1)S(1)} %get-tuple-element.66.chosen_ref, bf16[8,512,128]{2,1,0:T(8,128)(2,1)S(1)} %get-tuple-element.67.low_ref), custom_call_target="tpu_custom_call" | custom-call | flops 1000000 | bytes 10000 | tf_op jit(solution)/shard_map/pallas_call | solution.py:350
  32.2 3.0 %collective-permute-done.6.arrived_ref = bf16[512,128]{1,0:T(8,128)(2,1)S(1)} collective-permute-done((bf16[512,128]{1,0:T(8,128)(2,1)S(1)}, bf16[512,128]{1,0:T(8,128)(2,1)S(1)}, u32[]{:S(2)}, u32[]{:S(2)}) %collective-permute-start.6) | collective-permute-done | bytes 131104 | tf_op jit(solution)/shard_map/ppermute | solution.py:18
  35.2 0.5 %shard_map.94 = (bf16[512,256]{1,0:T(8,128)(2,1)S(1)}, bf16[512,128]{1,0:T(8,128)(2,1)S(1)}) custom-call(bf16[512,128]{1,0:T(8,128)(2,1)S(1)} %collective-permute-done.6.arrived_ref, bf16[512,256]{1,0:T(8,128)(2,1)S(1)} %shard_map.93.placed_ref, bf16[8,512,512]{2,1,0:T(8,128)(2,1)S(1)} %get-tuple-element.66.chosen_ref, ...), custom_call_target="tpu_custom_call" | custom-call | flops 1000000 | bytes 10000 | tf_op jit(solution)/shard_map/pallas_call | solution.py:350
  35.7 1.6 %collective-permute-start.7 = (bf16[512,128]{1,0:T(8,128)(2,1)S(1)}, bf16[512,128]{1,0:T(8,128)(2,1)S(1)}, u32[]{:S(2)}, u32[]{:S(2)}) collective-permute-start(bf16[512,128]{1,0:T(8,128)(2,1)S(1)} %get-tuple-element.71), channel_id=1, source_target_pairs={{0,2},{1,3},{2,0},{3,1},{4,6},{5,7},{6,4},{7,5},{8,10},{9,11},{10,... | collective-permute-start | bytes 393224 | tf_op jit(solution)/shard_map/ppermute | solution.py:18
  37.2 0.6 %shard_map.95.placed_ref = bf16[512,256]{1,0:T(8,128)(2,1)S(1)} custom-call(bf16[512,256]{1,0:T(8,128)(2,1)S(1)} %get-tuple-element.72.coef_ref, bf16[4,1,4,128,128]{4,3,2,1,0:T(8,128)(2,1)S(1)} %get-tuple-element.45.panel_ref, bf16[8,512,512]{2,1,0:T(8,128)(2,1)S(1)} %get-tuple-element.66.chosen_ref, bf16[8,512,128]{2,1,0:T(8,128)(2,1)S(1)} %get-tuple-element.67.low_ref), custom_call_target="tpu_custom_call" | custom-call | flops 1000000 | bytes 10000 | tf_op jit(solution)/shard_map/pallas_call | solution.py:350
  37.8 3.9 %collective-permute-done.7.arrived_ref = bf16[512,128]{1,0:T(8,128)(2,1)S(1)} collective-permute-done((bf16[512,128]{1,0:T(8,128)(2,1)S(1)}, bf16[512,128]{1,0:T(8,128)(2,1)S(1)}, u32[]{:S(2)}, u32[]{:S(2)}) %collective-permute-start.7) | collective-permute-done | bytes 131104 | tf_op jit(solution)/shard_map/ppermute | solution.py:18
  41.7 0.5 %shard_map.96 = (bf16[512,256]{1,0:T(8,128)(2,1)S(1)}, bf16[512,128]{1,0:T(8,128)(2,1)S(1)}) custom-call(bf16[512,128]{1,0:T(8,128)(2,1)S(1)} %collective-permute-done.7.arrived_ref, bf16[512,256]{1,0:T(8,128)(2,1)S(1)} %shard_map.95.placed_ref, bf16[8,512,512]{2,1,0:T(8,128)(2,1)S(1)} %get-tuple-element.66.chosen_ref, ...), custom_call_target="tpu_custom_call" | custom-call | flops 1000000 | bytes 10000 | tf_op jit(solution)/shard_map/pallas_call | solution.py:350
  42.3 0.6 %shard_map.97.placed_ref = bf16[512,256]{1,0:T(8,128)(2,1)S(1)} custom-call(bf16[512,256]{1,0:T(8,128)(2,1)S(1)} %get-tuple-element.74.coef_ref, bf16[4,1,4,128,128]{4,3,2,1,0:T(8,128)(2,1)S(1)} %get-tuple-element.45.panel_ref, bf16[8,512,512]{2,1,0:T(8,128)(2,1)S(1)} %get-tuple-element.66.chosen_ref, bf16[8,512,128]{2,1,0:T(8,128)(2,1)S(1)} %get-tuple-element.67.low_ref), custom_call_target="tpu_custom_call" | custom-call | flops 1000000 | bytes 10000 | tf_op jit(solution)/shard_map/pallas_call | solution.py:350
  42.8 0.8 %collective-permute-done.8.arrived_ref = bf16[512,128]{1,0:T(8,128)(2,1)S(1)} collective-permute-done((bf16[512,128]{1,0:T(8,128)(2,1)S(1)}, bf16[512,128]{1,0:T(8,128)(2,1)S(1)}, u32[]{:S(2)}, u32[]{:S(2)}) %collective-permute-start.8) | collective-permute-done | bytes 131104 | tf_op jit(solution)/shard_map/ppermute | solution.py:18
  43.6 1.6 %shard_map.98 = bf16[1024,512]{1,0:T(8,128)(2,1)} custom-call(bf16[512,128]{1,0:T(8,128)(2,1)S(1)} %collective-permute-done.8.arrived_ref, bf16[512,256]{1,0:T(8,128)(2,1)S(1)} %shard_map.97.placed_ref, bf16[8,512,512]{2,1,0:T(8,128)(2,1)S(1)} %get-tuple-element.66.chosen_ref, bf16[8,512,128]{2,1,0:T(8,128)(2,1)S(1)} %get-tuple-element.67.low_ref, ...), custom_call_target="tpu_custom_call" | custom-call | flops 1000000 | bytes 10000 | tf_op jit(solution)/shard_map/pallas_call | solution.py:350
  (3 shorter events, 0.1 us)
Async XLA Ops:
  2.1 1.5 %collective-permute-start = (bf16[512,128]{1,0:T(8,128)(2,1)S(1)}, bf16[512,128]{1,0:T(8,128)(2,1)S(1)}, u32[]{:S(2)}, u32[]{:S(2)}) collective-permute-start(bf16[512,128]{1,0:T(8,128)(2,1)S(1)} %get-tuple-element.41), channel_id=1, source_target_pairs={{0,1},{1,0},{2,3},{3,2},{4,5},{5,4},{6,7},{7,6},{8,9},{9,8},{10,11... | collective-permute-start | bytes 393224 | tf_op jit(solution)/shard_map/ppermute | solution.py:18
  4.2 6.8 %collective-permute-start.1 = (bf16[512,128]{1,0:T(8,128)(2,1)S(1)}, bf16[512,128]{1,0:T(8,128)(2,1)S(1)}, u32[]{:S(2)}, u32[]{:S(2)}) collective-permute-start(bf16[512,128]{1,0:T(8,128)(2,1)S(1)} %get-tuple-element.47), channel_id=1, source_target_pairs={{0,2},{1,3},{2,0},{3,1},{4,6},{5,7},{6,4},{7,5},{8,10},{9,11},{10,... | collective-permute-start | bytes 393224 | tf_op jit(solution)/shard_map/ppermute | solution.py:18
  11.5 5.4 %collective-permute-start.2 = (bf16[512,128]{1,0:T(8,128)(2,1)S(1)}, bf16[512,128]{1,0:T(8,128)(2,1)S(1)}, u32[]{:S(2)}, u32[]{:S(2)}) collective-permute-start(bf16[512,128]{1,0:T(8,128)(2,1)S(1)} %get-tuple-element.50), channel_id=1, source_target_pairs={{0,4},{1,5},{2,6},{3,7},{4,0},{5,1},{6,2},{7,3},{8,12},{9,13},{10,... | collective-permute-start | bytes 393224 | tf_op jit(solution)/shard_map/ppermute | solution.py:18
  13.3 6.7 %collective-permute-start.3 = (bf16[128,128]{1,0:T(8,128)(2,1)S(1)}, bf16[128,128]{1,0:T(8,128)(2,1)S(1)}, u32[]{:S(2)}, u32[]{:S(2)}) collective-permute-start(bf16[128,128]{1,0:T(8,128)(2,1)S(1)} %get-tuple-element.60), channel_id=1, source_target_pairs={{0,8},{1,9},{2,10},{3,11},{4,12},{5,13},{6,14},{7,15},{8,0},{9,1},... | collective-permute-start | bytes 98312 | tf_op jit(solution)/shard_map/ppermute | solution.py:18
  17.5 7.5 %collective-permute-start.5 = (bf16[512,128]{1,0:T(8,128)(2,1)S(1)}, bf16[512,128]{1,0:T(8,128)(2,1)S(1)}, u32[]{:S(2)}, u32[]{:S(2)}) collective-permute-start(bf16[512,128]{1,0:T(8,128)(2,1)S(1)} %get-tuple-element.59.sent_ref), channel_id=1, source_target_pairs={{0,8},{1,9},{2,10},{3,11},{4,12},{5,13},{6,14},{7,15},{8,0},{9,1},... | collective-permute-start | bytes 393224 | tf_op jit(solution)/shard_map/ppermute | solution.py:18
  20.8 5.9 %collective-permute-start.4 = (bf16[512,128]{1,0:T(8,128)(2,1)S(1)}, bf16[512,128]{1,0:T(8,128)(2,1)S(1)}, u32[]{:S(2)}, u32[]{:S(2)}) collective-permute-start(bf16[512,128]{1,0:T(8,128)(2,1)S(1)} %get-tuple-element.61), channel_id=1, source_target_pairs={{0,8},{1,9},{2,10},{3,11},{4,12},{5,13},{6,14},{7,15},{8,0},{9,1},... | collective-permute-start | bytes 393224 | tf_op jit(solution)/shard_map/ppermute | solution.py:18
  27.2 7.9 %collective-permute-start.6 = (bf16[512,128]{1,0:T(8,128)(2,1)S(1)}, bf16[512,128]{1,0:T(8,128)(2,1)S(1)}, u32[]{:S(2)}, u32[]{:S(2)}) collective-permute-start(bf16[512,128]{1,0:T(8,128)(2,1)S(1)} %get-tuple-element.69), channel_id=1, source_target_pairs={{0,4},{1,5},{2,6},{3,7},{4,0},{5,1},{6,2},{7,3},{8,12},{9,13},{10,... | collective-permute-start | bytes 393224 | tf_op jit(solution)/shard_map/ppermute | solution.py:18
  35.7 6.0 %collective-permute-start.7 = (bf16[512,128]{1,0:T(8,128)(2,1)S(1)}, bf16[512,128]{1,0:T(8,128)(2,1)S(1)}, u32[]{:S(2)}, u32[]{:S(2)}) collective-permute-start(bf16[512,128]{1,0:T(8,128)(2,1)S(1)} %get-tuple-element.71), channel_id=1, source_target_pairs={{0,2},{1,3},{2,0},{3,1},{4,6},{5,7},{6,4},{7,5},{8,10},{9,11},{10,... | collective-permute-start | bytes 393224 | tf_op jit(solution)/shard_map/ppermute | solution.py:18
  42.2 1.4 %collective-permute-start.8 = (bf16[512,128]{1,0:T(8,128)(2,1)S(1)}, bf16[512,128]{1,0:T(8,128)(2,1)S(1)}, u32[]{:S(2)}, u32[]{:S(2)}) collective-permute-start(bf16[512,128]{1,0:T(8,128)(2,1)S(1)} %get-tuple-element.73), channel_id=1, source_target_pairs={{0,1},{1,0},{2,3},{3,2},{4,5},{5,4},{6,7},{7,6},{8,9},{9,8},{10,11... | collective-permute-start | bytes 393224 | tf_op jit(solution)/shard_map/ppermute | solution.py:18

commit v7 on v6

--- a/solution.py
+++ b/solution.py
@@ -124,20 +124,27 @@
         pltpu.make_async_copy(source, target, done.at[at])
         for at, (source, target) in enumerate(pairs)
     ]
-    for load in loads:
-        load.start()
+    for at in (0, 1, 2, 3, 5, 4, 6, 7):
+        loads[at].start()
     loads[0].wait()
     loads[1].wait()
     slots = compose(pixel_ref[...], half_row(perm_ref, 0, 1 - bit_of(0)))
     slots_ref[...] = slots
-    for load in loads[2:-1]:
-        load.wait()
-    for at, part in enumerate(parts):
-        side, first = divmod(at * chunk, half)
-        leafed_ref[pl.ds(first, chunk), pl.ds(side * width, width)] = mul(
-            scene_ref[part], leaf_ref[...]
-        ).astype(thin)
-    out_ref[...] = take(take_plan(slots), leafed_ref[...]).astype(thin)
+    loads[2].wait()
+    chosen, low = take_plan(slots)
+    total = None
+    for at in range(0, half, chunk):
+        loads[3 + at // chunk].wait()
+        loads[3 + (half + at) // chunk].wait()
+        pieces = [
+            mul(scene_ref[pl.ds(side * half + at, chunk)], leaf_ref[...]).astype(thin)
+            for side in range(2)
+        ]
+        both = jnp.concatenate(pieces, axis=1)
+        leafed_ref[pl.ds(at, chunk)] = both
+        piece = mul(chosen[:, at : at + chunk], both)
+        total = piece if total is None else total + piece
+    out_ref[...] = jnp.where(low > 0.5, total[:, :width], total[:, width:]).astype(thin)
     loads[-1].wait()
 
 
@@ -176,16 +183,19 @@
     ]
 
 
-def echo_back(loads, echo, leaf, slots, back_ref):
+def echo_back(loads, echo, leaf, slots, back_ref, turns):
     half = echo.shape[0] // 2
     chunk = echo.shape[0] // scene_chunks
     loads[0].wait()
     plan = place_plan(slots[...], half)
     loads[1].wait()
     back = []
-    for at in range(scene_chunks):
-        loads[2 + at].wait()
-        back.append(mul_t(echo[pl.ds(at * chunk, chunk)], leaf[...]).astype(thin))
+    for turn in turns or (range(scene_chunks),):
+        for at in turn if turns else ():
+            loads[2 + at].start()
+        for at in turn:
+            loads[2 + at].wait()
+            back.append(mul_t(echo[pl.ds(at * chunk, chunk)], leaf[...]).astype(thin))
     back_ref[...] = place(plan, jnp.concatenate(back, axis=0)).astype(thin)
 
 
@@ -210,7 +220,7 @@
 
     @pl.when(early)
     def _():
-        echo_back(loads, echo, leaf, slots, back_ref)
+        echo_back(loads, echo, leaf, slots, back_ref, None)
 
     gram = split(mul_t(leaf[...], leaf[...]))
     both = pair_weights(panel_ref, last)
@@ -230,10 +240,18 @@
 
 
 def forward_kernel(level, arrived_ref, part_ref, panel_ref, perm_ref, coef_ref, out_ref):
-    coefficients = mix(level, arrived_ref, part_ref, panel_ref)
-    coef_ref[...] = coefficients
-    plan = take_plan(half_row(perm_ref, level + 1, 1 - bit_of(level + 1)))
-    out_ref[...] = take(plan, coefficients).astype(thin)
+    weight = pair_weight(panel_ref, level, 1 - bit_of(level))
+    chosen, low = take_plan(half_row(perm_ref, level + 1, 1 - bit_of(level + 1)))
+    half, width = arrived_ref.shape
+    step = half // 2
+    total = None
+    for at in range(0, half, step):
+        part = pl.ds(at, step)
+        mixture = (part_ref[part] + mul(arrived_ref[part], weight)).astype(thin)
+        coef_ref[part] = mixture
+        piece = mul(chosen[:, at : at + step], mixture)
+        total = piece if total is None else total + piece
+    out_ref[...] = jnp.where(low > 0.5, total[:, :width], total[:, width:]).astype(thin)
 
 
 def own_echo_kernel(
@@ -271,10 +289,10 @@
 
     @pl.when(jnp.logical_not(early))
     def _():
-        for load in loads:
+        for load in loads[:2]:
             load.start()
         make_plans(perm_ref, (own_slots_ref, out_slots_ref), chosen_ref, low_ref)
-        echo_back(loads, echo, leaf, slots, back_ref)
+        echo_back(loads, echo, leaf, slots, back_ref, ((0,), (1,), (2, 3)))
         echo_part_ref[...] = mul_t(back_ref[...], pair_weights(panel_ref, level))
 
     plan = take_plan(half_row(perm_ref, level, bit_of(level)))

time: 45.6 us -> 43.1 us (0.945)
  waiting for transfers between devices: 10.8 us -> 8.8 us
    ppermute x9, waiting for transfers between devices: 10.8 us -> 8.8 us  [swapped(): lax.ppermute(value, axis, [(i, i ^ 1 << apart) for i in range(lax.axis_si...]
  transfers between devices with their start and end apart: 9 -> 9, of which waited for: 7 -> 7; matrix products, arithmetic and copies ran while one was open for 0% -> 0% of each run, Pallas kernels for 24% -> 25%
where the time goes in v7:
time: 43.1 us; the launch traced here: 42.9 us
  Pallas kernels  16.9 us (39%)
  starting transfers between devices  16.9 us (39%)
  waiting for transfers between devices  8.8 us (20%)
    pallas_call x17, Pallas kernels, call(): pl.pallas_call(kernel, out_shape=shapes, in_specs=[near] * len(operands)...  16.9 us
    ppermute x9, starting transfers between devices, swapped(): lax.ppermute(value, axis, [(i, i ^ 1 << apart) for i in range(lax.axis_si...  16.9 us
    ppermute x9, waiting for transfers between devices, swapped(): lax.ppermute(value, axis, [(i, i ^ 1 << apart) for i in range(lax.axis_si...  8.8 us
  transfers between devices with their start and end apart: 9, of which 7 were waited for; matrix products, arithmetic and copies ran while one was open for 0% of the time, Pallas kernels for 25%

profile of v7, /device:TPU:0, one launch (start us, length us, event | category | flops | bytes accessed | tf_op | source)
XLA Modules:
  0.0 42.9 jit_solution(8017496661098579377)
XLA Ops:
  0.0 2.0 %shard_map.82 = (bf16[1024,512]{1,0:T(8,128)(2,1)S(1)}, bf16[512,128]{1,0:T(8,128)(2,1)S(1)}, s32[1,1024]{1,0:T(1,128)S(1)}, s32[4,1,1024]{2,1,0:T(1,128)S(1)}, ...) custom-call(bf16[1024,512]{1,0:T(8,128)(2,1)} %scene_in.1, ...), custom_call_target="tpu_custom_call" | custom-call | flops 1000000 | bytes 10000 | tf_op jit(solution)/shard_map/pallas_call | solution.py:368
  2.0 0.5 %collective-permute-start = (bf16[512,128]{1,0:T(8,128)(2,1)S(1)}, bf16[512,128]{1,0:T(8,128)(2,1)S(1)}, u32[]{:S(2)}, u32[]{:S(2)}) collective-permute-start(bf16[512,128]{1,0:T(8,128)(2,1)S(1)} %get-tuple-element.41), channel_id=1, source_target_pairs={{0,1},{1,0},{2,3},{3,2},{4,5},{5,4},{6,7},{7,6},{8,9},{9,8},{10,11... | collective-permute-start | bytes 393224 | tf_op jit(solution)/shard_map/ppermute | solution.py:18
  2.6 0.7 %shard_map.83 = (s32[1,512]{1,0:T(1,128)S(1)}, f32[512,256]{1,0:T(8,128)S(1)}) custom-call(bf16[512,256]{1,0:T(8,128)(2,1)S(1)} %get-tuple-element.42.leafed_ref, s32[1,1024]{1,0:T(1,128)S(1)} %get-tuple-element.43.pixel_ref, s32[4,1,1024]{2,1,0:T(1,128)S(1)} %get-tuple-element.44.perm_ref, bf16[4,1,4,128,128]{4,3,2,1,0:T(8,128)(2,1)S(1)} %get-tuple-element.45.panel_ref), custom_call_target="tpu_custom_call" | custom-call | flops 1000000 | bytes 10000 | tf_op jit(solution)/shard_map/pallas_call | solution.py:368
  3.3 0.3 collective-permute-done.arrived_ref
  3.6 0.5 %shard_map.84 = (bf16[512,256]{1,0:T(8,128)(2,1)S(1)}, bf16[512,128]{1,0:T(8,128)(2,1)S(1)}) custom-call(bf16[512,128]{1,0:T(8,128)(2,1)S(1)} %collective-permute-done.arrived_ref, f32[512,256]{1,0:T(8,128)S(1)} %get-tuple-element.46.part_ref, bf16[4,1,4,128,128]{4,3,2,1,0:T(8,128)(2,1)S(1)} %get-tuple-element.45.panel_ref, ...), custom_call_target="tpu_custom_call" | custom-call | flops 1000000 | bytes 10000 | tf_op jit(solution)/shard_map/pallas_call | solution.py:368
  4.1 2.9 %collective-permute-start.1 = (bf16[512,128]{1,0:T(8,128)(2,1)S(1)}, bf16[512,128]{1,0:T(8,128)(2,1)S(1)}, u32[]{:S(2)}, u32[]{:S(2)}) collective-permute-start(bf16[512,128]{1,0:T(8,128)(2,1)S(1)} %get-tuple-element.47), channel_id=1, source_target_pairs={{0,2},{1,3},{2,0},{3,1},{4,6},{5,7},{6,4},{7,5},{8,10},{9,11},{10,... | collective-permute-start | bytes 393224 | tf_op jit(solution)/shard_map/ppermute | solution.py:18
  7.0 3.8 %shard_map.85 = (f32[512,256]{1,0:T(8,128)S(1)}, bf16[256,256]{1,0:T(8,128)(2,1)S(1)}, bf16[256,128]{1,0:T(8,128)(2,1)S(1)}, bf16[128,128]{1,0:T(8,128)(2,1)S(1)}, bf16[512,256]{1,0:T(8,128)(2,1)S(1)}) custom-call(bf16[512,256]{1,0:T(8,128)(2,1)S(1)} %get-tuple-element.48.coef_ref, s32[4,1,1024]{2,1,0:T(1,128)S(1)} %get-tuple-element.44.perm_ref, ...), custom_call_target="tpu_custom_call" | custom-call | flops 1000000 | bytes 10000 | tf_op jit(solution)/shard_map/pallas_call | solution.py:368
  10.9 0.5 %shard_map.86 = (bf16[512,256]{1,0:T(8,128)(2,1)S(1)}, bf16[512,128]{1,0:T(8,128)(2,1)S(1)}) custom-call(bf16[512,128]{1,0:T(8,128)(2,1)S(1)} %collective-permute-done.1.arrived_ref, f32[512,256]{1,0:T(8,128)S(1)} %get-tuple-element.49.part_ref, bf16[4,1,4,128,128]{4,3,2,1,0:T(8,128)(2,1)S(1)} %get-tuple-element.45.panel_ref, ...), custom_call_target="tpu_custom_call" | custom-call | flops 1000000 | bytes 10000 | tf_op jit(solution)/shard_map/pallas_call | solution.py:368
  11.4 1.8 %collective-permute-start.2 = (bf16[512,128]{1,0:T(8,128)(2,1)S(1)}, bf16[512,128]{1,0:T(8,128)(2,1)S(1)}, u32[]{:S(2)}, u32[]{:S(2)}) collective-permute-start(bf16[512,128]{1,0:T(8,128)(2,1)S(1)} %get-tuple-element.50), channel_id=1, source_target_pairs={{0,4},{1,5},{2,6},{3,7},{4,0},{5,1},{6,2},{7,3},{8,12},{9,13},{10,... | collective-permute-start | bytes 393224 | tf_op jit(solution)/shard_map/ppermute | solution.py:18
  13.2 2.6 %collective-permute-start.3 = (bf16[128,128]{1,0:T(8,128)(2,1)S(1)}, bf16[128,128]{1,0:T(8,128)(2,1)S(1)}, u32[]{:S(2)}, u32[]{:S(2)}) collective-permute-start(bf16[128,128]{1,0:T(8,128)(2,1)S(1)} %get-tuple-element.60), channel_id=1, source_target_pairs={{0,8},{1,9},{2,10},{3,11},{4,12},{5,13},{6,14},{7,15},{8,0},{9,1},... | collective-permute-start | bytes 98312 | tf_op jit(solution)/shard_map/ppermute | solution.py:18
  15.8 0.8 %shard_map.87 = (f32[512,256]{1,0:T(8,128)S(1)}, f32[512,256]{1,0:T(8,128)S(1)}) custom-call(bf16[512,256]{1,0:T(8,128)(2,1)S(1)} %get-tuple-element.51.coef_ref, s32[4,1,1024]{2,1,0:T(1,128)S(1)} %get-tuple-element.44.perm_ref, bf16[4,1,4,128,128]{4,3,2,1,0:T(8,128)(2,1)S(1)} %get-tuple-element.45.panel_ref, bf16[512,256]{1,0:T(8,128)(2,1)S(1)} %get-tuple-element.52.back_ref), custom_call_target="tpu_custom_call" | custom-call | flops 1000000 | bytes 10000 | tf_op jit(solution)/shard_map/pallas_call | solution.py:368
  16.8 0.5 %shard_map.88 = (bf16[512,256]{1,0:T(8,128)(2,1)S(1)}, bf16[512,128]{1,0:T(8,128)(2,1)S(1)}) custom-call(bf16[512,128]{1,0:T(8,128)(2,1)S(1)} %collective-permute-done.2.arrived_ref, f32[512,256]{1,0:T(8,128)S(1)} %get-tuple-element.53.part_ref, bf16[4,1,4,128,128]{4,3,2,1,0:T(8,128)(2,1)S(1)} %get-tuple-element.45.panel_ref, ...), custom_call_target="tpu_custom_call" | custom-call | flops 1000000 | bytes 10000 | tf_op jit(solution)/shard_map/pallas_call | solution.py:368
  17.3 2.6 %collective-permute-start.5 = (bf16[512,128]{1,0:T(8,128)(2,1)S(1)}, bf16[512,128]{1,0:T(8,128)(2,1)S(1)}, u32[]{:S(2)}, u32[]{:S(2)}) collective-permute-start(bf16[512,128]{1,0:T(8,128)(2,1)S(1)} %get-tuple-element.59.sent_ref), channel_id=1, source_target_pairs={{0,8},{1,9},{2,10},{3,11},{4,12},{5,13},{6,14},{7,15},{8,0},{9,1},... | collective-permute-start | bytes 393224 | tf_op jit(solution)/shard_map/ppermute | solution.py:18
  19.9 0.7 %shard_map.89 = (f32[512,128]{1,0:T(8,128)S(1)}, f32[512,128]{1,0:T(8,128)S(1)}, bf16[512,128]{1,0:T(8,128)(2,1)S(1)}, bf16[8,512,512]{2,1,0:T(8,128)(2,1)S(1)}, bf16[8,512,128]{2,1,0:T(8,128)(2,1)S(1)}) custom-call(bf16[512,256]{1,0:T(8,128)(2,1)S(1)} %get-tuple-element.54.coef_ref, s32[4,1,1024]{2,1,0:T(1,128)S(1)} %get-tuple-element.44.perm_ref, ...), custom_call_target="tpu_custom_call" | custom-call | flops 1000000 | bytes 10000 | tf_op jit(solution)/shard_map/pallas_call | solution.py:368
  20.6 0.8 %collective-permute-start.4 = (bf16[512,128]{1,0:T(8,128)(2,1)S(1)}, bf16[512,128]{1,0:T(8,128)(2,1)S(1)}, u32[]{:S(2)}, u32[]{:S(2)}) collective-permute-start(bf16[512,128]{1,0:T(8,128)(2,1)S(1)} %get-tuple-element.61), channel_id=1, source_target_pairs={{0,8},{1,9},{2,10},{3,11},{4,12},{5,13},{6,14},{7,15},{8,0},{9,1},... | collective-permute-start | bytes 393224 | tf_op jit(solution)/shard_map/ppermute | solution.py:18
  21.4 2.0 %shard_map.90 = (bf16[8,512,512]{2,1,0:T(8,128)(2,1)S(1)}, bf16[8,512,128]{2,1,0:T(8,128)(2,1)S(1)}) custom-call(s32[4,1,1024]{2,1,0:T(1,128)S(1)} %get-tuple-element.44.perm_ref, s32[1,512]{1,0:T(1,128)S(1)} %get-tuple-element.57.own_slots_ref, s32[1,512]{1,0:T(1,128)S(1)} %get-tuple-element.58.out_slots_ref, ...), custom_call_target="tpu_custom_call", output_to_operand_aliasing={{0}: (3, {}), {1}: (4, {})} | custom-call | flops 1000000 | bytes 10000 | tf_op jit(solution)/shard_map/pallas_call | solution.py:368
  23.4 1.4 %collective-permute-done.5.arrived_ref = bf16[512,128]{1,0:T(8,128)(2,1)S(1)} collective-permute-done((bf16[512,128]{1,0:T(8,128)(2,1)S(1)}, bf16[512,128]{1,0:T(8,128)(2,1)S(1)}, u32[]{:S(2)}, u32[]{:S(2)}) %collective-permute-start.5) | collective-permute-done | bytes 131104 | tf_op jit(solution)/shard_map/ppermute | solution.py:18
  24.8 0.6 %shard_map.91.placed_ref = bf16[512,256]{1,0:T(8,128)(2,1)S(1)} custom-call(bf16[512,128]{1,0:T(8,128)(2,1)S(1)} %collective-permute-done.5.arrived_ref, f32[512,128]{1,0:T(8,128)S(1)} %get-tuple-element.62.part_ref, bf16[256,128]{1,0:T(8,128)(2,1)S(1)} %get-tuple-element.63.map_ref, bf16[8,512,512]{2,1,0:T(8,128)(2,1)S(1)} %get-tuple-element.66.chosen_ref, ...), custom_call_target="tpu_custom_call" | custom-call | flops 1000000 | bytes 10000 | tf_op jit(solution)/shard_map/pallas_call | solution.py:368
  25.4 1.2 %collective-permute-done.4.arrived_ref = bf16[512,128]{1,0:T(8,128)(2,1)S(1)} collective-permute-done((bf16[512,128]{1,0:T(8,128)(2,1)S(1)}, bf16[512,128]{1,0:T(8,128)(2,1)S(1)}, u32[]{:S(2)}, u32[]{:S(2)}) %collective-permute-start.4) | collective-permute-done | bytes 131104 | tf_op jit(solution)/shard_map/ppermute | solution.py:18
  26.5 0.5 %shard_map.92 = (bf16[512,256]{1,0:T(8,128)(2,1)S(1)}, bf16[512,128]{1,0:T(8,128)(2,1)S(1)}) custom-call(bf16[512,128]{1,0:T(8,128)(2,1)S(1)} %collective-permute-done.4.arrived_ref, bf16[512,256]{1,0:T(8,128)(2,1)S(1)} %shard_map.91.placed_ref, bf16[8,512,512]{2,1,0:T(8,128)(2,1)S(1)} %get-tuple-element.66.chosen_ref, ...), custom_call_target="tpu_custom_call" | custom-call | flops 1000000 | bytes 10000 | tf_op jit(solution)/shard_map/pallas_call | solution.py:368
  27.0 2.0 %collective-permute-start.6 = (bf16[512,128]{1,0:T(8,128)(2,1)S(1)}, bf16[512,128]{1,0:T(8,128)(2,1)S(1)}, u32[]{:S(2)}, u32[]{:S(2)}) collective-permute-start(bf16[512,128]{1,0:T(8,128)(2,1)S(1)} %get-tuple-element.69), channel_id=1, source_target_pairs={{0,4},{1,5},{2,6},{3,7},{4,0},{5,1},{6,2},{7,3},{8,12},{9,13},{10,... | collective-permute-start | bytes 393224 | tf_op jit(solution)/shard_map/ppermute | solution.py:18
  29.1 0.6 %shard_map.93.placed_ref = bf16[512,256]{1,0:T(8,128)(2,1)S(1)} custom-call(bf16[512,256]{1,0:T(8,128)(2,1)S(1)} %get-tuple-element.70.coef_ref, bf16[4,1,4,128,128]{4,3,2,1,0:T(8,128)(2,1)S(1)} %get-tuple-element.45.panel_ref, bf16[8,512,512]{2,1,0:T(8,128)(2,1)S(1)} %get-tuple-element.66.chosen_ref, bf16[8,512,128]{2,1,0:T(8,128)(2,1)S(1)} %get-tuple-element.67.low_ref), custom_call_target="tpu_custom_call" | custom-call | flops 1000000 | bytes 10000 | tf_op jit(solution)/shard_map/pallas_call | solution.py:368
  29.6 2.4 %collective-permute-done.6.arrived_ref = bf16[512,128]{1,0:T(8,128)(2,1)S(1)} collective-permute-done((bf16[512,128]{1,0:T(8,128)(2,1)S(1)}, bf16[512,128]{1,0:T(8,128)(2,1)S(1)}, u32[]{:S(2)}, u32[]{:S(2)}) %collective-permute-start.6) | collective-permute-done | bytes 131104 | tf_op jit(solution)/shard_map/ppermute | solution.py:18
  32.1 0.5 %shard_map.94 = (bf16[512,256]{1,0:T(8,128)(2,1)S(1)}, bf16[512,128]{1,0:T(8,128)(2,1)S(1)}) custom-call(bf16[512,128]{1,0:T(8,128)(2,1)S(1)} %collective-permute-done.6.arrived_ref, bf16[512,256]{1,0:T(8,128)(2,1)S(1)} %shard_map.93.placed_ref, bf16[8,512,512]{2,1,0:T(8,128)(2,1)S(1)} %get-tuple-element.66.chosen_ref, ...), custom_call_target="tpu_custom_call" | custom-call | flops 1000000 | bytes 10000 | tf_op jit(solution)/shard_map/pallas_call | solution.py:368
  32.5 1.6 %collective-permute-start.7 = (bf16[512,128]{1,0:T(8,128)(2,1)S(1)}, bf16[512,128]{1,0:T(8,128)(2,1)S(1)}, u32[]{:S(2)}, u32[]{:S(2)}) collective-permute-start(bf16[512,128]{1,0:T(8,128)(2,1)S(1)} %get-tuple-element.71), channel_id=1, source_target_pairs={{0,2},{1,3},{2,0},{3,1},{4,6},{5,7},{6,4},{7,5},{8,10},{9,11},{10,... | collective-permute-start | bytes 393224 | tf_op jit(solution)/shard_map/ppermute | solution.py:18
  34.1 0.6 %shard_map.95.placed_ref = bf16[512,256]{1,0:T(8,128)(2,1)S(1)} custom-call(bf16[512,256]{1,0:T(8,128)(2,1)S(1)} %get-tuple-element.72.coef_ref, bf16[4,1,4,128,128]{4,3,2,1,0:T(8,128)(2,1)S(1)} %get-tuple-element.45.panel_ref, bf16[8,512,512]{2,1,0:T(8,128)(2,1)S(1)} %get-tuple-element.66.chosen_ref, bf16[8,512,128]{2,1,0:T(8,128)(2,1)S(1)} %get-tuple-element.67.low_ref), custom_call_target="tpu_custom_call" | custom-call | flops 1000000 | bytes 10000 | tf_op jit(solution)/shard_map/pallas_call | solution.py:368
  34.7 2.9 %collective-permute-done.7.arrived_ref = bf16[512,128]{1,0:T(8,128)(2,1)S(1)} collective-permute-done((bf16[512,128]{1,0:T(8,128)(2,1)S(1)}, bf16[512,128]{1,0:T(8,128)(2,1)S(1)}, u32[]{:S(2)}, u32[]{:S(2)}) %collective-permute-start.7) | collective-permute-done | bytes 131104 | tf_op jit(solution)/shard_map/ppermute | solution.py:18
  37.6 0.5 %shard_map.96 = (bf16[512,256]{1,0:T(8,128)(2,1)S(1)}, bf16[512,128]{1,0:T(8,128)(2,1)S(1)}) custom-call(bf16[512,128]{1,0:T(8,128)(2,1)S(1)} %collective-permute-done.7.arrived_ref, bf16[512,256]{1,0:T(8,128)(2,1)S(1)} %shard_map.95.placed_ref, bf16[8,512,512]{2,1,0:T(8,128)(2,1)S(1)} %get-tuple-element.66.chosen_ref, ...), custom_call_target="tpu_custom_call" | custom-call | flops 1000000 | bytes 10000 | tf_op jit(solution)/shard_map/pallas_call | solution.py:368
  38.1 2.1 %collective-permute-start.8 = (bf16[512,128]{1,0:T(8,128)(2,1)S(1)}, bf16[512,128]{1,0:T(8,128)(2,1)S(1)}, u32[]{:S(2)}, u32[]{:S(2)}) collective-permute-start(bf16[512,128]{1,0:T(8,128)(2,1)S(1)} %get-tuple-element.73), channel_id=1, source_target_pairs={{0,1},{1,0},{2,3},{3,2},{4,5},{5,4},{6,7},{7,6},{8,9},{9,8},{10,11... | collective-permute-start | bytes 393224 | tf_op jit(solution)/shard_map/ppermute | solution.py:18
  40.1 0.6 %shard_map.97.placed_ref = bf16[512,256]{1,0:T(8,128)(2,1)S(1)} custom-call(bf16[512,256]{1,0:T(8,128)(2,1)S(1)} %get-tuple-element.74.coef_ref, bf16[4,1,4,128,128]{4,3,2,1,0:T(8,128)(2,1)S(1)} %get-tuple-element.45.panel_ref, bf16[8,512,512]{2,1,0:T(8,128)(2,1)S(1)} %get-tuple-element.66.chosen_ref, bf16[8,512,128]{2,1,0:T(8,128)(2,1)S(1)} %get-tuple-element.67.low_ref), custom_call_target="tpu_custom_call" | custom-call | flops 1000000 | bytes 10000 | tf_op jit(solution)/shard_map/pallas_call | solution.py:368
  40.7 0.4 collective-permute-done.8.arrived_ref
  41.1 1.6 %shard_map.98 = bf16[1024,512]{1,0:T(8,128)(2,1)} custom-call(bf16[512,128]{1,0:T(8,128)(2,1)S(1)} %collective-permute-done.8.arrived_ref, bf16[512,256]{1,0:T(8,128)(2,1)S(1)} %shard_map.97.placed_ref, bf16[8,512,512]{2,1,0:T(8,128)(2,1)S(1)} %get-tuple-element.66.chosen_ref, bf16[8,512,128]{2,1,0:T(8,128)(2,1)S(1)} %get-tuple-element.67.low_ref, ...), custom_call_target="tpu_custom_call" | custom-call | flops 1000000 | bytes 10000 | tf_op jit(solution)/shard_map/pallas_call | solution.py:368
  (3 shorter events, 0.2 us)
Async XLA Ops:
  2.0 1.5 %collective-permute-start = (bf16[512,128]{1,0:T(8,128)(2,1)S(1)}, bf16[512,128]{1,0:T(8,128)(2,1)S(1)}, u32[]{:S(2)}, u32[]{:S(2)}) collective-permute-start(bf16[512,128]{1,0:T(8,128)(2,1)S(1)} %get-tuple-element.41), channel_id=1, source_target_pairs={{0,1},{1,0},{2,3},{3,2},{4,5},{5,4},{6,7},{7,6},{8,9},{9,8},{10,11... | collective-permute-start | bytes 393224 | tf_op jit(solution)/shard_map/ppermute | solution.py:18
  4.1 6.8 %collective-permute-start.1 = (bf16[512,128]{1,0:T(8,128)(2,1)S(1)}, bf16[512,128]{1,0:T(8,128)(2,1)S(1)}, u32[]{:S(2)}, u32[]{:S(2)}) collective-permute-start(bf16[512,128]{1,0:T(8,128)(2,1)S(1)} %get-tuple-element.47), channel_id=1, source_target_pairs={{0,2},{1,3},{2,0},{3,1},{4,6},{5,7},{6,4},{7,5},{8,10},{9,11},{10,... | collective-permute-start | bytes 393224 | tf_op jit(solution)/shard_map/ppermute | solution.py:18
  11.4 5.4 %collective-permute-start.2 = (bf16[512,128]{1,0:T(8,128)(2,1)S(1)}, bf16[512,128]{1,0:T(8,128)(2,1)S(1)}, u32[]{:S(2)}, u32[]{:S(2)}) collective-permute-start(bf16[512,128]{1,0:T(8,128)(2,1)S(1)} %get-tuple-element.50), channel_id=1, source_target_pairs={{0,4},{1,5},{2,6},{3,7},{4,0},{5,1},{6,2},{7,3},{8,12},{9,13},{10,... | collective-permute-start | bytes 393224 | tf_op jit(solution)/shard_map/ppermute | solution.py:18
  13.2 6.7 %collective-permute-start.3 = (bf16[128,128]{1,0:T(8,128)(2,1)S(1)}, bf16[128,128]{1,0:T(8,128)(2,1)S(1)}, u32[]{:S(2)}, u32[]{:S(2)}) collective-permute-start(bf16[128,128]{1,0:T(8,128)(2,1)S(1)} %get-tuple-element.60), channel_id=1, source_target_pairs={{0,8},{1,9},{2,10},{3,11},{4,12},{5,13},{6,14},{7,15},{8,0},{9,1},... | collective-permute-start | bytes 98312 | tf_op jit(solution)/shard_map/ppermute | solution.py:18
  17.3 7.5 %collective-permute-start.5 = (bf16[512,128]{1,0:T(8,128)(2,1)S(1)}, bf16[512,128]{1,0:T(8,128)(2,1)S(1)}, u32[]{:S(2)}, u32[]{:S(2)}) collective-permute-start(bf16[512,128]{1,0:T(8,128)(2,1)S(1)} %get-tuple-element.59.sent_ref), channel_id=1, source_target_pairs={{0,8},{1,9},{2,10},{3,11},{4,12},{5,13},{6,14},{7,15},{8,0},{9,1},... | collective-permute-start | bytes 393224 | tf_op jit(solution)/shard_map/ppermute | solution.py:18
  20.6 5.9 %collective-permute-start.4 = (bf16[512,128]{1,0:T(8,128)(2,1)S(1)}, bf16[512,128]{1,0:T(8,128)(2,1)S(1)}, u32[]{:S(2)}, u32[]{:S(2)}) collective-permute-start(bf16[512,128]{1,0:T(8,128)(2,1)S(1)} %get-tuple-element.61), channel_id=1, source_target_pairs={{0,8},{1,9},{2,10},{3,11},{4,12},{5,13},{6,14},{7,15},{8,0},{9,1},... | collective-permute-start | bytes 393224 | tf_op jit(solution)/shard_map/ppermute | solution.py:18
  27.0 5.0 %collective-permute-start.6 = (bf16[512,128]{1,0:T(8,128)(2,1)S(1)}, bf16[512,128]{1,0:T(8,128)(2,1)S(1)}, u32[]{:S(2)}, u32[]{:S(2)}) collective-permute-start(bf16[512,128]{1,0:T(8,128)(2,1)S(1)} %get-tuple-element.69), channel_id=1, source_target_pairs={{0,4},{1,5},{2,6},{3,7},{4,0},{5,1},{6,2},{7,3},{8,12},{9,13},{10,... | collective-permute-start | bytes 393224 | tf_op jit(solution)/shard_map/ppermute | solution.py:18
  32.5 5.0 %collective-permute-start.7 = (bf16[512,128]{1,0:T(8,128)(2,1)S(1)}, bf16[512,128]{1,0:T(8,128)(2,1)S(1)}, u32[]{:S(2)}, u32[]{:S(2)}) collective-permute-start(bf16[512,128]{1,0:T(8,128)(2,1)S(1)} %get-tuple-element.71), channel_id=1, source_target_pairs={{0,2},{1,3},{2,0},{3,1},{4,6},{5,7},{6,4},{7,5},{8,10},{9,11},{10,... | collective-permute-start | bytes 393224 | tf_op jit(solution)/shard_map/ppermute | solution.py:18
  38.1 3.1 %collective-permute-start.8 = (bf16[512,128]{1,0:T(8,128)(2,1)S(1)}, bf16[512,128]{1,0:T(8,128)(2,1)S(1)}, u32[]{:S(2)}, u32[]{:S(2)}) collective-permute-start(bf16[512,128]{1,0:T(8,128)(2,1)S(1)} %get-tuple-element.73), channel_id=1, source_target_pairs={{0,1},{1,0},{2,3},{3,2},{4,5},{5,4},{6,7},{7,6},{8,9},{9,8},{10,11... | collective-permute-start | bytes 393224 | tf_op jit(solution)/shard_map/ppermute | solution.py:18

commit v8 on v7

--- a/solution.py
+++ b/solution.py
@@ -277,8 +277,9 @@
 
 def bracket_kernel(
     level, coef_ref, perm_ref, map_ref, panel_ref, early_ref, own_slots_ref, out_slots_ref,
-    sent_ref, arrived_map_ref, echo_in, leaf_in, slots_in,
-    part_ref, rest_ref, out_ref, chosen_ref, low_ref, echo_part_ref, back_ref, echo, leaf, slots, done,
+    arrived_map_ref, echo_in, leaf_in, slots_in,
+    part_ref, kept_map_ref, out_ref, chosen_ref, low_ref, echo_part_ref, back_ref,
+    echo, leaf, slots, done,
 ):
     loads = echo_loads(echo_in, leaf_in, slots_in, echo, leaf, slots, done)
     early = bit_of(0) == 0
@@ -301,13 +302,15 @@
     width = own.shape[1]
     part_ref[...] = both[:, :width]
     out_ref[...] = both[:, width:].astype(thin)
-    rest_ref[...] = mul(sent_ref[...], arrived_map_ref[...])
+    kept_map_ref[...] = arrived_map_ref[...]
 
 
 def plan_kernel(
-    perm_ref, own_slots_ref, out_slots_ref, chosen_in, low_in, chosen_ref, low_ref
+    perm_ref, own_slots_ref, out_slots_ref, chosen_in, low_in, sent_ref, map_ref,
+    chosen_ref, low_ref, rest_ref,
 ):
     del chosen_in, low_in
+    rest_ref[...] = mul(sent_ref[...], map_ref[...])
 
     @pl.when(bit_of(0) == 0)
     def _():
@@ -454,9 +457,9 @@
             )
     half_wide = ((half, width), wide)
     plan_like = [((2 * levels, half, half), thin), ((2 * levels, half, lanes), thin)]
-    part, rest, bracket, *plans = call(
+    part, arrived_map, bracket, *plans = call(
         functools.partial(bracket_kernel, last),
-        [half_wide, half_wide, sent] + plan_like,
+        [half_wide, ((width, width), thin), sent] + plan_like,
         coefficients,
         perms,
         own_map,
@@ -464,15 +467,22 @@
         early,
         own_slots,
         out_slots,
-        outgoing,
         arrived_map,
         far=(echoes, source_leaf, pulse_slot),
         scratch=[pltpu.VMEM((half, 2 * width), wide), pltpu.VMEM((half, 2 * width), thin)]
         + echo_scratch,
     )
     arrived_bracket = swapped(bracket, "box", last)
-    plans = call(
-        plan_kernel, plan_like, perms, own_slots, out_slots, *plans, aliases={3: 0, 4: 1}
+    *plans, rest = call(
+        plan_kernel,
+        plan_like + [half_wide],
+        perms,
+        own_slots,
+        out_slots,
+        *plans,
+        outgoing,
+        arrived_map,
+        aliases={3: 0, 4: 1},
     )
     placed = call(
         functools.partial(join_kernel, last), [column_of], arrived, part, other_map, *plans

time: 43.1 us -> 43 us (level)
  transfers between devices with their start and end apart: 9 -> 9, of which waited for: 7 -> 7; matrix products, arithmetic and copies ran while one was open for 0% -> 0% of each run, Pallas kernels for 25% -> 26%
where the time goes in v8:
time: 43 us; the launch traced here: 42.8 us
  Pallas kernels  17.2 us (40%)
  starting transfers between devices  16.9 us (39%)
  waiting for transfers between devices  8.46 us (20%)
    pallas_call x17, Pallas kernels, call(): pl.pallas_call(kernel, out_shape=shapes, in_specs=[near] * len(operands)...  17.2 us
    ppermute x9, starting transfers between devices, swapped(): lax.ppermute(value, axis, [(i, i ^ 1 << apart) for i in range(lax.axis_si...  16.9 us
    ppermute x9, waiting for transfers between devices, swapped(): lax.ppermute(value, axis, [(i, i ^ 1 << apart) for i in range(lax.axis_si...  8.46 us
  transfers between devices with their start and end apart: 9, of which 7 were waited for; matrix products, arithmetic and copies ran while one was open for 0% of the time, Pallas kernels for 26%

profile of v8, /device:TPU:0, one launch (start us, length us, event | category | flops | bytes accessed | tf_op | source)
XLA Modules:
  0.0 42.8 jit_solution(1295006222112687335)
XLA Ops:
  0.0 2.0 %shard_map.82 = (bf16[1024,512]{1,0:T(8,128)(2,1)S(1)}, bf16[512,128]{1,0:T(8,128)(2,1)S(1)}, s32[1,1024]{1,0:T(1,128)S(1)}, s32[4,1,1024]{2,1,0:T(1,128)S(1)}, ...) custom-call(bf16[1024,512]{1,0:T(8,128)(2,1)} %scene_in.1, ...), custom_call_target="tpu_custom_call" | custom-call | flops 1000000 | bytes 10000 | tf_op jit(solution)/shard_map/pallas_call | solution.py:371
  2.0 0.5 %collective-permute-start = (bf16[512,128]{1,0:T(8,128)(2,1)S(1)}, bf16[512,128]{1,0:T(8,128)(2,1)S(1)}, u32[]{:S(2)}, u32[]{:S(2)}) collective-permute-start(bf16[512,128]{1,0:T(8,128)(2,1)S(1)} %get-tuple-element.42), channel_id=1, source_target_pairs={{0,1},{1,0},{2,3},{3,2},{4,5},{5,4},{6,7},{7,6},{8,9},{9,8},{10,11... | collective-permute-start | bytes 393224 | tf_op jit(solution)/shard_map/ppermute | solution.py:18
  2.6 0.7 %shard_map.83 = (s32[1,512]{1,0:T(1,128)S(1)}, f32[512,256]{1,0:T(8,128)S(1)}) custom-call(bf16[512,256]{1,0:T(8,128)(2,1)S(1)} %get-tuple-element.43.leafed_ref, s32[1,1024]{1,0:T(1,128)S(1)} %get-tuple-element.44.pixel_ref, s32[4,1,1024]{2,1,0:T(1,128)S(1)} %get-tuple-element.45.perm_ref, bf16[4,1,4,128,128]{4,3,2,1,0:T(8,128)(2,1)S(1)} %get-tuple-element.46.panel_ref), custom_call_target="tpu_custom_call" | custom-call | flops 1000000 | bytes 10000 | tf_op jit(solution)/shard_map/pallas_call | solution.py:371
  3.3 0.3 collective-permute-done.arrived_ref
  3.6 0.5 %shard_map.84 = (bf16[512,256]{1,0:T(8,128)(2,1)S(1)}, bf16[512,128]{1,0:T(8,128)(2,1)S(1)}) custom-call(bf16[512,128]{1,0:T(8,128)(2,1)S(1)} %collective-permute-done.arrived_ref, f32[512,256]{1,0:T(8,128)S(1)} %get-tuple-element.47.part_ref, bf16[4,1,4,128,128]{4,3,2,1,0:T(8,128)(2,1)S(1)} %get-tuple-element.46.panel_ref, ...), custom_call_target="tpu_custom_call" | custom-call | flops 1000000 | bytes 10000 | tf_op jit(solution)/shard_map/pallas_call | solution.py:371
  4.1 2.9 %collective-permute-start.1 = (bf16[512,128]{1,0:T(8,128)(2,1)S(1)}, bf16[512,128]{1,0:T(8,128)(2,1)S(1)}, u32[]{:S(2)}, u32[]{:S(2)}) collective-permute-start(bf16[512,128]{1,0:T(8,128)(2,1)S(1)} %get-tuple-element.48), channel_id=1, source_target_pairs={{0,2},{1,3},{2,0},{3,1},{4,6},{5,7},{6,4},{7,5},{8,10},{9,11},{10,... | collective-permute-start | bytes 393224 | tf_op jit(solution)/shard_map/ppermute | solution.py:18
  7.0 3.8 %shard_map.85 = (f32[512,256]{1,0:T(8,128)S(1)}, bf16[256,256]{1,0:T(8,128)(2,1)S(1)}, bf16[256,128]{1,0:T(8,128)(2,1)S(1)}, bf16[128,128]{1,0:T(8,128)(2,1)S(1)}, bf16[512,256]{1,0:T(8,128)(2,1)S(1)}) custom-call(bf16[512,256]{1,0:T(8,128)(2,1)S(1)} %get-tuple-element.49.coef_ref, s32[4,1,1024]{2,1,0:T(1,128)S(1)} %get-tuple-element.45.perm_ref, ...), custom_call_target="tpu_custom_call" | custom-call | flops 1000000 | bytes 10000 | tf_op jit(solution)/shard_map/pallas_call | solution.py:371
  10.9 0.5 %shard_map.86 = (bf16[512,256]{1,0:T(8,128)(2,1)S(1)}, bf16[512,128]{1,0:T(8,128)(2,1)S(1)}) custom-call(bf16[512,128]{1,0:T(8,128)(2,1)S(1)} %collective-permute-done.1.arrived_ref, f32[512,256]{1,0:T(8,128)S(1)} %get-tuple-element.50.part_ref, bf16[4,1,4,128,128]{4,3,2,1,0:T(8,128)(2,1)S(1)} %get-tuple-element.46.panel_ref, ...), custom_call_target="tpu_custom_call" | custom-call | flops 1000000 | bytes 10000 | tf_op jit(solution)/shard_map/pallas_call | solution.py:371
  11.4 1.8 %collective-permute-start.2 = (bf16[512,128]{1,0:T(8,128)(2,1)S(1)}, bf16[512,128]{1,0:T(8,128)(2,1)S(1)}, u32[]{:S(2)}, u32[]{:S(2)}) collective-permute-start(bf16[512,128]{1,0:T(8,128)(2,1)S(1)} %get-tuple-element.51), channel_id=1, source_target_pairs={{0,4},{1,5},{2,6},{3,7},{4,0},{5,1},{6,2},{7,3},{8,12},{9,13},{10,... | collective-permute-start | bytes 393224 | tf_op jit(solution)/shard_map/ppermute | solution.py:18
  13.2 2.6 %collective-permute-start.3 = (bf16[128,128]{1,0:T(8,128)(2,1)S(1)}, bf16[128,128]{1,0:T(8,128)(2,1)S(1)}, u32[]{:S(2)}, u32[]{:S(2)}) collective-permute-start(bf16[128,128]{1,0:T(8,128)(2,1)S(1)} %get-tuple-element.60), channel_id=1, source_target_pairs={{0,8},{1,9},{2,10},{3,11},{4,12},{5,13},{6,14},{7,15},{8,0},{9,1},... | collective-permute-start | bytes 98312 | tf_op jit(solution)/shard_map/ppermute | solution.py:18
  15.8 0.8 %shard_map.87 = (f32[512,256]{1,0:T(8,128)S(1)}, f32[512,256]{1,0:T(8,128)S(1)}) custom-call(bf16[512,256]{1,0:T(8,128)(2,1)S(1)} %get-tuple-element.52.coef_ref, s32[4,1,1024]{2,1,0:T(1,128)S(1)} %get-tuple-element.45.perm_ref, bf16[4,1,4,128,128]{4,3,2,1,0:T(8,128)(2,1)S(1)} %get-tuple-element.46.panel_ref, bf16[512,256]{1,0:T(8,128)(2,1)S(1)} %get-tuple-element.53.back_ref), custom_call_target="tpu_custom_call" | custom-call | flops 1000000 | bytes 10000 | tf_op jit(solution)/shard_map/pallas_call | solution.py:371
  16.8 0.5 %shard_map.88 = (bf16[512,256]{1,0:T(8,128)(2,1)S(1)}, bf16[512,128]{1,0:T(8,128)(2,1)S(1)}) custom-call(bf16[512,128]{1,0:T(8,128)(2,1)S(1)} %collective-permute-done.2.arrived_ref, f32[512,256]{1,0:T(8,128)S(1)} %get-tuple-element.54.part_ref, bf16[4,1,4,128,128]{4,3,2,1,0:T(8,128)(2,1)S(1)} %get-tuple-element.46.panel_ref, ...), custom_call_target="tpu_custom_call" | custom-call | flops 1000000 | bytes 10000 | tf_op jit(solution)/shard_map/pallas_call | solution.py:371
  17.3 2.6 %collective-permute-start.5 = (bf16[512,128]{1,0:T(8,128)(2,1)S(1)}, bf16[512,128]{1,0:T(8,128)(2,1)S(1)}, u32[]{:S(2)}, u32[]{:S(2)}) collective-permute-start(bf16[512,128]{1,0:T(8,128)(2,1)S(1)} %get-tuple-element.62.sent_ref), channel_id=1, source_target_pairs={{0,8},{1,9},{2,10},{3,11},{4,12},{5,13},{6,14},{7,15},{8,0},{9,1},... | collective-permute-start | bytes 393224 | tf_op jit(solution)/shard_map/ppermute | solution.py:18
  19.9 0.6 %shard_map.89 = (f32[512,128]{1,0:T(8,128)S(1)}, bf16[128,128]{1,0:T(8,128)(2,1)S(1)}, bf16[512,128]{1,0:T(8,128)(2,1)S(1)}, bf16[8,512,512]{2,1,0:T(8,128)(2,1)S(1)}, bf16[8,512,128]{2,1,0:T(8,128)(2,1)S(1)}) custom-call(bf16[512,256]{1,0:T(8,128)(2,1)S(1)} %get-tuple-element.55.coef_ref, s32[4,1,1024]{2,1,0:T(1,128)S(1)} %get-tuple-element.45.perm_ref, ...), custom_call_target="tpu_custom_call" | custom-call | flops 1000000 | bytes 10000 | tf_op jit(solution)/shard_map/pallas_call | solution.py:371
  20.5 0.8 %collective-permute-start.4 = (bf16[512,128]{1,0:T(8,128)(2,1)S(1)}, bf16[512,128]{1,0:T(8,128)(2,1)S(1)}, u32[]{:S(2)}, u32[]{:S(2)}) collective-permute-start(bf16[512,128]{1,0:T(8,128)(2,1)S(1)} %get-tuple-element.61), channel_id=1, source_target_pairs={{0,8},{1,9},{2,10},{3,11},{4,12},{5,13},{6,14},{7,15},{8,0},{9,1},... | collective-permute-start | bytes 393224 | tf_op jit(solution)/shard_map/ppermute | solution.py:18
  21.3 2.3 %shard_map.90 = (bf16[8,512,512]{2,1,0:T(8,128)(2,1)S(1)}, bf16[8,512,128]{2,1,0:T(8,128)(2,1)S(1)}, f32[512,128]{1,0:T(8,128)S(1)}) custom-call(s32[4,1,1024]{2,1,0:T(1,128)S(1)} %get-tuple-element.45.perm_ref, s32[1,512]{1,0:T(1,128)S(1)} %get-tuple-element.58.own_slots_ref, ...), custom_call_target="tpu_custom_call", output_to_operand_aliasing={{0}: (3, {}), {1}: (4, {})} | custom-call | flops 1000000 | bytes 10000 | tf_op jit(solution)/shard_map/pallas_call | solution.py:371
  23.6 1.2 %collective-permute-done.5.arrived_ref = bf16[512,128]{1,0:T(8,128)(2,1)S(1)} collective-permute-done((bf16[512,128]{1,0:T(8,128)(2,1)S(1)}, bf16[512,128]{1,0:T(8,128)(2,1)S(1)}, u32[]{:S(2)}, u32[]{:S(2)}) %collective-permute-start.5) | collective-permute-done | bytes 131104 | tf_op jit(solution)/shard_map/ppermute | solution.py:18
  24.8 0.6 %shard_map.91.placed_ref = bf16[512,256]{1,0:T(8,128)(2,1)S(1)} custom-call(bf16[512,128]{1,0:T(8,128)(2,1)S(1)} %collective-permute-done.5.arrived_ref, f32[512,128]{1,0:T(8,128)S(1)} %get-tuple-element.63.part_ref, bf16[256,128]{1,0:T(8,128)(2,1)S(1)} %get-tuple-element.64.map_ref, bf16[8,512,512]{2,1,0:T(8,128)(2,1)S(1)} %get-tuple-element.68.chosen_ref, ...), custom_call_target="tpu_custom_call" | custom-call | flops 1000000 | bytes 10000 | tf_op jit(solution)/shard_map/pallas_call | solution.py:371
  25.4 1.1 %collective-permute-done.4.arrived_ref = bf16[512,128]{1,0:T(8,128)(2,1)S(1)} collective-permute-done((bf16[512,128]{1,0:T(8,128)(2,1)S(1)}, bf16[512,128]{1,0:T(8,128)(2,1)S(1)}, u32[]{:S(2)}, u32[]{:S(2)}) %collective-permute-start.4) | collective-permute-done | bytes 131104 | tf_op jit(solution)/shard_map/ppermute | solution.py:18
  26.4 0.5 %shard_map.92 = (bf16[512,256]{1,0:T(8,128)(2,1)S(1)}, bf16[512,128]{1,0:T(8,128)(2,1)S(1)}) custom-call(bf16[512,128]{1,0:T(8,128)(2,1)S(1)} %collective-permute-done.4.arrived_ref, bf16[512,256]{1,0:T(8,128)(2,1)S(1)} %shard_map.91.placed_ref, bf16[8,512,512]{2,1,0:T(8,128)(2,1)S(1)} %get-tuple-element.68.chosen_ref, ...), custom_call_target="tpu_custom_call" | custom-call | flops 1000000 | bytes 10000 | tf_op jit(solution)/shard_map/pallas_call | solution.py:371
  26.9 2.0 %collective-permute-start.6 = (bf16[512,128]{1,0:T(8,128)(2,1)S(1)}, bf16[512,128]{1,0:T(8,128)(2,1)S(1)}, u32[]{:S(2)}, u32[]{:S(2)}) collective-permute-start(bf16[512,128]{1,0:T(8,128)(2,1)S(1)} %get-tuple-element.71), channel_id=1, source_target_pairs={{0,4},{1,5},{2,6},{3,7},{4,0},{5,1},{6,2},{7,3},{8,12},{9,13},{10,... | collective-permute-start | bytes 393224 | tf_op jit(solution)/shard_map/ppermute | solution.py:18
  29.0 0.6 %shard_map.93.placed_ref = bf16[512,256]{1,0:T(8,128)(2,1)S(1)} custom-call(bf16[512,256]{1,0:T(8,128)(2,1)S(1)} %get-tuple-element.72.coef_ref, bf16[4,1,4,128,128]{4,3,2,1,0:T(8,128)(2,1)S(1)} %get-tuple-element.46.panel_ref, bf16[8,512,512]{2,1,0:T(8,128)(2,1)S(1)} %get-tuple-element.68.chosen_ref, bf16[8,512,128]{2,1,0:T(8,128)(2,1)S(1)} %get-tuple-element.69.low_ref), custom_call_target="tpu_custom_call" | custom-call | flops 1000000 | bytes 10000 | tf_op jit(solution)/shard_map/pallas_call | solution.py:371
  29.5 2.4 %collective-permute-done.6.arrived_ref = bf16[512,128]{1,0:T(8,128)(2,1)S(1)} collective-permute-done((bf16[512,128]{1,0:T(8,128)(2,1)S(1)}, bf16[512,128]{1,0:T(8,128)(2,1)S(1)}, u32[]{:S(2)}, u32[]{:S(2)}) %collective-permute-start.6) | collective-permute-done | bytes 131104 | tf_op jit(solution)/shard_map/ppermute | solution.py:18
  32.0 0.5 %shard_map.94 = (bf16[512,256]{1,0:T(8,128)(2,1)S(1)}, bf16[512,128]{1,0:T(8,128)(2,1)S(1)}) custom-call(bf16[512,128]{1,0:T(8,128)(2,1)S(1)} %collective-permute-done.6.arrived_ref, bf16[512,256]{1,0:T(8,128)(2,1)S(1)} %shard_map.93.placed_ref, bf16[8,512,512]{2,1,0:T(8,128)(2,1)S(1)} %get-tuple-element.68.chosen_ref, ...), custom_call_target="tpu_custom_call" | custom-call | flops 1000000 | bytes 10000 | tf_op jit(solution)/shard_map/pallas_call | solution.py:371
  32.4 1.6 %collective-permute-start.7 = (bf16[512,128]{1,0:T(8,128)(2,1)S(1)}, bf16[512,128]{1,0:T(8,128)(2,1)S(1)}, u32[]{:S(2)}, u32[]{:S(2)}) collective-permute-start(bf16[512,128]{1,0:T(8,128)(2,1)S(1)} %get-tuple-element.73), channel_id=1, source_target_pairs={{0,2},{1,3},{2,0},{3,1},{4,6},{5,7},{6,4},{7,5},{8,10},{9,11},{10,... | collective-permute-start | bytes 393224 | tf_op jit(solution)/shard_map/ppermute | solution.py:18
  34.0 0.6 %shard_map.95.placed_ref = bf16[512,256]{1,0:T(8,128)(2,1)S(1)} custom-call(bf16[512,256]{1,0:T(8,128)(2,1)S(1)} %get-tuple-element.74.coef_ref, bf16[4,1,4,128,128]{4,3,2,1,0:T(8,128)(2,1)S(1)} %get-tuple-element.46.panel_ref, bf16[8,512,512]{2,1,0:T(8,128)(2,1)S(1)} %get-tuple-element.68.chosen_ref, bf16[8,512,128]{2,1,0:T(8,128)(2,1)S(1)} %get-tuple-element.69.low_ref), custom_call_target="tpu_custom_call" | custom-call | flops 1000000 | bytes 10000 | tf_op jit(solution)/shard_map/pallas_call | solution.py:371
  34.6 2.9 %collective-permute-done.7.arrived_ref = bf16[512,128]{1,0:T(8,128)(2,1)S(1)} collective-permute-done((bf16[512,128]{1,0:T(8,128)(2,1)S(1)}, bf16[512,128]{1,0:T(8,128)(2,1)S(1)}, u32[]{:S(2)}, u32[]{:S(2)}) %collective-permute-start.7) | collective-permute-done | bytes 131104 | tf_op jit(solution)/shard_map/ppermute | solution.py:18
  37.5 0.5 %shard_map.96 = (bf16[512,256]{1,0:T(8,128)(2,1)S(1)}, bf16[512,128]{1,0:T(8,128)(2,1)S(1)}) custom-call(bf16[512,128]{1,0:T(8,128)(2,1)S(1)} %collective-permute-done.7.arrived_ref, bf16[512,256]{1,0:T(8,128)(2,1)S(1)} %shard_map.95.placed_ref, bf16[8,512,512]{2,1,0:T(8,128)(2,1)S(1)} %get-tuple-element.68.chosen_ref, ...), custom_call_target="tpu_custom_call" | custom-call | flops 1000000 | bytes 10000 | tf_op jit(solution)/shard_map/pallas_call | solution.py:371
  38.0 2.1 %collective-permute-start.8 = (bf16[512,128]{1,0:T(8,128)(2,1)S(1)}, bf16[512,128]{1,0:T(8,128)(2,1)S(1)}, u32[]{:S(2)}, u32[]{:S(2)}) collective-permute-start(bf16[512,128]{1,0:T(8,128)(2,1)S(1)} %get-tuple-element.75), channel_id=1, source_target_pairs={{0,1},{1,0},{2,3},{3,2},{4,5},{5,4},{6,7},{7,6},{8,9},{9,8},{10,11... | collective-permute-start | bytes 393224 | tf_op jit(solution)/shard_map/ppermute | solution.py:18
  40.0 0.6 %shard_map.97.placed_ref = bf16[512,256]{1,0:T(8,128)(2,1)S(1)} custom-call(bf16[512,256]{1,0:T(8,128)(2,1)S(1)} %get-tuple-element.76.coef_ref, bf16[4,1,4,128,128]{4,3,2,1,0:T(8,128)(2,1)S(1)} %get-tuple-element.46.panel_ref, bf16[8,512,512]{2,1,0:T(8,128)(2,1)S(1)} %get-tuple-element.68.chosen_ref, bf16[8,512,128]{2,1,0:T(8,128)(2,1)S(1)} %get-tuple-element.69.low_ref), custom_call_target="tpu_custom_call" | custom-call | flops 1000000 | bytes 10000 | tf_op jit(solution)/shard_map/pallas_call | solution.py:371
  40.6 0.4 collective-permute-done.8.arrived_ref
  41.0 1.6 %shard_map.98 = bf16[1024,512]{1,0:T(8,128)(2,1)} custom-call(bf16[512,128]{1,0:T(8,128)(2,1)S(1)} %collective-permute-done.8.arrived_ref, bf16[512,256]{1,0:T(8,128)(2,1)S(1)} %shard_map.97.placed_ref, bf16[8,512,512]{2,1,0:T(8,128)(2,1)S(1)} %get-tuple-element.68.chosen_ref, bf16[8,512,128]{2,1,0:T(8,128)(2,1)S(1)} %get-tuple-element.69.low_ref, ...), custom_call_target="tpu_custom_call" | custom-call | flops 1000000 | bytes 10000 | tf_op jit(solution)/shard_map/pallas_call | solution.py:371
  (3 shorter events, 0.2 us)
Async XLA Ops:
  2.0 1.5 %collective-permute-start = (bf16[512,128]{1,0:T(8,128)(2,1)S(1)}, bf16[512,128]{1,0:T(8,128)(2,1)S(1)}, u32[]{:S(2)}, u32[]{:S(2)}) collective-permute-start(bf16[512,128]{1,0:T(8,128)(2,1)S(1)} %get-tuple-element.42), channel_id=1, source_target_pairs={{0,1},{1,0},{2,3},{3,2},{4,5},{5,4},{6,7},{7,6},{8,9},{9,8},{10,11... | collective-permute-start | bytes 393224 | tf_op jit(solution)/shard_map/ppermute | solution.py:18
  4.1 6.8 %collective-permute-start.1 = (bf16[512,128]{1,0:T(8,128)(2,1)S(1)}, bf16[512,128]{1,0:T(8,128)(2,1)S(1)}, u32[]{:S(2)}, u32[]{:S(2)}) collective-permute-start(bf16[512,128]{1,0:T(8,128)(2,1)S(1)} %get-tuple-element.48), channel_id=1, source_target_pairs={{0,2},{1,3},{2,0},{3,1},{4,6},{5,7},{6,4},{7,5},{8,10},{9,11},{10,... | collective-permute-start | bytes 393224 | tf_op jit(solution)/shard_map/ppermute | solution.py:18
  11.4 5.4 %collective-permute-start.2 = (bf16[512,128]{1,0:T(8,128)(2,1)S(1)}, bf16[512,128]{1,0:T(8,128)(2,1)S(1)}, u32[]{:S(2)}, u32[]{:S(2)}) collective-permute-start(bf16[512,128]{1,0:T(8,128)(2,1)S(1)} %get-tuple-element.51), channel_id=1, source_target_pairs={{0,4},{1,5},{2,6},{3,7},{4,0},{5,1},{6,2},{7,3},{8,12},{9,13},{10,... | collective-permute-start | bytes 393224 | tf_op jit(solution)/shard_map/ppermute | solution.py:18
  13.2 6.7 %collective-permute-start.3 = (bf16[128,128]{1,0:T(8,128)(2,1)S(1)}, bf16[128,128]{1,0:T(8,128)(2,1)S(1)}, u32[]{:S(2)}, u32[]{:S(2)}) collective-permute-start(bf16[128,128]{1,0:T(8,128)(2,1)S(1)} %get-tuple-element.60), channel_id=1, source_target_pairs={{0,8},{1,9},{2,10},{3,11},{4,12},{5,13},{6,14},{7,15},{8,0},{9,1},... | collective-permute-start | bytes 98312 | tf_op jit(solution)/shard_map/ppermute | solution.py:18
  17.3 7.5 %collective-permute-start.5 = (bf16[512,128]{1,0:T(8,128)(2,1)S(1)}, bf16[512,128]{1,0:T(8,128)(2,1)S(1)}, u32[]{:S(2)}, u32[]{:S(2)}) collective-permute-start(bf16[512,128]{1,0:T(8,128)(2,1)S(1)} %get-tuple-element.62.sent_ref), channel_id=1, source_target_pairs={{0,8},{1,9},{2,10},{3,11},{4,12},{5,13},{6,14},{7,15},{8,0},{9,1},... | collective-permute-start | bytes 393224 | tf_op jit(solution)/shard_map/ppermute | solution.py:18
  20.5 5.9 %collective-permute-start.4 = (bf16[512,128]{1,0:T(8,128)(2,1)S(1)}, bf16[512,128]{1,0:T(8,128)(2,1)S(1)}, u32[]{:S(2)}, u32[]{:S(2)}) collective-permute-start(bf16[512,128]{1,0:T(8,128)(2,1)S(1)} %get-tuple-element.61), channel_id=1, source_target_pairs={{0,8},{1,9},{2,10},{3,11},{4,12},{5,13},{6,14},{7,15},{8,0},{9,1},... | collective-permute-start | bytes 393224 | tf_op jit(solution)/shard_map/ppermute | solution.py:18
  26.9 5.0 %collective-permute-start.6 = (bf16[512,128]{1,0:T(8,128)(2,1)S(1)}, bf16[512,128]{1,0:T(8,128)(2,1)S(1)}, u32[]{:S(2)}, u32[]{:S(2)}) collective-permute-start(bf16[512,128]{1,0:T(8,128)(2,1)S(1)} %get-tuple-element.71), channel_id=1, source_target_pairs={{0,4},{1,5},{2,6},{3,7},{4,0},{5,1},{6,2},{7,3},{8,12},{9,13},{10,... | collective-permute-start | bytes 393224 | tf_op jit(solution)/shard_map/ppermute | solution.py:18
  32.4 5.0 %collective-permute-start.7 = (bf16[512,128]{1,0:T(8,128)(2,1)S(1)}, bf16[512,128]{1,0:T(8,128)(2,1)S(1)}, u32[]{:S(2)}, u32[]{:S(2)}) collective-permute-start(bf16[512,128]{1,0:T(8,128)(2,1)S(1)} %get-tuple-element.73), channel_id=1, source_target_pairs={{0,2},{1,3},{2,0},{3,1},{4,6},{5,7},{6,4},{7,5},{8,10},{9,11},{10,... | collective-permute-start | bytes 393224 | tf_op jit(solution)/shard_map/ppermute | solution.py:18
  38.0 3.1 %collective-permute-start.8 = (bf16[512,128]{1,0:T(8,128)(2,1)S(1)}, bf16[512,128]{1,0:T(8,128)(2,1)S(1)}, u32[]{:S(2)}, u32[]{:S(2)}) collective-permute-start(bf16[512,128]{1,0:T(8,128)(2,1)S(1)} %get-tuple-element.75), channel_id=1, source_target_pairs={{0,1},{1,0},{2,3},{3,2},{4,5},{5,4},{6,7},{7,6},{8,9},{9,8},{10,11... | collective-permute-start | bytes 393224 | tf_op jit(solution)/shard_map/ppermute | solution.py:18

commit v9 on v8

--- a/solution.py
+++ b/solution.py
@@ -130,8 +130,8 @@
     loads[1].wait()
     slots = compose(pixel_ref[...], half_row(perm_ref, 0, 1 - bit_of(0)))
     slots_ref[...] = slots
+    chosen, low = take_plan(slots)
     loads[2].wait()
-    chosen, low = take_plan(slots)
     total = None
     for at in range(0, half, chunk):
         loads[3 + at // chunk].wait()
@@ -186,12 +186,14 @@
 def echo_back(loads, echo, leaf, slots, back_ref, turns):
     half = echo.shape[0] // 2
     chunk = echo.shape[0] // scene_chunks
+    for at in turns[0] if turns else ():
+        loads[2 + at].start()
     loads[0].wait()
     plan = place_plan(slots[...], half)
     loads[1].wait()
     back = []
     for turn in turns or (range(scene_chunks),):
-        for at in turn if turns else ():
+        for at in turn if turns and turn != turns[0] else ():
             loads[2 + at].start()
         for at in turn:
             loads[2 + at].wait()
@@ -293,7 +295,7 @@
         for load in loads[:2]:
             load.start()
         make_plans(perm_ref, (own_slots_ref, out_slots_ref), chosen_ref, low_ref)
-        echo_back(loads, echo, leaf, slots, back_ref, ((0,), (1,), (2, 3)))
+        echo_back(loads, echo, leaf, slots, back_ref, ((0,), (1,), (2,), (3,)))
         echo_part_ref[...] = mul_t(back_ref[...], pair_weights(panel_ref, level))
 
     plan = take_plan(half_row(perm_ref, level, bit_of(level)))

time: 43 us -> 42.9 us (level)
  no operation moved by 1% of the time
where the time goes in v9:
time: 42.9 us; the launch traced here: 42.6 us
  Pallas kernels  17.2 us (40%)
  starting transfers between devices  16.7 us (39%)
  waiting for transfers between devices  8.46 us (20%)
    pallas_call x17, Pallas kernels, call(): pl.pallas_call(kernel, out_shape=shapes, in_specs=[near] * len(operands)...  17.2 us
    ppermute x9, starting transfers between devices, swapped(): lax.ppermute(value, axis, [(i, i ^ 1 << apart) for i in range(lax.axis_si...  16.7 us
    ppermute x9, waiting for transfers between devices, swapped(): lax.ppermute(value, axis, [(i, i ^ 1 << apart) for i in range(lax.axis_si...  8.46 us
  transfers between devices with their start and end apart: 9, of which 7 were waited for; matrix products, arithmetic and copies ran while one was open for 0% of the time, Pallas kernels for 26%

profile of v9, /device:TPU:0, one launch (start us, length us, event | category | flops | bytes accessed | tf_op | source)
XLA Modules:
  0.0 42.6 jit_solution(7527560324620471570)
XLA Ops:
  0.0 2.0 %shard_map.82 = (bf16[1024,512]{1,0:T(8,128)(2,1)S(1)}, bf16[512,128]{1,0:T(8,128)(2,1)S(1)}, s32[1,1024]{1,0:T(1,128)S(1)}, s32[4,1,1024]{2,1,0:T(1,128)S(1)}, ...) custom-call(bf16[1024,512]{1,0:T(8,128)(2,1)} %scene_in.1, ...), custom_call_target="tpu_custom_call" | custom-call | flops 1000000 | bytes 10000 | tf_op jit(solution)/shard_map/pallas_call | solution.py:373
  2.0 0.5 %collective-permute-start = (bf16[512,128]{1,0:T(8,128)(2,1)S(1)}, bf16[512,128]{1,0:T(8,128)(2,1)S(1)}, u32[]{:S(2)}, u32[]{:S(2)}) collective-permute-start(bf16[512,128]{1,0:T(8,128)(2,1)S(1)} %get-tuple-element.42), channel_id=1, source_target_pairs={{0,1},{1,0},{2,3},{3,2},{4,5},{5,4},{6,7},{7,6},{8,9},{9,8},{10,11... | collective-permute-start | bytes 393224 | tf_op jit(solution)/shard_map/ppermute | solution.py:18
  2.6 0.7 %shard_map.83 = (s32[1,512]{1,0:T(1,128)S(1)}, f32[512,256]{1,0:T(8,128)S(1)}) custom-call(bf16[512,256]{1,0:T(8,128)(2,1)S(1)} %get-tuple-element.43.leafed_ref, s32[1,1024]{1,0:T(1,128)S(1)} %get-tuple-element.44.pixel_ref, s32[4,1,1024]{2,1,0:T(1,128)S(1)} %get-tuple-element.45.perm_ref, bf16[4,1,4,128,128]{4,3,2,1,0:T(8,128)(2,1)S(1)} %get-tuple-element.46.panel_ref), custom_call_target="tpu_custom_call" | custom-call | flops 1000000 | bytes 10000 | tf_op jit(solution)/shard_map/pallas_call | solution.py:373
  3.3 0.3 collective-permute-done.arrived_ref
  3.5 0.5 %shard_map.84 = (bf16[512,256]{1,0:T(8,128)(2,1)S(1)}, bf16[512,128]{1,0:T(8,128)(2,1)S(1)}) custom-call(bf16[512,128]{1,0:T(8,128)(2,1)S(1)} %collective-permute-done.arrived_ref, f32[512,256]{1,0:T(8,128)S(1)} %get-tuple-element.47.part_ref, bf16[4,1,4,128,128]{4,3,2,1,0:T(8,128)(2,1)S(1)} %get-tuple-element.46.panel_ref, ...), custom_call_target="tpu_custom_call" | custom-call | flops 1000000 | bytes 10000 | tf_op jit(solution)/shard_map/pallas_call | solution.py:373
  4.1 2.9 %collective-permute-start.1 = (bf16[512,128]{1,0:T(8,128)(2,1)S(1)}, bf16[512,128]{1,0:T(8,128)(2,1)S(1)}, u32[]{:S(2)}, u32[]{:S(2)}) collective-permute-start(bf16[512,128]{1,0:T(8,128)(2,1)S(1)} %get-tuple-element.48), channel_id=1, source_target_pairs={{0,2},{1,3},{2,0},{3,1},{4,6},{5,7},{6,4},{7,5},{8,10},{9,11},{10,... | collective-permute-start | bytes 393224 | tf_op jit(solution)/shard_map/ppermute | solution.py:18
  7.0 3.8 %shard_map.85 = (f32[512,256]{1,0:T(8,128)S(1)}, bf16[256,256]{1,0:T(8,128)(2,1)S(1)}, bf16[256,128]{1,0:T(8,128)(2,1)S(1)}, bf16[128,128]{1,0:T(8,128)(2,1)S(1)}, bf16[512,256]{1,0:T(8,128)(2,1)S(1)}) custom-call(bf16[512,256]{1,0:T(8,128)(2,1)S(1)} %get-tuple-element.49.coef_ref, s32[4,1,1024]{2,1,0:T(1,128)S(1)} %get-tuple-element.45.perm_ref, ...), custom_call_target="tpu_custom_call" | custom-call | flops 1000000 | bytes 10000 | tf_op jit(solution)/shard_map/pallas_call | solution.py:373
  10.9 0.5 %shard_map.86 = (bf16[512,256]{1,0:T(8,128)(2,1)S(1)}, bf16[512,128]{1,0:T(8,128)(2,1)S(1)}) custom-call(bf16[512,128]{1,0:T(8,128)(2,1)S(1)} %collective-permute-done.1.arrived_ref, f32[512,256]{1,0:T(8,128)S(1)} %get-tuple-element.50.part_ref, bf16[4,1,4,128,128]{4,3,2,1,0:T(8,128)(2,1)S(1)} %get-tuple-element.46.panel_ref, ...), custom_call_target="tpu_custom_call" | custom-call | flops 1000000 | bytes 10000 | tf_op jit(solution)/shard_map/pallas_call | solution.py:373
  11.4 1.8 %collective-permute-start.2 = (bf16[512,128]{1,0:T(8,128)(2,1)S(1)}, bf16[512,128]{1,0:T(8,128)(2,1)S(1)}, u32[]{:S(2)}, u32[]{:S(2)}) collective-permute-start(bf16[512,128]{1,0:T(8,128)(2,1)S(1)} %get-tuple-element.51), channel_id=1, source_target_pairs={{0,4},{1,5},{2,6},{3,7},{4,0},{5,1},{6,2},{7,3},{8,12},{9,13},{10,... | collective-permute-start | bytes 393224 | tf_op jit(solution)/shard_map/ppermute | solution.py:18
  13.2 2.6 %collective-permute-start.3 = (bf16[128,128]{1,0:T(8,128)(2,1)S(1)}, bf16[128,128]{1,0:T(8,128)(2,1)S(1)}, u32[]{:S(2)}, u32[]{:S(2)}) collective-permute-start(bf16[128,128]{1,0:T(8,128)(2,1)S(1)} %get-tuple-element.60), channel_id=1, source_target_pairs={{0,8},{1,9},{2,10},{3,11},{4,12},{5,13},{6,14},{7,15},{8,0},{9,1},... | collective-permute-start | bytes 98312 | tf_op jit(solution)/shard_map/ppermute | solution.py:18
  15.8 0.8 %shard_map.87 = (f32[512,256]{1,0:T(8,128)S(1)}, f32[512,256]{1,0:T(8,128)S(1)}) custom-call(bf16[512,256]{1,0:T(8,128)(2,1)S(1)} %get-tuple-element.52.coef_ref, s32[4,1,1024]{2,1,0:T(1,128)S(1)} %get-tuple-element.45.perm_ref, bf16[4,1,4,128,128]{4,3,2,1,0:T(8,128)(2,1)S(1)} %get-tuple-element.46.panel_ref, bf16[512,256]{1,0:T(8,128)(2,1)S(1)} %get-tuple-element.53.back_ref), custom_call_target="tpu_custom_call" | custom-call | flops 1000000 | bytes 10000 | tf_op jit(solution)/shard_map/pallas_call | solution.py:373
  16.8 0.5 %shard_map.88 = (bf16[512,256]{1,0:T(8,128)(2,1)S(1)}, bf16[512,128]{1,0:T(8,128)(2,1)S(1)}) custom-call(bf16[512,128]{1,0:T(8,128)(2,1)S(1)} %collective-permute-done.2.arrived_ref, f32[512,256]{1,0:T(8,128)S(1)} %get-tuple-element.54.part_ref, bf16[4,1,4,128,128]{4,3,2,1,0:T(8,128)(2,1)S(1)} %get-tuple-element.46.panel_ref, ...), custom_call_target="tpu_custom_call" | custom-call | flops 1000000 | bytes 10000 | tf_op jit(solution)/shard_map/pallas_call | solution.py:373
  17.3 2.6 %collective-permute-start.5 = (bf16[512,128]{1,0:T(8,128)(2,1)S(1)}, bf16[512,128]{1,0:T(8,128)(2,1)S(1)}, u32[]{:S(2)}, u32[]{:S(2)}) collective-permute-start(bf16[512,128]{1,0:T(8,128)(2,1)S(1)} %get-tuple-element.62.sent_ref), channel_id=1, source_target_pairs={{0,8},{1,9},{2,10},{3,11},{4,12},{5,13},{6,14},{7,15},{8,0},{9,1},... | collective-permute-start | bytes 393224 | tf_op jit(solution)/shard_map/ppermute | solution.py:18
  19.9 0.6 %shard_map.89 = (f32[512,128]{1,0:T(8,128)S(1)}, bf16[128,128]{1,0:T(8,128)(2,1)S(1)}, bf16[512,128]{1,0:T(8,128)(2,1)S(1)}, bf16[8,512,512]{2,1,0:T(8,128)(2,1)S(1)}, bf16[8,512,128]{2,1,0:T(8,128)(2,1)S(1)}) custom-call(bf16[512,256]{1,0:T(8,128)(2,1)S(1)} %get-tuple-element.55.coef_ref, s32[4,1,1024]{2,1,0:T(1,128)S(1)} %get-tuple-element.45.perm_ref, ...), custom_call_target="tpu_custom_call" | custom-call | flops 1000000 | bytes 10000 | tf_op jit(solution)/shard_map/pallas_call | solution.py:373
  20.5 0.8 %collective-permute-start.4 = (bf16[512,128]{1,0:T(8,128)(2,1)S(1)}, bf16[512,128]{1,0:T(8,128)(2,1)S(1)}, u32[]{:S(2)}, u32[]{:S(2)}) collective-permute-start(bf16[512,128]{1,0:T(8,128)(2,1)S(1)} %get-tuple-element.61), channel_id=1, source_target_pairs={{0,8},{1,9},{2,10},{3,11},{4,12},{5,13},{6,14},{7,15},{8,0},{9,1},... | collective-permute-start | bytes 393224 | tf_op jit(solution)/shard_map/ppermute | solution.py:18
  21.3 2.3 %shard_map.90 = (bf16[8,512,512]{2,1,0:T(8,128)(2,1)S(1)}, bf16[8,512,128]{2,1,0:T(8,128)(2,1)S(1)}, f32[512,128]{1,0:T(8,128)S(1)}) custom-call(s32[4,1,1024]{2,1,0:T(1,128)S(1)} %get-tuple-element.45.perm_ref, s32[1,512]{1,0:T(1,128)S(1)} %get-tuple-element.58.own_slots_ref, ...), custom_call_target="tpu_custom_call", output_to_operand_aliasing={{0}: (3, {}), {1}: (4, {})} | custom-call | flops 1000000 | bytes 10000 | tf_op jit(solution)/shard_map/pallas_call | solution.py:373
  23.6 1.2 %collective-permute-done.5.arrived_ref = bf16[512,128]{1,0:T(8,128)(2,1)S(1)} collective-permute-done((bf16[512,128]{1,0:T(8,128)(2,1)S(1)}, bf16[512,128]{1,0:T(8,128)(2,1)S(1)}, u32[]{:S(2)}, u32[]{:S(2)}) %collective-permute-start.5) | collective-permute-done | bytes 131104 | tf_op jit(solution)/shard_map/ppermute | solution.py:18
  24.8 0.6 %shard_map.91.placed_ref = bf16[512,256]{1,0:T(8,128)(2,1)S(1)} custom-call(bf16[512,128]{1,0:T(8,128)(2,1)S(1)} %collective-permute-done.5.arrived_ref, f32[512,128]{1,0:T(8,128)S(1)} %get-tuple-element.63.part_ref, bf16[256,128]{1,0:T(8,128)(2,1)S(1)} %get-tuple-element.64.map_ref, bf16[8,512,512]{2,1,0:T(8,128)(2,1)S(1)} %get-tuple-element.68.chosen_ref, ...), custom_call_target="tpu_custom_call" | custom-call | flops 1000000 | bytes 10000 | tf_op jit(solution)/shard_map/pallas_call | solution.py:373
  25.4 1.1 %collective-permute-done.4.arrived_ref = bf16[512,128]{1,0:T(8,128)(2,1)S(1)} collective-permute-done((bf16[512,128]{1,0:T(8,128)(2,1)S(1)}, bf16[512,128]{1,0:T(8,128)(2,1)S(1)}, u32[]{:S(2)}, u32[]{:S(2)}) %collective-permute-start.4) | collective-permute-done | bytes 131104 | tf_op jit(solution)/shard_map/ppermute | solution.py:18
  26.4 0.5 %shard_map.92 = (bf16[512,256]{1,0:T(8,128)(2,1)S(1)}, bf16[512,128]{1,0:T(8,128)(2,1)S(1)}) custom-call(bf16[512,128]{1,0:T(8,128)(2,1)S(1)} %collective-permute-done.4.arrived_ref, bf16[512,256]{1,0:T(8,128)(2,1)S(1)} %shard_map.91.placed_ref, bf16[8,512,512]{2,1,0:T(8,128)(2,1)S(1)} %get-tuple-element.68.chosen_ref, ...), custom_call_target="tpu_custom_call" | custom-call | flops 1000000 | bytes 10000 | tf_op jit(solution)/shard_map/pallas_call | solution.py:373
  26.9 2.0 %collective-permute-start.6 = (bf16[512,128]{1,0:T(8,128)(2,1)S(1)}, bf16[512,128]{1,0:T(8,128)(2,1)S(1)}, u32[]{:S(2)}, u32[]{:S(2)}) collective-permute-start(bf16[512,128]{1,0:T(8,128)(2,1)S(1)} %get-tuple-element.71), channel_id=1, source_target_pairs={{0,4},{1,5},{2,6},{3,7},{4,0},{5,1},{6,2},{7,3},{8,12},{9,13},{10,... | collective-permute-start | bytes 393224 | tf_op jit(solution)/shard_map/ppermute | solution.py:18
  28.9 0.6 %shard_map.93.placed_ref = bf16[512,256]{1,0:T(8,128)(2,1)S(1)} custom-call(bf16[512,256]{1,0:T(8,128)(2,1)S(1)} %get-tuple-element.72.coef_ref, bf16[4,1,4,128,128]{4,3,2,1,0:T(8,128)(2,1)S(1)} %get-tuple-element.46.panel_ref, bf16[8,512,512]{2,1,0:T(8,128)(2,1)S(1)} %get-tuple-element.68.chosen_ref, bf16[8,512,128]{2,1,0:T(8,128)(2,1)S(1)} %get-tuple-element.69.low_ref), custom_call_target="tpu_custom_call" | custom-call | flops 1000000 | bytes 10000 | tf_op jit(solution)/shard_map/pallas_call | solution.py:373
  29.5 2.4 %collective-permute-done.6.arrived_ref = bf16[512,128]{1,0:T(8,128)(2,1)S(1)} collective-permute-done((bf16[512,128]{1,0:T(8,128)(2,1)S(1)}, bf16[512,128]{1,0:T(8,128)(2,1)S(1)}, u32[]{:S(2)}, u32[]{:S(2)}) %collective-permute-start.6) | collective-permute-done | bytes 131104 | tf_op jit(solution)/shard_map/ppermute | solution.py:18
  32.0 0.5 %shard_map.94 = (bf16[512,256]{1,0:T(8,128)(2,1)S(1)}, bf16[512,128]{1,0:T(8,128)(2,1)S(1)}) custom-call(bf16[512,128]{1,0:T(8,128)(2,1)S(1)} %collective-permute-done.6.arrived_ref, bf16[512,256]{1,0:T(8,128)(2,1)S(1)} %shard_map.93.placed_ref, bf16[8,512,512]{2,1,0:T(8,128)(2,1)S(1)} %get-tuple-element.68.chosen_ref, ...), custom_call_target="tpu_custom_call" | custom-call | flops 1000000 | bytes 10000 | tf_op jit(solution)/shard_map/pallas_call | solution.py:373
  32.4 1.6 %collective-permute-start.7 = (bf16[512,128]{1,0:T(8,128)(2,1)S(1)}, bf16[512,128]{1,0:T(8,128)(2,1)S(1)}, u32[]{:S(2)}, u32[]{:S(2)}) collective-permute-start(bf16[512,128]{1,0:T(8,128)(2,1)S(1)} %get-tuple-element.73), channel_id=1, source_target_pairs={{0,2},{1,3},{2,0},{3,1},{4,6},{5,7},{6,4},{7,5},{8,10},{9,11},{10,... | collective-permute-start | bytes 393224 | tf_op jit(solution)/shard_map/ppermute | solution.py:18
  34.0 0.6 %shard_map.95.placed_ref = bf16[512,256]{1,0:T(8,128)(2,1)S(1)} custom-call(bf16[512,256]{1,0:T(8,128)(2,1)S(1)} %get-tuple-element.74.coef_ref, bf16[4,1,4,128,128]{4,3,2,1,0:T(8,128)(2,1)S(1)} %get-tuple-element.46.panel_ref, bf16[8,512,512]{2,1,0:T(8,128)(2,1)S(1)} %get-tuple-element.68.chosen_ref, bf16[8,512,128]{2,1,0:T(8,128)(2,1)S(1)} %get-tuple-element.69.low_ref), custom_call_target="tpu_custom_call" | custom-call | flops 1000000 | bytes 10000 | tf_op jit(solution)/shard_map/pallas_call | solution.py:373
  34.6 2.9 %collective-permute-done.7.arrived_ref = bf16[512,128]{1,0:T(8,128)(2,1)S(1)} collective-permute-done((bf16[512,128]{1,0:T(8,128)(2,1)S(1)}, bf16[512,128]{1,0:T(8,128)(2,1)S(1)}, u32[]{:S(2)}, u32[]{:S(2)}) %collective-permute-start.7) | collective-permute-done | bytes 131104 | tf_op jit(solution)/shard_map/ppermute | solution.py:18
  37.5 0.5 %shard_map.96 = (bf16[512,256]{1,0:T(8,128)(2,1)S(1)}, bf16[512,128]{1,0:T(8,128)(2,1)S(1)}) custom-call(bf16[512,128]{1,0:T(8,128)(2,1)S(1)} %collective-permute-done.7.arrived_ref, bf16[512,256]{1,0:T(8,128)(2,1)S(1)} %shard_map.95.placed_ref, bf16[8,512,512]{2,1,0:T(8,128)(2,1)S(1)} %get-tuple-element.68.chosen_ref, ...), custom_call_target="tpu_custom_call" | custom-call | flops 1000000 | bytes 10000 | tf_op jit(solution)/shard_map/pallas_call | solution.py:373
  38.0 1.9 %collective-permute-start.8 = (bf16[512,128]{1,0:T(8,128)(2,1)S(1)}, bf16[512,128]{1,0:T(8,128)(2,1)S(1)}, u32[]{:S(2)}, u32[]{:S(2)}) collective-permute-start(bf16[512,128]{1,0:T(8,128)(2,1)S(1)} %get-tuple-element.75), channel_id=1, source_target_pairs={{0,1},{1,0},{2,3},{3,2},{4,5},{5,4},{6,7},{7,6},{8,9},{9,8},{10,11... | collective-permute-start | bytes 393224 | tf_op jit(solution)/shard_map/ppermute | solution.py:18
  39.9 0.6 %shard_map.97.placed_ref = bf16[512,256]{1,0:T(8,128)(2,1)S(1)} custom-call(bf16[512,256]{1,0:T(8,128)(2,1)S(1)} %get-tuple-element.76.coef_ref, bf16[4,1,4,128,128]{4,3,2,1,0:T(8,128)(2,1)S(1)} %get-tuple-element.46.panel_ref, bf16[8,512,512]{2,1,0:T(8,128)(2,1)S(1)} %get-tuple-element.68.chosen_ref, bf16[8,512,128]{2,1,0:T(8,128)(2,1)S(1)} %get-tuple-element.69.low_ref), custom_call_target="tpu_custom_call" | custom-call | flops 1000000 | bytes 10000 | tf_op jit(solution)/shard_map/pallas_call | solution.py:373
  40.5 0.4 collective-permute-done.8.arrived_ref
  40.9 1.6 %shard_map.98 = bf16[1024,512]{1,0:T(8,128)(2,1)} custom-call(bf16[512,128]{1,0:T(8,128)(2,1)S(1)} %collective-permute-done.8.arrived_ref, bf16[512,256]{1,0:T(8,128)(2,1)S(1)} %shard_map.97.placed_ref, bf16[8,512,512]{2,1,0:T(8,128)(2,1)S(1)} %get-tuple-element.68.chosen_ref, bf16[8,512,128]{2,1,0:T(8,128)(2,1)S(1)} %get-tuple-element.69.low_ref, ...), custom_call_target="tpu_custom_call" | custom-call | flops 1000000 | bytes 10000 | tf_op jit(solution)/shard_map/pallas_call | solution.py:373
  (3 shorter events, 0.2 us)
Async XLA Ops:
  2.0 1.5 %collective-permute-start = (bf16[512,128]{1,0:T(8,128)(2,1)S(1)}, bf16[512,128]{1,0:T(8,128)(2,1)S(1)}, u32[]{:S(2)}, u32[]{:S(2)}) collective-permute-start(bf16[512,128]{1,0:T(8,128)(2,1)S(1)} %get-tuple-element.42), channel_id=1, source_target_pairs={{0,1},{1,0},{2,3},{3,2},{4,5},{5,4},{6,7},{7,6},{8,9},{9,8},{10,11... | collective-permute-start | bytes 393224 | tf_op jit(solution)/shard_map/ppermute | solution.py:18
  4.1 6.8 %collective-permute-start.1 = (bf16[512,128]{1,0:T(8,128)(2,1)S(1)}, bf16[512,128]{1,0:T(8,128)(2,1)S(1)}, u32[]{:S(2)}, u32[]{:S(2)}) collective-permute-start(bf16[512,128]{1,0:T(8,128)(2,1)S(1)} %get-tuple-element.48), channel_id=1, source_target_pairs={{0,2},{1,3},{2,0},{3,1},{4,6},{5,7},{6,4},{7,5},{8,10},{9,11},{10,... | collective-permute-start | bytes 393224 | tf_op jit(solution)/shard_map/ppermute | solution.py:18
  11.4 5.4 %collective-permute-start.2 = (bf16[512,128]{1,0:T(8,128)(2,1)S(1)}, bf16[512,128]{1,0:T(8,128)(2,1)S(1)}, u32[]{:S(2)}, u32[]{:S(2)}) collective-permute-start(bf16[512,128]{1,0:T(8,128)(2,1)S(1)} %get-tuple-element.51), channel_id=1, source_target_pairs={{0,4},{1,5},{2,6},{3,7},{4,0},{5,1},{6,2},{7,3},{8,12},{9,13},{10,... | collective-permute-start | bytes 393224 | tf_op jit(solution)/shard_map/ppermute | solution.py:18
  13.2 6.7 %collective-permute-start.3 = (bf16[128,128]{1,0:T(8,128)(2,1)S(1)}, bf16[128,128]{1,0:T(8,128)(2,1)S(1)}, u32[]{:S(2)}, u32[]{:S(2)}) collective-permute-start(bf16[128,128]{1,0:T(8,128)(2,1)S(1)} %get-tuple-element.60), channel_id=1, source_target_pairs={{0,8},{1,9},{2,10},{3,11},{4,12},{5,13},{6,14},{7,15},{8,0},{9,1},... | collective-permute-start | bytes 98312 | tf_op jit(solution)/shard_map/ppermute | solution.py:18
  17.3 7.5 %collective-permute-start.5 = (bf16[512,128]{1,0:T(8,128)(2,1)S(1)}, bf16[512,128]{1,0:T(8,128)(2,1)S(1)}, u32[]{:S(2)}, u32[]{:S(2)}) collective-permute-start(bf16[512,128]{1,0:T(8,128)(2,1)S(1)} %get-tuple-element.62.sent_ref), channel_id=1, source_target_pairs={{0,8},{1,9},{2,10},{3,11},{4,12},{5,13},{6,14},{7,15},{8,0},{9,1},... | collective-permute-start | bytes 393224 | tf_op jit(solution)/shard_map/ppermute | solution.py:18
  20.5 5.9 %collective-permute-start.4 = (bf16[512,128]{1,0:T(8,128)(2,1)S(1)}, bf16[512,128]{1,0:T(8,128)(2,1)S(1)}, u32[]{:S(2)}, u32[]{:S(2)}) collective-permute-start(bf16[512,128]{1,0:T(8,128)(2,1)S(1)} %get-tuple-element.61), channel_id=1, source_target_pairs={{0,8},{1,9},{2,10},{3,11},{4,12},{5,13},{6,14},{7,15},{8,0},{9,1},... | collective-permute-start | bytes 393224 | tf_op jit(solution)/shard_map/ppermute | solution.py:18
  26.9 5.0 %collective-permute-start.6 = (bf16[512,128]{1,0:T(8,128)(2,1)S(1)}, bf16[512,128]{1,0:T(8,128)(2,1)S(1)}, u32[]{:S(2)}, u32[]{:S(2)}) collective-permute-start(bf16[512,128]{1,0:T(8,128)(2,1)S(1)} %get-tuple-element.71), channel_id=1, source_target_pairs={{0,4},{1,5},{2,6},{3,7},{4,0},{5,1},{6,2},{7,3},{8,12},{9,13},{10,... | collective-permute-start | bytes 393224 | tf_op jit(solution)/shard_map/ppermute | solution.py:18
  32.4 5.0 %collective-permute-start.7 = (bf16[512,128]{1,0:T(8,128)(2,1)S(1)}, bf16[512,128]{1,0:T(8,128)(2,1)S(1)}, u32[]{:S(2)}, u32[]{:S(2)}) collective-permute-start(bf16[512,128]{1,0:T(8,128)(2,1)S(1)} %get-tuple-element.73), channel_id=1, source_target_pairs={{0,2},{1,3},{2,0},{3,1},{4,6},{5,7},{6,4},{7,5},{8,10},{9,11},{10,... | collective-permute-start | bytes 393224 | tf_op jit(solution)/shard_map/ppermute | solution.py:18
  38.0 2.9 %collective-permute-start.8 = (bf16[512,128]{1,0:T(8,128)(2,1)S(1)}, bf16[512,128]{1,0:T(8,128)(2,1)S(1)}, u32[]{:S(2)}, u32[]{:S(2)}) collective-permute-start(bf16[512,128]{1,0:T(8,128)(2,1)S(1)} %get-tuple-element.75), channel_id=1, source_target_pairs={{0,1},{1,0},{2,3},{3,2},{4,5},{5,4},{6,7},{7,6},{8,9},{9,8},{10,11... | collective-permute-start | bytes 393224 | tf_op jit(solution)/shard_map/ppermute | solution.py:18

commit v10 on v9

--- a/solution.py
+++ b/solution.py
@@ -190,20 +190,26 @@
         loads[2 + at].start()
     loads[0].wait()
     plan = place_plan(slots[...], half)
-    loads[1].wait()
+    if turns:
+        loads[1].wait()
+    else:
+        for load in loads[2:]:
+            load.wait()
     back = []
     for turn in turns or (range(scene_chunks),):
         for at in turn if turns and turn != turns[0] else ():
             loads[2 + at].start()
         for at in turn:
-            loads[2 + at].wait()
+            if turns:
+                loads[2 + at].wait()
             back.append(mul_t(echo[pl.ds(at * chunk, chunk)], leaf[...]).astype(thin))
     back_ref[...] = place(plan, jnp.concatenate(back, axis=0)).astype(thin)
 
 
 def own_map_kernel(
     level, last, coef_ref, perm_ref, panel_ref, echo_in, leaf_in, slots_in,
-    part_ref, own_map_ref, other_map_ref, sent_map_ref, back_ref, echo, leaf, slots, done,
+    part_ref, own_map_ref, other_map_ref, sent_map_ref, echo_part_ref, back_ref,
+    echo, leaf, slots, done,
 ):
     loads = echo_loads(echo_in, leaf_in, slots_in, echo, leaf, slots, done)
     early = bit_of(0) == 0
@@ -216,14 +222,9 @@
     @pl.when(jnp.logical_not(early))
     def _():
         loads[1].start()
-        loads[1].wait()
 
     own_kernel(level, coef_ref, perm_ref, panel_ref, part_ref)
-
-    @pl.when(early)
-    def _():
-        echo_back(loads, echo, leaf, slots, back_ref, None)
-
+    loads[1].wait()
     gram = split(mul_t(leaf[...], leaf[...]))
     both = pair_weights(panel_ref, last)
     width = both.shape[0] // 2
@@ -233,6 +234,11 @@
     own_map_ref[...] = split(maps[:width])
     other_map_ref[...] = split(maps[width:, :width])
     sent_map_ref[...] = maps[width:, width:].astype(thin)
+
+    @pl.when(early)
+    def _():
+        echo_back(loads, echo, leaf, slots, back_ref, None)
+        echo_part_ref[...] = mul_t(back_ref[...], both)
 
 
 def mix(level, arrived_ref, part_ref, panel_ref):
@@ -254,16 +260,6 @@
         piece = mul(chosen[:, at : at + step], mixture)
         total = piece if total is None else total + piece
     out_ref[...] = jnp.where(low > 0.5, total[:, :width], total[:, width:]).astype(thin)
-
-
-def own_echo_kernel(
-    level, last, coef_ref, perm_ref, panel_ref, back_ref, part_ref, echo_part_ref
-):
-    own_kernel(level, coef_ref, perm_ref, panel_ref, part_ref)
-
-    @pl.when(bit_of(0) == 0)
-    def _():
-        echo_part_ref[...] = mul_t(back_ref[...], pair_weights(panel_ref, last))
 
 
 def make_plans(perm_ref, slots_refs, chosen_ref, low_ref):
@@ -432,23 +428,14 @@
             narrow_map = ((2 * width, width), thin)
             part, own_map, other_map, sent_map, early = call(
                 functools.partial(own_map_kernel, level, last),
-                [mixed, ((2 * width, 2 * width), thin), narrow_map, ((width, width), thin), column_of],
+                [mixed, ((2 * width, 2 * width), thin), narrow_map, ((width, width), thin), mixed],
                 coefficients,
                 perms,
                 blocks,
                 far=(echoes, source_leaf, pulse_slot),
-                scratch=echo_scratch,
+                scratch=[pltpu.VMEM((half, 2 * width), thin)] + echo_scratch,
             )
             arrived_map = swapped(sent_map, "box", last)
-        elif level == 2:
-            part, early = call(
-                functools.partial(own_echo_kernel, level, last),
-                [mixed, mixed],
-                coefficients,
-                perms,
-                blocks,
-                early,
-            )
         elif level < last:
             part = call(
                 functools.partial(own_kernel, level),

time: 42.9 us -> 42.9 us (level)
  Pallas kernels: 17.2 us -> 16.4 us
  waiting for transfers between devices: 8.46 us -> 9.19 us
    pallas_call x17, Pallas kernels: 17.2 us -> 16.4 us  [call(): pl.pallas_call(kernel, out_shape=shapes, in_specs=[near] * len(operands)...]
    ppermute x9, waiting for transfers between devices: 8.46 us -> 9.19 us  [swapped(): lax.ppermute(value, axis, [(i, i ^ 1 << apart) for i in range(lax.axis_si...]
  transfers between devices with their start and end apart: 9 -> 9, of which waited for: 7 -> 8; matrix products, arithmetic and copies ran while one was open for 0% -> 0% of each run, Pallas kernels for 26% -> 24%
where the time goes in v10:
time: 42.9 us; the launch traced here: 42.6 us
  starting transfers between devices  16.8 us (39%)
  Pallas kernels  16.4 us (38%)
  waiting for transfers between devices  9.19 us (21%)
    ppermute x9, starting transfers between devices, swapped(): lax.ppermute(value, axis, [(i, i ^ 1 << apart) for i in range(lax.axis_si...  16.8 us
    pallas_call x17, Pallas kernels, call(): pl.pallas_call(kernel, out_shape=shapes, in_specs=[near] * len(operands)...  16.4 us
    ppermute x9, waiting for transfers between devices, swapped(): lax.ppermute(value, axis, [(i, i ^ 1 << apart) for i in range(lax.axis_si...  9.19 us
  transfers between devices with their start and end apart: 9, of which 8 were waited for; matrix products, arithmetic and copies ran while one was open for 0% of the time, Pallas kernels for 24%

profile of v10, /device:TPU:0, one launch (start us, length us, event | category | flops | bytes accessed | tf_op | source)
XLA Modules:
  0.0 42.6 jit_solution(480335638543680179)
XLA Ops:
  0.0 2.0 %shard_map.82 = (bf16[1024,512]{1,0:T(8,128)(2,1)S(1)}, bf16[512,128]{1,0:T(8,128)(2,1)S(1)}, s32[1,1024]{1,0:T(1,128)S(1)}, s32[4,1,1024]{2,1,0:T(1,128)S(1)}, ...) custom-call(bf16[1024,512]{1,0:T(8,128)(2,1)} %scene_in.1, ...), custom_call_target="tpu_custom_call" | custom-call | flops 1000000 | bytes 10000 | tf_op jit(solution)/shard_map/pallas_call | solution.py:369
  2.0 0.5 %collective-permute-start = (bf16[512,128]{1,0:T(8,128)(2,1)S(1)}, bf16[512,128]{1,0:T(8,128)(2,1)S(1)}, u32[]{:S(2)}, u32[]{:S(2)}) collective-permute-start(bf16[512,128]{1,0:T(8,128)(2,1)S(1)} %get-tuple-element.40), channel_id=1, source_target_pairs={{0,1},{1,0},{2,3},{3,2},{4,5},{5,4},{6,7},{7,6},{8,9},{9,8},{10,11... | collective-permute-start | bytes 393224 | tf_op jit(solution)/shard_map/ppermute | solution.py:18
  2.6 0.7 %shard_map.83 = (s32[1,512]{1,0:T(1,128)S(1)}, f32[512,256]{1,0:T(8,128)S(1)}) custom-call(bf16[512,256]{1,0:T(8,128)(2,1)S(1)} %get-tuple-element.41.leafed_ref, s32[1,1024]{1,0:T(1,128)S(1)} %get-tuple-element.42.pixel_ref, s32[4,1,1024]{2,1,0:T(1,128)S(1)} %get-tuple-element.43.perm_ref, bf16[4,1,4,128,128]{4,3,2,1,0:T(8,128)(2,1)S(1)} %get-tuple-element.44.panel_ref), custom_call_target="tpu_custom_call" | custom-call | flops 1000000 | bytes 10000 | tf_op jit(solution)/shard_map/pallas_call | solution.py:369
  3.5 0.5 %shard_map.84 = (bf16[512,256]{1,0:T(8,128)(2,1)S(1)}, bf16[512,128]{1,0:T(8,128)(2,1)S(1)}) custom-call(bf16[512,128]{1,0:T(8,128)(2,1)S(1)} %collective-permute-done.arrived_ref, f32[512,256]{1,0:T(8,128)S(1)} %get-tuple-element.45.part_ref, bf16[4,1,4,128,128]{4,3,2,1,0:T(8,128)(2,1)S(1)} %get-tuple-element.44.panel_ref, ...), custom_call_target="tpu_custom_call" | custom-call | flops 1000000 | bytes 10000 | tf_op jit(solution)/shard_map/pallas_call | solution.py:369
  4.1 2.9 %collective-permute-start.1 = (bf16[512,128]{1,0:T(8,128)(2,1)S(1)}, bf16[512,128]{1,0:T(8,128)(2,1)S(1)}, u32[]{:S(2)}, u32[]{:S(2)}) collective-permute-start(bf16[512,128]{1,0:T(8,128)(2,1)S(1)} %get-tuple-element.46), channel_id=1, source_target_pairs={{0,2},{1,3},{2,0},{3,1},{4,6},{5,7},{6,4},{7,5},{8,10},{9,11},{10,... | collective-permute-start | bytes 393224 | tf_op jit(solution)/shard_map/ppermute | solution.py:18
  7.0 3.3 %shard_map.85 = (f32[512,256]{1,0:T(8,128)S(1)}, bf16[256,256]{1,0:T(8,128)(2,1)S(1)}, bf16[256,128]{1,0:T(8,128)(2,1)S(1)}, bf16[128,128]{1,0:T(8,128)(2,1)S(1)}, f32[512,256]{1,0:T(8,128)S(1)}) custom-call(bf16[512,256]{1,0:T(8,128)(2,1)S(1)} %get-tuple-element.47.coef_ref, s32[4,1,1024]{2,1,0:T(1,128)S(1)} %get-tuple-element.43.perm_ref, ...), custom_call_target="tpu_custom_call" | custom-call | flops 1000000 | bytes 10000 | tf_op jit(solution)/shard_map/pallas_call | solution.py:369
  10.3 0.5 %collective-permute-done.1.arrived_ref = bf16[512,128]{1,0:T(8,128)(2,1)S(1)} collective-permute-done((bf16[512,128]{1,0:T(8,128)(2,1)S(1)}, bf16[512,128]{1,0:T(8,128)(2,1)S(1)}, u32[]{:S(2)}, u32[]{:S(2)}) %collective-permute-start.1) | collective-permute-done | bytes 131104 | tf_op jit(solution)/shard_map/ppermute | solution.py:18
  10.8 0.5 %shard_map.86 = (bf16[512,256]{1,0:T(8,128)(2,1)S(1)}, bf16[512,128]{1,0:T(8,128)(2,1)S(1)}) custom-call(bf16[512,128]{1,0:T(8,128)(2,1)S(1)} %collective-permute-done.1.arrived_ref, f32[512,256]{1,0:T(8,128)S(1)} %get-tuple-element.48.part_ref, bf16[4,1,4,128,128]{4,3,2,1,0:T(8,128)(2,1)S(1)} %get-tuple-element.44.panel_ref, ...), custom_call_target="tpu_custom_call" | custom-call | flops 1000000 | bytes 10000 | tf_op jit(solution)/shard_map/pallas_call | solution.py:369
  11.3 1.9 %collective-permute-start.2 = (bf16[512,128]{1,0:T(8,128)(2,1)S(1)}, bf16[512,128]{1,0:T(8,128)(2,1)S(1)}, u32[]{:S(2)}, u32[]{:S(2)}) collective-permute-start(bf16[512,128]{1,0:T(8,128)(2,1)S(1)} %get-tuple-element.49), channel_id=1, source_target_pairs={{0,4},{1,5},{2,6},{3,7},{4,0},{5,1},{6,2},{7,3},{8,12},{9,13},{10,... | collective-permute-start | bytes 393224 | tf_op jit(solution)/shard_map/ppermute | solution.py:18
  13.2 2.6 %collective-permute-start.3 = (bf16[128,128]{1,0:T(8,128)(2,1)S(1)}, bf16[128,128]{1,0:T(8,128)(2,1)S(1)}, u32[]{:S(2)}, u32[]{:S(2)}) collective-permute-start(bf16[128,128]{1,0:T(8,128)(2,1)S(1)} %get-tuple-element.56), channel_id=1, source_target_pairs={{0,8},{1,9},{2,10},{3,11},{4,12},{5,13},{6,14},{7,15},{8,0},{9,1},... | collective-permute-start | bytes 98312 | tf_op jit(solution)/shard_map/ppermute | solution.py:18
  15.8 0.5 %shard_map.87.part_ref = f32[512,256]{1,0:T(8,128)S(1)} custom-call(bf16[512,256]{1,0:T(8,128)(2,1)S(1)} %get-tuple-element.50.coef_ref, s32[4,1,1024]{2,1,0:T(1,128)S(1)} %get-tuple-element.43.perm_ref, bf16[4,1,4,128,128]{4,3,2,1,0:T(8,128)(2,1)S(1)} %get-tuple-element.44.panel_ref), custom_call_target="tpu_custom_call" | custom-call | flops 1000000 | bytes 10000 | tf_op jit(solution)/shard_map/pallas_call | solution.py:369
  16.3 0.5 %collective-permute-done.2.arrived_ref = bf16[512,128]{1,0:T(8,128)(2,1)S(1)} collective-permute-done((bf16[512,128]{1,0:T(8,128)(2,1)S(1)}, bf16[512,128]{1,0:T(8,128)(2,1)S(1)}, u32[]{:S(2)}, u32[]{:S(2)}) %collective-permute-start.2) | collective-permute-done | bytes 131104 | tf_op jit(solution)/shard_map/ppermute | solution.py:18
  16.8 0.5 %shard_map.88 = (bf16[512,256]{1,0:T(8,128)(2,1)S(1)}, bf16[512,128]{1,0:T(8,128)(2,1)S(1)}) custom-call(bf16[512,128]{1,0:T(8,128)(2,1)S(1)} %collective-permute-done.2.arrived_ref, f32[512,256]{1,0:T(8,128)S(1)} %shard_map.87.part_ref, bf16[4,1,4,128,128]{4,3,2,1,0:T(8,128)(2,1)S(1)} %get-tuple-element.44.panel_ref, ...), custom_call_target="tpu_custom_call" | custom-call | flops 1000000 | bytes 10000 | tf_op jit(solution)/shard_map/pallas_call | solution.py:369
  17.3 2.6 %collective-permute-start.5 = (bf16[512,128]{1,0:T(8,128)(2,1)S(1)}, bf16[512,128]{1,0:T(8,128)(2,1)S(1)}, u32[]{:S(2)}, u32[]{:S(2)}) collective-permute-start(bf16[512,128]{1,0:T(8,128)(2,1)S(1)} %get-tuple-element.58.sent_ref), channel_id=1, source_target_pairs={{0,8},{1,9},{2,10},{3,11},{4,12},{5,13},{6,14},{7,15},{8,0},{9,1},... | collective-permute-start | bytes 393224 | tf_op jit(solution)/shard_map/ppermute | solution.py:18
  19.9 0.6 %shard_map.89 = (f32[512,128]{1,0:T(8,128)S(1)}, bf16[128,128]{1,0:T(8,128)(2,1)S(1)}, bf16[512,128]{1,0:T(8,128)(2,1)S(1)}, bf16[8,512,512]{2,1,0:T(8,128)(2,1)S(1)}, bf16[8,512,128]{2,1,0:T(8,128)(2,1)S(1)}) custom-call(bf16[512,256]{1,0:T(8,128)(2,1)S(1)} %get-tuple-element.51.coef_ref, s32[4,1,1024]{2,1,0:T(1,128)S(1)} %get-tuple-element.43.perm_ref, ...), custom_call_target="tpu_custom_call" | custom-call | flops 1000000 | bytes 10000 | tf_op jit(solution)/shard_map/pallas_call | solution.py:369
  20.5 0.8 %collective-permute-start.4 = (bf16[512,128]{1,0:T(8,128)(2,1)S(1)}, bf16[512,128]{1,0:T(8,128)(2,1)S(1)}, u32[]{:S(2)}, u32[]{:S(2)}) collective-permute-start(bf16[512,128]{1,0:T(8,128)(2,1)S(1)} %get-tuple-element.57), channel_id=1, source_target_pairs={{0,8},{1,9},{2,10},{3,11},{4,12},{5,13},{6,14},{7,15},{8,0},{9,1},... | collective-permute-start | bytes 393224 | tf_op jit(solution)/shard_map/ppermute | solution.py:18
  21.3 2.3 %shard_map.90 = (bf16[8,512,512]{2,1,0:T(8,128)(2,1)S(1)}, bf16[8,512,128]{2,1,0:T(8,128)(2,1)S(1)}, f32[512,128]{1,0:T(8,128)S(1)}) custom-call(s32[4,1,1024]{2,1,0:T(1,128)S(1)} %get-tuple-element.43.perm_ref, s32[1,512]{1,0:T(1,128)S(1)} %get-tuple-element.54.own_slots_ref, ...), custom_call_target="tpu_custom_call", output_to_operand_aliasing={{0}: (3, {}), {1}: (4, {})} | custom-call | flops 1000000 | bytes 10000 | tf_op jit(solution)/shard_map/pallas_call | solution.py:369
  23.6 1.2 %collective-permute-done.5.arrived_ref = bf16[512,128]{1,0:T(8,128)(2,1)S(1)} collective-permute-done((bf16[512,128]{1,0:T(8,128)(2,1)S(1)}, bf16[512,128]{1,0:T(8,128)(2,1)S(1)}, u32[]{:S(2)}, u32[]{:S(2)}) %collective-permute-start.5) | collective-permute-done | bytes 131104 | tf_op jit(solution)/shard_map/ppermute | solution.py:18
  24.9 0.6 %shard_map.91.placed_ref = bf16[512,256]{1,0:T(8,128)(2,1)S(1)} custom-call(bf16[512,128]{1,0:T(8,128)(2,1)S(1)} %collective-permute-done.5.arrived_ref, f32[512,128]{1,0:T(8,128)S(1)} %get-tuple-element.59.part_ref, bf16[256,128]{1,0:T(8,128)(2,1)S(1)} %get-tuple-element.60.map_ref, bf16[8,512,512]{2,1,0:T(8,128)(2,1)S(1)} %get-tuple-element.64.chosen_ref, ...), custom_call_target="tpu_custom_call" | custom-call | flops 1000000 | bytes 10000 | tf_op jit(solution)/shard_map/pallas_call | solution.py:369
  25.4 1.0 %collective-permute-done.4.arrived_ref = bf16[512,128]{1,0:T(8,128)(2,1)S(1)} collective-permute-done((bf16[512,128]{1,0:T(8,128)(2,1)S(1)}, bf16[512,128]{1,0:T(8,128)(2,1)S(1)}, u32[]{:S(2)}, u32[]{:S(2)}) %collective-permute-start.4) | collective-permute-done | bytes 131104 | tf_op jit(solution)/shard_map/ppermute | solution.py:18
  26.4 0.5 %shard_map.92 = (bf16[512,256]{1,0:T(8,128)(2,1)S(1)}, bf16[512,128]{1,0:T(8,128)(2,1)S(1)}) custom-call(bf16[512,128]{1,0:T(8,128)(2,1)S(1)} %collective-permute-done.4.arrived_ref, bf16[512,256]{1,0:T(8,128)(2,1)S(1)} %shard_map.91.placed_ref, bf16[8,512,512]{2,1,0:T(8,128)(2,1)S(1)} %get-tuple-element.64.chosen_ref, ...), custom_call_target="tpu_custom_call" | custom-call | flops 1000000 | bytes 10000 | tf_op jit(solution)/shard_map/pallas_call | solution.py:369
  26.9 2.0 %collective-permute-start.6 = (bf16[512,128]{1,0:T(8,128)(2,1)S(1)}, bf16[512,128]{1,0:T(8,128)(2,1)S(1)}, u32[]{:S(2)}, u32[]{:S(2)}) collective-permute-start(bf16[512,128]{1,0:T(8,128)(2,1)S(1)} %get-tuple-element.67), channel_id=1, source_target_pairs={{0,4},{1,5},{2,6},{3,7},{4,0},{5,1},{6,2},{7,3},{8,12},{9,13},{10,... | collective-permute-start | bytes 393224 | tf_op jit(solution)/shard_map/ppermute | solution.py:18
  28.9 0.6 %shard_map.93.placed_ref = bf16[512,256]{1,0:T(8,128)(2,1)S(1)} custom-call(bf16[512,256]{1,0:T(8,128)(2,1)S(1)} %get-tuple-element.68.coef_ref, bf16[4,1,4,128,128]{4,3,2,1,0:T(8,128)(2,1)S(1)} %get-tuple-element.44.panel_ref, bf16[8,512,512]{2,1,0:T(8,128)(2,1)S(1)} %get-tuple-element.64.chosen_ref, bf16[8,512,128]{2,1,0:T(8,128)(2,1)S(1)} %get-tuple-element.65.low_ref), custom_call_target="tpu_custom_call" | custom-call | flops 1000000 | bytes 10000 | tf_op jit(solution)/shard_map/pallas_call | solution.py:369
  29.5 2.4 %collective-permute-done.6.arrived_ref = bf16[512,128]{1,0:T(8,128)(2,1)S(1)} collective-permute-done((bf16[512,128]{1,0:T(8,128)(2,1)S(1)}, bf16[512,128]{1,0:T(8,128)(2,1)S(1)}, u32[]{:S(2)}, u32[]{:S(2)}) %collective-permute-start.6) | collective-permute-done | bytes 131104 | tf_op jit(solution)/shard_map/ppermute | solution.py:18
  32.0 0.5 %shard_map.94 = (bf16[512,256]{1,0:T(8,128)(2,1)S(1)}, bf16[512,128]{1,0:T(8,128)(2,1)S(1)}) custom-call(bf16[512,128]{1,0:T(8,128)(2,1)S(1)} %collective-permute-done.6.arrived_ref, bf16[512,256]{1,0:T(8,128)(2,1)S(1)} %shard_map.93.placed_ref, bf16[8,512,512]{2,1,0:T(8,128)(2,1)S(1)} %get-tuple-element.64.chosen_ref, ...), custom_call_target="tpu_custom_call" | custom-call | flops 1000000 | bytes 10000 | tf_op jit(solution)/shard_map/pallas_call | solution.py:369
  32.4 1.6 %collective-permute-start.7 = (bf16[512,128]{1,0:T(8,128)(2,1)S(1)}, bf16[512,128]{1,0:T(8,128)(2,1)S(1)}, u32[]{:S(2)}, u32[]{:S(2)}) collective-permute-start(bf16[512,128]{1,0:T(8,128)(2,1)S(1)} %get-tuple-element.69), channel_id=1, source_target_pairs={{0,2},{1,3},{2,0},{3,1},{4,6},{5,7},{6,4},{7,5},{8,10},{9,11},{10,... | collective-permute-start | bytes 393224 | tf_op jit(solution)/shard_map/ppermute | solution.py:18
  34.0 0.6 %shard_map.95.placed_ref = bf16[512,256]{1,0:T(8,128)(2,1)S(1)} custom-call(bf16[512,256]{1,0:T(8,128)(2,1)S(1)} %get-tuple-element.70.coef_ref, bf16[4,1,4,128,128]{4,3,2,1,0:T(8,128)(2,1)S(1)} %get-tuple-element.44.panel_ref, bf16[8,512,512]{2,1,0:T(8,128)(2,1)S(1)} %get-tuple-element.64.chosen_ref, bf16[8,512,128]{2,1,0:T(8,128)(2,1)S(1)} %get-tuple-element.65.low_ref), custom_call_target="tpu_custom_call" | custom-call | flops 1000000 | bytes 10000 | tf_op jit(solution)/shard_map/pallas_call | solution.py:369
  34.6 2.9 %collective-permute-done.7.arrived_ref = bf16[512,128]{1,0:T(8,128)(2,1)S(1)} collective-permute-done((bf16[512,128]{1,0:T(8,128)(2,1)S(1)}, bf16[512,128]{1,0:T(8,128)(2,1)S(1)}, u32[]{:S(2)}, u32[]{:S(2)}) %collective-permute-start.7) | collective-permute-done | bytes 131104 | tf_op jit(solution)/shard_map/ppermute | solution.py:18
  37.5 0.5 %shard_map.96 = (bf16[512,256]{1,0:T(8,128)(2,1)S(1)}, bf16[512,128]{1,0:T(8,128)(2,1)S(1)}) custom-call(bf16[512,128]{1,0:T(8,128)(2,1)S(1)} %collective-permute-done.7.arrived_ref, bf16[512,256]{1,0:T(8,128)(2,1)S(1)} %shard_map.95.placed_ref, bf16[8,512,512]{2,1,0:T(8,128)(2,1)S(1)} %get-tuple-element.64.chosen_ref, ...), custom_call_target="tpu_custom_call" | custom-call | flops 1000000 | bytes 10000 | tf_op jit(solution)/shard_map/pallas_call | solution.py:369
  38.0 1.9 %collective-permute-start.8 = (bf16[512,128]{1,0:T(8,128)(2,1)S(1)}, bf16[512,128]{1,0:T(8,128)(2,1)S(1)}, u32[]{:S(2)}, u32[]{:S(2)}) collective-permute-start(bf16[512,128]{1,0:T(8,128)(2,1)S(1)} %get-tuple-element.71), channel_id=1, source_target_pairs={{0,1},{1,0},{2,3},{3,2},{4,5},{5,4},{6,7},{7,6},{8,9},{9,8},{10,11... | collective-permute-start | bytes 393224 | tf_op jit(solution)/shard_map/ppermute | solution.py:18
  39.9 0.6 %shard_map.97.placed_ref = bf16[512,256]{1,0:T(8,128)(2,1)S(1)} custom-call(bf16[512,256]{1,0:T(8,128)(2,1)S(1)} %get-tuple-element.72.coef_ref, bf16[4,1,4,128,128]{4,3,2,1,0:T(8,128)(2,1)S(1)} %get-tuple-element.44.panel_ref, bf16[8,512,512]{2,1,0:T(8,128)(2,1)S(1)} %get-tuple-element.64.chosen_ref, bf16[8,512,128]{2,1,0:T(8,128)(2,1)S(1)} %get-tuple-element.65.low_ref), custom_call_target="tpu_custom_call" | custom-call | flops 1000000 | bytes 10000 | tf_op jit(solution)/shard_map/pallas_call | solution.py:369
  40.9 1.6 %shard_map.98 = bf16[1024,512]{1,0:T(8,128)(2,1)} custom-call(bf16[512,128]{1,0:T(8,128)(2,1)S(1)} %collective-permute-done.8.arrived_ref, bf16[512,256]{1,0:T(8,128)(2,1)S(1)} %shard_map.97.placed_ref, bf16[8,512,512]{2,1,0:T(8,128)(2,1)S(1)} %get-tuple-element.64.chosen_ref, bf16[8,512,128]{2,1,0:T(8,128)(2,1)S(1)} %get-tuple-element.65.low_ref, ...), custom_call_target="tpu_custom_call" | custom-call | flops 1000000 | bytes 10000 | tf_op jit(solution)/shard_map/pallas_call | solution.py:369
  (3 shorter events, 0.7 us)
Async XLA Ops:
  2.0 1.5 %collective-permute-start = (bf16[512,128]{1,0:T(8,128)(2,1)S(1)}, bf16[512,128]{1,0:T(8,128)(2,1)S(1)}, u32[]{:S(2)}, u32[]{:S(2)}) collective-permute-start(bf16[512,128]{1,0:T(8,128)(2,1)S(1)} %get-tuple-element.40), channel_id=1, source_target_pairs={{0,1},{1,0},{2,3},{3,2},{4,5},{5,4},{6,7},{7,6},{8,9},{9,8},{10,11... | collective-permute-start | bytes 393224 | tf_op jit(solution)/shard_map/ppermute | solution.py:18
  4.1 6.7 %collective-permute-start.1 = (bf16[512,128]{1,0:T(8,128)(2,1)S(1)}, bf16[512,128]{1,0:T(8,128)(2,1)S(1)}, u32[]{:S(2)}, u32[]{:S(2)}) collective-permute-start(bf16[512,128]{1,0:T(8,128)(2,1)S(1)} %get-tuple-element.46), channel_id=1, source_target_pairs={{0,2},{1,3},{2,0},{3,1},{4,6},{5,7},{6,4},{7,5},{8,10},{9,11},{10,... | collective-permute-start | bytes 393224 | tf_op jit(solution)/shard_map/ppermute | solution.py:18
  11.3 5.5 %collective-permute-start.2 = (bf16[512,128]{1,0:T(8,128)(2,1)S(1)}, bf16[512,128]{1,0:T(8,128)(2,1)S(1)}, u32[]{:S(2)}, u32[]{:S(2)}) collective-permute-start(bf16[512,128]{1,0:T(8,128)(2,1)S(1)} %get-tuple-element.49), channel_id=1, source_target_pairs={{0,4},{1,5},{2,6},{3,7},{4,0},{5,1},{6,2},{7,3},{8,12},{9,13},{10,... | collective-permute-start | bytes 393224 | tf_op jit(solution)/shard_map/ppermute | solution.py:18
  13.2 6.7 %collective-permute-start.3 = (bf16[128,128]{1,0:T(8,128)(2,1)S(1)}, bf16[128,128]{1,0:T(8,128)(2,1)S(1)}, u32[]{:S(2)}, u32[]{:S(2)}) collective-permute-start(bf16[128,128]{1,0:T(8,128)(2,1)S(1)} %get-tuple-element.56), channel_id=1, source_target_pairs={{0,8},{1,9},{2,10},{3,11},{4,12},{5,13},{6,14},{7,15},{8,0},{9,1},... | collective-permute-start | bytes 98312 | tf_op jit(solution)/shard_map/ppermute | solution.py:18
  17.3 7.6 %collective-permute-start.5 = (bf16[512,128]{1,0:T(8,128)(2,1)S(1)}, bf16[512,128]{1,0:T(8,128)(2,1)S(1)}, u32[]{:S(2)}, u32[]{:S(2)}) collective-permute-start(bf16[512,128]{1,0:T(8,128)(2,1)S(1)} %get-tuple-element.58.sent_ref), channel_id=1, source_target_pairs={{0,8},{1,9},{2,10},{3,11},{4,12},{5,13},{6,14},{7,15},{8,0},{9,1},... | collective-permute-start | bytes 393224 | tf_op jit(solution)/shard_map/ppermute | solution.py:18
  20.5 5.9 %collective-permute-start.4 = (bf16[512,128]{1,0:T(8,128)(2,1)S(1)}, bf16[512,128]{1,0:T(8,128)(2,1)S(1)}, u32[]{:S(2)}, u32[]{:S(2)}) collective-permute-start(bf16[512,128]{1,0:T(8,128)(2,1)S(1)} %get-tuple-element.57), channel_id=1, source_target_pairs={{0,8},{1,9},{2,10},{3,11},{4,12},{5,13},{6,14},{7,15},{8,0},{9,1},... | collective-permute-start | bytes 393224 | tf_op jit(solution)/shard_map/ppermute | solution.py:18
  26.9 5.0 %collective-permute-start.6 = (bf16[512,128]{1,0:T(8,128)(2,1)S(1)}, bf16[512,128]{1,0:T(8,128)(2,1)S(1)}, u32[]{:S(2)}, u32[]{:S(2)}) collective-permute-start(bf16[512,128]{1,0:T(8,128)(2,1)S(1)} %get-tuple-element.67), channel_id=1, source_target_pairs={{0,4},{1,5},{2,6},{3,7},{4,0},{5,1},{6,2},{7,3},{8,12},{9,13},{10,... | collective-permute-start | bytes 393224 | tf_op jit(solution)/shard_map/ppermute | solution.py:18
  32.4 5.0 %collective-permute-start.7 = (bf16[512,128]{1,0:T(8,128)(2,1)S(1)}, bf16[512,128]{1,0:T(8,128)(2,1)S(1)}, u32[]{:S(2)}, u32[]{:S(2)}) collective-permute-start(bf16[512,128]{1,0:T(8,128)(2,1)S(1)} %get-tuple-element.69), channel_id=1, source_target_pairs={{0,2},{1,3},{2,0},{3,1},{4,6},{5,7},{6,4},{7,5},{8,10},{9,11},{10,... | collective-permute-start | bytes 393224 | tf_op jit(solution)/shard_map/ppermute | solution.py:18
  38.0 2.9 %collective-permute-start.8 = (bf16[512,128]{1,0:T(8,128)(2,1)S(1)}, bf16[512,128]{1,0:T(8,128)(2,1)S(1)}, u32[]{:S(2)}, u32[]{:S(2)}) collective-permute-start(bf16[512,128]{1,0:T(8,128)(2,1)S(1)} %get-tuple-element.71), channel_id=1, source_target_pairs={{0,1},{1,0},{2,3},{3,2},{4,5},{5,4},{6,7},{7,6},{8,9},{9,8},{10,11... | collective-permute-start | bytes 393224 | tf_op jit(solution)/shard_map/ppermute | solution.py:18

commit v11 on v9

--- a/solution.py
+++ b/solution.py
@@ -190,13 +190,18 @@
         loads[2 + at].start()
     loads[0].wait()
     plan = place_plan(slots[...], half)
-    loads[1].wait()
+    if turns:
+        loads[1].wait()
+    else:
+        for load in loads[2:]:
+            load.wait()
     back = []
     for turn in turns or (range(scene_chunks),):
         for at in turn if turns and turn != turns[0] else ():
             loads[2 + at].start()
         for at in turn:
-            loads[2 + at].wait()
+            if turns:
+                loads[2 + at].wait()
             back.append(mul_t(echo[pl.ds(at * chunk, chunk)], leaf[...]).astype(thin))
     back_ref[...] = place(plan, jnp.concatenate(back, axis=0)).astype(thin)
 
@@ -216,14 +221,9 @@
     @pl.when(jnp.logical_not(early))
     def _():
         loads[1].start()
-        loads[1].wait()
 
     own_kernel(level, coef_ref, perm_ref, panel_ref, part_ref)
-
-    @pl.when(early)
-    def _():
-        echo_back(loads, echo, leaf, slots, back_ref, None)
-
+    loads[1].wait()
     gram = split(mul_t(leaf[...], leaf[...]))
     both = pair_weights(panel_ref, last)
     width = both.shape[0] // 2
@@ -233,6 +233,10 @@
     own_map_ref[...] = split(maps[:width])
     other_map_ref[...] = split(maps[width:, :width])
     sent_map_ref[...] = maps[width:, width:].astype(thin)
+
+    @pl.when(early)
+    def _():
+        echo_back(loads, echo, leaf, slots, back_ref, None)
 
 
 def mix(level, arrived_ref, part_ref, panel_ref):

time: 42.9 us -> 42.9 us (level)
  Pallas kernels: 17.2 us -> 16.6 us
  waiting for transfers between devices: 8.46 us -> 9 us
    pallas_call x17, Pallas kernels: 17.2 us -> 16.6 us  [call(): pl.pallas_call(kernel, out_shape=shapes, in_specs=[near] * len(operands)...]
    ppermute x9, waiting for transfers between devices: 8.46 us -> 9 us  [swapped(): lax.ppermute(value, axis, [(i, i ^ 1 << apart) for i in range(lax.axis_si...]
  transfers between devices with their start and end apart: 9 -> 9, of which waited for: 7 -> 8; matrix products, arithmetic and copies ran while one was open for 0% -> 0% of each run, Pallas kernels for 26% -> 25%
where the time goes in v11:
time: 42.9 us; the launch traced here: 42.6 us
  starting transfers between devices  16.8 us (39%)
  Pallas kernels  16.6 us (39%)
  waiting for transfers between devices  9 us (21%)
    ppermute x9, starting transfers between devices, swapped(): lax.ppermute(value, axis, [(i, i ^ 1 << apart) for i in range(lax.axis_si...  16.8 us
    pallas_call x17, Pallas kernels, call(): pl.pallas_call(kernel, out_shape=shapes, in_specs=[near] * len(operands)...  16.6 us
    ppermute x9, waiting for transfers between devices, swapped(): lax.ppermute(value, axis, [(i, i ^ 1 << apart) for i in range(lax.axis_si...  9 us
  transfers between devices with their start and end apart: 9, of which 8 were waited for; matrix products, arithmetic and copies ran while one was open for 0% of the time, Pallas kernels for 25%

profile of v11, /device:TPU:0, one launch (start us, length us, event | category | flops | bytes accessed | tf_op | source)
XLA Modules:
  0.0 42.6 jit_solution(1057842946783937069)
XLA Ops:
  0.0 2.0 %shard_map.82 = (bf16[1024,512]{1,0:T(8,128)(2,1)S(1)}, bf16[512,128]{1,0:T(8,128)(2,1)S(1)}, s32[1,1024]{1,0:T(1,128)S(1)}, s32[4,1,1024]{2,1,0:T(1,128)S(1)}, ...) custom-call(bf16[1024,512]{1,0:T(8,128)(2,1)} %scene_in.1, ...), custom_call_target="tpu_custom_call" | custom-call | flops 1000000 | bytes 10000 | tf_op jit(solution)/shard_map/pallas_call | solution.py:377
  2.0 0.5 %collective-permute-start = (bf16[512,128]{1,0:T(8,128)(2,1)S(1)}, bf16[512,128]{1,0:T(8,128)(2,1)S(1)}, u32[]{:S(2)}, u32[]{:S(2)}) collective-permute-start(bf16[512,128]{1,0:T(8,128)(2,1)S(1)} %get-tuple-element.42), channel_id=1, source_target_pairs={{0,1},{1,0},{2,3},{3,2},{4,5},{5,4},{6,7},{7,6},{8,9},{9,8},{10,11... | collective-permute-start | bytes 393224 | tf_op jit(solution)/shard_map/ppermute | solution.py:18
  2.6 0.7 %shard_map.83 = (s32[1,512]{1,0:T(1,128)S(1)}, f32[512,256]{1,0:T(8,128)S(1)}) custom-call(bf16[512,256]{1,0:T(8,128)(2,1)S(1)} %get-tuple-element.43.leafed_ref, s32[1,1024]{1,0:T(1,128)S(1)} %get-tuple-element.44.pixel_ref, s32[4,1,1024]{2,1,0:T(1,128)S(1)} %get-tuple-element.45.perm_ref, bf16[4,1,4,128,128]{4,3,2,1,0:T(8,128)(2,1)S(1)} %get-tuple-element.46.panel_ref), custom_call_target="tpu_custom_call" | custom-call | flops 1000000 | bytes 10000 | tf_op jit(solution)/shard_map/pallas_call | solution.py:377
  3.5 0.5 %shard_map.84 = (bf16[512,256]{1,0:T(8,128)(2,1)S(1)}, bf16[512,128]{1,0:T(8,128)(2,1)S(1)}) custom-call(bf16[512,128]{1,0:T(8,128)(2,1)S(1)} %collective-permute-done.arrived_ref, f32[512,256]{1,0:T(8,128)S(1)} %get-tuple-element.47.part_ref, bf16[4,1,4,128,128]{4,3,2,1,0:T(8,128)(2,1)S(1)} %get-tuple-element.46.panel_ref, ...), custom_call_target="tpu_custom_call" | custom-call | flops 1000000 | bytes 10000 | tf_op jit(solution)/shard_map/pallas_call | solution.py:377
  4.1 2.9 %collective-permute-start.1 = (bf16[512,128]{1,0:T(8,128)(2,1)S(1)}, bf16[512,128]{1,0:T(8,128)(2,1)S(1)}, u32[]{:S(2)}, u32[]{:S(2)}) collective-permute-start(bf16[512,128]{1,0:T(8,128)(2,1)S(1)} %get-tuple-element.48), channel_id=1, source_target_pairs={{0,2},{1,3},{2,0},{3,1},{4,6},{5,7},{6,4},{7,5},{8,10},{9,11},{10,... | collective-permute-start | bytes 393224 | tf_op jit(solution)/shard_map/ppermute | solution.py:18
  7.0 3.3 %shard_map.85 = (f32[512,256]{1,0:T(8,128)S(1)}, bf16[256,256]{1,0:T(8,128)(2,1)S(1)}, bf16[256,128]{1,0:T(8,128)(2,1)S(1)}, bf16[128,128]{1,0:T(8,128)(2,1)S(1)}, bf16[512,256]{1,0:T(8,128)(2,1)S(1)}) custom-call(bf16[512,256]{1,0:T(8,128)(2,1)S(1)} %get-tuple-element.49.coef_ref, s32[4,1,1024]{2,1,0:T(1,128)S(1)} %get-tuple-element.45.perm_ref, ...), custom_call_target="tpu_custom_call" | custom-call | flops 1000000 | bytes 10000 | tf_op jit(solution)/shard_map/pallas_call | solution.py:377
  10.3 0.5 %collective-permute-done.1.arrived_ref = bf16[512,128]{1,0:T(8,128)(2,1)S(1)} collective-permute-done((bf16[512,128]{1,0:T(8,128)(2,1)S(1)}, bf16[512,128]{1,0:T(8,128)(2,1)S(1)}, u32[]{:S(2)}, u32[]{:S(2)}) %collective-permute-start.1) | collective-permute-done | bytes 131104 | tf_op jit(solution)/shard_map/ppermute | solution.py:18
  10.8 0.5 %shard_map.86 = (bf16[512,256]{1,0:T(8,128)(2,1)S(1)}, bf16[512,128]{1,0:T(8,128)(2,1)S(1)}) custom-call(bf16[512,128]{1,0:T(8,128)(2,1)S(1)} %collective-permute-done.1.arrived_ref, f32[512,256]{1,0:T(8,128)S(1)} %get-tuple-element.50.part_ref, bf16[4,1,4,128,128]{4,3,2,1,0:T(8,128)(2,1)S(1)} %get-tuple-element.46.panel_ref, ...), custom_call_target="tpu_custom_call" | custom-call | flops 1000000 | bytes 10000 | tf_op jit(solution)/shard_map/pallas_call | solution.py:377
  11.3 1.9 %collective-permute-start.2 = (bf16[512,128]{1,0:T(8,128)(2,1)S(1)}, bf16[512,128]{1,0:T(8,128)(2,1)S(1)}, u32[]{:S(2)}, u32[]{:S(2)}) collective-permute-start(bf16[512,128]{1,0:T(8,128)(2,1)S(1)} %get-tuple-element.51), channel_id=1, source_target_pairs={{0,4},{1,5},{2,6},{3,7},{4,0},{5,1},{6,2},{7,3},{8,12},{9,13},{10,... | collective-permute-start | bytes 393224 | tf_op jit(solution)/shard_map/ppermute | solution.py:18
  13.2 2.6 %collective-permute-start.3 = (bf16[128,128]{1,0:T(8,128)(2,1)S(1)}, bf16[128,128]{1,0:T(8,128)(2,1)S(1)}, u32[]{:S(2)}, u32[]{:S(2)}) collective-permute-start(bf16[128,128]{1,0:T(8,128)(2,1)S(1)} %get-tuple-element.60), channel_id=1, source_target_pairs={{0,8},{1,9},{2,10},{3,11},{4,12},{5,13},{6,14},{7,15},{8,0},{9,1},... | collective-permute-start | bytes 98312 | tf_op jit(solution)/shard_map/ppermute | solution.py:18
  15.8 0.8 %shard_map.87 = (f32[512,256]{1,0:T(8,128)S(1)}, f32[512,256]{1,0:T(8,128)S(1)}) custom-call(bf16[512,256]{1,0:T(8,128)(2,1)S(1)} %get-tuple-element.52.coef_ref, s32[4,1,1024]{2,1,0:T(1,128)S(1)} %get-tuple-element.45.perm_ref, bf16[4,1,4,128,128]{4,3,2,1,0:T(8,128)(2,1)S(1)} %get-tuple-element.46.panel_ref, bf16[512,256]{1,0:T(8,128)(2,1)S(1)} %get-tuple-element.53.back_ref), custom_call_target="tpu_custom_call" | custom-call | flops 1000000 | bytes 10000 | tf_op jit(solution)/shard_map/pallas_call | solution.py:377
  16.8 0.5 %shard_map.88 = (bf16[512,256]{1,0:T(8,128)(2,1)S(1)}, bf16[512,128]{1,0:T(8,128)(2,1)S(1)}) custom-call(bf16[512,128]{1,0:T(8,128)(2,1)S(1)} %collective-permute-done.2.arrived_ref, f32[512,256]{1,0:T(8,128)S(1)} %get-tuple-element.54.part_ref, bf16[4,1,4,128,128]{4,3,2,1,0:T(8,128)(2,1)S(1)} %get-tuple-element.46.panel_ref, ...), custom_call_target="tpu_custom_call" | custom-call | flops 1000000 | bytes 10000 | tf_op jit(solution)/shard_map/pallas_call | solution.py:377
  17.3 2.6 %collective-permute-start.5 = (bf16[512,128]{1,0:T(8,128)(2,1)S(1)}, bf16[512,128]{1,0:T(8,128)(2,1)S(1)}, u32[]{:S(2)}, u32[]{:S(2)}) collective-permute-start(bf16[512,128]{1,0:T(8,128)(2,1)S(1)} %get-tuple-element.62.sent_ref), channel_id=1, source_target_pairs={{0,8},{1,9},{2,10},{3,11},{4,12},{5,13},{6,14},{7,15},{8,0},{9,1},... | collective-permute-start | bytes 393224 | tf_op jit(solution)/shard_map/ppermute | solution.py:18
  19.9 0.6 %shard_map.89 = (f32[512,128]{1,0:T(8,128)S(1)}, bf16[128,128]{1,0:T(8,128)(2,1)S(1)}, bf16[512,128]{1,0:T(8,128)(2,1)S(1)}, bf16[8,512,512]{2,1,0:T(8,128)(2,1)S(1)}, bf16[8,512,128]{2,1,0:T(8,128)(2,1)S(1)}) custom-call(bf16[512,256]{1,0:T(8,128)(2,1)S(1)} %get-tuple-element.55.coef_ref, s32[4,1,1024]{2,1,0:T(1,128)S(1)} %get-tuple-element.45.perm_ref, ...), custom_call_target="tpu_custom_call" | custom-call | flops 1000000 | bytes 10000 | tf_op jit(solution)/shard_map/pallas_call | solution.py:377
  20.5 0.8 %collective-permute-start.4 = (bf16[512,128]{1,0:T(8,128)(2,1)S(1)}, bf16[512,128]{1,0:T(8,128)(2,1)S(1)}, u32[]{:S(2)}, u32[]{:S(2)}) collective-permute-start(bf16[512,128]{1,0:T(8,128)(2,1)S(1)} %get-tuple-element.61), channel_id=1, source_target_pairs={{0,8},{1,9},{2,10},{3,11},{4,12},{5,13},{6,14},{7,15},{8,0},{9,1},... | collective-permute-start | bytes 393224 | tf_op jit(solution)/shard_map/ppermute | solution.py:18
  21.3 2.3 %shard_map.90 = (bf16[8,512,512]{2,1,0:T(8,128)(2,1)S(1)}, bf16[8,512,128]{2,1,0:T(8,128)(2,1)S(1)}, f32[512,128]{1,0:T(8,128)S(1)}) custom-call(s32[4,1,1024]{2,1,0:T(1,128)S(1)} %get-tuple-element.45.perm_ref, s32[1,512]{1,0:T(1,128)S(1)} %get-tuple-element.58.own_slots_ref, ...), custom_call_target="tpu_custom_call", output_to_operand_aliasing={{0}: (3, {}), {1}: (4, {})} | custom-call | flops 1000000 | bytes 10000 | tf_op jit(solution)/shard_map/pallas_call | solution.py:377
  23.6 1.2 %collective-permute-done.5.arrived_ref = bf16[512,128]{1,0:T(8,128)(2,1)S(1)} collective-permute-done((bf16[512,128]{1,0:T(8,128)(2,1)S(1)}, bf16[512,128]{1,0:T(8,128)(2,1)S(1)}, u32[]{:S(2)}, u32[]{:S(2)}) %collective-permute-start.5) | collective-permute-done | bytes 131104 | tf_op jit(solution)/shard_map/ppermute | solution.py:18
  24.9 0.6 %shard_map.91.placed_ref = bf16[512,256]{1,0:T(8,128)(2,1)S(1)} custom-call(bf16[512,128]{1,0:T(8,128)(2,1)S(1)} %collective-permute-done.5.arrived_ref, f32[512,128]{1,0:T(8,128)S(1)} %get-tuple-element.63.part_ref, bf16[256,128]{1,0:T(8,128)(2,1)S(1)} %get-tuple-element.64.map_ref, bf16[8,512,512]{2,1,0:T(8,128)(2,1)S(1)} %get-tuple-element.68.chosen_ref, ...), custom_call_target="tpu_custom_call" | custom-call | flops 1000000 | bytes 10000 | tf_op jit(solution)/shard_map/pallas_call | solution.py:377
  25.4 1.0 %collective-permute-done.4.arrived_ref = bf16[512,128]{1,0:T(8,128)(2,1)S(1)} collective-permute-done((bf16[512,128]{1,0:T(8,128)(2,1)S(1)}, bf16[512,128]{1,0:T(8,128)(2,1)S(1)}, u32[]{:S(2)}, u32[]{:S(2)}) %collective-permute-start.4) | collective-permute-done | bytes 131104 | tf_op jit(solution)/shard_map/ppermute | solution.py:18
  26.4 0.5 %shard_map.92 = (bf16[512,256]{1,0:T(8,128)(2,1)S(1)}, bf16[512,128]{1,0:T(8,128)(2,1)S(1)}) custom-call(bf16[512,128]{1,0:T(8,128)(2,1)S(1)} %collective-permute-done.4.arrived_ref, bf16[512,256]{1,0:T(8,128)(2,1)S(1)} %shard_map.91.placed_ref, bf16[8,512,512]{2,1,0:T(8,128)(2,1)S(1)} %get-tuple-element.68.chosen_ref, ...), custom_call_target="tpu_custom_call" | custom-call | flops 1000000 | bytes 10000 | tf_op jit(solution)/shard_map/pallas_call | solution.py:377
  26.9 2.0 %collective-permute-start.6 = (bf16[512,128]{1,0:T(8,128)(2,1)S(1)}, bf16[512,128]{1,0:T(8,128)(2,1)S(1)}, u32[]{:S(2)}, u32[]{:S(2)}) collective-permute-start(bf16[512,128]{1,0:T(8,128)(2,1)S(1)} %get-tuple-element.71), channel_id=1, source_target_pairs={{0,4},{1,5},{2,6},{3,7},{4,0},{5,1},{6,2},{7,3},{8,12},{9,13},{10,... | collective-permute-start | bytes 393224 | tf_op jit(solution)/shard_map/ppermute | solution.py:18
  28.9 0.6 %shard_map.93.placed_ref = bf16[512,256]{1,0:T(8,128)(2,1)S(1)} custom-call(bf16[512,256]{1,0:T(8,128)(2,1)S(1)} %get-tuple-element.72.coef_ref, bf16[4,1,4,128,128]{4,3,2,1,0:T(8,128)(2,1)S(1)} %get-tuple-element.46.panel_ref, bf16[8,512,512]{2,1,0:T(8,128)(2,1)S(1)} %get-tuple-element.68.chosen_ref, bf16[8,512,128]{2,1,0:T(8,128)(2,1)S(1)} %get-tuple-element.69.low_ref), custom_call_target="tpu_custom_call" | custom-call | flops 1000000 | bytes 10000 | tf_op jit(solution)/shard_map/pallas_call | solution.py:377
  29.5 2.4 %collective-permute-done.6.arrived_ref = bf16[512,128]{1,0:T(8,128)(2,1)S(1)} collective-permute-done((bf16[512,128]{1,0:T(8,128)(2,1)S(1)}, bf16[512,128]{1,0:T(8,128)(2,1)S(1)}, u32[]{:S(2)}, u32[]{:S(2)}) %collective-permute-start.6) | collective-permute-done | bytes 131104 | tf_op jit(solution)/shard_map/ppermute | solution.py:18
  32.0 0.5 %shard_map.94 = (bf16[512,256]{1,0:T(8,128)(2,1)S(1)}, bf16[512,128]{1,0:T(8,128)(2,1)S(1)}) custom-call(bf16[512,128]{1,0:T(8,128)(2,1)S(1)} %collective-permute-done.6.arrived_ref, bf16[512,256]{1,0:T(8,128)(2,1)S(1)} %shard_map.93.placed_ref, bf16[8,512,512]{2,1,0:T(8,128)(2,1)S(1)} %get-tuple-element.68.chosen_ref, ...), custom_call_target="tpu_custom_call" | custom-call | flops 1000000 | bytes 10000 | tf_op jit(solution)/shard_map/pallas_call | solution.py:377
  32.4 1.6 %collective-permute-start.7 = (bf16[512,128]{1,0:T(8,128)(2,1)S(1)}, bf16[512,128]{1,0:T(8,128)(2,1)S(1)}, u32[]{:S(2)}, u32[]{:S(2)}) collective-permute-start(bf16[512,128]{1,0:T(8,128)(2,1)S(1)} %get-tuple-element.73), channel_id=1, source_target_pairs={{0,2},{1,3},{2,0},{3,1},{4,6},{5,7},{6,4},{7,5},{8,10},{9,11},{10,... | collective-permute-start | bytes 393224 | tf_op jit(solution)/shard_map/ppermute | solution.py:18
  34.0 0.6 %shard_map.95.placed_ref = bf16[512,256]{1,0:T(8,128)(2,1)S(1)} custom-call(bf16[512,256]{1,0:T(8,128)(2,1)S(1)} %get-tuple-element.74.coef_ref, bf16[4,1,4,128,128]{4,3,2,1,0:T(8,128)(2,1)S(1)} %get-tuple-element.46.panel_ref, bf16[8,512,512]{2,1,0:T(8,128)(2,1)S(1)} %get-tuple-element.68.chosen_ref, bf16[8,512,128]{2,1,0:T(8,128)(2,1)S(1)} %get-tuple-element.69.low_ref), custom_call_target="tpu_custom_call" | custom-call | flops 1000000 | bytes 10000 | tf_op jit(solution)/shard_map/pallas_call | solution.py:377
  34.6 2.9 %collective-permute-done.7.arrived_ref = bf16[512,128]{1,0:T(8,128)(2,1)S(1)} collective-permute-done((bf16[512,128]{1,0:T(8,128)(2,1)S(1)}, bf16[512,128]{1,0:T(8,128)(2,1)S(1)}, u32[]{:S(2)}, u32[]{:S(2)}) %collective-permute-start.7) | collective-permute-done | bytes 131104 | tf_op jit(solution)/shard_map/ppermute | solution.py:18
  37.5 0.5 %shard_map.96 = (bf16[512,256]{1,0:T(8,128)(2,1)S(1)}, bf16[512,128]{1,0:T(8,128)(2,1)S(1)}) custom-call(bf16[512,128]{1,0:T(8,128)(2,1)S(1)} %collective-permute-done.7.arrived_ref, bf16[512,256]{1,0:T(8,128)(2,1)S(1)} %shard_map.95.placed_ref, bf16[8,512,512]{2,1,0:T(8,128)(2,1)S(1)} %get-tuple-element.68.chosen_ref, ...), custom_call_target="tpu_custom_call" | custom-call | flops 1000000 | bytes 10000 | tf_op jit(solution)/shard_map/pallas_call | solution.py:377
  38.0 1.9 %collective-permute-start.8 = (bf16[512,128]{1,0:T(8,128)(2,1)S(1)}, bf16[512,128]{1,0:T(8,128)(2,1)S(1)}, u32[]{:S(2)}, u32[]{:S(2)}) collective-permute-start(bf16[512,128]{1,0:T(8,128)(2,1)S(1)} %get-tuple-element.75), channel_id=1, source_target_pairs={{0,1},{1,0},{2,3},{3,2},{4,5},{5,4},{6,7},{7,6},{8,9},{9,8},{10,11... | collective-permute-start | bytes 393224 | tf_op jit(solution)/shard_map/ppermute | solution.py:18
  39.9 0.6 %shard_map.97.placed_ref = bf16[512,256]{1,0:T(8,128)(2,1)S(1)} custom-call(bf16[512,256]{1,0:T(8,128)(2,1)S(1)} %get-tuple-element.76.coef_ref, bf16[4,1,4,128,128]{4,3,2,1,0:T(8,128)(2,1)S(1)} %get-tuple-element.46.panel_ref, bf16[8,512,512]{2,1,0:T(8,128)(2,1)S(1)} %get-tuple-element.68.chosen_ref, bf16[8,512,128]{2,1,0:T(8,128)(2,1)S(1)} %get-tuple-element.69.low_ref), custom_call_target="tpu_custom_call" | custom-call | flops 1000000 | bytes 10000 | tf_op jit(solution)/shard_map/pallas_call | solution.py:377
  40.5 0.4 collective-permute-done.8.arrived_ref
  40.9 1.6 %shard_map.98 = bf16[1024,512]{1,0:T(8,128)(2,1)} custom-call(bf16[512,128]{1,0:T(8,128)(2,1)S(1)} %collective-permute-done.8.arrived_ref, bf16[512,256]{1,0:T(8,128)(2,1)S(1)} %shard_map.97.placed_ref, bf16[8,512,512]{2,1,0:T(8,128)(2,1)S(1)} %get-tuple-element.68.chosen_ref, bf16[8,512,128]{2,1,0:T(8,128)(2,1)S(1)} %get-tuple-element.69.low_ref, ...), custom_call_target="tpu_custom_call" | custom-call | flops 1000000 | bytes 10000 | tf_op jit(solution)/shard_map/pallas_call | solution.py:377
  (3 shorter events, 0.5 us)
Async XLA Ops:
  2.0 1.5 %collective-permute-start = (bf16[512,128]{1,0:T(8,128)(2,1)S(1)}, bf16[512,128]{1,0:T(8,128)(2,1)S(1)}, u32[]{:S(2)}, u32[]{:S(2)}) collective-permute-start(bf16[512,128]{1,0:T(8,128)(2,1)S(1)} %get-tuple-element.42), channel_id=1, source_target_pairs={{0,1},{1,0},{2,3},{3,2},{4,5},{5,4},{6,7},{7,6},{8,9},{9,8},{10,11... | collective-permute-start | bytes 393224 | tf_op jit(solution)/shard_map/ppermute | solution.py:18
  4.1 6.7 %collective-permute-start.1 = (bf16[512,128]{1,0:T(8,128)(2,1)S(1)}, bf16[512,128]{1,0:T(8,128)(2,1)S(1)}, u32[]{:S(2)}, u32[]{:S(2)}) collective-permute-start(bf16[512,128]{1,0:T(8,128)(2,1)S(1)} %get-tuple-element.48), channel_id=1, source_target_pairs={{0,2},{1,3},{2,0},{3,1},{4,6},{5,7},{6,4},{7,5},{8,10},{9,11},{10,... | collective-permute-start | bytes 393224 | tf_op jit(solution)/shard_map/ppermute | solution.py:18
  11.3 5.5 %collective-permute-start.2 = (bf16[512,128]{1,0:T(8,128)(2,1)S(1)}, bf16[512,128]{1,0:T(8,128)(2,1)S(1)}, u32[]{:S(2)}, u32[]{:S(2)}) collective-permute-start(bf16[512,128]{1,0:T(8,128)(2,1)S(1)} %get-tuple-element.51), channel_id=1, source_target_pairs={{0,4},{1,5},{2,6},{3,7},{4,0},{5,1},{6,2},{7,3},{8,12},{9,13},{10,... | collective-permute-start | bytes 393224 | tf_op jit(solution)/shard_map/ppermute | solution.py:18
  13.2 6.7 %collective-permute-start.3 = (bf16[128,128]{1,0:T(8,128)(2,1)S(1)}, bf16[128,128]{1,0:T(8,128)(2,1)S(1)}, u32[]{:S(2)}, u32[]{:S(2)}) collective-permute-start(bf16[128,128]{1,0:T(8,128)(2,1)S(1)} %get-tuple-element.60), channel_id=1, source_target_pairs={{0,8},{1,9},{2,10},{3,11},{4,12},{5,13},{6,14},{7,15},{8,0},{9,1},... | collective-permute-start | bytes 98312 | tf_op jit(solution)/shard_map/ppermute | solution.py:18
  17.3 7.6 %collective-permute-start.5 = (bf16[512,128]{1,0:T(8,128)(2,1)S(1)}, bf16[512,128]{1,0:T(8,128)(2,1)S(1)}, u32[]{:S(2)}, u32[]{:S(2)}) collective-permute-start(bf16[512,128]{1,0:T(8,128)(2,1)S(1)} %get-tuple-element.62.sent_ref), channel_id=1, source_target_pairs={{0,8},{1,9},{2,10},{3,11},{4,12},{5,13},{6,14},{7,15},{8,0},{9,1},... | collective-permute-start | bytes 393224 | tf_op jit(solution)/shard_map/ppermute | solution.py:18
  20.5 5.9 %collective-permute-start.4 = (bf16[512,128]{1,0:T(8,128)(2,1)S(1)}, bf16[512,128]{1,0:T(8,128)(2,1)S(1)}, u32[]{:S(2)}, u32[]{:S(2)}) collective-permute-start(bf16[512,128]{1,0:T(8,128)(2,1)S(1)} %get-tuple-element.61), channel_id=1, source_target_pairs={{0,8},{1,9},{2,10},{3,11},{4,12},{5,13},{6,14},{7,15},{8,0},{9,1},... | collective-permute-start | bytes 393224 | tf_op jit(solution)/shard_map/ppermute | solution.py:18
  26.9 5.0 %collective-permute-start.6 = (bf16[512,128]{1,0:T(8,128)(2,1)S(1)}, bf16[512,128]{1,0:T(8,128)(2,1)S(1)}, u32[]{:S(2)}, u32[]{:S(2)}) collective-permute-start(bf16[512,128]{1,0:T(8,128)(2,1)S(1)} %get-tuple-element.71), channel_id=1, source_target_pairs={{0,4},{1,5},{2,6},{3,7},{4,0},{5,1},{6,2},{7,3},{8,12},{9,13},{10,... | collective-permute-start | bytes 393224 | tf_op jit(solution)/shard_map/ppermute | solution.py:18
  32.4 5.0 %collective-permute-start.7 = (bf16[512,128]{1,0:T(8,128)(2,1)S(1)}, bf16[512,128]{1,0:T(8,128)(2,1)S(1)}, u32[]{:S(2)}, u32[]{:S(2)}) collective-permute-start(bf16[512,128]{1,0:T(8,128)(2,1)S(1)} %get-tuple-element.73), channel_id=1, source_target_pairs={{0,2},{1,3},{2,0},{3,1},{4,6},{5,7},{6,4},{7,5},{8,10},{9,11},{10,... | collective-permute-start | bytes 393224 | tf_op jit(solution)/shard_map/ppermute | solution.py:18
  38.0 2.9 %collective-permute-start.8 = (bf16[512,128]{1,0:T(8,128)(2,1)S(1)}, bf16[512,128]{1,0:T(8,128)(2,1)S(1)}, u32[]{:S(2)}, u32[]{:S(2)}) collective-permute-start(bf16[512,128]{1,0:T(8,128)(2,1)S(1)} %get-tuple-element.75), channel_id=1, source_target_pairs={{0,1},{1,0},{2,3},{3,2},{4,5},{5,4},{6,7},{7,6},{8,9},{9,8},{10,11... | collective-permute-start | bytes 393224 | tf_op jit(solution)/shard_map/ppermute | solution.py:18
